TPU v7x, 32 devices: a whole 2x2x4 slice. The times are simulated.
32 devices in a mesh: row: 2 (over x), col: 16 (over z, y, core).
Axes of the slice: x: 2, y: 2, z: 4, core: 2. Of those that a mesh axis runs over, the one named last changes fastest.
Arguments:
- amplitudes: bfloat16 [2048, 65536], P('row', 'col'), may hold values from -6 to 6
- residual_in: bfloat16 [2048, 65536], P('row', 'col'), may hold values from -6 to 6
- cholesky: bfloat16 [65536, 1280], P('col', 'row'), may hold values from -0.0625 to 0.0625
Outputs:
- residual_out: bfloat16 [2048, 65536], P('row', 'col')
All inputs are finite; a program needn't handle non-finite values.
Results may differ from a plain program's by a relative error of at most 0.004.
Values may be sent and summed in bfloat16 or wider, within the bound.
No kernel may reach another device: no remote copies, remote signals or barrier semaphores. Data moves between devices by JAX's collectives and lax.ppermute only.
A program may use at most 128 MiB of HBM per device.

v0:
```python
import jax
import jax.numpy as jnp
from jax import lax
from jax.sharding import PartitionSpec as P


def project_back(chi_block, vectors):
    return lax.dot_general(
        chi_block, vectors, (((1,), (1,)), ((), ())), preferred_element_type=jnp.float32
    )


def body(amplitudes, residual_in, cholesky):
    full_panel = lax.all_gather(cholesky, "row", axis=1, tiled=True)
    partial_value = jnp.dot(amplitudes, full_panel, preferred_element_type=jnp.float32)
    chi = lax.psum(partial_value, "col").astype(jnp.bfloat16)
    update = project_back(chi, full_panel)
    return (residual_in.astype(jnp.float32) + update).astype(jnp.bfloat16)


def solution(mesh):
    in_specs = (P("row", "col"), P("row", "col"), P("col", "row"))
    out_specs = P("row", "col")
    return jax.shard_map(body, mesh=mesh, in_specs=in_specs, out_specs=out_specs, check_vma=False)
```

profile of v0, /device:TPU:0, one launch (start us, length us, event | category | flops | bytes accessed | tf_op | source)
XLA Modules:
  0.0 299.9 jit_solution(10045682270345817966)
XLA Ops:
  6.5 0.0 all-gather.2.cloned.1.call-start
  6.5 0.7 all-gather.2.cloned.1.call-update
  7.3 133.9 %all-gather.2.cloned.1.call-done = bf16[4096,1280]{1,0:T(8,128)(2,1)} async-done(((bf16[4096,640]{1,0:T(8,128)(2,1)}), bf16[4096,1280]{1,0:T(8,128)(2,1)}) %all-gather.2.cloned.1.call-update) | async-done | bytes 10485776 | tf_op jit(solution)/shard_map/all_gather | solution.py:14
  141.1 17.9 %fusion.1 = f32[1024,1280]{1,0:T(8,128)} fusion(bf16[1024,4096]{1,0:T(8,128)(2,1)} %param.3, bf16[4096,1280]{1,0:T(8,128)(2,1)} %all-gather.2.cloned.1.call-done), kind=kOutput, calls=%fused_computation.2 | convolution fusion | flops 10737418240 | bytes 24117248 | tf_op jit(solution)/shard_map/dot_general | solution.py:15
  159.0 116.1 %all-reduce.1 = bf16[1024,1280]{1,0:T(8,128)(2,1)S(1)} all-reduce(f32[1024,1280]{1,0:T(8,128)} %fusion.1), channel_id=1, replica_groups=mesh['row'=2,'col'=16] {'col'}, use_global_device_ids=true, to_apply=%region_0.0 | all-reduce | flops 1310720 | bytes 7864320 | tf_op jit(solution)/shard_map/psum | solution.py:16
  275.1 18.0 %add_convert_fusion = bf16[1024,4096]{1,0:T(8,128)(2,1)} fusion(bf16[1024,4096]{1,0:T(8,128)(2,1)} %param.4, bf16[4096,1280]{1,0:T(8,128)(2,1)} %all-gather.2.cloned.1.call-done, bf16[1024,1280]{1,0:T(8,128)(2,1)S(1)} %all-reduce.1), kind=kOutput, calls=%fused_computation | convolution fusion | flops 10750001152 | bytes 29884416 | tf_op jit(solution)/shard_map/dot_general | solution.py:8
Async XLA Ops:
  6.5 134.6 %all-gather.2.cloned.1.call-start = ((), (), s32[]{:S(2)}) async-start(), calls=%async_computation | async-start | bytes 15728640 | tf_op jit(solution)/shard_map/all_gather | solution.py:14
Sparse Core Ops, SparseCore 0:
  8.9 132.1 all-gather.1
where the time goes:
time: 302 us; the launch traced here: 300 us
  waiting for transfers between devices  135 us (45%)
  blocking collectives  116 us (38%)
  matrix products  35.8 us (12%)
  between operations  13.4 us (4%)
    all_gather x1, waiting for transfers between devices, body(): full_panel = lax.all_gather(cholesky, 'row', axis=1, tiled=True)  134 us
    psum x1, blocking collectives, body(): chi = lax.psum(partial_value, 'col').astype(jnp.bfloat16)  116 us
    dot_general x1, matrix products, project_back(): lax.dot_general(chi_block, vectors, (((1,), (1,)), ((), ())), preferred_e...  18 us
    dot_general x1, matrix products, body(): jnp.dot(amplitudes, full_panel, preferred_element_type=jnp.float32)  17.9 us
  transfers between devices with their start and end apart: 1, of which 1 were waited for; matrix products, arithmetic and copies ran while one was open for 0% of the time, Pallas kernels for 0%

commit v1 on v0

v1 whole, which is shorter than its diff:
```python
import jax
import jax.numpy as jnp
from jax import lax
from jax.experimental import pallas as pl
from jax.experimental.layout import Layout, with_layout_constraint
from jax.experimental.pallas import tpu as pltpu
from jax.sharding import PartitionSpec as P

GROUPS = (128, 256, 256)
VMEM_BYTES = 30 * 1024 * 1024


def after(value, *others):
    return lax.optimization_barrier((value, *others))[0]


def block_of(extent, target):
    while extent % target:
        target //= 2
    return target


def project(amplitudes, vectors):
    part = jnp.dot(amplitudes, vectors, preferred_element_type=jnp.float32)
    return with_layout_constraint(part, Layout(major_to_minor=(0, 1)))


def project_back(base, groups, kind):
    rows, columns = base.shape
    block = block_of(columns, 1024)
    chis = [chi for chi, _ in groups]
    pieces = [piece for _, members in groups for piece in members]

    def kernel(base_ref, *refs):
        left = jnp.concatenate([c[...] for c in refs[: len(chis)]], axis=1)
        right = jnp.concatenate([p[...] for p in refs[len(chis) : -1]], axis=1)
        term = lax.dot_general(left, right, (((1,), (1,)), ((), ())), preferred_element_type=jnp.float32)
        refs[-1][...] = (base_ref[...].astype(jnp.float32) + term).astype(kind)

    return pl.pallas_call(
        kernel,
        grid=(columns // block,),
        in_specs=[pl.BlockSpec((rows, block), lambda i: (0, i))]
        + [pl.BlockSpec(chi.shape, lambda i: (0, 0), pipeline_mode=pl.Buffered(1)) for chi in chis]
        + [pl.BlockSpec((block, piece.shape[1]), lambda i: (i, 0)) for piece in pieces],
        out_specs=pl.BlockSpec((rows, block), lambda i: (0, i)),
        out_shape=jax.ShapeDtypeStruct(base.shape, kind),
        compiler_params=pltpu.CompilerParams(vmem_limit_bytes=VMEM_BYTES),
        cost_estimate=pl.CostEstimate(flops=0, bytes_accessed=0, transcendentals=0),
    )(base, *chis, *pieces)


def solution(mesh):
    rows, cols = mesh.shape["row"], mesh.shape["col"]
    bits = [1 << k for k in range(cols.bit_length() - 1)]

    def exchange(value, bit):
        return lax.ppermute(value, "col", [(i, i ^ bit) for i in range(cols)])

    def body(amplitudes, residual_in, cholesky):
        me = lax.axis_index("col")
        upper = [(me & bit) != 0 for bit in bits]
        once = 1 + (me >> 20)

        def boxed(run, *values):
            shapes = jax.eval_shape(run, *values)
            zeros = jax.tree.map(lambda s: jnp.zeros(s.shape, s.dtype), shapes)
            return lax.while_loop(lambda s: s[0] < once, lambda s: (s[0] + 1, run(*values)), (jnp.int32(0), zeros))[1]

        def halve(value, step, narrow):
            half = value.shape[0] // 2
            low, high = value[:half], value[half:]
            send = jnp.where(upper[step], low, high)
            got = exchange(send.astype(narrow) if step else send, bits[step])
            return jnp.where(upper[step], high, low) + got.astype(jnp.float32)

        def double(value, step):
            up = upper[step]
            got = exchange(value, bits[step])
            return jnp.concatenate([jnp.where(up, got, value), jnp.where(up, value, got)])

        steps = range(len(bits))

        def scatter(value, narrow=jnp.float32):
            for step in steps:
                value = halve(value, step, narrow)
            return value.astype(jnp.bfloat16)

        def gather(value):
            for step in steps[::-1]:
                value = double(value, step)
            return value

        def send_row(vectors, shift):
            return lax.ppermute(vectors, "row", [(i, (i + shift) % rows) for i in range(rows)])

        if rows != 2 or len(bits) != 4 or sum(GROUPS) != cholesky.shape[1]:
            rest = jnp.concatenate([send_row(cholesky, shift) for shift in range(1, rows)], axis=1)
            chi = gather(scatter(project(amplitudes, cholesky)))
            total = project_back(residual_in, [(chi, [cholesky])], jnp.float32)
            rest = after(rest, total)
            return project_back(total, [(gather(scatter(project(amplitudes, rest))), [rest])], jnp.bfloat16)

        ends = [sum(GROUPS[: k + 1]) for k in range(len(GROUPS))]
        out_a, out_b, out_c = [cholesky[:, end - size : end] for end, size in zip(ends, GROUPS)]
        a = send_row(out_a, 1)
        part_own = project(amplitudes, after(cholesky, out_a))
        own = lax.psum_scatter(part_own, "col", scatter_dimension=0, tiled=True).astype(jnp.bfloat16)
        b = send_row(after(out_b, part_own), 1)
        part_a = project(amplitudes, after(a, part_own))
        chi_a = boxed(lambda v: gather(scatter(v)), part_a)
        c = send_row(after(out_c, chi_a), 1)
        part_b = project(amplitudes, after(b, chi_a))
        own = after(own, part_b)
        chi_own = lax.all_gather(own, "col", axis=0, tiled=True)
        chi_b = boxed(lambda v: gather(scatter(v)), after(part_b, own))
        chi_c = gather(scatter(project(amplitudes, after(c, chi_b, chi_own)), jnp.bfloat16))
        groups = [(chi_own, [cholesky]), (chi_a, [a]), (chi_b, [b]), (chi_c, [c])]
        return project_back(residual_in, groups, jnp.bfloat16)

    in_specs = (P("row", "col"), P("row", "col"), P("col", "row"))
    return jax.shard_map(body, mesh=mesh, in_specs=in_specs, out_specs=P("row", "col"), check_vma=False)
```

time: 302 us -> 235 us (0.78)
  blocking collectives: 116 us -> 0 us
  starting transfers between devices: 0.01 us -> 41.7 us
  waiting for transfers between devices: 135 us -> 114 us
  Pallas kernels: 0 us -> 14.5 us
  other arithmetic: 0 us -> 10.7 us
  local copies, waits for them, and re-layouts: 0 us -> 8.44 us
  matrix products: 35.8 us -> 31.7 us
    all_gather x1, waiting for transfers between devices: 134 us -> 0.01 us  [body(): chi_own = lax.all_gather(own, 'col', axis=0, tiled=True)]
    psum x1 -> x0, blocking collectives: 116 us -> none  [body(): chi = lax.psum(partial_value, 'col').astype(jnp.bfloat16)]
    ppermute x0 -> x27, waiting for transfers between devices: none -> 114 us  [the longest x24 67.9 us: exchange(): return lax.ppermute(value, 'col', [(i, i ^ bit) for i in range(cols)])]
    ppermute x0 -> x27, starting transfers between devices: none -> 41.5 us  [the longest x24 37 us: exchange(): return lax.ppermute(value, 'col', [(i, i ^ bit) for i in range(cols)])]
    pallas_call x0 -> x1, Pallas kernels: none -> 14.5 us  [project_back(): pl.pallas_call(kernel, grid=(columns // block,), in_specs=[pl.BlockSpec((...]
    slice x0 -> x2, local copies, waits for them, and re-layouts: none -> 6.78 us  [body(): cholesky[:, end - size:end]]
    dot_general x2 -> x4, matrix products: 35.8 us -> 31.7 us  [project(): part = jnp.dot(amplitudes, vectors, preferred_element_type=jnp.float32)]
    select_n x0 -> x21, other arithmetic: none -> 3.91 us  [the longest x9 2.5 us: halve(): send = jnp.where(upper[step], low, high)]
  transfers between devices with their start and end apart: 1 -> 29, of which waited for: 1 -> 26; matrix products, arithmetic and copies ran while one was open for 0% -> 18% of each run, Pallas kernels for 0% -> 0%
where the time goes in v1:
time: 235 us
  waiting for transfers between devices  114 us (49%)
  starting transfers between devices  41.7 us (18%)
  matrix products  31.7 us (13%)
  Pallas kernels  14.5 us (6%)
  between operations  13.6 us (6%)
  other arithmetic  10.7 us (5%)
  local copies, waits for them, and re-layouts  8.44 us (4%)
    ppermute x24, waiting for transfers between devices, exchange(): return lax.ppermute(value, 'col', [(i, i ^ bit) for i in range(cols)])  67.9 us
    ppermute x3, waiting for transfers between devices, send_row(): lax.ppermute(vectors, 'row', [(i, (i + shift) % rows) for i in range(rows)])  46 us
    ppermute x24, starting transfers between devices, exchange(): return lax.ppermute(value, 'col', [(i, i ^ bit) for i in range(cols)])  37 us
    dot_general x4, matrix products, project(): part = jnp.dot(amplitudes, vectors, preferred_element_type=jnp.float32)  31.7 us
    pallas_call x1, Pallas kernels, project_back(): pl.pallas_call(kernel, grid=(columns // block,), in_specs=[pl.BlockSpec((...  14.5 us
    slice x2, local copies, waits for them, and re-layouts, body(): cholesky[:, end - size:end]  6.78 us
  transfers between devices with their start and end apart: 29, of which 26 were waited for; matrix products, arithmetic and copies ran while one was open for 18% of the time, Pallas kernels for 0%

profile of v1, /device:TPU:0, one launch (start us, length us, event | category | flops | bytes accessed | tf_op | source)
XLA Modules:
  0.0 234.6 jit_solution(13224456657216653118)
XLA Ops:
  6.5 2.3 slice.81
  8.8 2.9 %collective-permute-start.17 = (bf16[4096,128]{1,0:T(8,128)(2,1)}, bf16[4096,128]{1,0:T(8,128)(2,1)S(1)}, u32[]{:S(2)}, u32[]{:S(2)}) collective-permute-start(bf16[4096,128]{1,0:T(8,128)(2,1)} %slice.81), channel_id=1, source_target_pairs={{0,16},{16,0},{1,17},{17,1},{2,18},{18,2},{3,19},{19,3},{4,20},{20... | collective-permute-start | bytes 3145736 | tf_op jit(solution)/shard_map/ppermute | solution.py:95
  11.8 11.6 %convolution_bitcast_fusion = f32[1024,640]{1,0:T(8,128)} fusion(bf16[1024,4096]{1,0:T(8,128)(2,1)} %param.7, bf16[4096,640]{1,0:T(8,128)(2,1)} %refs_4_.1), kind=kOutput, calls=%fused_computation.40 | convolution fusion | flops 5368709120 | bytes 16252928 | tf_op jit(solution)/shard_map/dot_general | solution.py:24
  23.7 4.5 %fusion = (bf16[4096,256]{1,0:T(8,128)(2,1)}, bf16[4096,256]{1,0:T(8,128)(2,1)}) fusion(bf16[4096,640]{1,0:T(8,128)(2,1)} %refs_4_.1), kind=kLoop, calls=%fused_computation.64 | loop fusion | bytes 8388608 | tf_op jit(solution)/shard_map/slice | solution.py:105
  28.2 7.8 %collective-permute-done.17.refs_5_ = bf16[4096,128]{1,0:T(8,128)(2,1)S(1)} collective-permute-done((bf16[4096,128]{1,0:T(8,128)(2,1)}, bf16[4096,128]{1,0:T(8,128)(2,1)S(1)}, u32[]{:S(2)}, u32[]{:S(2)}) %collective-permute-start.17) | collective-permute-done | bytes 1048608 | tf_op jit(solution)/shard_map/ppermute | solution.py:95
  36.0 6.8 %convolution_bitcast_fusion.3 = f32[1024,128]{1,0:T(8,128)} fusion(bf16[1024,4096]{1,0:T(8,128)(2,1)} %param.7, bf16[4096,128]{1,0:T(8,128)(2,1)S(1)} %collective-permute-done.17.refs_5_), kind=kOutput, calls=%fused_computation.43 | convolution fusion | flops 1073741824 | bytes 9961472 | tf_op jit(solution)/shard_map/dot_general | solution.py:24
  42.8 0.8 broadcast_in_dim.6
  43.6 38.5 %while.20 = (s32[]{:T(128)}, bf16[1024,128]{1,0:T(8,128)(2,1)}, s32[]{:T(128)}, pred[]{:T(512)}, pred[]{:T(512)}, /*index=5*/pred[]{:T(512)}, pred[]{:T(512)}, f32[1024,128]{1,0:T(8,128)}, s32[]{:T(128)}) while((s32[]{:T(128)}, bf16[1024,128]{1,0:T(8,128)(2,1)}, s32[]{:T(128)}, pred[]{:T(512)}, pred[]{:T(512)}, /*index=5*/pred[]{:T(512)}, ...), condition=%wide.region_2.3_spmd, body=%wide.region_1.2_spmd.sunk | while | flops 2064386 | bytes 8339881 | solution.py:68
  43.6 1.1 slice_select_fusion.17
  44.7 1.5 collective-permute-done
  46.2 1.1 select_add_fusion.13
  47.3 2.2 collective-permute-start.1
  49.5 4.2 %collective-permute-done.1 = f32[256,128]{1,0:T(8,128)S(1)} collective-permute-done((f32[256,128]{1,0:T(8,128)S(1)}, f32[256,128]{1,0:T(8,128)S(1)}, u32[]{:S(2)}, u32[]{:S(2)}) %collective-permute-start.1) | collective-permute-done | bytes 131104 | tf_op jit(solution)/shard_map/while/body/ppermute | solution.py:58
  53.7 1.5 collective-permute-start.2
  55.2 4.1 %collective-permute-done.2 = f32[128,128]{1,0:T(8,128)S(1)} collective-permute-done((f32[128,128]{1,0:T(8,128)S(1)}, f32[128,128]{1,0:T(8,128)S(1)}, u32[]{:S(2)}, u32[]{:S(2)}) %collective-permute-start.2) | collective-permute-done | bytes 65568 | tf_op jit(solution)/shard_map/while/body/ppermute | solution.py:58
  59.3 2.6 %collective-permute-start.3 = (f32[64,128]{1,0:T(8,128)S(1)}, f32[64,128]{1,0:T(8,128)S(1)}, u32[]{:S(2)}, u32[]{:S(2)}) collective-permute-start(f32[64,128]{1,0:T(8,128)S(1)} %slice_select_fusion.20), channel_id=1, source_target_pairs={{0,8},{1,9},{2,10},{3,11},{4,12},{5,13},{6,14},{7,15},{8,0},{9,1},... | collective-permute-start | bytes 98312 | tf_op jit(solution)/shard_map/while/body/ppermute | solution.py:58
  61.9 3.5 %collective-permute-done.3 = f32[64,128]{1,0:T(8,128)S(1)} collective-permute-done((f32[64,128]{1,0:T(8,128)S(1)}, f32[64,128]{1,0:T(8,128)S(1)}, u32[]{:S(2)}, u32[]{:S(2)}) %collective-permute-start.3) | collective-permute-done | bytes 32800 | tf_op jit(solution)/shard_map/while/body/ppermute | solution.py:58
  65.4 1.9 collective-permute-start.4
  67.3 2.8 %collective-permute-done.4 = bf16[64,128]{1,0:T(8,128)(2,1)S(1)} collective-permute-done((bf16[64,128]{1,0:T(8,128)(2,1)S(1)}, bf16[64,128]{1,0:T(8,128)(2,1)S(1)}, u32[]{:S(2)}, u32[]{:S(2)}) %collective-permute-start.4) | collective-permute-done | bytes 16416 | tf_op jit(solution)/shard_map/while/body/ppermute | solution.py:58
  70.2 1.5 collective-permute-start.5
  71.7 2.5 %collective-permute-done.5 = bf16[128,128]{1,0:T(8,128)(2,1)S(1)} collective-permute-done((bf16[128,128]{1,0:T(8,128)(2,1)S(1)}, bf16[128,128]{1,0:T(8,128)(2,1)S(1)}, u32[]{:S(2)}, u32[]{:S(2)}) %collective-permute-start.5) | collective-permute-done | bytes 32800 | tf_op jit(solution)/shard_map/while/body/ppermute | solution.py:58
  74.2 2.4 %collective-permute-start.6 = (bf16[256,128]{1,0:T(8,128)(2,1)S(1)}, bf16[256,128]{1,0:T(8,128)(2,1)S(1)}, u32[]{:S(2)}, u32[]{:S(2)}) collective-permute-start(bf16[256,128]{1,0:T(8,128)(2,1)S(1)} %pad_maximum_fusion.21), channel_id=1, source_target_pairs={{0,2},{1,3},{2,0},{3,1},{4,6},{5,7},{6,4},{7,5},{8,10},{9,11},{10,... | collective-permute-start | bytes 196616 | tf_op jit(solution)/shard_map/while/body/ppermute | solution.py:58
  76.6 3.1 %collective-permute-done.6 = bf16[256,128]{1,0:T(8,128)(2,1)S(1)} collective-permute-done((bf16[256,128]{1,0:T(8,128)(2,1)S(1)}, bf16[256,128]{1,0:T(8,128)(2,1)S(1)}, u32[]{:S(2)}, u32[]{:S(2)}) %collective-permute-start.6) | collective-permute-done | bytes 65568 | tf_op jit(solution)/shard_map/while/body/ppermute | solution.py:58
  79.9 1.3 collective-permute-done.7
  82.1 1.5 collective-permute-start.18
  83.6 6.7 %convolution_bitcast_fusion.2 = f32[1024,256]{1,0:T(8,128)} fusion(bf16[1024,4096]{1,0:T(8,128)(2,1)} %param.7, bf16[4096,256]{1,0:T(8,128)(2,1)S(1)} %collective-permute-done.16.refs_6_), kind=kOutput, calls=%fused_computation.42 | convolution fusion | flops 2147483648 | bytes 11534336 | tf_op jit(solution)/shard_map/dot_general | solution.py:24
  90.3 1.6 convert_element_type.30
  91.9 38.2 %collective-permute-done.18.refs_7_ = bf16[4096,256]{1,0:T(8,128)(2,1)} collective-permute-done((bf16[4096,256]{1,0:T(8,128)(2,1)}, bf16[4096,256]{1,0:T(8,128)(2,1)}, u32[]{:S(2)}, u32[]{:S(2)}) %collective-permute-start.18) | collective-permute-done | bytes 2097184 | tf_op jit(solution)/shard_map/ppermute | solution.py:95
  130.1 0.8 broadcast_in_dim.7
  130.9 42.3 %while.21 = (s32[]{:T(128)}, bf16[1024,256]{1,0:T(8,128)(2,1)}, s32[]{:T(128)}, pred[]{:T(512)}, pred[]{:T(512)}, /*index=5*/pred[]{:T(512)}, pred[]{:T(512)}, f32[1024,256]{1,0:T(8,128)}, s32[]{:T(128)}) while((s32[]{:T(128)}, bf16[1024,256]{1,0:T(8,128)(2,1)}, s32[]{:T(128)}, pred[]{:T(512)}, pred[]{:T(512)}, /*index=5*/pred[]{:T(512)}, ...), condition=%wide.region_4.5_spmd, body=%wide.region_3.4_spmd.sunk | while | flops 4128770 | bytes 16679337 | solution.py:68
  130.9 1.3 slice_select_fusion.21
  132.2 1.9 collective-permute-done.8
  134.1 1.3 select_add_fusion.16
  135.5 1.2 collective-permute-start.9
  136.7 7.2 %collective-permute-done.9 = f32[256,256]{1,0:T(8,128)S(1)} collective-permute-done((f32[256,256]{1,0:T(8,128)S(1)}, f32[256,256]{1,0:T(8,128)S(1)}, u32[]{:S(2)}, u32[]{:S(2)}) %collective-permute-start.9) | collective-permute-done | bytes 262176 | tf_op jit(solution)/shard_map/while/body/ppermute | solution.py:58
  144.0 1.6 collective-permute-start.10
  145.6 3.4 %collective-permute-done.10 = f32[128,256]{1,0:T(8,128)S(1)} collective-permute-done((f32[128,256]{1,0:T(8,128)S(1)}, f32[128,256]{1,0:T(8,128)S(1)}, u32[]{:S(2)}, u32[]{:S(2)}) %collective-permute-start.10) | collective-permute-done | bytes 131104 | tf_op jit(solution)/shard_map/while/body/ppermute | solution.py:58
  149.0 2.7 %collective-permute-start.11 = (f32[64,256]{1,0:T(8,128)S(1)}, f32[64,256]{1,0:T(8,128)S(1)}, u32[]{:S(2)}, u32[]{:S(2)}) collective-permute-start(f32[64,256]{1,0:T(8,128)S(1)} %slice_select_fusion.24), channel_id=1, source_target_pairs={{0,8},{1,9},{2,10},{3,11},{4,12},{5,13},{6,14},{7,15},{8,0},{9,1},... | collective-permute-start | bytes 196616 | tf_op jit(solution)/shard_map/while/body/ppermute | solution.py:58
  151.8 2.5 %collective-permute-done.11 = f32[64,256]{1,0:T(8,128)S(1)} collective-permute-done((f32[64,256]{1,0:T(8,128)S(1)}, f32[64,256]{1,0:T(8,128)S(1)}, u32[]{:S(2)}, u32[]{:S(2)}) %collective-permute-start.11) | collective-permute-done | bytes 65568 | tf_op jit(solution)/shard_map/while/body/ppermute | solution.py:58
  154.3 2.8 %collective-permute-start.12 = (bf16[64,256]{1,0:T(8,128)(2,1)S(1)}, bf16[64,256]{1,0:T(8,128)(2,1)S(1)}, u32[]{:S(2)}, u32[]{:S(2)}) collective-permute-start(bf16[64,256]{1,0:T(8,128)(2,1)S(1)} %add_convert_fusion.6), channel_id=1, source_target_pairs={{0,8},{1,9},{2,10},{3,11},{4,12},{5,13},{6,14},{7,15},{8,0},{9,1},... | collective-permute-start | bytes 98312 | tf_op jit(solution)/shard_map/while/body/ppermute | solution.py:58
  157.1 2.1 collective-permute-done.12
  159.2 1.9 collective-permute-start.13
  161.2 2.4 %collective-permute-done.13 = bf16[128,256]{1,0:T(8,128)(2,1)S(1)} collective-permute-done((bf16[128,256]{1,0:T(8,128)(2,1)S(1)}, bf16[128,256]{1,0:T(8,128)(2,1)S(1)}, u32[]{:S(2)}, u32[]{:S(2)}) %collective-permute-start.13) | collective-permute-done | bytes 65568 | tf_op jit(solution)/shard_map/while/body/ppermute | solution.py:58
  163.6 1.4 collective-permute-start.14
  165.0 3.7 %collective-permute-done.14 = bf16[256,256]{1,0:T(8,128)(2,1)S(1)} collective-permute-done((bf16[256,256]{1,0:T(8,128)(2,1)S(1)}, bf16[256,256]{1,0:T(8,128)(2,1)S(1)}, u32[]{:S(2)}, u32[]{:S(2)}) %collective-permute-start.14) | collective-permute-done | bytes 131104 | tf_op jit(solution)/shard_map/while/body/ppermute | solution.py:58
  169.4 1.9 collective-permute-done.15
  171.3 1.0 broadcast_select_fusion.39
  172.3 0.8 pad_maximum_fusion.27
  173.2 6.5 %convolution_bitcast_fusion.1 = f32[1024,256]{1,0:T(8,128)S(1)} fusion(bf16[1024,4096]{1,0:T(8,128)(2,1)} %param.7, bf16[4096,256]{1,0:T(8,128)(2,1)} %collective-permute-done.18.refs_7_), kind=kOutput, calls=%fused_computation.41 | convolution fusion | flops 2147483648 | bytes 11534336 | tf_op jit(solution)/shard_map/dot_general | solution.py:24
  180.0 1.8 collective-permute-done.19
  181.9 1.4 collective-permute-start.20
  183.2 4.2 %collective-permute-done.20 = bf16[256,256]{1,0:T(8,128)(2,1)S(1)} collective-permute-done((bf16[256,256]{1,0:T(8,128)(2,1)S(1)}, bf16[256,256]{1,0:T(8,128)(2,1)S(1)}, u32[]{:S(2)}, u32[]{:S(2)}) %collective-permute-start.20) | collective-permute-done | bytes 131104 | tf_op jit(solution)/shard_map/ppermute | solution.py:58
  187.6 1.9 collective-permute-start.21
  189.5 2.4 %collective-permute-done.21 = bf16[128,256]{1,0:T(8,128)(2,1)S(1)} collective-permute-done((bf16[128,256]{1,0:T(8,128)(2,1)S(1)}, bf16[128,256]{1,0:T(8,128)(2,1)S(1)}, u32[]{:S(2)}, u32[]{:S(2)}) %collective-permute-start.21) | collective-permute-done | bytes 65568 | tf_op jit(solution)/shard_map/ppermute | solution.py:58
  191.9 3.1 %collective-permute-start.22 = (bf16[64,256]{1,0:T(8,128)(2,1)S(1)}, bf16[64,256]{1,0:T(8,128)(2,1)S(1)}, u32[]{:S(2)}, u32[]{:S(2)}) collective-permute-start(bf16[64,256]{1,0:T(8,128)(2,1)S(1)} %select_convert_fusion.2), channel_id=1, source_target_pairs={{0,8},{1,9},{2,10},{3,11},{4,12},{5,13},{6,14},{7,15},{8,0},{9,1},... | collective-permute-start | bytes 98312 | tf_op jit(solution)/shard_map/ppermute | solution.py:58
  195.0 1.9 collective-permute-done.22
  196.9 3.0 %collective-permute-start.23 = (bf16[64,256]{1,0:T(8,128)(2,1)S(1)}, bf16[64,256]{1,0:T(8,128)(2,1)S(1)}, u32[]{:S(2)}, u32[]{:S(2)}) collective-permute-start(bf16[64,256]{1,0:T(8,128)(2,1)S(1)} %add_convert_fusion.2), channel_id=1, source_target_pairs={{0,8},{1,9},{2,10},{3,11},{4,12},{5,13},{6,14},{7,15},{8,0},{9,1},... | collective-permute-start | bytes 98312 | tf_op jit(solution)/shard_map/ppermute | solution.py:58
  199.9 2.0 collective-permute-done.23
  202.0 2.1 collective-permute-start.24
  204.1 2.2 collective-permute-done.24
  206.4 1.4 collective-permute-start.25
  207.8 3.6 %collective-permute-done.25 = bf16[256,256]{1,0:T(8,128)(2,1)S(1)} collective-permute-done((bf16[256,256]{1,0:T(8,128)(2,1)S(1)}, bf16[256,256]{1,0:T(8,128)(2,1)S(1)}, u32[]{:S(2)}, u32[]{:S(2)}) %collective-permute-start.25) | collective-permute-done | bytes 131104 | tf_op jit(solution)/shard_map/ppermute | solution.py:58
  211.5 1.5 collective-permute-done.26
  213.3 14.5 %shard_map.37 = bf16[1024,4096]{1,0:T(8,128)(2,1)} custom-call(bf16[1024,4096]{1,0:T(8,128)(2,1)S(1)} %bitcast.19, bf16[1024,640]{1,0:T(8,128)(2,1)S(1)} %copy-done, bf16[1024,128]{1,0:T(8,128)(2,1)S(1)} %copy-done.2, bf16[1024,256]{1,0:T(8,128)(2,1)S(1)} %copy-done.1, bf16[1024,256]{1,0:T(8,128)(2,1)S(1)} %pad_maximum_fusion.8.refs_3_, ...), custom_call_target="tpu_custom_call" | custom-call | tf_op jit(solution)/shard_map/pallas_call | solution.py:40
  (72 shorter events, 3.3 us)
Async XLA Ops:
  6.5 83.8 %reduce-scatter.2.cloned.1.call-start = ((), (), s32[]{:S(2)}) async-start(), calls=%async_computation.1 | async-start | bytes 2785280 | tf_op jit(solution)/shard_map/reduce_scatter | solution.py:108
  8.8 27.1 %collective-permute-start.17 = (bf16[4096,128]{1,0:T(8,128)(2,1)}, bf16[4096,128]{1,0:T(8,128)(2,1)S(1)}, u32[]{:S(2)}, u32[]{:S(2)}) collective-permute-start(bf16[4096,128]{1,0:T(8,128)(2,1)} %slice.81), channel_id=1, source_target_pairs={{0,16},{16,0},{1,17},{17,1},{2,18},{18,2},{3,19},{19,3},{4,20},{20... | collective-permute-start | bytes 3145736 | tf_op jit(solution)/shard_map/ppermute | solution.py:95
  23.4 149.7 %all-gather.2.cloned.1.call-start = ((), (), s32[]{:S(2)}) async-start(), calls=%async_computation.2 | async-start | bytes 1392640 | tf_op jit(solution)/shard_map/all_gather | solution.py:115
  28.2 55.4 %collective-permute-start.16 = (bf16[4096,256]{1,0:T(8,128)(2,1)}, bf16[4096,256]{1,0:T(8,128)(2,1)S(1)}, u32[]{:S(2)}, u32[]{:S(2)}) collective-permute-start(bf16[4096,256]{1,0:T(8,128)(2,1)} %get-tuple-element.98), channel_id=1, source_target_pairs={{0,16},{16,0},{1,17},{17,1},{2,18},{18,2},{3,19},{19,3},{4,20},{20... | collective-permute-start | bytes 6291464 | tf_op jit(solution)/shard_map/ppermute | solution.py:95
  44.6 1.6 collective-permute-start
  47.3 6.3 %collective-permute-start.1 = (f32[256,128]{1,0:T(8,128)S(1)}, f32[256,128]{1,0:T(8,128)S(1)}, u32[]{:S(2)}, u32[]{:S(2)}) collective-permute-start(f32[256,128]{1,0:T(8,128)S(1)} %slice_select_fusion.18), channel_id=1, source_target_pairs={{0,2},{1,3},{2,0},{3,1},{4,6},{5,7},{6,4},{7,5},{8,10},{9,11},{10,... | collective-permute-start | bytes 393224 | tf_op jit(solution)/shard_map/while/body/ppermute | solution.py:58
  53.7 5.6 %collective-permute-start.2 = (f32[128,128]{1,0:T(8,128)S(1)}, f32[128,128]{1,0:T(8,128)S(1)}, u32[]{:S(2)}, u32[]{:S(2)}) collective-permute-start(f32[128,128]{1,0:T(8,128)S(1)} %slice_select_fusion.19), channel_id=1, source_target_pairs={{0,4},{1,5},{2,6},{3,7},{4,0},{5,1},{6,2},{7,3},{8,12},{9,13},{10,... | collective-permute-start | bytes 196616 | tf_op jit(solution)/shard_map/while/body/ppermute | solution.py:58
  59.3 6.1 %collective-permute-start.3 = (f32[64,128]{1,0:T(8,128)S(1)}, f32[64,128]{1,0:T(8,128)S(1)}, u32[]{:S(2)}, u32[]{:S(2)}) collective-permute-start(f32[64,128]{1,0:T(8,128)S(1)} %slice_select_fusion.20), channel_id=1, source_target_pairs={{0,8},{1,9},{2,10},{3,11},{4,12},{5,13},{6,14},{7,15},{8,0},{9,1},... | collective-permute-start | bytes 98312 | tf_op jit(solution)/shard_map/while/body/ppermute | solution.py:58
  65.4 4.7 %collective-permute-start.4 = (bf16[64,128]{1,0:T(8,128)(2,1)S(1)}, bf16[64,128]{1,0:T(8,128)(2,1)S(1)}, u32[]{:S(2)}, u32[]{:S(2)}) collective-permute-start(bf16[64,128]{1,0:T(8,128)(2,1)S(1)} %add_convert_fusion.5), channel_id=1, source_target_pairs={{0,8},{1,9},{2,10},{3,11},{4,12},{5,13},{6,14},{7,15},{8,0},{9,1},... | collective-permute-start | bytes 49160 | tf_op jit(solution)/shard_map/while/body/ppermute | solution.py:58
  70.2 4.0 %collective-permute-start.5 = (bf16[128,128]{1,0:T(8,128)(2,1)S(1)}, bf16[128,128]{1,0:T(8,128)(2,1)S(1)}, u32[]{:S(2)}, u32[]{:S(2)}) collective-permute-start(bf16[128,128]{1,0:T(8,128)(2,1)S(1)} %pad_maximum_fusion.20), channel_id=1, source_target_pairs={{0,4},{1,5},{2,6},{3,7},{4,0},{5,1},{6,2},{7,3},{8,12},{9,13},{10,... | collective-permute-start | bytes 98312 | tf_op jit(solution)/shard_map/while/body/ppermute | solution.py:58
  74.2 5.6 %collective-permute-start.6 = (bf16[256,128]{1,0:T(8,128)(2,1)S(1)}, bf16[256,128]{1,0:T(8,128)(2,1)S(1)}, u32[]{:S(2)}, u32[]{:S(2)}) collective-permute-start(bf16[256,128]{1,0:T(8,128)(2,1)S(1)} %pad_maximum_fusion.21), channel_id=1, source_target_pairs={{0,2},{1,3},{2,0},{3,1},{4,6},{5,7},{6,4},{7,5},{8,10},{9,11},{10,... | collective-permute-start | bytes 196616 | tf_op jit(solution)/shard_map/while/body/ppermute | solution.py:58
  79.8 1.4 collective-permute-start.7
  82.1 48.0 %collective-permute-start.18 = (bf16[4096,256]{1,0:T(8,128)(2,1)}, bf16[4096,256]{1,0:T(8,128)(2,1)}, u32[]{:S(2)}, u32[]{:S(2)}) collective-permute-start(bf16[4096,256]{1,0:T(8,128)(2,1)} %get-tuple-element.105), channel_id=1, source_target_pairs={{0,16},{16,0},{1,17},{17,1},{2,18},{18,2},{3,19},{19,3},{4,20},{20... | collective-permute-start | bytes 6291464 | tf_op jit(solution)/shard_map/ppermute | solution.py:95
  132.2 2.0 collective-permute-start.8
  135.5 8.4 %collective-permute-start.9 = (f32[256,256]{1,0:T(8,128)S(1)}, f32[256,256]{1,0:T(8,128)S(1)}, u32[]{:S(2)}, u32[]{:S(2)}) collective-permute-start(f32[256,256]{1,0:T(8,128)S(1)} %slice_select_fusion.22), channel_id=1, source_target_pairs={{0,2},{1,3},{2,0},{3,1},{4,6},{5,7},{6,4},{7,5},{8,10},{9,11},{10,... | collective-permute-start | bytes 786440 | tf_op jit(solution)/shard_map/while/body/ppermute | solution.py:58
  144.0 5.0 %collective-permute-start.10 = (f32[128,256]{1,0:T(8,128)S(1)}, f32[128,256]{1,0:T(8,128)S(1)}, u32[]{:S(2)}, u32[]{:S(2)}) collective-permute-start(f32[128,256]{1,0:T(8,128)S(1)} %slice_select_fusion.23), channel_id=1, source_target_pairs={{0,4},{1,5},{2,6},{3,7},{4,0},{5,1},{6,2},{7,3},{8,12},{9,13},{10,... | collective-permute-start | bytes 393224 | tf_op jit(solution)/shard_map/while/body/ppermute | solution.py:58
  149.0 5.2 %collective-permute-start.11 = (f32[64,256]{1,0:T(8,128)S(1)}, f32[64,256]{1,0:T(8,128)S(1)}, u32[]{:S(2)}, u32[]{:S(2)}) collective-permute-start(f32[64,256]{1,0:T(8,128)S(1)} %slice_select_fusion.24), channel_id=1, source_target_pairs={{0,8},{1,9},{2,10},{3,11},{4,12},{5,13},{6,14},{7,15},{8,0},{9,1},... | collective-permute-start | bytes 196616 | tf_op jit(solution)/shard_map/while/body/ppermute | solution.py:58
  154.3 4.9 %collective-permute-start.12 = (bf16[64,256]{1,0:T(8,128)(2,1)S(1)}, bf16[64,256]{1,0:T(8,128)(2,1)S(1)}, u32[]{:S(2)}, u32[]{:S(2)}) collective-permute-start(bf16[64,256]{1,0:T(8,128)(2,1)S(1)} %add_convert_fusion.6), channel_id=1, source_target_pairs={{0,8},{1,9},{2,10},{3,11},{4,12},{5,13},{6,14},{7,15},{8,0},{9,1},... | collective-permute-start | bytes 98312 | tf_op jit(solution)/shard_map/while/body/ppermute | solution.py:58
  159.2 4.3 %collective-permute-start.13 = (bf16[128,256]{1,0:T(8,128)(2,1)S(1)}, bf16[128,256]{1,0:T(8,128)(2,1)S(1)}, u32[]{:S(2)}, u32[]{:S(2)}) collective-permute-start(bf16[128,256]{1,0:T(8,128)(2,1)S(1)} %pad_maximum_fusion.24), channel_id=1, source_target_pairs={{0,4},{1,5},{2,6},{3,7},{4,0},{5,1},{6,2},{7,3},{8,12},{9,13},{10,... | collective-permute-start | bytes 196616 | tf_op jit(solution)/shard_map/while/body/ppermute | solution.py:58
  163.6 5.0 %collective-permute-start.14 = (bf16[256,256]{1,0:T(8,128)(2,1)S(1)}, bf16[256,256]{1,0:T(8,128)(2,1)S(1)}, u32[]{:S(2)}, u32[]{:S(2)}) collective-permute-start(bf16[256,256]{1,0:T(8,128)(2,1)S(1)} %pad_maximum_fusion.25), channel_id=1, source_target_pairs={{0,2},{1,3},{2,0},{3,1},{4,6},{5,7},{6,4},{7,5},{8,10},{9,11},{10,... | collective-permute-start | bytes 393224 | tf_op jit(solution)/shard_map/while/body/ppermute | solution.py:58
  169.4 1.9 collective-permute-start.15
  173.2 40.0 %slice-start = ((s8[5242880]{0:T(1024)(128)(4,1)}), s8[4194304]{0:T(1024)(128)(4,1)S(1)}, s32[]{:S(2)}) async-start(s8[5242880]{0:T(1024)(128)(4,1)} %bitcast.16), calls=%async_computation.3 | async-start | bytes 8388608
  173.2 40.0 %slice-start.2 = ((s8[8388608]{0:T(1024)(128)(4,1)}), s8[4194304]{0:T(1024)(128)(4,1)S(1)}, s32[]{:S(2)}) async-start(s8[8388608]{0:T(1024)(128)(4,1)} %bitcast.18), calls=%async_computation.5 | async-start | bytes 8388608
  173.2 40.1 %slice-start.1 = ((s8[5242880]{0:T(1024)(128)(4,1)}), s8[1048576]{0:T(1024)(128)(4,1)S(1)}, s32[]{:S(2)}) async-start(s8[5242880]{0:T(1024)(128)(4,1)} %bitcast.16), calls=%async_computation.4 | async-start | bytes 2097152
  173.2 40.1 %slice-start.3 = ((s8[8388608]{0:T(1024)(128)(4,1)}), s8[4194304]{0:T(1024)(128)(4,1)S(1)}, s32[]{:S(2)}) async-start(s8[8388608]{0:T(1024)(128)(4,1)} %bitcast.18), calls=%async_computation.6 | async-start | bytes 8388608
  179.7 33.6 %copy-start = (bf16[1024,640]{1,0:T(8,128)(2,1)S(1)}, bf16[1024,640]{1,0:T(8,128)(2,1)}, u32[]{:S(2)}) copy-start(bf16[1024,640]{1,0:T(8,128)(2,1)} %all-gather.2.cloned.1.call-done.refs_0_) | copy-start | bytes 3932164
  179.7 33.6 %copy-start.1 = (bf16[1024,256]{1,0:T(8,128)(2,1)S(1)}, bf16[1024,256]{1,0:T(8,128)(2,1)}, u32[]{:S(2)}) copy-start(bf16[1024,256]{1,0:T(8,128)(2,1)} %get-tuple-element.104.refs_2_) | copy-start | bytes 1572868
  179.7 33.6 %copy-start.2 = (bf16[1024,128]{1,0:T(8,128)(2,1)S(1)}, bf16[1024,128]{1,0:T(8,128)(2,1)}, u32[]{:S(2)}) copy-start(bf16[1024,128]{1,0:T(8,128)(2,1)} %get-tuple-element.100.refs_1_) | copy-start | bytes 786436
  179.8 2.0 collective-permute-start.19
  181.9 5.6 %collective-permute-start.20 = (bf16[256,256]{1,0:T(8,128)(2,1)S(1)}, bf16[256,256]{1,0:T(8,128)(2,1)S(1)}, u32[]{:S(2)}, u32[]{:S(2)}) collective-permute-start(bf16[256,256]{1,0:T(8,128)(2,1)S(1)} %select_convert_fusion), channel_id=1, source_target_pairs={{0,2},{1,3},{2,0},{3,1},{4,6},{5,7},{6,4},{7,5},{8,10},{9,11},{10,... | collective-permute-start | bytes 393224 | tf_op jit(solution)/shard_map/ppermute | solution.py:58
  187.6 4.3 %collective-permute-start.21 = (bf16[128,256]{1,0:T(8,128)(2,1)S(1)}, bf16[128,256]{1,0:T(8,128)(2,1)S(1)}, u32[]{:S(2)}, u32[]{:S(2)}) collective-permute-start(bf16[128,256]{1,0:T(8,128)(2,1)S(1)} %select_convert_fusion.1), channel_id=1, source_target_pairs={{0,4},{1,5},{2,6},{3,7},{4,0},{5,1},{6,2},{7,3},{8,12},{9,13},{10,... | collective-permute-start | bytes 196616 | tf_op jit(solution)/shard_map/ppermute | solution.py:58
  191.9 5.0 %collective-permute-start.22 = (bf16[64,256]{1,0:T(8,128)(2,1)S(1)}, bf16[64,256]{1,0:T(8,128)(2,1)S(1)}, u32[]{:S(2)}, u32[]{:S(2)}) collective-permute-start(bf16[64,256]{1,0:T(8,128)(2,1)S(1)} %select_convert_fusion.2), channel_id=1, source_target_pairs={{0,8},{1,9},{2,10},{3,11},{4,12},{5,13},{6,14},{7,15},{8,0},{9,1},... | collective-permute-start | bytes 98312 | tf_op jit(solution)/shard_map/ppermute | solution.py:58
  196.9 5.0 %collective-permute-start.23 = (bf16[64,256]{1,0:T(8,128)(2,1)S(1)}, bf16[64,256]{1,0:T(8,128)(2,1)S(1)}, u32[]{:S(2)}, u32[]{:S(2)}) collective-permute-start(bf16[64,256]{1,0:T(8,128)(2,1)S(1)} %add_convert_fusion.2), channel_id=1, source_target_pairs={{0,8},{1,9},{2,10},{3,11},{4,12},{5,13},{6,14},{7,15},{8,0},{9,1},... | collective-permute-start | bytes 98312 | tf_op jit(solution)/shard_map/ppermute | solution.py:58
  202.0 4.4 %collective-permute-start.24 = (bf16[128,256]{1,0:T(8,128)(2,1)S(1)}, bf16[128,256]{1,0:T(8,128)(2,1)S(1)}, u32[]{:S(2)}, u32[]{:S(2)}) collective-permute-start(bf16[128,256]{1,0:T(8,128)(2,1)S(1)} %pad_maximum_fusion.11), channel_id=1, source_target_pairs={{0,4},{1,5},{2,6},{3,7},{4,0},{5,1},{6,2},{7,3},{8,12},{9,13},{10,... | collective-permute-start | bytes 196616 | tf_op jit(solution)/shard_map/ppermute | solution.py:58
  206.4 5.0 %collective-permute-start.25 = (bf16[256,256]{1,0:T(8,128)(2,1)S(1)}, bf16[256,256]{1,0:T(8,128)(2,1)S(1)}, u32[]{:S(2)}, u32[]{:S(2)}) collective-permute-start(bf16[256,256]{1,0:T(8,128)(2,1)S(1)} %pad_maximum_fusion.10), channel_id=1, source_target_pairs={{0,2},{1,3},{2,0},{3,1},{4,6},{5,7},{6,4},{7,5},{8,10},{9,11},{10,... | collective-permute-start | bytes 393224 | tf_op jit(solution)/shard_map/ppermute | solution.py:58
  211.5 1.6 collective-permute-start.26
Sparse Core Ops, SparseCore 0:
  23.6 64.7 reduce-scatter.1
  92.0 39.5 all-gather.1

commit v2 on v1

v2 whole, which is shorter than its diff:
```python
import jax
import jax.numpy as jnp
from jax import lax
from jax.experimental import pallas as pl
from jax.experimental.layout import Layout, with_layout_constraint
from jax.experimental.pallas import tpu as pltpu
from jax.sharding import PartitionSpec as P

GROUPS = (128, 256, 256)
KINDS = (jnp.float32, jnp.bfloat16, jnp.bfloat16)
TURN = 1
VMEM_BYTES = 58 * 1024 * 1024


def after(value, *others):
    return lax.optimization_barrier((value, *others))[0]


def block_of(extent, target):
    while extent % target:
        target //= 2
    return target


def project(amplitudes, vectors):
    part = jnp.dot(amplitudes, vectors, preferred_element_type=jnp.float32)
    return with_layout_constraint(part, Layout(major_to_minor=(0, 1)))


def project_back(base, groups, kind):
    rows, columns = base.shape
    block = block_of(columns, 1024)
    chis = [chi for chi, _ in groups]
    pieces = [piece for _, members in groups for piece in members]

    def kernel(base_ref, *refs):
        left = jnp.concatenate([c[...] for c in refs[: len(chis)]], axis=1)
        right = jnp.concatenate([p[...] for p in refs[len(chis) : -1]], axis=1)
        term = lax.dot_general(left, right, (((1,), (1,)), ((), ())), preferred_element_type=jnp.float32)
        refs[-1][...] = (base_ref[...].astype(jnp.float32) + term).astype(kind)

    return pl.pallas_call(
        kernel,
        grid=(columns // block,),
        in_specs=[pl.BlockSpec((rows, block), lambda i: (0, i))]
        + [pl.BlockSpec(chi.shape, lambda i: (0, 0), pipeline_mode=pl.Buffered(1)) for chi in chis]
        + [pl.BlockSpec((block, piece.shape[1]), lambda i: (i, 0)) for piece in pieces],
        out_specs=pl.BlockSpec((rows, block), lambda i: (0, i)),
        out_shape=jax.ShapeDtypeStruct(base.shape, kind),
        compiler_params=pltpu.CompilerParams(vmem_limit_bytes=VMEM_BYTES),
        cost_estimate=pl.CostEstimate(flops=0, bytes_accessed=0, transcendentals=0),
    )(base, *chis, *pieces)


def solution(mesh):
    rows, cols = mesh.shape["row"], mesh.shape["col"]

    def exchange(value, bit):
        return lax.ppermute(value, "col", [(i, i ^ bit) for i in range(cols)])

    def body(amplitudes, residual_in, cholesky):
        me = lax.axis_index("col")
        once = 1 + (me >> 20)

        def boxed(run, *values):
            shapes = jax.eval_shape(run, *values)
            zeros = jax.tree.map(lambda s: jnp.zeros(s.shape, s.dtype), shapes)

            def trip(state):
                return state[0] + 1, run(*[after(value, state[0]) for value in values])

            return lax.while_loop(lambda state: state[0] < once, trip, (jnp.int32(0), zeros))[1]

        bits = [1 << k for k in range(cols.bit_length() - 1)]
        upper = [(me & bit) != 0 for bit in bits]

        def halve(value, step, kind):
            half = value.shape[0] // 2
            low, high = value[:half], value[half:]
            got = exchange(jnp.where(upper[step], low, high).astype(kind), bits[step])
            return jnp.where(upper[step], high, low) + got.astype(jnp.float32)

        def double(value, step):
            got = exchange(value, bits[step])
            return jnp.concatenate([jnp.where(upper[step], got, value), jnp.where(upper[step], value, got)])

        mates = [[i for i in range(cols) if i % 2 == core] for core in range(2)]
        count = cols // 2

        def spread(value):
            return lax.all_to_all(value, "col", 0, 0, tiled=True, axis_index_groups=mates)

        def scatter(value, kind=jnp.float32):
            value = halve(value, 0, jnp.float32)
            parts = spread(value.astype(kind)).astype(jnp.float32)
            return jnp.sum(parts.reshape(count, parts.shape[0] // count, -1), axis=0).astype(jnp.bfloat16)

        def gather(value):
            return spread(jnp.tile(value, (count, 1)))

        def send_row(vectors, shift):
            return lax.ppermute(vectors, "row", [(i, (i + shift) % rows) for i in range(rows)])

        if rows != 2 or sum(GROUPS) != cholesky.shape[1]:
            rest = jnp.concatenate([send_row(cholesky, shift) for shift in range(1, rows)], axis=1)
            chi = double(gather(scatter(project(amplitudes, cholesky))), 0)
            total = project_back(residual_in, [(chi, [cholesky])], jnp.float32)
            rest = after(rest, total)
            chi = double(gather(scatter(project(amplitudes, rest))), 0)
            return project_back(total, [(chi, [rest])], jnp.bfloat16)

        ends = [sum(GROUPS[: k + 1]) for k in range(len(GROUPS))]
        outs = [cholesky[:, end - size : end] for end, size in zip(ends, GROUPS)]
        pieces = [send_row(outs[0], 1)]
        part = project(amplitudes, after(cholesky, outs[0]))
        pieces.append(send_row(after(outs[1], part), 1))
        own = lax.psum_scatter(part, "col", scatter_dimension=0, tiled=True).astype(jnp.bfloat16)
        groups = []
        waits = [part]
        for k, kind in enumerate(KINDS):
            part = project(amplitudes, after(pieces[k], *waits))
            if k == TURN:
                own = after(own, part)
                chi_own = lax.all_gather(own, "col", axis=0, tiled=True)
                part = after(part, own)
            if k < len(GROUPS) - 1:
                chi = double(boxed(lambda v: gather(scatter(v, kind)), part), 0)
            else:
                chi = double(gather(scatter(part, kind)), 0)
            if len(pieces) < len(GROUPS):
                pieces.append(send_row(after(outs[len(pieces)], chi), 1))
            waits = [chi] if k + 2 < len(GROUPS) else [chi, chi_own]
            groups.append((chi, [pieces[k]]))
        return project_back(residual_in, [(chi_own, [cholesky])] + groups, jnp.bfloat16)

    in_specs = (P("row", "col"), P("row", "col"), P("col", "row"))
    return jax.shard_map(body, mesh=mesh, in_specs=in_specs, out_specs=P("row", "col"), check_vma=False)
```

time: 235 us -> 191 us (0.81)
  waiting for transfers between devices: 114 us -> 40.2 us
  blocking collectives: 0 us -> 59.6 us
  starting transfers between devices: 41.7 us -> 13.2 us
  other arithmetic: 10.7 us -> 6.52 us
    all_to_all x0 -> x4, blocking collectives: none -> 59.6 us  [spread(): lax.all_to_all(value, 'col', 0, 0, tiled=True, axis_index_groups=mates)]
    ppermute x24 -> x6, waiting for transfers between devices: 67.9 us -> 9.9 us  [exchange(): return lax.ppermute(value, 'col', [(i, i ^ bit) for i in range(cols)])]
    ppermute x3, waiting for transfers between devices: 46 us -> 8.51 us  [send_row(): lax.ppermute(vectors, 'row', [(i, (i + shift) % rows) for i in range(rows)])]
    ppermute x24 -> x6, starting transfers between devices: 37 us -> 0.47 us  [exchange(): return lax.ppermute(value, 'col', [(i, i ^ bit) for i in range(cols)])]
    all_to_all x0 -> x2, waiting for transfers between devices: none -> 18.2 us  [spread(): lax.all_to_all(value, 'col', 0, 0, tiled=True, axis_index_groups=mates)]
    all_to_all x0 -> x2, starting transfers between devices: none -> 8.16 us  [spread(): lax.all_to_all(value, 'col', 0, 0, tiled=True, axis_index_groups=mates)]
    add x9 -> x1, other arithmetic: 2.66 us -> 0.05 us  [halve(): return jnp.where(upper[step], high, low) + got.astype(jnp.float32)]
    all_gather x1, waiting for transfers between devices: 0.01 us -> 2.58 us  [body(): chi_own = lax.all_gather(own, 'col', axis=0, tiled=True)]
  transfers between devices with their start and end apart: 29 -> 13, of which waited for: 26 -> 12; matrix products, arithmetic and copies ran while one was open for 18% -> 19% of each run, Pallas kernels for 0% -> 0%
where the time goes in v2:
time: 191 us; the launch traced here: 190 us
  blocking collectives  59.6 us (31%)
  waiting for transfers between devices  40.2 us (21%)
  matrix products  30.7 us (16%)
  Pallas kernels  16.8 us (9%)
  between operations  13.5 us (7%)
  starting transfers between devices  13.2 us (7%)
  local copies, waits for them, and re-layouts  9.95 us (5%)
  other arithmetic  6.52 us (3%)
    all_to_all x4, blocking collectives, spread(): lax.all_to_all(value, 'col', 0, 0, tiled=True, axis_index_groups=mates)  59.6 us
    dot_general x4, matrix products, project(): part = jnp.dot(amplitudes, vectors, preferred_element_type=jnp.float32)  30.7 us
    all_to_all x2, waiting for transfers between devices, spread(): lax.all_to_all(value, 'col', 0, 0, tiled=True, axis_index_groups=mates)  18.2 us
    pallas_call x1, Pallas kernels, project_back(): pl.pallas_call(kernel, grid=(columns // block,), in_specs=[pl.BlockSpec((...  16.8 us
    ppermute x6, waiting for transfers between devices, exchange(): return lax.ppermute(value, 'col', [(i, i ^ bit) for i in range(cols)])  9.9 us
    ppermute x3, waiting for transfers between devices, send_row(): lax.ppermute(vectors, 'row', [(i, (i + shift) % rows) for i in range(rows)])  8.51 us
    all_to_all x2, starting transfers between devices, spread(): lax.all_to_all(value, 'col', 0, 0, tiled=True, axis_index_groups=mates)  8.16 us
    slice x2, local copies, waits for them, and re-layouts, body(): outs = [cholesky[:, end - size:end] for end, size in zip(ends, GROUPS)]  5.77 us
  transfers between devices with their start and end apart: 13, of which 12 were waited for; matrix products, arithmetic and copies ran while one was open for 19% of the time, Pallas kernels for 0%

profile of v2, /device:TPU:0, one launch (start us, length us, event | category | flops | bytes accessed | tf_op | source)
XLA Modules:
  0.0 190.5 jit_solution(13614285360576486210)
XLA Ops:
  6.5 0.0 reduce-scatter.2.cloned.1.call-start
  6.5 1.3 slice.33
  7.8 3.0 %collective-permute-start.3 = (bf16[4096,128]{1,0:T(8,128)(2,1)S(1)}, bf16[4096,128]{1,0:T(8,128)(2,1)}, u32[]{:S(2)}, u32[]{:S(2)}) collective-permute-start(bf16[4096,128]{1,0:T(8,128)(2,1)S(1)} %slice.33), channel_id=1, source_target_pairs={{0,16},{16,0},{1,17},{17,1},{2,18},{18,2},{3,19},{19,3},{4,20},{20... | collective-permute-start | bytes 3145736 | tf_op jit(solution)/shard_map/ppermute | solution.py:102
  10.8 11.6 %convolution_bitcast_fusion = f32[1024,640]{1,0:T(8,128)} fusion(bf16[1024,4096]{1,0:T(8,128)(2,1)} %param.7, bf16[4096,640]{1,0:T(8,128)(2,1)} %refs_4_.1), kind=kOutput, calls=%fused_computation.4 | convolution fusion | flops 5368709120 | bytes 16252928 | tf_op jit(solution)/shard_map/dot_general | solution.py:26
  22.5 0.0 reduce-scatter.2.cloned.1.call-update
  22.5 0.0 all-gather.2.cloned.1.call-start
  22.6 4.5 %fusion = (bf16[4096,256]{1,0:T(8,128)(2,1)}, bf16[4096,256]{1,0:T(8,128)(2,1)}) fusion(bf16[4096,640]{1,0:T(8,128)(2,1)} %refs_4_.1), kind=kLoop, calls=%fused_computation.19 | loop fusion | bytes 8388608 | tf_op jit(solution)/shard_map/slice | solution.py:113
  27.0 0.0 collective-permute-start.2
  27.1 7.9 %collective-permute-done.3.refs_5_ = bf16[4096,128]{1,0:T(8,128)(2,1)} collective-permute-done((bf16[4096,128]{1,0:T(8,128)(2,1)S(1)}, bf16[4096,128]{1,0:T(8,128)(2,1)}, u32[]{:S(2)}, u32[]{:S(2)}) %collective-permute-start.3) | collective-permute-done | bytes 1048608 | tf_op jit(solution)/shard_map/ppermute | solution.py:102
  34.9 6.3 %convolution_bitcast_fusion.3 = f32[1024,128]{1,0:T(8,128)S(1)} fusion(bf16[1024,4096]{1,0:T(8,128)(2,1)} %param.7, bf16[4096,128]{1,0:T(8,128)(2,1)} %collective-permute-done.3.refs_5_), kind=kOutput, calls=%fused_computation.7 | convolution fusion | flops 1073741824 | bytes 9961472 | tf_op jit(solution)/shard_map/dot_general | solution.py:26
  41.2 0.7 broadcast_in_dim.6
  41.9 35.3 %while.22 = (s32[]{:T(128)}, bf16[512,128]{1,0:T(8,128)(2,1)}, s32[]{:T(128)}, pred[]{:T(512)}, f32[1024,128]{1,0:T(8,128)S(1)}, /*index=5*/s32[]{:T(128)}, f32[]{:T(128)}) while((s32[]{:T(128)}, bf16[512,128]{1,0:T(8,128)(2,1)}, s32[]{:T(128)}, pred[]{:T(512)}, f32[1024,128]{1,0:T(8,128)S(1)}, /*index=5*/s32[]{:T(128)}, f32[]{:T(128)}) %tuple.65), condition=%wide.region_3.4_spmd, body=%wide.region_1.3_spmd.sunk | while | flops 253954 | bytes 4751543 | solution.py:72
  41.9 0.1 collective-permute-start
  42.0 1.5 collective-permute-done
  43.6 20.2 %all_to_all.62 = f32[8,64,128]{2,1,0:T(8,128)S(1)} all-to-all(f32[8,64,128]{2,1,0:T(8,128)S(1)} %bitcast.32), channel_id=1, replica_groups={{0,2,4,6,8,10,12,14},{1,3,5,7,9,11,13,15},{16,18,20,22,24,26,28,30},{17..., dimensions={0} | all-to-all | bytes 524288 | tf_op jit(solution)/shard_map/while/body/all_to_all | solution.py:91
  63.8 0.7 tile.14
  64.5 4.6 %all-to-all-start.1 = ((bf16[8,64,128]{2,1,0:T(8,128)(2,1)}), bf16[8,64,128]{2,1,0:T(8,128)(2,1)S(1)}, u32[]{:S(2)}, u32[]{:S(2)}) async-start(bf16[8,64,128]{2,1,0:T(8,128)(2,1)} %tile.14), calls=%async_computation.1 | async-start | bytes 262144 | tf_op jit(solution)/shard_map/while/body/all_to_all | solution.py:91
  69.1 7.3 %all-to-all-done.1 = bf16[8,64,128]{2,1,0:T(8,128)(2,1)S(1)} async-done(((bf16[8,64,128]{2,1,0:T(8,128)(2,1)}), bf16[8,64,128]{2,1,0:T(8,128)(2,1)S(1)}, u32[]{:S(2)}, u32[]{:S(2)}) %all-to-all-start.1) | async-done | bytes 131104 | tf_op jit(solution)/shard_map/while/body/all_to_all | solution.py:91
  76.5 0.0 copy-start.2
  76.5 0.7 copy-done.2
  77.1 0.0 collective-permute-start.4
  77.2 1.6 collective-permute-done.4
  78.7 0.9 broadcast_select_fusion.5
  79.6 0.7 pad_maximum_fusion.2.refs_1_
  80.4 1.5 collective-permute-start.6
  81.9 0.0 collective-permute-done.2.refs_6_
  81.9 0.0 copy-start
  81.9 6.5 %convolution_bitcast_fusion.2 = f32[1024,256]{1,0:T(8,128)S(1)} fusion(bf16[1024,4096]{1,0:T(8,128)(2,1)} %param.7, bf16[4096,256]{1,0:T(8,128)(2,1)S(1)} %collective-permute-done.2.refs_6_), kind=kOutput, calls=%fused_computation.6 | convolution fusion | flops 2147483648 | bytes 11534336 | tf_op jit(solution)/shard_map/dot_general | solution.py:26
  88.4 0.0 copy-done
  88.4 0.9 reduce-scatter.2.cloned.1.call-done
  89.4 1.6 convert_element_type.33
  90.9 0.0 all-gather.2.cloned.1.call-update
  90.9 0.7 broadcast_in_dim.7
  91.7 32.4 %while.23 = (s32[]{:T(128)}, bf16[512,256]{1,0:T(8,128)(2,1)}, s32[]{:T(128)}, pred[]{:T(512)}, f32[1024,256]{1,0:T(8,128)S(1)}, /*index=5*/s32[]{:T(128)}, bf16[]{:T(256)}) while((s32[]{:T(128)}, bf16[512,256]{1,0:T(8,128)(2,1)}, s32[]{:T(128)}, pred[]{:T(512)}, f32[1024,256]{1,0:T(8,128)S(1)}, /*index=5*/s32[]{:T(128)}, bf16[]{:T(256)}) %tuple.68), condition=%wide.region_6.7_spmd, body=%wide.region_4.6_spmd.sunk | while | flops 638978 | bytes 8454325 | solution.py:72
  91.7 0.1 slice_select_fusion.6
  91.7 0.1 collective-permute-start.1
  91.8 1.9 collective-permute-done.1
  93.7 0.1 add_convert_fusion.3
  93.8 14.4 %all_to_all.63 = bf16[8,64,256]{2,1,0:T(8,128)(2,1)S(1)} all-to-all(bf16[8,64,256]{2,1,0:T(8,128)(2,1)S(1)} %bitcast.33), channel_id=1, replica_groups={{0,2,4,6,8,10,12,14},{1,3,5,7,9,11,13,15},{16,18,20,22,24,26,28,30},{17..., dimensions={0} | all-to-all | bytes 524288 | tf_op jit(solution)/shard_map/while/body/all_to_all | solution.py:91
  108.2 0.7 tile.20
  108.9 3.5 %all-to-all-start.3 = ((bf16[8,64,256]{2,1,0:T(8,128)(2,1)}), bf16[8,64,256]{2,1,0:T(8,128)(2,1)S(1)}, u32[]{:S(2)}, u32[]{:S(2)}) async-start(bf16[8,64,256]{2,1,0:T(8,128)(2,1)} %tile.20), calls=%async_computation.3 | async-start | bytes 524288 | tf_op jit(solution)/shard_map/while/body/all_to_all | solution.py:91
  112.5 10.9 %all-to-all-done.3 = bf16[8,64,256]{2,1,0:T(8,128)(2,1)S(1)} async-done(((bf16[8,64,256]{2,1,0:T(8,128)(2,1)}), bf16[8,64,256]{2,1,0:T(8,128)(2,1)S(1)}, u32[]{:S(2)}, u32[]{:S(2)}) %all-to-all-start.3) | async-done | bytes 262176 | tf_op jit(solution)/shard_map/while/body/all_to_all | solution.py:91
  123.4 0.0 copy-start.1
  123.4 0.7 copy-done.1
  124.1 0.0 collective-permute-start.5
  124.1 1.7 collective-permute-done.5
  125.8 1.0 broadcast_select_fusion.3
  126.8 0.9 pad_maximum_fusion.refs_2_
  127.7 0.6 collective-permute-done.6.refs_7_
  128.4 2.6 %all-gather.2.cloned.1.call-done.refs_0_ = bf16[1024,640]{1,0:T(8,128)(2,1)} async-done(((bf16[64,640]{1,0:T(8,128)(2,1)}), bf16[1024,640]{1,0:T(8,128)(2,1)}) %all-gather.2.cloned.1.call-update) | async-done | bytes 1310736 | tf_op jit(solution)/shard_map/all_gather | solution.py:124
  130.9 6.3 %convolution_bitcast_fusion.1 = f32[1024,256]{1,0:T(8,128)S(1)} fusion(bf16[1024,4096]{1,0:T(8,128)(2,1)} %param.7, bf16[4096,256]{1,0:T(8,128)(2,1)} %collective-permute-done.6.refs_7_), kind=kOutput, calls=%fused_computation.5 | convolution fusion | flops 2147483648 | bytes 11534336 | tf_op jit(solution)/shard_map/dot_general | solution.py:26
  137.3 0.1 slice_select_fusion.2
  137.3 0.3 collective-permute-start.7
  137.7 1.7 collective-permute-done.7
  139.3 0.1 add_convert_fusion.1
  139.4 12.7 %all_to_all.60 = bf16[8,64,256]{2,1,0:T(8,128)(2,1)S(1)} all-to-all(bf16[8,64,256]{2,1,0:T(8,128)(2,1)S(1)} %bitcast.36), channel_id=1, replica_groups={{0,2,4,6,8,10,12,14},{1,3,5,7,9,11,13,15},{16,18,20,22,24,26,28,30},{17..., dimensions={0} | all-to-all | bytes 524288 | tf_op jit(solution)/shard_map/all_to_all | solution.py:91
  152.1 12.3 %all_to_all.61 = bf16[8,64,256]{2,1,0:T(8,128)(2,1)S(1)} all-to-all(bf16[8,64,256]{2,1,0:T(8,128)(2,1)S(1)} %tile.11), channel_id=1, replica_groups={{0,2,4,6,8,10,12,14},{1,3,5,7,9,11,13,15},{16,18,20,22,24,26,28,30},{17..., dimensions={0} | all-to-all | bytes 524288 | tf_op jit(solution)/shard_map/all_to_all | solution.py:91
  164.4 0.0 collective-permute-start.8
  164.4 1.5 collective-permute-done.8
  166.0 0.1 broadcast_select_fusion.1
  166.0 0.8 pad_maximum_fusion.1.refs_3_
  166.9 16.8 %shard_map.37 = bf16[1024,4096]{1,0:T(8,128)(2,1)} custom-call(bf16[1024,4096]{1,0:T(8,128)(2,1)} %base_ref.1, bf16[1024,640]{1,0:T(8,128)(2,1)} %all-gather.2.cloned.1.call-done.refs_0_, bf16[1024,128]{1,0:T(8,128)(2,1)} %pad_maximum_fusion.2.refs_1_, bf16[1024,256]{1,0:T(8,128)(2,1)} %pad_maximum_fusion.refs_2_, ...), custom_call_target="tpu_custom_call" | custom-call | tf_op jit(solution)/shard_map/pallas_call | solution.py:42
  (6 shorter events, 0.2 us)
Async XLA Ops:
  6.5 82.8 %reduce-scatter.2.cloned.1.call-start = ((), (), s32[]{:S(2)}) async-start(), calls=%async_computation.7 | async-start | bytes 2785280 | tf_op jit(solution)/shard_map/reduce_scatter | solution.py:117
  7.8 27.1 %collective-permute-start.3 = (bf16[4096,128]{1,0:T(8,128)(2,1)S(1)}, bf16[4096,128]{1,0:T(8,128)(2,1)}, u32[]{:S(2)}, u32[]{:S(2)}) collective-permute-start(bf16[4096,128]{1,0:T(8,128)(2,1)S(1)} %slice.33), channel_id=1, source_target_pairs={{0,16},{16,0},{1,17},{17,1},{2,18},{18,2},{3,19},{19,3},{4,20},{20... | collective-permute-start | bytes 3145736 | tf_op jit(solution)/shard_map/ppermute | solution.py:102
  22.5 108.4 %all-gather.2.cloned.1.call-start = ((), (), s32[]{:S(2)}) async-start(), calls=%async_computation.8 | async-start | bytes 1392640 | tf_op jit(solution)/shard_map/all_gather | solution.py:124
  27.0 54.8 %collective-permute-start.2 = (bf16[4096,256]{1,0:T(8,128)(2,1)}, bf16[4096,256]{1,0:T(8,128)(2,1)S(1)}, u32[]{:S(2)}, u32[]{:S(2)}) collective-permute-start(bf16[4096,256]{1,0:T(8,128)(2,1)} %get-tuple-element.107), channel_id=1, source_target_pairs={{0,16},{16,0},{1,17},{17,1},{2,18},{18,2},{3,19},{19,3},{4,20},{20... | collective-permute-start | bytes 6291464 | tf_op jit(solution)/shard_map/ppermute | solution.py:102
  41.9 1.6 collective-permute-start
  64.5 12.0 %all-to-all-start.1 = ((bf16[8,64,128]{2,1,0:T(8,128)(2,1)}), bf16[8,64,128]{2,1,0:T(8,128)(2,1)S(1)}, u32[]{:S(2)}, u32[]{:S(2)}) async-start(bf16[8,64,128]{2,1,0:T(8,128)(2,1)} %tile.14), calls=%async_computation.1 | async-start | bytes 262144 | tf_op jit(solution)/shard_map/while/body/all_to_all | solution.py:91
  76.5 0.7 copy-start.2
  77.1 1.6 collective-permute-start.4
  80.4 48.0 %collective-permute-start.6 = (bf16[4096,256]{1,0:T(8,128)(2,1)}, bf16[4096,256]{1,0:T(8,128)(2,1)}, u32[]{:S(2)}, u32[]{:S(2)}) collective-permute-start(bf16[4096,256]{1,0:T(8,128)(2,1)} %get-tuple-element.114), channel_id=1, source_target_pairs={{0,16},{16,0},{1,17},{17,1},{2,18},{18,2},{3,19},{19,3},{4,20},{20... | collective-permute-start | bytes 6291464 | tf_op jit(solution)/shard_map/ppermute | solution.py:102
  81.9 6.5 %copy-start = (bf16[4096,256]{1,0:T(8,128)(2,1)}, bf16[4096,256]{1,0:T(8,128)(2,1)S(1)}, u32[]{:S(2)}) copy-start(bf16[4096,256]{1,0:T(8,128)(2,1)S(1)} %collective-permute-done.2.refs_6_) | copy-start | bytes 6291460
  91.7 2.0 %collective-permute-start.1 = (f32[512,256]{1,0:T(8,128)S(1)}, f32[512,256]{1,0:T(8,128)S(1)}, u32[]{:S(2)}, u32[]{:S(2)}) collective-permute-start(f32[512,256]{1,0:T(8,128)S(1)} %slice_select_fusion.6), channel_id=1, source_target_pairs={{0,1},{1,0},{2,3},{3,2},{4,5},{5,4},{6,7},{7,6},{8,9},{9,8},{10,11... | collective-permute-start | bytes 1572872 | tf_op jit(solution)/shard_map/while/body/ppermute | solution.py:59
  108.9 14.4 %all-to-all-start.3 = ((bf16[8,64,256]{2,1,0:T(8,128)(2,1)}), bf16[8,64,256]{2,1,0:T(8,128)(2,1)S(1)}, u32[]{:S(2)}, u32[]{:S(2)}) async-start(bf16[8,64,256]{2,1,0:T(8,128)(2,1)} %tile.20), calls=%async_computation.3 | async-start | bytes 524288 | tf_op jit(solution)/shard_map/while/body/all_to_all | solution.py:91
  123.4 0.7 copy-start.1
  124.1 1.7 collective-permute-start.5
  137.3 2.0 %collective-permute-start.7 = (f32[512,256]{1,0:T(8,128)S(1)}, f32[512,256]{1,0:T(8,128)S(1)}, u32[]{:S(2)}, u32[]{:S(2)}) collective-permute-start(f32[512,256]{1,0:T(8,128)S(1)} %slice_select_fusion.2), channel_id=1, source_target_pairs={{0,1},{1,0},{2,3},{3,2},{4,5},{5,4},{6,7},{7,6},{8,9},{9,8},{10,11... | collective-permute-start | bytes 1572872 | tf_op jit(solution)/shard_map/ppermute | solution.py:59
  164.4 1.5 collective-permute-start.8
Sparse Core Ops, SparseCore 0:
  22.6 66.6 reduce-scatter.1
  91.6 39.2 all-gather.1

commit v3 on v2

v3 whole, which is shorter than its diff:
```python
import jax
import jax.numpy as jnp
from jax import lax
from jax.experimental import pallas as pl
from jax.experimental.layout import Layout, with_layout_constraint
from jax.experimental.pallas import tpu as pltpu
from jax.sharding import PartitionSpec as P

GROUPS = (128, 256, 256)
VMEM_BYTES = 58 * 1024 * 1024
FREE = pl.CostEstimate(flops=0, bytes_accessed=0, transcendentals=0)


def after(value, *others):
    return lax.optimization_barrier((value, *others))[0]


def block_of(extent, target):
    while extent % target:
        target //= 2
    return target


def project(amplitudes, vectors):
    part = jnp.dot(amplitudes, vectors, preferred_element_type=jnp.float32)
    return with_layout_constraint(part, Layout(major_to_minor=(0, 1)))


def project_wide(amplitudes, vectors):
    rows, depth = amplitudes.shape
    width = vectors.shape[1]
    block = block_of(depth, 1024)
    steps = depth // block

    def kernel(left_ref, right_ref, out_ref, total_ref):
        step = pl.program_id(0)
        term = lax.dot_general(right_ref[...].T, left_ref[...], (((1,), (1,)), ((), ())), preferred_element_type=jnp.float32)

        @pl.when(step == 0)
        def _():
            total_ref[...] = term

        @pl.when((step > 0) & (step < steps - 1))
        def _():
            total_ref[...] += term

        @pl.when(step == steps - 1)
        def _():
            out_ref[...] = (total_ref[...] + term).T

    return pl.pallas_call(
        kernel,
        grid=(steps,),
        in_specs=[pl.BlockSpec((rows, block), lambda k: (0, k)), pl.BlockSpec((block, width), lambda k: (k, 0))],
        out_specs=pl.BlockSpec((rows, width), lambda k: (0, 0)),
        out_shape=jax.ShapeDtypeStruct((rows, width), jnp.float32),
        scratch_shapes=[pltpu.VMEM((width, rows), jnp.float32)],
        compiler_params=pltpu.CompilerParams(vmem_limit_bytes=VMEM_BYTES),
        cost_estimate=FREE,
    )(amplitudes, vectors)


def project_back(base, chis, pieces, kind):
    rows, columns = base.shape
    block = block_of(columns, 1024)

    def kernel(base_ref, *refs):
        left = jnp.concatenate([c[...] for c in refs[: len(chis)]], axis=1)
        right = jnp.concatenate([p[...] for p in refs[len(chis) : -1]], axis=1)
        term = lax.dot_general(left, right, (((1,), (1,)), ((), ())), preferred_element_type=jnp.float32)
        refs[-1][...] = (base_ref[...].astype(jnp.float32) + term).astype(kind)

    return pl.pallas_call(
        kernel,
        grid=(columns // block,),
        in_specs=[pl.BlockSpec((rows, block), lambda i: (0, i))]
        + [pl.BlockSpec(chi.shape, lambda i: (0, 0), pipeline_mode=pl.Buffered(1)) for chi in chis]
        + [pl.BlockSpec((block, piece.shape[1]), lambda i: (i, 0)) for piece in pieces],
        out_specs=pl.BlockSpec((rows, block), lambda i: (0, i)),
        out_shape=jax.ShapeDtypeStruct(base.shape, kind),
        compiler_params=pltpu.CompilerParams(vmem_limit_bytes=VMEM_BYTES),
        cost_estimate=FREE,
    )(base, *chis, *pieces)


def solution(mesh):
    rows, cols = mesh.shape["row"], mesh.shape["col"]

    def exchange(value, bit):
        return lax.ppermute(value, "col", [(i, i ^ bit) for i in range(cols)])

    def body(amplitudes, residual_in, cholesky):
        me = lax.axis_index("col")
        once = 1 + (me >> 20)

        def boxed(run, *values):
            shapes = jax.eval_shape(run, *values)
            zeros = jax.tree.map(lambda s: jnp.zeros(s.shape, s.dtype), shapes)

            def trip(state):
                return state[0] + 1, run(*[after(value, state[0]) for value in values])

            return lax.while_loop(lambda state: state[0] < once, trip, (jnp.int32(0), zeros))[1]

        bits = [1 << k for k in range(cols.bit_length() - 1)]
        upper = [(me & bit) != 0 for bit in bits]

        def split(value, step):
            low, high = jnp.split(value, 2)
            return jnp.where(upper[step], high, low), jnp.where(upper[step], low, high)

        def halve(value, step, kind):
            keep, send = split(value, step)
            return keep + exchange(send.astype(kind), bits[step]).astype(jnp.float32)

        def double(value, step):
            got = exchange(value, bits[step])
            mine = lax.broadcasted_iota(jnp.int32, (2, 1, 1), 0) == upper[step].astype(jnp.int32)
            return jnp.where(mine, value, got).reshape(2 * value.shape[0], value.shape[1])

        def finish(value):
            value = halve(halve(value, 2, jnp.bfloat16), 3, jnp.bfloat16).astype(jnp.bfloat16)
            return double(double(double(value, 3), 2), 1)

        mates = [[i for i in range(cols) if i % 2 == core] for core in range(2)]
        count = cols // 2

        def spread(value):
            return lax.all_to_all(value, "col", 0, 0, tiled=True, axis_index_groups=mates)

        def scatter(value, kind=jnp.float32):
            value = halve(value, 0, jnp.float32)
            parts = spread(value.astype(kind)).astype(jnp.float32)
            return jnp.sum(parts.reshape(count, parts.shape[0] // count, -1), axis=0).astype(jnp.bfloat16)

        def gather(value):
            return spread(jnp.tile(value, (count, 1)))

        def send_row(vectors, shift):
            return lax.ppermute(vectors, "row", [(i, (i + shift) % rows) for i in range(rows)])

        if rows != 2 or len(bits) != 4 or sum(GROUPS) != cholesky.shape[1]:
            rest = jnp.concatenate([send_row(cholesky, shift) for shift in range(1, rows)], axis=1)
            chi = double(gather(scatter(project(amplitudes, cholesky))), 0)
            total = project_back(residual_in, [chi], [cholesky], jnp.float32)
            rest = after(rest, total)
            chi = double(gather(scatter(project(amplitudes, rest))), 0)
            return project_back(total, [chi], [rest], jnp.bfloat16)

        ends = [sum(GROUPS[: k + 1]) for k in range(len(GROUPS))]
        out_a, out_b, out_c = [cholesky[:, end - size : end] for end, size in zip(ends, GROUPS)]
        a = send_row(out_a, 1)
        part_own = project_wide(amplitudes, after(cholesky, out_a))
        keep, send = split(boxed(lambda v: halve(v, 0, jnp.float32), part_own), 1)
        got = exchange(send, bits[1])
        out_b = after(out_b, send)
        b = send_row(out_b, 1)
        part_a = project(amplitudes, after(a, out_b))
        half_own = boxed(finish, after(keep, part_a) + got)
        c = send_row(after(out_c, half_own), 1)
        chi_own = double(half_own, 0)
        part = jnp.concatenate([part_a, project(amplitudes, after(b, chi_own))], axis=1)
        chi_ab = double(boxed(lambda v: gather(scatter(v, jnp.bfloat16)), part), 0)
        chi_c = double(gather(scatter(project(amplitudes, after(c, chi_ab)), jnp.bfloat16)), 0)
        return project_back(residual_in, [chi_own, chi_ab, chi_c], [cholesky, a, b, c], jnp.bfloat16)

    in_specs = (P("row", "col"), P("row", "col"), P("col", "row"))
    return jax.shard_map(body, mesh=mesh, in_specs=in_specs, out_specs=P("row", "col"), check_vma=False)
```

time: 191 us -> 182 us (0.953)
  blocking collectives: 59.6 us -> 43.2 us
  between operations: 13.5 us -> 0.09 us
  matrix products: 30.7 us -> 18.7 us
  Pallas kernels: 16.8 us -> 26.6 us
  other arithmetic: 6.52 us -> 13.8 us
  starting transfers between devices: 13.2 us -> 20.1 us
  waiting for transfers between devices: 40.2 us -> 45.9 us
  local copies, waits for them, and re-layouts: 9.95 us -> 12.9 us
    ppermute x6 -> x12, waiting for transfers between devices: 9.9 us -> 33.9 us  [exchange(): return lax.ppermute(value, 'col', [(i, i ^ bit) for i in range(cols)])]
    all_to_all x4 -> x3, blocking collectives: 59.6 us -> 43.2 us  [spread(): lax.all_to_all(value, 'col', 0, 0, tiled=True, axis_index_groups=mates)]
    ppermute x6 -> x12, starting transfers between devices: 0.47 us -> 12.5 us  [exchange(): return lax.ppermute(value, 'col', [(i, i ^ bit) for i in range(cols)])]
    dot_general x4 -> x3, matrix products: 30.7 us -> 18.7 us  [project(): part = jnp.dot(amplitudes, vectors, preferred_element_type=jnp.float32)]
    pallas_call x0 -> x1, Pallas kernels: none -> 9.81 us  [project_wide(): pl.pallas_call(kernel, grid=(steps,), in_specs=[pl.BlockSpec((rows, block...]
    ppermute x3, waiting for transfers between devices: 8.51 us -> 0.6 us  [send_row(): lax.ppermute(vectors, 'row', [(i, (i + shift) % rows) for i in range(rows)])]
    select_n x6 -> x10, other arithmetic: 2.13 us -> 9.49 us  [the longest x6 6.78 us: double(): jnp.where(mine, value, got).reshape(2 * value.shape[0], value.shape[1])]
    all_to_all x2 -> x1, waiting for transfers between devices: 18.2 us -> 11.3 us  [spread(): lax.all_to_all(value, 'col', 0, 0, tiled=True, axis_index_groups=mates)]
  transfers between devices with their start and end apart: 13 -> 16, of which waited for: 12 -> 14; matrix products, arithmetic and copies ran while one was open for 19% -> 19% of each run, Pallas kernels for 0% -> 5%
where the time goes in v3:
time: 182 us; the launch traced here: 181 us
  waiting for transfers between devices  45.9 us (25%)
  blocking collectives  43.2 us (24%)
  Pallas kernels  26.6 us (15%)
  starting transfers between devices  20.1 us (11%)
  matrix products  18.7 us (10%)
  other arithmetic  13.8 us (8%)
  local copies, waits for them, and re-layouts  12.9 us (7%)
    all_to_all x3, blocking collectives, spread(): lax.all_to_all(value, 'col', 0, 0, tiled=True, axis_index_groups=mates)  43.2 us
    ppermute x12, waiting for transfers between devices, exchange(): return lax.ppermute(value, 'col', [(i, i ^ bit) for i in range(cols)])  33.9 us
    dot_general x3, matrix products, project(): part = jnp.dot(amplitudes, vectors, preferred_element_type=jnp.float32)  18.7 us
    pallas_call x1, Pallas kernels, project_back(): pl.pallas_call(kernel, grid=(columns // block,), in_specs=[pl.BlockSpec((...  16.8 us
    ppermute x12, starting transfers between devices, exchange(): return lax.ppermute(value, 'col', [(i, i ^ bit) for i in range(cols)])  12.5 us
    all_to_all x1, waiting for transfers between devices, spread(): lax.all_to_all(value, 'col', 0, 0, tiled=True, axis_index_groups=mates)  11.3 us
    pallas_call x1, Pallas kernels, project_wide(): pl.pallas_call(kernel, grid=(steps,), in_specs=[pl.BlockSpec((rows, block...  9.81 us
    select_n x6, other arithmetic, double(): jnp.where(mine, value, got).reshape(2 * value.shape[0], value.shape[1])  6.78 us
  transfers between devices with their start and end apart: 16, of which 14 were waited for; matrix products, arithmetic and copies ran while one was open for 19% of the time, Pallas kernels for 5%

profile of v3, /device:TPU:0, one launch (start us, length us, event | category | flops | bytes accessed | tf_op | source)
XLA Modules:
  0.0 181.3 jit_solution(5562152236740857629)
XLA Ops:
  0.0 2.3 %slice.9 = bf16[4096,128]{1,0:T(8,128)(2,1)} slice(bf16[4096,640]{1,0:T(8,128)(2,1)} %refs_3_.1), slice={[0:4096], [0:128]} | slice | bytes 2097152 | tf_op jit(solution)/shard_map/slice | solution.py:151
  2.3 2.9 %collective-permute-start.7 = (bf16[4096,128]{1,0:T(8,128)(2,1)}, bf16[4096,128]{1,0:T(8,128)(2,1)}, u32[]{:S(2)}, u32[]{:S(2)}) collective-permute-start(bf16[4096,128]{1,0:T(8,128)(2,1)} %slice.9), channel_id=1, source_target_pairs={{0,16},{16,0},{1,17},{17,1},{2,18},{18,2},{3,19},{19,3},{4,20},{20... | collective-permute-start | bytes 3145736 | tf_op jit(solution)/shard_map/ppermute | solution.py:140
  5.2 9.8 %shard_map.37 = f32[1024,640]{1,0:T(8,128)S(1)} custom-call(bf16[1024,4096]{1,0:T(8,128)(2,1)} %left_ref.1, bf16[4096,640]{1,0:T(8,128)(2,1)} %refs_3_.1), custom_call_target="tpu_custom_call" | custom-call | tf_op jit(solution)/shard_map/pallas_call | solution.py:51
  15.0 1.1 broadcast_in_dim.149
  16.2 7.1 %while.32 = (s32[]{:T(128)}, f32[512,640]{1,0:T(8,128)}, s32[]{:T(128)}, pred[]{:T(512)}, f32[1024,640]{1,0:T(8,128)S(1)}, /*index=5*/s32[]{:T(128)}) while((s32[]{:T(128)}, f32[512,640]{1,0:T(8,128)}, s32[]{:T(128)}, pred[]{:T(512)}, f32[1024,640]{1,0:T(8,128)S(1)}, /*index=5*/s32[]{:T(128)}) %tuple.77), condition=%wide.region_1.2_spmd, body=%wide.region_0.1_spmd.sunk | while | flops 983042 | bytes 14418031 | solution.py:103
  16.2 1.2 slice_select_fusion.7
  17.4 3.4 %collective-permute-done = f32[512,640]{1,0:T(8,128)} collective-permute-done((f32[512,640]{1,0:T(8,128)}, f32[512,640]{1,0:T(8,128)}, u32[]{:S(2)}, u32[]{:S(2)}) %collective-permute-start) | collective-permute-done | bytes 1310752 | tf_op jit(solution)/shard_map/while/body/ppermute | solution.py:90
  20.7 2.6 %select_add_fusion.2 = f32[512,640]{1,0:T(8,128)} fusion(f32[512,640]{1,0:T(8,128)} %collective-permute-done, f32[1024,640]{1,0:T(8,128)S(1)} %get-tuple-element.286, pred[]{:T(512)} %get-tuple-element.314), kind=kLoop, calls=%fused_computation.clone.1 | loop fusion | flops 655360 | bytes 5242881 | tf_op jit(solution)/shard_map/while/body/add | solution.py:114
  23.3 1.4 slice_select_fusion.2
  24.7 1.6 collective-permute-start.8
  26.3 4.5 %fusion = (bf16[4096,256]{1,0:T(8,128)(2,1)}, bf16[4096,256]{1,0:T(8,128)(2,1)}) fusion(bf16[4096,640]{1,0:T(8,128)(2,1)} %refs_3_.1), kind=kLoop, calls=%fused_computation.27 | loop fusion | bytes 8388608 | tf_op jit(solution)/shard_map/slice | solution.py:151
  30.8 0.5 collective-permute-start.10
  31.3 6.7 %convolution_bitcast_fusion.2 = f32[1024,128]{1,0:T(8,128)} fusion(bf16[1024,4096]{1,0:T(8,128)(2,1)} %left_ref.1, bf16[4096,128]{1,0:T(8,128)(2,1)} %collective-permute-done.7.refs_4_), kind=kOutput, calls=%fused_computation.19 | convolution fusion | flops 1073741824 | bytes 9961472 | tf_op jit(solution)/shard_map/dot_general | solution.py:25
  38.0 3.6 %collective-permute-done.8 = f32[256,640]{1,0:T(8,128)} collective-permute-done((f32[256,640]{1,0:T(8,128)S(1)}, f32[256,640]{1,0:T(8,128)}, u32[]{:S(2)}, u32[]{:S(2)}) %collective-permute-start.8) | collective-permute-done | bytes 655392 | tf_op jit(solution)/shard_map/ppermute | solution.py:90
  41.6 1.2 add.37
  42.8 0.9 broadcast_in_dim.148
  43.7 30.2 %while.33 = (s32[]{:T(128)}, bf16[512,640]{1,0:T(8,128)(2,1)}, s32[]{:T(128)}, pred[]{:T(512)}, pred[]{:T(512)}, /*index=5*/pred[]{:T(512)}, f32[256,640]{1,0:T(8,128)S(1)}, s32[]{:T(128)}) while((s32[]{:T(128)}, bf16[512,640]{1,0:T(8,128)(2,1)}, s32[]{:T(128)}, pred[]{:T(512)}, pred[]{:T(512)}, /*index=5*/pred[]{:T(512)}, ...), condition=%wide.region_3.4_spmd, body=%wide.region_2.3_spmd.sunk | while | flops 1105931 | bytes 7949640 | solution.py:103
  43.7 1.6 collective-permute-start.1
  45.3 3.8 %collective-permute-done.1 = bf16[128,640]{1,0:T(8,128)(2,1)S(1)} collective-permute-done((bf16[128,640]{1,0:T(8,128)(2,1)S(1)}, bf16[128,640]{1,0:T(8,128)(2,1)S(1)}, u32[]{:S(2)}, u32[]{:S(2)}) %collective-permute-start.1) | collective-permute-done | bytes 163872 | tf_op jit(solution)/shard_map/while/body/ppermute | solution.py:90
  49.3 2.7 %collective-permute-start.2 = (bf16[64,640]{1,0:T(8,128)(2,1)S(1)}, bf16[64,640]{1,0:T(8,128)(2,1)S(1)}, u32[]{:S(2)}, u32[]{:S(2)}) collective-permute-start(bf16[64,640]{1,0:T(8,128)(2,1)S(1)} %select_convert_fusion.5), channel_id=1, source_target_pairs={{0,8},{1,9},{2,10},{3,11},{4,12},{5,13},{6,14},{7,15},{8,0},{9,1},... | collective-permute-start | bytes 245768 | tf_op jit(solution)/shard_map/while/body/ppermute | solution.py:90
  51.9 0.1 broadcast_in_dim.210
  52.0 0.1 broadcast_in_dim.211
  52.1 2.6 %collective-permute-done.2 = bf16[64,640]{1,0:T(8,128)(2,1)S(1)} collective-permute-done((bf16[64,640]{1,0:T(8,128)(2,1)S(1)}, bf16[64,640]{1,0:T(8,128)(2,1)S(1)}, u32[]{:S(2)}, u32[]{:S(2)}) %collective-permute-start.2) | collective-permute-done | bytes 81952 | tf_op jit(solution)/shard_map/while/body/ppermute | solution.py:90
  54.7 2.7 %collective-permute-start.3 = (bf16[64,640]{1,0:T(8,128)(2,1)S(1)}, bf16[64,640]{1,0:T(8,128)(2,1)S(1)}, u32[]{:S(2)}, u32[]{:S(2)}) collective-permute-start(bf16[64,640]{1,0:T(8,128)(2,1)S(1)} %add_convert_fusion.5), channel_id=1, source_target_pairs={{0,8},{1,9},{2,10},{3,11},{4,12},{5,13},{6,14},{7,15},{8,0},{9,1},... | collective-permute-start | bytes 245768 | tf_op jit(solution)/shard_map/while/body/ppermute | solution.py:90
  57.4 2.7 %collective-permute-done.3 = bf16[64,640]{1,0:T(8,128)(2,1)S(1)} collective-permute-done((bf16[64,640]{1,0:T(8,128)(2,1)S(1)}, bf16[64,640]{1,0:T(8,128)(2,1)S(1)}, u32[]{:S(2)}, u32[]{:S(2)}) %collective-permute-start.3) | collective-permute-done | bytes 81952 | tf_op jit(solution)/shard_map/while/body/ppermute | solution.py:90
  60.2 0.1 bitcast_select_fusion.9
  60.3 2.0 %collective-permute-start.4 = (bf16[128,640]{1,0:T(8,128)(2,1)S(1)}, bf16[128,640]{1,0:T(8,128)(2,1)S(1)}, u32[]{:S(2)}, u32[]{:S(2)}) collective-permute-start(bf16[128,640]{1,0:T(8,128)(2,1)S(1)} %bitcast_select_fusion.9), channel_id=1, source_target_pairs={{0,4},{1,5},{2,6},{3,7},{4,0},{5,1},{6,2},{7,3},{8,12},{9,13},{10,... | collective-permute-start | bytes 491528 | tf_op jit(solution)/shard_map/while/body/ppermute | solution.py:90
  62.3 0.1 broadcast_bitcast_fusion.2
  62.3 3.3 %collective-permute-done.4 = bf16[128,640]{1,0:T(8,128)(2,1)S(1)} collective-permute-done((bf16[128,640]{1,0:T(8,128)(2,1)S(1)}, bf16[128,640]{1,0:T(8,128)(2,1)S(1)}, u32[]{:S(2)}, u32[]{:S(2)}) %collective-permute-start.4) | collective-permute-done | bytes 163872 | tf_op jit(solution)/shard_map/while/body/ppermute | solution.py:90
  65.6 0.1 bitcast_select_fusion.10
  65.8 1.6 collective-permute-start.5
  67.4 0.1 broadcast_in_dim.208
  67.5 5.5 %collective-permute-done.5 = bf16[256,640]{1,0:T(8,128)(2,1)S(1)} collective-permute-done((bf16[256,640]{1,0:T(8,128)(2,1)S(1)}, bf16[256,640]{1,0:T(8,128)(2,1)S(1)}, u32[]{:S(2)}, u32[]{:S(2)}) %collective-permute-start.5) | collective-permute-done | bytes 327712 | tf_op jit(solution)/shard_map/while/body/ppermute | solution.py:90
  72.9 1.0 bitcast_select_fusion.11
  73.9 0.1 broadcast_in_dim.145
  74.0 0.6 collective-permute-start.12
  74.7 1.6 collective-permute-done.9
  76.2 2.5 %bitcast_select_fusion.3.refs_0_ = bf16[1024,640]{1,0:T(8,128)(2,1)} fusion(pred[1024]{0:T(1024)(128)(4,1)S(1)} %broadcast_in_dim.146, bf16[512,640]{1,0:T(8,128)(2,1)S(1)} %collective-permute-done.9, bf16[512,640]{1,0:T(8,128)(2,1)} %get-tuple-element.148), kind=kLoop, calls=%fused_computation.18 | loop fusion | flops 655360 | bytes 2622464 | tf_op jit(solution)/shard_map/jit(_where)/select_n | solution.py:119
  78.7 0.6 collective-permute-done.10.refs_5_
  79.3 1.3 copy-done
  80.6 5.7 %convolution_bitcast_fusion.1 = f32[1024,256]{1,0:T(8,128)S(1)} fusion(bf16[1024,4096]{1,0:T(8,128)(2,1)} %left_ref.1, bf16[4096,256]{1,0:T(8,128)(2,1)S(1)} %collective-permute-done.10.refs_5_), kind=kOutput, calls=%fused_computation.17 | convolution fusion | flops 2147483648 | bytes 11534336 | tf_op jit(solution)/shard_map/dot_general | solution.py:25
  86.3 0.1 pad_maximum_fusion
  86.4 0.8 broadcast_in_dim.155
  87.2 37.5 %while.34 = (s32[]{:T(128)}, bf16[512,384]{1,0:T(8,128)(2,1)}, s32[]{:T(128)}, pred[]{:T(512)}, f32[1024,384]{1,0:T(8,128)S(1)}, /*index=5*/s32[]{:T(128)}, bf16[]{:T(256)}) while((s32[]{:T(128)}, bf16[512,384]{1,0:T(8,128)(2,1)}, s32[]{:T(128)}, pred[]{:T(512)}, f32[1024,384]{1,0:T(8,128)S(1)}, /*index=5*/s32[]{:T(128)}, bf16[]{:T(256)}) %tuple.83), condition=%wide.region_6.7_spmd, body=%wide.region_4.6_spmd.sunk | while | flops 958466 | bytes 12681397 | solution.py:103
  87.2 0.1 slice_select_fusion.8
  87.3 0.1 collective-permute-start.6
  87.4 2.3 %collective-permute-done.6 = f32[512,384]{1,0:T(8,128)S(1)} collective-permute-done((f32[512,384]{1,0:T(8,128)S(1)}, f32[512,384]{1,0:T(8,128)S(1)}, u32[]{:S(2)}, u32[]{:S(2)}) %collective-permute-start.6) | collective-permute-done | bytes 786464 | tf_op jit(solution)/shard_map/while/body/ppermute | solution.py:90
  89.7 0.1 add_convert_fusion.6
  89.8 18.6 %all_to_all.44 = bf16[8,64,384]{2,1,0:T(8,128)(2,1)S(1)} all-to-all(bf16[8,64,384]{2,1,0:T(8,128)(2,1)S(1)} %bitcast.60), channel_id=1, replica_groups={{0,2,4,6,8,10,12,14},{1,3,5,7,9,11,13,15},{16,18,20,22,24,26,28,30},{17..., dimensions={0} | all-to-all | bytes 786432 | tf_op jit(solution)/shard_map/while/body/all_to_all | solution.py:129
  108.4 0.8 tile.11
  109.2 3.5 %all-to-all-start.1 = ((bf16[8,64,384]{2,1,0:T(8,128)(2,1)}), bf16[8,64,384]{2,1,0:T(8,128)(2,1)S(1)}, u32[]{:S(2)}, u32[]{:S(2)}) async-start(bf16[8,64,384]{2,1,0:T(8,128)(2,1)} %tile.11), calls=%async_computation.1 | async-start | bytes 786432 | tf_op jit(solution)/shard_map/while/body/all_to_all | solution.py:129
  112.7 11.3 %all-to-all-done.1 = bf16[8,64,384]{2,1,0:T(8,128)(2,1)S(1)} async-done(((bf16[8,64,384]{2,1,0:T(8,128)(2,1)}), bf16[8,64,384]{2,1,0:T(8,128)(2,1)S(1)}, u32[]{:S(2)}, u32[]{:S(2)}) %all-to-all-start.1) | async-done | bytes 393248 | tf_op jit(solution)/shard_map/while/body/all_to_all | solution.py:129
  124.0 0.8 copy-done.1
  124.8 1.9 %collective-permute-done.11 = bf16[512,384]{1,0:T(8,128)(2,1)S(1)} collective-permute-done((bf16[512,384]{1,0:T(8,128)(2,1)}, bf16[512,384]{1,0:T(8,128)(2,1)S(1)}, u32[]{:S(2)}, u32[]{:S(2)}) %collective-permute-start.11) | collective-permute-done | bytes 393248 | tf_op jit(solution)/shard_map/ppermute | solution.py:90
  126.7 2.1 %bitcast_select_fusion.4.refs_1_ = bf16[1024,384]{1,0:T(8,128)(2,1)} fusion(pred[1024]{0:T(1024)(128)(4,1)S(1)} %broadcast_in_dim.146, bf16[512,384]{1,0:T(8,128)(2,1)S(1)} %collective-permute-done.11, bf16[512,384]{1,0:T(8,128)(2,1)} %get-tuple-element.150), kind=kLoop, calls=%fused_computation.20 | loop fusion | flops 393216 | bytes 1573888 | tf_op jit(solution)/shard_map/jit(_where)/select_n | solution.py:119
  128.8 6.3 %convolution_bitcast_fusion = f32[1024,256]{1,0:T(8,128)S(1)} fusion(bf16[1024,4096]{1,0:T(8,128)(2,1)} %left_ref.1, bf16[4096,256]{1,0:T(8,128)(2,1)} %collective-permute-done.12.refs_6_), kind=kOutput, calls=%fused_computation.16 | convolution fusion | flops 2147483648 | bytes 11534336 | tf_op jit(solution)/shard_map/dot_general | solution.py:25
  135.2 0.2 collective-permute-start.13
  135.4 1.8 collective-permute-done.13
  137.2 0.1 add_convert_fusion.2
  137.3 12.7 %all_to_all.42 = bf16[8,64,256]{2,1,0:T(8,128)(2,1)S(1)} all-to-all(bf16[8,64,256]{2,1,0:T(8,128)(2,1)S(1)} %bitcast.64), channel_id=1, replica_groups={{0,2,4,6,8,10,12,14},{1,3,5,7,9,11,13,15},{16,18,20,22,24,26,28,30},{17..., dimensions={0} | all-to-all | bytes 524288 | tf_op jit(solution)/shard_map/all_to_all | solution.py:129
  150.0 12.0 %all_to_all.43 = bf16[8,64,256]{2,1,0:T(8,128)(2,1)S(1)} all-to-all(bf16[8,64,256]{2,1,0:T(8,128)(2,1)S(1)} %tile.4), channel_id=1, replica_groups={{0,2,4,6,8,10,12,14},{1,3,5,7,9,11,13,15},{16,18,20,22,24,26,28,30},{17..., dimensions={0} | all-to-all | bytes 524288 | tf_op jit(solution)/shard_map/all_to_all | solution.py:129
  162.0 1.5 collective-permute-done.14
  163.5 1.0 bitcast_select_fusion.5.refs_2_
  164.5 16.8 %shard_map.38 = bf16[1024,4096]{1,0:T(8,128)(2,1)} custom-call(bf16[1024,4096]{1,0:T(8,128)(2,1)} %base_ref.1, bf16[1024,640]{1,0:T(8,128)(2,1)} %bitcast_select_fusion.3.refs_0_, bf16[1024,384]{1,0:T(8,128)(2,1)} %bitcast_select_fusion.4.refs_1_, bf16[1024,256]{1,0:T(8,128)(2,1)} %bitcast_select_fusion.5.refs_2_, bf16[4096,640]{1,0:T(8,128)(2,1)} %refs_3_.1, ...), custom_call_target="tpu_custom_call" | custom-call | tf_op jit(solution)/shard_map/pallas_call | solution.py:73
  (24 shorter events, 0.4 us)
Async XLA Ops:
  2.3 29.0 %collective-permute-start.7 = (bf16[4096,128]{1,0:T(8,128)(2,1)}, bf16[4096,128]{1,0:T(8,128)(2,1)}, u32[]{:S(2)}, u32[]{:S(2)}) collective-permute-start(bf16[4096,128]{1,0:T(8,128)(2,1)} %slice.9), channel_id=1, source_target_pairs={{0,16},{16,0},{1,17},{17,1},{2,18},{18,2},{3,19},{19,3},{4,20},{20... | collective-permute-start | bytes 3145736 | tf_op jit(solution)/shard_map/ppermute | solution.py:140
  17.4 3.4 %collective-permute-start = (f32[512,640]{1,0:T(8,128)}, f32[512,640]{1,0:T(8,128)}, u32[]{:S(2)}, u32[]{:S(2)}) collective-permute-start(f32[512,640]{1,0:T(8,128)} %slice_select_fusion.7), channel_id=1, source_target_pairs={{0,1},{1,0},{2,3},{3,2},{4,5},{5,4},{6,7},{7,6},{8,9},{9,8},{10,11... | collective-permute-start | bytes 3932168 | tf_op jit(solution)/shard_map/while/body/ppermute | solution.py:90
  24.7 16.9 %collective-permute-start.8 = (f32[256,640]{1,0:T(8,128)S(1)}, f32[256,640]{1,0:T(8,128)}, u32[]{:S(2)}, u32[]{:S(2)}) collective-permute-start(f32[256,640]{1,0:T(8,128)S(1)} %get-tuple-element.189), channel_id=1, source_target_pairs={{0,2},{1,3},{2,0},{3,1},{4,6},{5,7},{6,4},{7,5},{8,10},{9,11},{10,... | collective-permute-start | bytes 1966088 | tf_op jit(solution)/shard_map/ppermute | solution.py:90
  30.8 48.5 %collective-permute-start.10 = (bf16[4096,256]{1,0:T(8,128)(2,1)}, bf16[4096,256]{1,0:T(8,128)(2,1)S(1)}, u32[]{:S(2)}, u32[]{:S(2)}) collective-permute-start(bf16[4096,256]{1,0:T(8,128)(2,1)} %get-tuple-element.145), channel_id=1, source_target_pairs={{0,16},{16,0},{1,17},{17,1},{2,18},{18,2},{3,19},{19,3},{4,20},{20... | collective-permute-start | bytes 6291464 | tf_op jit(solution)/shard_map/ppermute | solution.py:140
  43.7 5.5 %collective-permute-start.1 = (bf16[128,640]{1,0:T(8,128)(2,1)S(1)}, bf16[128,640]{1,0:T(8,128)(2,1)S(1)}, u32[]{:S(2)}, u32[]{:S(2)}) collective-permute-start(bf16[128,640]{1,0:T(8,128)(2,1)S(1)} %select_convert_fusion.4), channel_id=1, source_target_pairs={{0,4},{1,5},{2,6},{3,7},{4,0},{5,1},{6,2},{7,3},{8,12},{9,13},{10,... | collective-permute-start | bytes 491528 | tf_op jit(solution)/shard_map/while/body/ppermute | solution.py:90
  49.3 5.4 %collective-permute-start.2 = (bf16[64,640]{1,0:T(8,128)(2,1)S(1)}, bf16[64,640]{1,0:T(8,128)(2,1)S(1)}, u32[]{:S(2)}, u32[]{:S(2)}) collective-permute-start(bf16[64,640]{1,0:T(8,128)(2,1)S(1)} %select_convert_fusion.5), channel_id=1, source_target_pairs={{0,8},{1,9},{2,10},{3,11},{4,12},{5,13},{6,14},{7,15},{8,0},{9,1},... | collective-permute-start | bytes 245768 | tf_op jit(solution)/shard_map/while/body/ppermute | solution.py:90
  54.7 5.5 %collective-permute-start.3 = (bf16[64,640]{1,0:T(8,128)(2,1)S(1)}, bf16[64,640]{1,0:T(8,128)(2,1)S(1)}, u32[]{:S(2)}, u32[]{:S(2)}) collective-permute-start(bf16[64,640]{1,0:T(8,128)(2,1)S(1)} %add_convert_fusion.5), channel_id=1, source_target_pairs={{0,8},{1,9},{2,10},{3,11},{4,12},{5,13},{6,14},{7,15},{8,0},{9,1},... | collective-permute-start | bytes 245768 | tf_op jit(solution)/shard_map/while/body/ppermute | solution.py:90
  60.3 5.4 %collective-permute-start.4 = (bf16[128,640]{1,0:T(8,128)(2,1)S(1)}, bf16[128,640]{1,0:T(8,128)(2,1)S(1)}, u32[]{:S(2)}, u32[]{:S(2)}) collective-permute-start(bf16[128,640]{1,0:T(8,128)(2,1)S(1)} %bitcast_select_fusion.9), channel_id=1, source_target_pairs={{0,4},{1,5},{2,6},{3,7},{4,0},{5,1},{6,2},{7,3},{8,12},{9,13},{10,... | collective-permute-start | bytes 491528 | tf_op jit(solution)/shard_map/while/body/ppermute | solution.py:90
  65.8 7.1 %collective-permute-start.5 = (bf16[256,640]{1,0:T(8,128)(2,1)S(1)}, bf16[256,640]{1,0:T(8,128)(2,1)S(1)}, u32[]{:S(2)}, u32[]{:S(2)}) collective-permute-start(bf16[256,640]{1,0:T(8,128)(2,1)S(1)} %bitcast_select_fusion.10), channel_id=1, source_target_pairs={{0,2},{1,3},{2,0},{3,1},{4,6},{5,7},{6,4},{7,5},{8,10},{9,11},{10,... | collective-permute-start | bytes 983048 | tf_op jit(solution)/shard_map/while/body/ppermute | solution.py:90
  73.9 2.3 %collective-permute-start.9 = (bf16[512,640]{1,0:T(8,128)(2,1)}, bf16[512,640]{1,0:T(8,128)(2,1)S(1)}, u32[]{:S(2)}, u32[]{:S(2)}) collective-permute-start(bf16[512,640]{1,0:T(8,128)(2,1)} %get-tuple-element.148), channel_id=1, source_target_pairs={{0,1},{1,0},{2,3},{3,2},{4,5},{5,4},{6,7},{7,6},{8,9},{9,8},{10,11... | collective-permute-start | bytes 1966088 | tf_op jit(solution)/shard_map/ppermute | solution.py:90
  74.0 54.8 %collective-permute-start.12 = (bf16[4096,256]{1,0:T(8,128)(2,1)}, bf16[4096,256]{1,0:T(8,128)(2,1)}, u32[]{:S(2)}, u32[]{:S(2)}) collective-permute-start(bf16[4096,256]{1,0:T(8,128)(2,1)} %get-tuple-element.151), channel_id=1, source_target_pairs={{0,16},{16,0},{1,17},{17,1},{2,18},{18,2},{3,19},{19,3},{4,20},{20... | collective-permute-start | bytes 6291464 | tf_op jit(solution)/shard_map/ppermute | solution.py:140
  78.7 7.6 %copy-start.2 = (f32[1024,128]{1,0:T(8,128)S(1)}, f32[1024,128]{1,0:T(8,128)}, u32[]{:S(2)}) copy-start(f32[1024,128]{1,0:T(8,128)} %convolution_bitcast_fusion.2) | copy-start | bytes 1572868
  79.3 1.3 copy-start
  87.3 2.4 %collective-permute-start.6 = (f32[512,384]{1,0:T(8,128)S(1)}, f32[512,384]{1,0:T(8,128)S(1)}, u32[]{:S(2)}, u32[]{:S(2)}) collective-permute-start(f32[512,384]{1,0:T(8,128)S(1)} %slice_select_fusion.8), channel_id=1, source_target_pairs={{0,1},{1,0},{2,3},{3,2},{4,5},{5,4},{6,7},{7,6},{8,9},{9,8},{10,11... | collective-permute-start | bytes 2359304 | tf_op jit(solution)/shard_map/while/body/ppermute | solution.py:90
  109.2 14.8 %all-to-all-start.1 = ((bf16[8,64,384]{2,1,0:T(8,128)(2,1)}), bf16[8,64,384]{2,1,0:T(8,128)(2,1)S(1)}, u32[]{:S(2)}, u32[]{:S(2)}) async-start(bf16[8,64,384]{2,1,0:T(8,128)(2,1)} %tile.11), calls=%async_computation.1 | async-start | bytes 786432 | tf_op jit(solution)/shard_map/while/body/all_to_all | solution.py:129
  124.0 0.8 copy-start.1
  124.8 1.9 %collective-permute-start.11 = (bf16[512,384]{1,0:T(8,128)(2,1)}, bf16[512,384]{1,0:T(8,128)(2,1)S(1)}, u32[]{:S(2)}, u32[]{:S(2)}) collective-permute-start(bf16[512,384]{1,0:T(8,128)(2,1)} %get-tuple-element.150), channel_id=1, source_target_pairs={{0,1},{1,0},{2,3},{3,2},{4,5},{5,4},{6,7},{7,6},{8,9},{9,8},{10,11... | collective-permute-start | bytes 1179656 | tf_op jit(solution)/shard_map/ppermute | solution.py:90
  135.2 2.0 %collective-permute-start.13 = (f32[512,256]{1,0:T(8,128)S(1)}, f32[512,256]{1,0:T(8,128)S(1)}, u32[]{:S(2)}, u32[]{:S(2)}) collective-permute-start(f32[512,256]{1,0:T(8,128)S(1)} %slice_select_fusion.4), channel_id=1, source_target_pairs={{0,1},{1,0},{2,3},{3,2},{4,5},{5,4},{6,7},{7,6},{8,9},{9,8},{10,11... | collective-permute-start | bytes 1572872 | tf_op jit(solution)/shard_map/ppermute | solution.py:90
  162.0 1.5 collective-permute-start.14

commit v4 on v3

--- a/solution.py
+++ b/solution.py
@@ -91,16 +91,13 @@
 
     def body(amplitudes, residual_in, cholesky):
         me = lax.axis_index("col")
-        once = 1 + (me >> 20)
+        boxes = (me >> 20) == 0
 
         def boxed(run, *values):
-            shapes = jax.eval_shape(run, *values)
-            zeros = jax.tree.map(lambda s: jnp.zeros(s.shape, s.dtype), shapes)
+            def never(*values):
+                return jax.tree.map(lambda s: jnp.zeros(s.shape, s.dtype), jax.eval_shape(run, *values))
 
-            def trip(state):
-                return state[0] + 1, run(*[after(value, state[0]) for value in values])
-
-            return lax.while_loop(lambda state: state[0] < once, trip, (jnp.int32(0), zeros))[1]
+            return lax.cond(boxes, run, never, *values)
 
         bits = [1 << k for k in range(cols.bit_length() - 1)]
         upper = [(me & bit) != 0 for bit in bits]
@@ -120,7 +117,7 @@
 
         def finish(value):
             value = halve(halve(value, 2, jnp.bfloat16), 3, jnp.bfloat16).astype(jnp.bfloat16)
-            return double(double(double(value, 3), 2), 1)
+            return double(double(value, 3), 2)
 
         mates = [[i for i in range(cols) if i % 2 == core] for core in range(2)]
         count = cols // 2
@@ -128,23 +125,20 @@
         def spread(value):
             return lax.all_to_all(value, "col", 0, 0, tiled=True, axis_index_groups=mates)
 
-        def scatter(value, kind=jnp.float32):
-            value = halve(value, 0, jnp.float32)
-            parts = spread(value.astype(kind)).astype(jnp.float32)
-            return jnp.sum(parts.reshape(count, parts.shape[0] // count, -1), axis=0).astype(jnp.bfloat16)
-
-        def gather(value):
-            return spread(jnp.tile(value, (count, 1)))
+        def chain(value):
+            parts = spread(halve(value, 0, jnp.float32).astype(jnp.bfloat16)).astype(jnp.float32)
+            mine = jnp.sum(parts.reshape(count, parts.shape[0] // count, -1), axis=0).astype(jnp.bfloat16)
+            return spread(jnp.tile(mine, (count, 1)))
 
         def send_row(vectors, shift):
             return lax.ppermute(vectors, "row", [(i, (i + shift) % rows) for i in range(rows)])
 
         if rows != 2 or len(bits) != 4 or sum(GROUPS) != cholesky.shape[1]:
             rest = jnp.concatenate([send_row(cholesky, shift) for shift in range(1, rows)], axis=1)
-            chi = double(gather(scatter(project(amplitudes, cholesky))), 0)
+            chi = double(chain(project(amplitudes, cholesky)), 0)
             total = project_back(residual_in, [chi], [cholesky], jnp.float32)
             rest = after(rest, total)
-            chi = double(gather(scatter(project(amplitudes, rest))), 0)
+            chi = double(chain(project(amplitudes, rest)), 0)
             return project_back(total, [chi], [rest], jnp.bfloat16)
 
         ends = [sum(GROUPS[: k + 1]) for k in range(len(GROUPS))]
@@ -156,13 +150,14 @@
         out_b = after(out_b, send)
         b = send_row(out_b, 1)
         part_a = project(amplitudes, after(a, out_b))
-        half_own = boxed(finish, after(keep, part_a) + got)
-        c = send_row(after(out_c, half_own), 1)
-        chi_own = double(half_own, 0)
-        part = jnp.concatenate([part_a, project(amplitudes, after(b, chi_own))], axis=1)
-        chi_ab = double(boxed(lambda v: gather(scatter(v, jnp.bfloat16)), part), 0)
-        chi_c = double(gather(scatter(project(amplitudes, after(c, chi_ab)), jnp.bfloat16)), 0)
-        return project_back(residual_in, [chi_own, chi_ab, chi_c], [cholesky, a, b, c], jnp.bfloat16)
+        quarter = boxed(finish, after(keep, part_a) + got)
+        c = send_row(after(out_c, quarter), 1)
+        chi_a = double(boxed(chain, after(part_a, quarter)), 0)
+        part_b = project(amplitudes, after(b, chi_a))
+        chi_own, half_b = boxed(lambda u, v: (double(double(u, 1), 0), chain(v)), quarter, part_b)
+        chi_b = double(half_b, 0)
+        chi_c = double(chain(project(amplitudes, after(c, chi_b))), 0)
+        return project_back(residual_in, [chi_own, chi_a, chi_b, chi_c], [cholesky, a, b, c], jnp.bfloat16)
 
     in_specs = (P("row", "col"), P("row", "col"), P("col", "row"))
     return jax.shard_map(body, mesh=mesh, in_specs=in_specs, out_specs=P("row", "col"), check_vma=False)

time: 182 us -> 186 us (1.022)
  other arithmetic: 13.8 us -> 7.51 us
  blocking collectives: 43.2 us -> 48.5 us
  waiting for transfers between devices: 45.9 us -> 50.8 us
  starting transfers between devices: 20.1 us -> 24.2 us
  local copies, waits for them, and re-layouts: 12.9 us -> 9.49 us
    all_to_all x3 -> x4, blocking collectives: 43.2 us -> 48.5 us  [spread(): lax.all_to_all(value, 'col', 0, 0, tiled=True, axis_index_groups=mates)]
    all_to_all x1 -> x2, starting transfers between devices: 3.45 us -> 7.47 us  [spread(): lax.all_to_all(value, 'col', 0, 0, tiled=True, axis_index_groups=mates)]
    broadcast_in_dim x3 -> x0, local copies, waits for them, and re-layouts: 2.83 us -> none  [boxed(): zeros = jax.tree.map(lambda s: jnp.zeros(s.shape, s.dtype), shapes)]
    ppermute x12 -> x14, waiting for transfers between devices: 33.9 us -> 36.6 us  [exchange(): return lax.ppermute(value, 'col', [(i, i ^ bit) for i in range(cols)])]
    select_n x4 -> x5, other arithmetic: 2.71 us -> 0.39 us  [split(): jnp.where(upper[step], low, high)]
    select_n x6 -> x7, other arithmetic: 6.78 us -> 4.5 us  [double(): jnp.where(mine, value, got).reshape(2 * value.shape[0], value.shape[1])]
    all_to_all x1 -> x2, waiting for transfers between devices: 11.3 us -> 12.8 us  [spread(): lax.all_to_all(value, 'col', 0, 0, tiled=True, axis_index_groups=mates)]
    ppermute x12 -> x14, starting transfers between devices: 12.5 us -> 12.1 us  [exchange(): return lax.ppermute(value, 'col', [(i, i ^ bit) for i in range(cols)])]
  transfers between devices with their start and end apart: 16 -> 19, of which waited for: 14 -> 16; matrix products, arithmetic and copies ran while one was open for 19% -> 14% of each run, Pallas kernels for 5% -> 5%
where the time goes in v4:
time: 186 us
  waiting for transfers between devices  50.8 us (27%)
  blocking collectives  48.5 us (26%)
  Pallas kernels  26.2 us (14%)
  starting transfers between devices  24.2 us (13%)
  matrix products  18.7 us (10%)
  local copies, waits for them, and re-layouts  9.49 us (5%)
  other arithmetic  7.51 us (4%)
    all_to_all x4, blocking collectives, spread(): lax.all_to_all(value, 'col', 0, 0, tiled=True, axis_index_groups=mates)  48.5 us
    ppermute x14, waiting for transfers between devices, exchange(): return lax.ppermute(value, 'col', [(i, i ^ bit) for i in range(cols)])  36.6 us
    dot_general x3, matrix products, project(): part = jnp.dot(amplitudes, vectors, preferred_element_type=jnp.float32)  18.7 us
    pallas_call x1, Pallas kernels, project_back(): pl.pallas_call(kernel, grid=(columns // block,), in_specs=[pl.BlockSpec((...  16.4 us
    all_to_all x2, waiting for transfers between devices, spread(): lax.all_to_all(value, 'col', 0, 0, tiled=True, axis_index_groups=mates)  12.8 us
    ppermute x14, starting transfers between devices, exchange(): return lax.ppermute(value, 'col', [(i, i ^ bit) for i in range(cols)])  12.1 us
    pallas_call x1, Pallas kernels, project_wide(): pl.pallas_call(kernel, grid=(steps,), in_specs=[pl.BlockSpec((rows, block...  9.81 us
    all_to_all x2, starting transfers between devices, spread(): lax.all_to_all(value, 'col', 0, 0, tiled=True, axis_index_groups=mates)  7.47 us
  transfers between devices with their start and end apart: 19, of which 16 were waited for; matrix products, arithmetic and copies ran while one was open for 14% of the time, Pallas kernels for 5%

profile of v4, /device:TPU:0, one launch (start us, length us, event | category | flops | bytes accessed | tf_op | source)
XLA Modules:
  0.0 185.7 jit_solution(1663702778663510246)
XLA Ops:
  0.0 2.3 %slice.9 = bf16[4096,128]{1,0:T(8,128)(2,1)} slice(bf16[4096,640]{1,0:T(8,128)(2,1)} %refs_4_.1), slice={[0:4096], [0:128]} | slice | bytes 2097152 | tf_op jit(solution)/shard_map/slice | solution.py:145
  2.3 2.9 %collective-permute-start.9 = (bf16[4096,128]{1,0:T(8,128)(2,1)}, bf16[4096,128]{1,0:T(8,128)(2,1)S(1)}, u32[]{:S(2)}, u32[]{:S(2)}) collective-permute-start(bf16[4096,128]{1,0:T(8,128)(2,1)} %slice.9), channel_id=1, source_target_pairs={{0,16},{16,0},{1,17},{17,1},{2,18},{18,2},{3,19},{19,3},{4,20},{20... | collective-permute-start | bytes 3145736 | tf_op jit(solution)/shard_map/ppermute | solution.py:134
  5.2 4.5 %fusion.1 = (bf16[4096,256]{1,0:T(8,128)(2,1)}, bf16[4096,256]{1,0:T(8,128)(2,1)}) fusion(bf16[4096,640]{1,0:T(8,128)(2,1)} %refs_4_.1), kind=kLoop, calls=%fused_computation.31 | loop fusion | bytes 8388608 | tf_op jit(solution)/shard_map/slice | solution.py:145
  9.8 9.8 %shard_map.37 = f32[1024,640]{1,0:T(8,128)S(1)} custom-call(bf16[1024,4096]{1,0:T(8,128)(2,1)} %left_ref.1, bf16[4096,640]{1,0:T(8,128)(2,1)} %refs_4_.1), custom_call_target="tpu_custom_call" | custom-call | tf_op jit(solution)/shard_map/pallas_call | solution.py:51
  19.6 5.9 %conditional.4 = (f32[512,640]{1,0:T(8,128)}, f32[256,640]{1,0:T(8,128)S(1)}, f32[256,640]{1,0:T(8,128)S(1)}) conditional(s32[]{:T(128)} %convert_element_type.68, () %tuple.48, (pred[]{:T(512)}, f32[1024,640]{1,0:T(8,128)S(1)}) %tuple.50), branch_computations={%region_0.0_spmd, %region_1.2_spmd} | conditional | flops 983040 | bytes 17039426 | solution.py:100
  19.6 0.1 slice_select_fusion
  19.8 3.0 %collective-permute-done.8 = f32[512,640]{1,0:T(8,128)S(1)} collective-permute-done((f32[512,640]{1,0:T(8,128)S(1)}, f32[512,640]{1,0:T(8,128)S(1)}, u32[]{:S(2)}, u32[]{:S(2)}) %collective-permute-start.8) | collective-permute-done | bytes 1310752 | tf_op jit(solution)/shard_map/cond/branch_1_fun/ppermute | solution.py:90
  22.8 1.3 select_add_fusion
  24.1 1.4 fusion
  25.5 0.1 broadcast_select_fusion
  25.6 0.1 collective-permute-start.11
  25.7 2.0 %collective-permute-start.10 = (f32[256,640]{1,0:T(8,128)S(1)}, f32[256,640]{1,0:T(8,128)S(1)}, u32[]{:S(2)}, u32[]{:S(2)}) collective-permute-start(f32[256,640]{1,0:T(8,128)S(1)} %get-tuple-element.85), channel_id=1, source_target_pairs={{0,2},{1,3},{2,0},{3,1},{4,6},{5,7},{6,4},{7,5},{8,10},{9,11},{10,... | collective-permute-start | bytes 1966088 | tf_op jit(solution)/shard_map/ppermute | solution.py:90
  27.7 1.4 collective-permute-done.9.refs_5_
  29.1 6.1 %convolution_bitcast_fusion.2 = f32[1024,128]{1,0:T(8,128)S(1)} fusion(bf16[1024,4096]{1,0:T(8,128)(2,1)} %left_ref.1, bf16[4096,128]{1,0:T(8,128)(2,1)S(1)} %collective-permute-done.9.refs_5_), kind=kOutput, calls=%fused_computation.21 | convolution fusion | flops 1073741824 | bytes 9961472 | tf_op jit(solution)/shard_map/dot_general | solution.py:25
  35.2 7.3 %collective-permute-done.10 = f32[256,640]{1,0:T(8,128)S(1)} collective-permute-done((f32[256,640]{1,0:T(8,128)S(1)}, f32[256,640]{1,0:T(8,128)S(1)}, u32[]{:S(2)}, u32[]{:S(2)}) %collective-permute-start.10) | collective-permute-done | bytes 655392 | tf_op jit(solution)/shard_map/ppermute | solution.py:90
  42.5 22.2 %conditional.5 = (bf16[256,640]{1,0:T(8,128)(2,1)S(1)}) conditional(s32[]{:T(128)} %convert_element_type.68, () %tuple.47, (s32[]{:T(128)}, f32[256,640]{1,0:T(8,128)S(1)}, f32[256,640]{1,0:T(8,128)S(1)}) %tuple.54), branch_computations={%region_2.3_spmd, %region_3.4_spmd} | conditional | flops 942090 | bytes 7292144 | solution.py:100
  42.6 1.8 collective-permute-start
  44.5 3.8 %collective-permute-done = bf16[128,640]{1,0:T(8,128)(2,1)S(1)} collective-permute-done((bf16[128,640]{1,0:T(8,128)(2,1)S(1)}, bf16[128,640]{1,0:T(8,128)(2,1)S(1)}, u32[]{:S(2)}, u32[]{:S(2)}) %collective-permute-start) | collective-permute-done | bytes 163872 | tf_op jit(solution)/shard_map/cond/branch_1_fun/ppermute | solution.py:90
  48.3 2.6 %collective-permute-start.1 = (bf16[64,640]{1,0:T(8,128)(2,1)S(1)}, bf16[64,640]{1,0:T(8,128)(2,1)S(1)}, u32[]{:S(2)}, u32[]{:S(2)}) collective-permute-start(bf16[64,640]{1,0:T(8,128)(2,1)S(1)} %select_convert_fusion.1), channel_id=1, source_target_pairs={{0,8},{1,9},{2,10},{3,11},{4,12},{5,13},{6,14},{7,15},{8,0},{9,1},... | collective-permute-start | bytes 245768 | tf_op jit(solution)/shard_map/cond/branch_1_fun/ppermute | solution.py:90
  50.9 0.1 broadcast_in_dim.112
  51.0 0.1 broadcast_in_dim.113
  51.1 2.6 %collective-permute-done.1 = bf16[64,640]{1,0:T(8,128)(2,1)S(1)} collective-permute-done((bf16[64,640]{1,0:T(8,128)(2,1)S(1)}, bf16[64,640]{1,0:T(8,128)(2,1)S(1)}, u32[]{:S(2)}, u32[]{:S(2)}) %collective-permute-start.1) | collective-permute-done | bytes 81952 | tf_op jit(solution)/shard_map/cond/branch_1_fun/ppermute | solution.py:90
  53.7 2.7 %collective-permute-start.2 = (bf16[64,640]{1,0:T(8,128)(2,1)S(1)}, bf16[64,640]{1,0:T(8,128)(2,1)S(1)}, u32[]{:S(2)}, u32[]{:S(2)}) collective-permute-start(bf16[64,640]{1,0:T(8,128)(2,1)S(1)} %add_convert_fusion), channel_id=1, source_target_pairs={{0,8},{1,9},{2,10},{3,11},{4,12},{5,13},{6,14},{7,15},{8,0},{9,1},... | collective-permute-start | bytes 245768 | tf_op jit(solution)/shard_map/cond/branch_1_fun/ppermute | solution.py:90
  56.5 2.7 %collective-permute-done.2 = bf16[64,640]{1,0:T(8,128)(2,1)S(1)} collective-permute-done((bf16[64,640]{1,0:T(8,128)(2,1)S(1)}, bf16[64,640]{1,0:T(8,128)(2,1)S(1)}, u32[]{:S(2)}, u32[]{:S(2)}) %collective-permute-start.2) | collective-permute-done | bytes 81952 | tf_op jit(solution)/shard_map/cond/branch_1_fun/ppermute | solution.py:90
  59.1 0.1 bitcast_select_fusion.1
  59.2 2.1 %collective-permute-start.3 = (bf16[128,640]{1,0:T(8,128)(2,1)S(1)}, bf16[128,640]{1,0:T(8,128)(2,1)S(1)}, u32[]{:S(2)}, u32[]{:S(2)}) collective-permute-start(bf16[128,640]{1,0:T(8,128)(2,1)S(1)} %bitcast_select_fusion.1), channel_id=1, source_target_pairs={{0,4},{1,5},{2,6},{3,7},{4,0},{5,1},{6,2},{7,3},{8,12},{9,13},{10,... | collective-permute-start | bytes 491528 | tf_op jit(solution)/shard_map/cond/branch_1_fun/ppermute | solution.py:90
  61.3 0.1 broadcast_bitcast_fusion
  61.4 3.3 %collective-permute-done.3 = bf16[128,640]{1,0:T(8,128)(2,1)S(1)} collective-permute-done((bf16[128,640]{1,0:T(8,128)(2,1)S(1)}, bf16[128,640]{1,0:T(8,128)(2,1)S(1)}, u32[]{:S(2)}, u32[]{:S(2)}) %collective-permute-start.3) | collective-permute-done | bytes 163872 | tf_op jit(solution)/shard_map/cond/branch_1_fun/ppermute | solution.py:90
  64.6 0.1 bitcast_select_fusion
  64.8 1.6 collective-permute-start.14
  66.4 25.7 %conditional.6 = (bf16[512,128]{1,0:T(8,128)(2,1)S(1)}) conditional(s32[]{:T(128)} %convert_element_type.68, () %tuple.55, (pred[]{:T(512)}, f32[1024,128]{1,0:T(8,128)S(1)}) %tuple.57), branch_computations={%region_4.5_spmd, %region_5.7_spmd} | conditional | flops 319488 | bytes 3571764 | solution.py:100
  66.5 1.5 collective-permute-done.4
  68.1 14.2 %all_to_all.46 = bf16[8,64,128]{2,1,0:T(8,128)(2,1)S(1)} all-to-all(bf16[8,64,128]{2,1,0:T(8,128)(2,1)S(1)} %bitcast.51), channel_id=1, replica_groups={{0,2,4,6,8,10,12,14},{1,3,5,7,9,11,13,15},{16,18,20,22,24,26,28,30},{17..., dimensions={0} | all-to-all | bytes 262144 | tf_op jit(solution)/shard_map/cond/branch_1_fun/all_to_all | solution.py:126
  82.3 9.8 %all_to_all.47 = bf16[8,64,128]{2,1,0:T(8,128)(2,1)S(1)} all-to-all(bf16[8,64,128]{2,1,0:T(8,128)(2,1)S(1)} %tile.2), channel_id=1, replica_groups={{0,2,4,6,8,10,12,14},{1,3,5,7,9,11,13,15},{16,18,20,22,24,26,28,30},{17..., dimensions={0} | all-to-all | bytes 262144 | tf_op jit(solution)/shard_map/cond/branch_1_fun/all_to_all | solution.py:126
  92.1 0.1 broadcast_in_dim.153
  92.2 1.2 collective-permute-done.12
  93.4 0.9 bitcast_select_fusion.6.refs_1_
  94.3 6.3 %convolution_bitcast_fusion.1 = f32[1024,256]{1,0:T(8,128)S(1)} fusion(bf16[1024,4096]{1,0:T(8,128)(2,1)} %left_ref.1, bf16[4096,256]{1,0:T(8,128)(2,1)} %collective-permute-done.11.refs_6_), kind=kOutput, calls=%fused_computation.20 | convolution fusion | flops 2147483648 | bytes 11534336 | tf_op jit(solution)/shard_map/dot_general | solution.py:25
  100.6 29.3 %conditional.7 = (bf16[1024,640]{1,0:T(8,128)(2,1)S(1)}, bf16[512,256]{1,0:T(8,128)(2,1)}) conditional(s32[]{:T(128)} %convert_element_type.68, () %tuple.46, (pred[]{:T(512)}, pred[]{:T(512)}, bf16[256,640]{1,0:T(8,128)(2,1)S(1)}, f32[1024,256]{1,0:T(8,128)S(1)}) %tuple.59), branch_computations={%region_7.8_spmd, %region_8.10_spmd} | conditional | flops 1622022 | bytes 15538406 | solution.py:100
  100.7 0.2 collective-permute-start.7
  100.9 0.2 collective-permute-start.5
  101.2 1.5 collective-permute-done.7
  102.7 0.8 add_convert_fusion.2
  103.5 3.4 %all-to-all-start.2 = ((bf16[8,64,256]{2,1,0:T(8,128)(2,1)}), bf16[8,64,256]{2,1,0:T(8,128)(2,1)S(1)}, u32[]{:S(2)}, u32[]{:S(2)}) async-start(bf16[8,64,256]{2,1,0:T(8,128)(2,1)} %bitcast.11), calls=%async_computation.2 | async-start | bytes 524288 | tf_op jit(solution)/shard_map/cond/branch_1_fun/all_to_all | solution.py:126
  107.0 0.1 broadcast_in_dim.126
  107.1 4.6 %collective-permute-done.5 = bf16[256,640]{1,0:T(8,128)(2,1)S(1)} collective-permute-done((bf16[256,640]{1,0:T(8,128)(2,1)S(1)}, bf16[256,640]{1,0:T(8,128)(2,1)S(1)}, u32[]{:S(2)}, u32[]{:S(2)}) %collective-permute-start.5) | collective-permute-done | bytes 327712 | tf_op jit(solution)/shard_map/cond/branch_1_fun/ppermute | solution.py:90
  111.6 0.2 bitcast_select_fusion.3
  111.9 4.5 %all-to-all-done.2 = bf16[8,64,256]{2,1,0:T(8,128)(2,1)S(1)} async-done(((bf16[8,64,256]{2,1,0:T(8,128)(2,1)}), bf16[8,64,256]{2,1,0:T(8,128)(2,1)S(1)}, u32[]{:S(2)}, u32[]{:S(2)}) %all-to-all-start.2) | async-done | bytes 262176 | tf_op jit(solution)/shard_map/cond/branch_1_fun/all_to_all | solution.py:126
  116.4 0.7 tile.4
  117.2 4.1 %all-to-all-start.3 = ((bf16[8,64,256]{2,1,0:T(8,128)(2,1)}), bf16[8,64,256]{2,1,0:T(8,128)(2,1)}, u32[]{:S(2)}, u32[]{:S(2)}) async-start(bf16[8,64,256]{2,1,0:T(8,128)(2,1)} %tile.4), calls=%async_computation.3 | async-start | bytes 524288 | tf_op jit(solution)/shard_map/cond/branch_1_fun/all_to_all | solution.py:126
  121.3 0.1 broadcast_in_dim.123
  121.4 0.3 bitcast_select_fusion.2
  121.6 8.3 %all-to-all-done.3 = bf16[8,64,256]{2,1,0:T(8,128)(2,1)} async-done(((bf16[8,64,256]{2,1,0:T(8,128)(2,1)}), bf16[8,64,256]{2,1,0:T(8,128)(2,1)}, u32[]{:S(2)}, u32[]{:S(2)}) %all-to-all-start.3) | async-done | bytes 262176 | tf_op jit(solution)/shard_map/cond/branch_1_fun/all_to_all | solution.py:126
  129.9 1.7 collective-permute-done.13
  131.7 2.0 %bitcast_select_fusion.5.refs_2_ = bf16[1024,256]{1,0:T(8,128)(2,1)} fusion(pred[1024]{0:T(1024)(128)(4,1)S(1)} %broadcast_in_dim.154, bf16[512,256]{1,0:T(8,128)(2,1)S(1)} %collective-permute-done.13, bf16[512,256]{1,0:T(8,128)(2,1)} %get-tuple-element.78), kind=kLoop, calls=%fused_computation.23 | loop fusion | flops 262144 | bytes 1049600 | tf_op jit(solution)/shard_map/jit(_where)/select_n | solution.py:116
  133.6 6.3 %convolution_bitcast_fusion = f32[1024,256]{1,0:T(8,128)S(1)} fusion(bf16[1024,4096]{1,0:T(8,128)(2,1)} %left_ref.1, bf16[4096,256]{1,0:T(8,128)(2,1)} %collective-permute-done.14.refs_7_), kind=kOutput, calls=%fused_computation.19 | convolution fusion | flops 2147483648 | bytes 11534336 | tf_op jit(solution)/shard_map/dot_general | solution.py:25
  140.0 0.2 collective-permute-start.15
  140.2 1.8 collective-permute-done.15
  142.0 0.1 add_convert_fusion.3
  142.1 12.6 %all_to_all.48 = bf16[8,64,256]{2,1,0:T(8,128)(2,1)S(1)} all-to-all(bf16[8,64,256]{2,1,0:T(8,128)(2,1)S(1)} %bitcast.50), channel_id=1, replica_groups={{0,2,4,6,8,10,12,14},{1,3,5,7,9,11,13,15},{16,18,20,22,24,26,28,30},{17..., dimensions={0} | all-to-all | bytes 524288 | tf_op jit(solution)/shard_map/all_to_all | solution.py:126
  154.8 12.0 %all_to_all.49 = bf16[8,64,256]{2,1,0:T(8,128)(2,1)S(1)} all-to-all(bf16[8,64,256]{2,1,0:T(8,128)(2,1)S(1)} %tile.11), channel_id=1, replica_groups={{0,2,4,6,8,10,12,14},{1,3,5,7,9,11,13,15},{16,18,20,22,24,26,28,30},{17..., dimensions={0} | all-to-all | bytes 524288 | tf_op jit(solution)/shard_map/all_to_all | solution.py:126
  166.7 1.5 collective-permute-done.16
  168.3 1.0 bitcast_select_fusion.4.refs_3_
  169.3 16.4 %shard_map.38 = bf16[1024,4096]{1,0:T(8,128)(2,1)} custom-call(bf16[1024,4096]{1,0:T(8,128)(2,1)} %base_ref.1, bf16[1024,640]{1,0:T(8,128)(2,1)S(1)} %get-tuple-element.77.refs_0_, bf16[1024,128]{1,0:T(8,128)(2,1)} %bitcast_select_fusion.6.refs_1_, bf16[1024,256]{1,0:T(8,128)(2,1)} %bitcast_select_fusion.5.refs_2_, ...), custom_call_target="tpu_custom_call" | custom-call | tf_op jit(solution)/shard_map/pallas_call | solution.py:73
  (33 shorter events, 0.9 us)
Async XLA Ops:
  2.3 26.8 %collective-permute-start.9 = (bf16[4096,128]{1,0:T(8,128)(2,1)}, bf16[4096,128]{1,0:T(8,128)(2,1)S(1)}, u32[]{:S(2)}, u32[]{:S(2)}) collective-permute-start(bf16[4096,128]{1,0:T(8,128)(2,1)} %slice.9), channel_id=1, source_target_pairs={{0,16},{16,0},{1,17},{17,1},{2,18},{18,2},{3,19},{19,3},{4,20},{20... | collective-permute-start | bytes 3145736 | tf_op jit(solution)/shard_map/ppermute | solution.py:134
  19.7 3.1 %collective-permute-start.8 = (f32[512,640]{1,0:T(8,128)S(1)}, f32[512,640]{1,0:T(8,128)S(1)}, u32[]{:S(2)}, u32[]{:S(2)}) collective-permute-start(f32[512,640]{1,0:T(8,128)S(1)} %slice_select_fusion), channel_id=1, source_target_pairs={{0,1},{1,0},{2,3},{3,2},{4,5},{5,4},{6,7},{7,6},{8,9},{9,8},{10,11... | collective-permute-start | bytes 3932168 | tf_op jit(solution)/shard_map/cond/branch_1_fun/ppermute | solution.py:90
  25.6 68.7 %collective-permute-start.11 = (bf16[4096,256]{1,0:T(8,128)(2,1)}, bf16[4096,256]{1,0:T(8,128)(2,1)}, u32[]{:S(2)}, u32[]{:S(2)}) collective-permute-start(bf16[4096,256]{1,0:T(8,128)(2,1)} %get-tuple-element.72), channel_id=1, source_target_pairs={{0,16},{16,0},{1,17},{17,1},{2,18},{18,2},{3,19},{19,3},{4,20},{20... | collective-permute-start | bytes 6291464 | tf_op jit(solution)/shard_map/ppermute | solution.py:134
  25.7 16.8 %collective-permute-start.10 = (f32[256,640]{1,0:T(8,128)S(1)}, f32[256,640]{1,0:T(8,128)S(1)}, u32[]{:S(2)}, u32[]{:S(2)}) collective-permute-start(f32[256,640]{1,0:T(8,128)S(1)} %get-tuple-element.85), channel_id=1, source_target_pairs={{0,2},{1,3},{2,0},{3,1},{4,6},{5,7},{6,4},{7,5},{8,10},{9,11},{10,... | collective-permute-start | bytes 1966088 | tf_op jit(solution)/shard_map/ppermute | solution.py:90
  29.1 6.1 %copy-start = (bf16[4096,128]{1,0:T(8,128)(2,1)}, bf16[4096,128]{1,0:T(8,128)(2,1)S(1)}, u32[]{:S(2)}) copy-start(bf16[4096,128]{1,0:T(8,128)(2,1)S(1)} %collective-permute-done.9.refs_5_) | copy-start | bytes 3145732
  42.6 5.6 %collective-permute-start = (bf16[128,640]{1,0:T(8,128)(2,1)S(1)}, bf16[128,640]{1,0:T(8,128)(2,1)S(1)}, u32[]{:S(2)}, u32[]{:S(2)}) collective-permute-start(bf16[128,640]{1,0:T(8,128)(2,1)S(1)} %select_convert_fusion), channel_id=1, source_target_pairs={{0,4},{1,5},{2,6},{3,7},{4,0},{5,1},{6,2},{7,3},{8,12},{9,13},{10,... | collective-permute-start | bytes 491528 | tf_op jit(solution)/shard_map/cond/branch_1_fun/ppermute | solution.py:90
  48.3 5.4 %collective-permute-start.1 = (bf16[64,640]{1,0:T(8,128)(2,1)S(1)}, bf16[64,640]{1,0:T(8,128)(2,1)S(1)}, u32[]{:S(2)}, u32[]{:S(2)}) collective-permute-start(bf16[64,640]{1,0:T(8,128)(2,1)S(1)} %select_convert_fusion.1), channel_id=1, source_target_pairs={{0,8},{1,9},{2,10},{3,11},{4,12},{5,13},{6,14},{7,15},{8,0},{9,1},... | collective-permute-start | bytes 245768 | tf_op jit(solution)/shard_map/cond/branch_1_fun/ppermute | solution.py:90
  53.7 5.4 %collective-permute-start.2 = (bf16[64,640]{1,0:T(8,128)(2,1)S(1)}, bf16[64,640]{1,0:T(8,128)(2,1)S(1)}, u32[]{:S(2)}, u32[]{:S(2)}) collective-permute-start(bf16[64,640]{1,0:T(8,128)(2,1)S(1)} %add_convert_fusion), channel_id=1, source_target_pairs={{0,8},{1,9},{2,10},{3,11},{4,12},{5,13},{6,14},{7,15},{8,0},{9,1},... | collective-permute-start | bytes 245768 | tf_op jit(solution)/shard_map/cond/branch_1_fun/ppermute | solution.py:90
  59.2 5.4 %collective-permute-start.3 = (bf16[128,640]{1,0:T(8,128)(2,1)S(1)}, bf16[128,640]{1,0:T(8,128)(2,1)S(1)}, u32[]{:S(2)}, u32[]{:S(2)}) collective-permute-start(bf16[128,640]{1,0:T(8,128)(2,1)S(1)} %bitcast_select_fusion.1), channel_id=1, source_target_pairs={{0,4},{1,5},{2,6},{3,7},{4,0},{5,1},{6,2},{7,3},{8,12},{9,13},{10,... | collective-permute-start | bytes 491528 | tf_op jit(solution)/shard_map/cond/branch_1_fun/ppermute | solution.py:90
  64.8 68.9 %collective-permute-start.14 = (bf16[4096,256]{1,0:T(8,128)(2,1)}, bf16[4096,256]{1,0:T(8,128)(2,1)}, u32[]{:S(2)}, u32[]{:S(2)}) collective-permute-start(bf16[4096,256]{1,0:T(8,128)(2,1)} %get-tuple-element.79), channel_id=1, source_target_pairs={{0,16},{16,0},{1,17},{17,1},{2,18},{18,2},{3,19},{19,3},{4,20},{20... | collective-permute-start | bytes 6291464 | tf_op jit(solution)/shard_map/ppermute | solution.py:134
  66.4 1.6 collective-permute-start.4
  92.1 1.3 collective-permute-start.12
  100.7 2.0 %collective-permute-start.7 = (f32[512,256]{1,0:T(8,128)S(1)}, f32[512,256]{1,0:T(8,128)S(1)}, u32[]{:S(2)}, u32[]{:S(2)}) collective-permute-start(f32[512,256]{1,0:T(8,128)S(1)} %slice_select_fusion.2), channel_id=1, source_target_pairs={{0,1},{1,0},{2,3},{3,2},{4,5},{5,4},{6,7},{7,6},{8,9},{9,8},{10,11... | collective-permute-start | bytes 1572872 | tf_op jit(solution)/shard_map/cond/branch_1_fun/ppermute | solution.py:90
  100.9 10.7 %collective-permute-start.5 = (bf16[256,640]{1,0:T(8,128)(2,1)S(1)}, bf16[256,640]{1,0:T(8,128)(2,1)S(1)}, u32[]{:S(2)}, u32[]{:S(2)}) collective-permute-start(bf16[256,640]{1,0:T(8,128)(2,1)S(1)} %get-tuple-element.55), channel_id=1, source_target_pairs={{0,2},{1,3},{2,0},{3,1},{4,6},{5,7},{6,4},{7,5},{8,10},{9,11},{10,... | collective-permute-start | bytes 983048 | tf_op jit(solution)/shard_map/cond/branch_1_fun/ppermute | solution.py:90
  103.5 12.9 %all-to-all-start.2 = ((bf16[8,64,256]{2,1,0:T(8,128)(2,1)}), bf16[8,64,256]{2,1,0:T(8,128)(2,1)S(1)}, u32[]{:S(2)}, u32[]{:S(2)}) async-start(bf16[8,64,256]{2,1,0:T(8,128)(2,1)} %bitcast.11), calls=%async_computation.2 | async-start | bytes 524288 | tf_op jit(solution)/shard_map/cond/branch_1_fun/all_to_all | solution.py:126
  111.8 9.6 %collective-permute-start.6 = (bf16[512,640]{1,0:T(8,128)(2,1)S(1)}, bf16[512,640]{1,0:T(8,128)(2,1)S(1)}, u32[]{:S(2)}, u32[]{:S(2)}) collective-permute-start(bf16[512,640]{1,0:T(8,128)(2,1)S(1)} %bitcast_select_fusion.3), channel_id=1, source_target_pairs={{0,1},{1,0},{2,3},{3,2},{4,5},{5,4},{6,7},{7,6},{8,9},{9,8},{10,11... | collective-permute-start | bytes 1966088 | tf_op jit(solution)/shard_map/cond/branch_1_fun/ppermute | solution.py:90
  117.2 12.7 %all-to-all-start.3 = ((bf16[8,64,256]{2,1,0:T(8,128)(2,1)}), bf16[8,64,256]{2,1,0:T(8,128)(2,1)}, u32[]{:S(2)}, u32[]{:S(2)}) async-start(bf16[8,64,256]{2,1,0:T(8,128)(2,1)} %tile.4), calls=%async_computation.3 | async-start | bytes 524288 | tf_op jit(solution)/shard_map/cond/branch_1_fun/all_to_all | solution.py:126
  129.9 1.7 collective-permute-start.13
  140.0 2.0 %collective-permute-start.15 = (f32[512,256]{1,0:T(8,128)S(1)}, f32[512,256]{1,0:T(8,128)S(1)}, u32[]{:S(2)}, u32[]{:S(2)}) collective-permute-start(f32[512,256]{1,0:T(8,128)S(1)} %slice_select_fusion.3), channel_id=1, source_target_pairs={{0,1},{1,0},{2,3},{3,2},{4,5},{5,4},{6,7},{7,6},{8,9},{9,8},{10,11... | collective-permute-start | bytes 1572872 | tf_op jit(solution)/shard_map/ppermute | solution.py:90
  166.7 1.5 collective-permute-start.16

commit v5 on v4

--- a/solution.py
+++ b/solution.py
@@ -60,27 +60,45 @@
     )(amplitudes, vectors)
 
 
-def project_back(base, chis, pieces, kind):
+def project_back(base, chis, pieces, upper, kind):
     rows, columns = base.shape
     block = block_of(columns, 1024)
+    half = rows // 2
+    widths = [mine.shape[1] for mine, _ in chis]
 
-    def kernel(base_ref, *refs):
-        left = jnp.concatenate([c[...] for c in refs[: len(chis)]], axis=1)
-        right = jnp.concatenate([p[...] for p in refs[len(chis) : -1]], axis=1)
-        term = lax.dot_general(left, right, (((1,), (1,)), ((), ())), preferred_element_type=jnp.float32)
-        refs[-1][...] = (base_ref[...].astype(jnp.float32) + term).astype(kind)
+    def kernel(upper_ref, base_ref, *refs):
+        chi_refs, piece_refs, (out_ref, left_ref) = refs[: 2 * len(chis)], refs[2 * len(chis) : -2], refs[-2:]
 
+        @pl.when(pl.program_id(0) == 0)
+        def _():
+            own = pl.multiple_of(upper_ref[0] * half, half)
+            other = pl.multiple_of((1 - upper_ref[0]) * half, half)
+            at = 0
+            for k, width in enumerate(widths):
+                left_ref[pl.ds(own, half), at : at + width] = chi_refs[2 * k][...]
+                left_ref[pl.ds(other, half), at : at + width] = chi_refs[2 * k + 1][...]
+                at += width
+
+        right = jnp.concatenate([p[...] for p in piece_refs], axis=1)
+        term = lax.dot_general(left_ref[...], right, (((1,), (1,)), ((), ())), preferred_element_type=jnp.float32)
+        out_ref[...] = (base_ref[...].astype(jnp.float32) + term).astype(kind)
+
+    halves = [h for pair in chis for h in pair]
     return pl.pallas_call(
         kernel,
-        grid=(columns // block,),
-        in_specs=[pl.BlockSpec((rows, block), lambda i: (0, i))]
-        + [pl.BlockSpec(chi.shape, lambda i: (0, 0), pipeline_mode=pl.Buffered(1)) for chi in chis]
-        + [pl.BlockSpec((block, piece.shape[1]), lambda i: (i, 0)) for piece in pieces],
-        out_specs=pl.BlockSpec((rows, block), lambda i: (0, i)),
+        grid_spec=pltpu.PrefetchScalarGridSpec(
+            num_scalar_prefetch=1,
+            grid=(columns // block,),
+            in_specs=[pl.BlockSpec((rows, block), lambda i, u: (0, i))]
+            + [pl.BlockSpec(h.shape, lambda i, u: (0, 0), pipeline_mode=pl.Buffered(1)) for h in halves]
+            + [pl.BlockSpec((block, piece.shape[1]), lambda i, u: (i, 0)) for piece in pieces],
+            out_specs=pl.BlockSpec((rows, block), lambda i, u: (0, i)),
+            scratch_shapes=[pltpu.VMEM((rows, sum(widths)), jnp.bfloat16)],
+        ),
         out_shape=jax.ShapeDtypeStruct(base.shape, kind),
         compiler_params=pltpu.CompilerParams(vmem_limit_bytes=VMEM_BYTES),
         cost_estimate=FREE,
-    )(base, *chis, *pieces)
+    )(upper, base, *halves, *pieces)
 
 
 def solution(mesh):
@@ -119,27 +137,40 @@
             value = halve(halve(value, 2, jnp.bfloat16), 3, jnp.bfloat16).astype(jnp.bfloat16)
             return double(double(value, 3), 2)
 
+        def both(value):
+            return value, exchange(value, 1)
+
+        flag = jnp.reshape(me & 1, (1,))
         mates = [[i for i in range(cols) if i % 2 == core] for core in range(2)]
         count = cols // 2
 
         def spread(value):
             return lax.all_to_all(value, "col", 0, 0, tiled=True, axis_index_groups=mates)
 
+        def scatter(value):
+            parts = spread(halve(value, 0, jnp.float32).astype(jnp.bfloat16)).astype(jnp.float32)
+            return jnp.sum(parts.reshape(count, parts.shape[0] // count, -1), axis=0).astype(jnp.bfloat16)
+
+        def gather(mine):
+            return spread(jnp.tile(mine, (count, 1)))
+
         def chain(value):
-            parts = spread(halve(value, 0, jnp.float32).astype(jnp.bfloat16)).astype(jnp.float32)
-            mine = jnp.sum(parts.reshape(count, parts.shape[0] // count, -1), axis=0).astype(jnp.bfloat16)
-            return spread(jnp.tile(mine, (count, 1)))
+            return gather(scatter(value))
+
+        def last(quarter, part):
+            mine = scatter(part)
+            return both(after(double(quarter, 1), mine)), gather(mine)
 
         def send_row(vectors, shift):
             return lax.ppermute(vectors, "row", [(i, (i + shift) % rows) for i in range(rows)])
 
         if rows != 2 or len(bits) != 4 or sum(GROUPS) != cholesky.shape[1]:
             rest = jnp.concatenate([send_row(cholesky, shift) for shift in range(1, rows)], axis=1)
-            chi = double(chain(project(amplitudes, cholesky)), 0)
-            total = project_back(residual_in, [chi], [cholesky], jnp.float32)
+            pair = both(chain(project(amplitudes, cholesky)))
+            total = project_back(residual_in, [pair], [cholesky], flag, jnp.float32)
             rest = after(rest, total)
-            chi = double(chain(project(amplitudes, rest)), 0)
-            return project_back(total, [chi], [rest], jnp.bfloat16)
+            pair = both(chain(project(amplitudes, rest)))
+            return project_back(total, [pair], [rest], flag, jnp.bfloat16)
 
         ends = [sum(GROUPS[: k + 1]) for k in range(len(GROUPS))]
         out_a, out_b, out_c = [cholesky[:, end - size : end] for end, size in zip(ends, GROUPS)]
@@ -152,12 +183,11 @@
         part_a = project(amplitudes, after(a, out_b))
         quarter = boxed(finish, after(keep, part_a) + got)
         c = send_row(after(out_c, quarter), 1)
-        chi_a = double(boxed(chain, after(part_a, quarter)), 0)
-        part_b = project(amplitudes, after(b, chi_a))
-        chi_own, half_b = boxed(lambda u, v: (double(double(u, 1), 0), chain(v)), quarter, part_b)
-        chi_b = double(half_b, 0)
-        chi_c = double(chain(project(amplitudes, after(c, chi_b))), 0)
-        return project_back(residual_in, [chi_own, chi_a, chi_b, chi_c], [cholesky, a, b, c], jnp.bfloat16)
+        part = jnp.concatenate([part_a, project(amplitudes, after(b, quarter))], axis=1)
+        own, half_ab = boxed(last, quarter, part)
+        pair_ab = both(half_ab)
+        pair_c = both(chain(project(amplitudes, after(c, *pair_ab))))
+        return project_back(residual_in, [own, pair_ab, pair_c], [cholesky, a, b, c], flag, jnp.bfloat16)
 
     in_specs = (P("row", "col"), P("row", "col"), P("col", "row"))
     return jax.shard_map(body, mesh=mesh, in_specs=in_specs, out_specs=P("row", "col"), check_vma=False)

time: 186 us -> 174 us (0.935)
  blocking collectives: 48.5 us -> 25 us
  waiting for transfers between devices: 50.8 us -> 60 us
  starting transfers between devices: 24.2 us -> 28.2 us
  other arithmetic: 7.51 us -> 4.29 us
    all_to_all x4 -> x2, blocking collectives: 48.5 us -> 25 us  [spread(): lax.all_to_all(value, 'col', 0, 0, tiled=True, axis_index_groups=mates)]
    ppermute x3, waiting for transfers between devices: 1.38 us -> 9.51 us  [send_row(): lax.ppermute(vectors, 'row', [(i, (i + shift) % rows) for i in range(rows)])]
    all_to_all x2, waiting for transfers between devices: 12.8 us -> 17.9 us  [spread(): lax.all_to_all(value, 'col', 0, 0, tiled=True, axis_index_groups=mates)]
    ppermute x14 -> x12, waiting for transfers between devices: 36.6 us -> 32.6 us  [exchange(): return lax.ppermute(value, 'col', [(i, i ^ bit) for i in range(cols)])]
    select_n x7 -> x3, other arithmetic: 4.5 us -> 1.22 us  [double(): jnp.where(mine, value, got).reshape(2 * value.shape[0], value.shape[1])]
    all_to_all x2, starting transfers between devices: 7.47 us -> 9.93 us  [spread(): lax.all_to_all(value, 'col', 0, 0, tiled=True, axis_index_groups=mates)]
    ppermute x14 -> x12, starting transfers between devices: 12.1 us -> 13.6 us  [exchange(): return lax.ppermute(value, 'col', [(i, i ^ bit) for i in range(cols)])]
  transfers between devices with their start and end apart: 19 -> 17, of which waited for: 16 -> 15; matrix products, arithmetic and copies ran while one was open for 14% -> 14% of each run, Pallas kernels for 5% -> 6%
where the time goes in v5:
time: 174 us; the launch traced here: 173 us
  waiting for transfers between devices  60 us (34%)
  starting transfers between devices  28.2 us (16%)
  Pallas kernels  26.8 us (15%)
  blocking collectives  25 us (14%)
  matrix products  19 us (11%)
  local copies, waits for them, and re-layouts  9.99 us (6%)
  other arithmetic  4.29 us (2%)
    ppermute x12, waiting for transfers between devices, exchange(): return lax.ppermute(value, 'col', [(i, i ^ bit) for i in range(cols)])  32.6 us
    all_to_all x2, blocking collectives, spread(): lax.all_to_all(value, 'col', 0, 0, tiled=True, axis_index_groups=mates)  25 us
    dot_general x3, matrix products, project(): part = jnp.dot(amplitudes, vectors, preferred_element_type=jnp.float32)  19 us
    all_to_all x2, waiting for transfers between devices, spread(): lax.all_to_all(value, 'col', 0, 0, tiled=True, axis_index_groups=mates)  17.9 us
    pallas_call x1, Pallas kernels, project_back(): pl.pallas_call(kernel, grid_spec=pltpu.PrefetchScalarGridSpec(num_scalar_...  17 us
    ppermute x12, starting transfers between devices, exchange(): return lax.ppermute(value, 'col', [(i, i ^ bit) for i in range(cols)])  13.6 us
    all_to_all x2, starting transfers between devices, spread(): lax.all_to_all(value, 'col', 0, 0, tiled=True, axis_index_groups=mates)  9.93 us
    pallas_call x1, Pallas kernels, project_wide(): pl.pallas_call(kernel, grid=(steps,), in_specs=[pl.BlockSpec((rows, block...  9.81 us
  transfers between devices with their start and end apart: 17, of which 15 were waited for; matrix products, arithmetic and copies ran while one was open for 14% of the time, Pallas kernels for 6%

profile of v5, /device:TPU:0, one launch (start us, length us, event | category | flops | bytes accessed | tf_op | source)
XLA Modules:
  0.0 173.5 jit_solution(16285381732144490102)
XLA Ops:
  0.0 2.3 %slice.9 = bf16[4096,128]{1,0:T(8,128)(2,1)} slice(bf16[4096,640]{1,0:T(8,128)(2,1)} %refs_6_.1), slice={[0:4096], [0:128]} | slice | bytes 2097152 | tf_op jit(solution)/shard_map/slice | solution.py:176
  2.3 2.9 %collective-permute-start.8 = (bf16[4096,128]{1,0:T(8,128)(2,1)}, bf16[4096,128]{1,0:T(8,128)(2,1)S(1)}, u32[]{:S(2)}, u32[]{:S(2)}) collective-permute-start(bf16[4096,128]{1,0:T(8,128)(2,1)} %slice.9), channel_id=1, source_target_pairs={{0,16},{16,0},{1,17},{17,1},{2,18},{18,2},{3,19},{19,3},{4,20},{20... | collective-permute-start | bytes 3145736 | tf_op jit(solution)/shard_map/ppermute | solution.py:165
  5.2 4.5 %fusion.1 = (bf16[4096,256]{1,0:T(8,128)(2,1)}, bf16[4096,256]{1,0:T(8,128)(2,1)}) fusion(bf16[4096,640]{1,0:T(8,128)(2,1)} %refs_6_.1), kind=kLoop, calls=%fused_computation.24 | loop fusion | bytes 8388608 | tf_op jit(solution)/shard_map/slice | solution.py:176
  9.7 9.8 %shard_map.37 = f32[1024,640]{1,0:T(8,128)S(1)} custom-call(bf16[1024,4096]{1,0:T(8,128)(2,1)} %left_ref.1, bf16[4096,640]{1,0:T(8,128)(2,1)} %refs_6_.1), custom_call_target="tpu_custom_call" | custom-call | tf_op jit(solution)/shard_map/pallas_call | solution.py:51
  19.5 5.9 %conditional.3 = (f32[512,640]{1,0:T(8,128)}, f32[256,640]{1,0:T(8,128)S(1)}, f32[256,640]{1,0:T(8,128)S(1)}) conditional(s32[]{:T(128)} %convert_element_type.49, () %tuple.42, (pred[]{:T(512)}, f32[1024,640]{1,0:T(8,128)S(1)}) %tuple.44), branch_computations={%region_0.0_spmd, %region_1.2_spmd} | conditional | flops 983040 | bytes 17039426 | solution.py:118
  19.6 0.1 slice_select_fusion
  19.7 0.1 collective-permute-start.7
  19.8 3.0 %collective-permute-done.7 = f32[512,640]{1,0:T(8,128)S(1)} collective-permute-done((f32[512,640]{1,0:T(8,128)S(1)}, f32[512,640]{1,0:T(8,128)S(1)}, u32[]{:S(2)}, u32[]{:S(2)}) %collective-permute-start.7) | collective-permute-done | bytes 1310752 | tf_op jit(solution)/shard_map/cond/branch_1_fun/ppermute | solution.py:108
  22.8 1.3 select_add_fusion
  24.1 1.4 fusion
  25.5 0.1 broadcast_select_fusion
  25.6 0.1 collective-permute-start.10
  25.7 2.0 %collective-permute-start.9 = (f32[256,640]{1,0:T(8,128)S(1)}, f32[256,640]{1,0:T(8,128)S(1)}, u32[]{:S(2)}, u32[]{:S(2)}) collective-permute-start(f32[256,640]{1,0:T(8,128)S(1)} %get-tuple-element.76), channel_id=1, source_target_pairs={{0,2},{1,3},{2,0},{3,1},{4,6},{5,7},{6,4},{7,5},{8,10},{9,11},{10,... | collective-permute-start | bytes 1966088 | tf_op jit(solution)/shard_map/ppermute | solution.py:108
  27.7 1.4 collective-permute-done.8.refs_7_
  29.1 6.1 %convolution_bitcast_fusion.2 = f32[1024,128]{1,0:T(8,128)S(1)} fusion(bf16[1024,4096]{1,0:T(8,128)(2,1)} %left_ref.1, bf16[4096,128]{1,0:T(8,128)(2,1)S(1)} %collective-permute-done.8.refs_7_), kind=kOutput, calls=%fused_computation.18 | convolution fusion | flops 1073741824 | bytes 9961472 | tf_op jit(solution)/shard_map/dot_general | solution.py:25
  35.2 7.3 %collective-permute-done.9 = f32[256,640]{1,0:T(8,128)S(1)} collective-permute-done((f32[256,640]{1,0:T(8,128)S(1)}, f32[256,640]{1,0:T(8,128)S(1)}, u32[]{:S(2)}, u32[]{:S(2)}) %collective-permute-start.9) | collective-permute-done | bytes 655392 | tf_op jit(solution)/shard_map/ppermute | solution.py:108
  42.5 22.2 %conditional.4 = (bf16[256,640]{1,0:T(8,128)(2,1)S(1)}) conditional(s32[]{:T(128)} %convert_element_type.49, () %tuple.41, (s32[]{:T(128)}, f32[256,640]{1,0:T(8,128)S(1)}, f32[256,640]{1,0:T(8,128)S(1)}) %tuple.48), branch_computations={%region_2.3_spmd, %region_3.4_spmd} | conditional | flops 942090 | bytes 7292144 | solution.py:118
  42.5 0.1 add.14
  42.6 1.8 %collective-permute-start = (bf16[128,640]{1,0:T(8,128)(2,1)S(1)}, bf16[128,640]{1,0:T(8,128)(2,1)S(1)}, u32[]{:S(2)}, u32[]{:S(2)}) collective-permute-start(bf16[128,640]{1,0:T(8,128)(2,1)S(1)} %select_convert_fusion), channel_id=1, source_target_pairs={{0,4},{1,5},{2,6},{3,7},{4,0},{5,1},{6,2},{7,3},{8,12},{9,13},{10,... | collective-permute-start | bytes 491528 | tf_op jit(solution)/shard_map/cond/branch_1_fun/ppermute | solution.py:108
  44.4 3.8 %collective-permute-done = bf16[128,640]{1,0:T(8,128)(2,1)S(1)} collective-permute-done((bf16[128,640]{1,0:T(8,128)(2,1)S(1)}, bf16[128,640]{1,0:T(8,128)(2,1)S(1)}, u32[]{:S(2)}, u32[]{:S(2)}) %collective-permute-start) | collective-permute-done | bytes 163872 | tf_op jit(solution)/shard_map/cond/branch_1_fun/ppermute | solution.py:108
  48.3 2.6 %collective-permute-start.1 = (bf16[64,640]{1,0:T(8,128)(2,1)S(1)}, bf16[64,640]{1,0:T(8,128)(2,1)S(1)}, u32[]{:S(2)}, u32[]{:S(2)}) collective-permute-start(bf16[64,640]{1,0:T(8,128)(2,1)S(1)} %select_convert_fusion.1), channel_id=1, source_target_pairs={{0,8},{1,9},{2,10},{3,11},{4,12},{5,13},{6,14},{7,15},{8,0},{9,1},... | collective-permute-start | bytes 245768 | tf_op jit(solution)/shard_map/cond/branch_1_fun/ppermute | solution.py:108
  50.9 0.1 broadcast_in_dim.54
  51.0 0.1 broadcast_in_dim.55
  51.1 2.6 %collective-permute-done.1 = bf16[64,640]{1,0:T(8,128)(2,1)S(1)} collective-permute-done((bf16[64,640]{1,0:T(8,128)(2,1)S(1)}, bf16[64,640]{1,0:T(8,128)(2,1)S(1)}, u32[]{:S(2)}, u32[]{:S(2)}) %collective-permute-start.1) | collective-permute-done | bytes 81952 | tf_op jit(solution)/shard_map/cond/branch_1_fun/ppermute | solution.py:108
  53.7 2.7 %collective-permute-start.2 = (bf16[64,640]{1,0:T(8,128)(2,1)S(1)}, bf16[64,640]{1,0:T(8,128)(2,1)S(1)}, u32[]{:S(2)}, u32[]{:S(2)}) collective-permute-start(bf16[64,640]{1,0:T(8,128)(2,1)S(1)} %add_convert_fusion), channel_id=1, source_target_pairs={{0,8},{1,9},{2,10},{3,11},{4,12},{5,13},{6,14},{7,15},{8,0},{9,1},... | collective-permute-start | bytes 245768 | tf_op jit(solution)/shard_map/cond/branch_1_fun/ppermute | solution.py:108
  56.4 2.7 %collective-permute-done.2 = bf16[64,640]{1,0:T(8,128)(2,1)S(1)} collective-permute-done((bf16[64,640]{1,0:T(8,128)(2,1)S(1)}, bf16[64,640]{1,0:T(8,128)(2,1)S(1)}, u32[]{:S(2)}, u32[]{:S(2)}) %collective-permute-start.2) | collective-permute-done | bytes 81952 | tf_op jit(solution)/shard_map/cond/branch_1_fun/ppermute | solution.py:108
  59.1 0.1 bitcast_select_fusion.1
  59.2 2.1 %collective-permute-start.3 = (bf16[128,640]{1,0:T(8,128)(2,1)S(1)}, bf16[128,640]{1,0:T(8,128)(2,1)S(1)}, u32[]{:S(2)}, u32[]{:S(2)}) collective-permute-start(bf16[128,640]{1,0:T(8,128)(2,1)S(1)} %bitcast_select_fusion.1), channel_id=1, source_target_pairs={{0,4},{1,5},{2,6},{3,7},{4,0},{5,1},{6,2},{7,3},{8,12},{9,13},{10,... | collective-permute-start | bytes 491528 | tf_op jit(solution)/shard_map/cond/branch_1_fun/ppermute | solution.py:108
  61.3 0.1 broadcast_bitcast_fusion
  61.4 3.3 %collective-permute-done.3 = bf16[128,640]{1,0:T(8,128)(2,1)S(1)} collective-permute-done((bf16[128,640]{1,0:T(8,128)(2,1)S(1)}, bf16[128,640]{1,0:T(8,128)(2,1)S(1)}, u32[]{:S(2)}, u32[]{:S(2)}) %collective-permute-start.3) | collective-permute-done | bytes 163872 | tf_op jit(solution)/shard_map/cond/branch_1_fun/ppermute | solution.py:108
  64.6 0.1 bitcast_select_fusion
  64.7 1.6 collective-permute-start.12
  66.3 8.1 %collective-permute-done.10.refs_8_ = bf16[4096,256]{1,0:T(8,128)(2,1)} collective-permute-done((bf16[4096,256]{1,0:T(8,128)(2,1)}, bf16[4096,256]{1,0:T(8,128)(2,1)}, u32[]{:S(2)}, u32[]{:S(2)}) %collective-permute-start.10) | collective-permute-done | bytes 2097184 | tf_op jit(solution)/shard_map/ppermute | solution.py:165
  74.4 6.3 %convolution_bitcast_fusion.1 = f32[1024,256]{1,0:T(8,128)S(1)} fusion(bf16[1024,4096]{1,0:T(8,128)(2,1)} %left_ref.1, bf16[4096,256]{1,0:T(8,128)(2,1)} %collective-permute-done.10.refs_8_), kind=kOutput, calls=%fused_computation.17 | convolution fusion | flops 2147483648 | bytes 11534336 | tf_op jit(solution)/shard_map/dot_general | solution.py:25
  80.8 0.1 pad_maximum_fusion
  80.9 37.6 %conditional.5 = (bf16[512,640]{1,0:T(8,128)(2,1)}, bf16[512,640]{1,0:T(8,128)(2,1)}, bf16[512,384]{1,0:T(8,128)(2,1)}) conditional(s32[]{:T(128)} %convert_element_type.49, () %tuple.40, (pred[]{:T(512)}, bf16[256,640]{1,0:T(8,128)(2,1)S(1)}, pred[]{:T(512)}, f32[1024,384]{1,0:T(8,128)S(1)}) %tuple.50), branch_computations={%region_4.5_spmd, %region_5.7_spmd} | conditional | flops 1286147 | bytes 16746721 | solution.py:118
  80.9 0.1 slice_select_fusion.1
  81.0 0.1 collective-permute-start.6
  81.1 2.3 %collective-permute-done.6 = f32[512,384]{1,0:T(8,128)S(1)} collective-permute-done((f32[512,384]{1,0:T(8,128)S(1)}, f32[512,384]{1,0:T(8,128)S(1)}, u32[]{:S(2)}, u32[]{:S(2)}) %collective-permute-start.6) | collective-permute-done | bytes 786464 | tf_op jit(solution)/shard_map/cond/branch_1_fun/ppermute | solution.py:108
  83.3 0.9 add_convert_fusion.1
  84.2 5.8 %all-to-all-start = ((bf16[8,64,384]{2,1,0:T(8,128)(2,1)}), bf16[8,64,384]{2,1,0:T(8,128)(2,1)S(1)}, u32[]{:S(2)}, u32[]{:S(2)}) async-start(bf16[8,64,384]{2,1,0:T(8,128)(2,1)} %bitcast.7), calls=%async_computation | async-start | bytes 786432 | tf_op jit(solution)/shard_map/cond/branch_1_fun/all_to_all | solution.py:148
  90.0 2.0 %collective-permute-start.4 = (bf16[256,640]{1,0:T(8,128)(2,1)S(1)}, bf16[256,640]{1,0:T(8,128)(2,1)S(1)}, u32[]{:S(2)}, u32[]{:S(2)}) collective-permute-start(bf16[256,640]{1,0:T(8,128)(2,1)S(1)} %get-tuple-element.45), channel_id=1, source_target_pairs={{0,2},{1,3},{2,0},{3,1},{4,6},{5,7},{6,4},{7,5},{8,10},{9,11},{10,... | collective-permute-start | bytes 983048 | tf_op jit(solution)/shard_map/cond/branch_1_fun/ppermute | solution.py:108
  92.0 10.0 %all-to-all-done = bf16[8,64,384]{2,1,0:T(8,128)(2,1)S(1)} async-done(((bf16[8,64,384]{2,1,0:T(8,128)(2,1)}), bf16[8,64,384]{2,1,0:T(8,128)(2,1)S(1)}, u32[]{:S(2)}, u32[]{:S(2)}) %all-to-all-start) | async-done | bytes 393248 | tf_op jit(solution)/shard_map/cond/branch_1_fun/all_to_all | solution.py:148
  102.0 0.1 reduce_sum.22
  102.1 0.8 tile.0
  102.8 4.1 %all-to-all-start.1 = ((bf16[8,64,384]{2,1,0:T(8,128)(2,1)}), bf16[8,64,384]{2,1,0:T(8,128)(2,1)}, u32[]{:S(2)}, u32[]{:S(2)}) async-start(bf16[8,64,384]{2,1,0:T(8,128)(2,1)} %tile.0), calls=%async_computation.1 | async-start | bytes 786432 | tf_op jit(solution)/shard_map/cond/branch_1_fun/all_to_all | solution.py:148
  107.0 0.1 broadcast_in_dim.65
  107.1 0.0 collective-permute-done.4
  107.1 1.0 bitcast_select_fusion.2
  108.1 0.0 collective-permute-start.5
  108.1 2.4 %collective-permute-done.5 = bf16[512,640]{1,0:T(8,128)(2,1)} collective-permute-done((bf16[512,640]{1,0:T(8,128)(2,1)}, bf16[512,640]{1,0:T(8,128)(2,1)}, u32[]{:S(2)}, u32[]{:S(2)}) %collective-permute-start.5) | collective-permute-done | bytes 655392 | tf_op jit(solution)/shard_map/cond/branch_1_fun/ppermute | solution.py:108
  110.5 8.0 %all-to-all-done.1 = bf16[8,64,384]{2,1,0:T(8,128)(2,1)} async-done(((bf16[8,64,384]{2,1,0:T(8,128)(2,1)}), bf16[8,64,384]{2,1,0:T(8,128)(2,1)}, u32[]{:S(2)}, u32[]{:S(2)}) %all-to-all-start.1) | async-done | bytes 393248 | tf_op jit(solution)/shard_map/cond/branch_1_fun/all_to_all | solution.py:148
  118.5 0.0 collective-permute-start.11
  118.5 1.9 %collective-permute-done.11.refs_3_ = bf16[512,384]{1,0:T(8,128)(2,1)S(1)} collective-permute-done((bf16[512,384]{1,0:T(8,128)(2,1)}, bf16[512,384]{1,0:T(8,128)(2,1)S(1)}, u32[]{:S(2)}, u32[]{:S(2)}) %collective-permute-start.11) | collective-permute-done | bytes 393248 | tf_op jit(solution)/shard_map/ppermute | solution.py:108
  120.4 6.6 %convolution_bitcast_fusion = f32[1024,256]{1,0:T(8,128)S(1)} fusion(bf16[1024,4096]{1,0:T(8,128)(2,1)} %left_ref.1, bf16[4096,256]{1,0:T(8,128)(2,1)S(1)} %collective-permute-done.12.refs_9_), kind=kOutput, calls=%fused_computation.16 | convolution fusion | flops 2147483648 | bytes 11534336 | tf_op jit(solution)/shard_map/dot_general | solution.py:25
  127.1 0.1 slice_select_fusion.2
  127.1 0.2 collective-permute-start.13
  127.3 1.8 %collective-permute-done.13 = f32[512,256]{1,0:T(8,128)S(1)} collective-permute-done((f32[512,256]{1,0:T(8,128)S(1)}, f32[512,256]{1,0:T(8,128)S(1)}, u32[]{:S(2)}, u32[]{:S(2)}) %collective-permute-start.13) | collective-permute-done | bytes 524320 | tf_op jit(solution)/shard_map/ppermute | solution.py:108
  129.1 0.1 add_convert_fusion.2
  129.2 13.0 %all_to_all.31 = bf16[8,64,256]{2,1,0:T(8,128)(2,1)S(1)} all-to-all(bf16[8,64,256]{2,1,0:T(8,128)(2,1)S(1)} %bitcast.33), channel_id=1, replica_groups={{0,2,4,6,8,10,12,14},{1,3,5,7,9,11,13,15},{16,18,20,22,24,26,28,30},{17..., dimensions={0} | all-to-all | bytes 524288 | tf_op jit(solution)/shard_map/all_to_all | solution.py:148
  142.3 12.0 %all_to_all.32 = bf16[8,64,256]{2,1,0:T(8,128)(2,1)S(1)} all-to-all(bf16[8,64,256]{2,1,0:T(8,128)(2,1)S(1)} %tile.4), channel_id=1, replica_groups={{0,2,4,6,8,10,12,14},{1,3,5,7,9,11,13,15},{16,18,20,22,24,26,28,30},{17..., dimensions={0} | all-to-all | bytes 524288 | tf_op jit(solution)/shard_map/all_to_all | solution.py:148
  154.3 1.5 collective-permute-done.14.refs_5_
  155.8 0.7 copy-done.4
  156.5 17.0 %shard_map.38 = bf16[1024,4096]{1,0:T(8,128)(2,1)} custom-call(s32[1]{0:T(128)} %bitcast.9.upper_ref, bf16[1024,4096]{1,0:T(8,128)(2,1)} %base_ref.1, bf16[512,640]{1,0:T(8,128)(2,1)} %get-tuple-element.67.refs_0_, bf16[512,640]{1,0:T(8,128)(2,1)} %get-tuple-element.68.refs_1_, bf16[512,384]{1,0:T(8,128)(2,1)} %get-tuple-element.69.refs_2_, ...), custom_call_target="tpu_custom_call" | custom-call | tf_op jit(solution)/shard_map/pallas_call | solution.py:87
  (21 shorter events, 0.2 us)
Async XLA Ops:
  2.3 26.8 %collective-permute-start.8 = (bf16[4096,128]{1,0:T(8,128)(2,1)}, bf16[4096,128]{1,0:T(8,128)(2,1)S(1)}, u32[]{:S(2)}, u32[]{:S(2)}) collective-permute-start(bf16[4096,128]{1,0:T(8,128)(2,1)} %slice.9), channel_id=1, source_target_pairs={{0,16},{16,0},{1,17},{17,1},{2,18},{18,2},{3,19},{19,3},{4,20},{20... | collective-permute-start | bytes 3145736 | tf_op jit(solution)/shard_map/ppermute | solution.py:165
  19.7 3.1 %collective-permute-start.7 = (f32[512,640]{1,0:T(8,128)S(1)}, f32[512,640]{1,0:T(8,128)S(1)}, u32[]{:S(2)}, u32[]{:S(2)}) collective-permute-start(f32[512,640]{1,0:T(8,128)S(1)} %slice_select_fusion), channel_id=1, source_target_pairs={{0,1},{1,0},{2,3},{3,2},{4,5},{5,4},{6,7},{7,6},{8,9},{9,8},{10,11... | collective-permute-start | bytes 3932168 | tf_op jit(solution)/shard_map/cond/branch_1_fun/ppermute | solution.py:108
  25.6 48.9 %collective-permute-start.10 = (bf16[4096,256]{1,0:T(8,128)(2,1)}, bf16[4096,256]{1,0:T(8,128)(2,1)}, u32[]{:S(2)}, u32[]{:S(2)}) collective-permute-start(bf16[4096,256]{1,0:T(8,128)(2,1)} %get-tuple-element.63), channel_id=1, source_target_pairs={{0,16},{16,0},{1,17},{17,1},{2,18},{18,2},{3,19},{19,3},{4,20},{20... | collective-permute-start | bytes 6291464 | tf_op jit(solution)/shard_map/ppermute | solution.py:165
  25.7 16.8 %collective-permute-start.9 = (f32[256,640]{1,0:T(8,128)S(1)}, f32[256,640]{1,0:T(8,128)S(1)}, u32[]{:S(2)}, u32[]{:S(2)}) collective-permute-start(f32[256,640]{1,0:T(8,128)S(1)} %get-tuple-element.76), channel_id=1, source_target_pairs={{0,2},{1,3},{2,0},{3,1},{4,6},{5,7},{6,4},{7,5},{8,10},{9,11},{10,... | collective-permute-start | bytes 1966088 | tf_op jit(solution)/shard_map/ppermute | solution.py:108
  29.1 6.1 %copy-start.2 = (bf16[4096,128]{1,0:T(8,128)(2,1)}, bf16[4096,128]{1,0:T(8,128)(2,1)S(1)}, u32[]{:S(2)}) copy-start(bf16[4096,128]{1,0:T(8,128)(2,1)S(1)} %collective-permute-done.8.refs_7_) | copy-start | bytes 3145732
  42.6 5.6 %collective-permute-start = (bf16[128,640]{1,0:T(8,128)(2,1)S(1)}, bf16[128,640]{1,0:T(8,128)(2,1)S(1)}, u32[]{:S(2)}, u32[]{:S(2)}) collective-permute-start(bf16[128,640]{1,0:T(8,128)(2,1)S(1)} %select_convert_fusion), channel_id=1, source_target_pairs={{0,4},{1,5},{2,6},{3,7},{4,0},{5,1},{6,2},{7,3},{8,12},{9,13},{10,... | collective-permute-start | bytes 491528 | tf_op jit(solution)/shard_map/cond/branch_1_fun/ppermute | solution.py:108
  48.3 5.4 %collective-permute-start.1 = (bf16[64,640]{1,0:T(8,128)(2,1)S(1)}, bf16[64,640]{1,0:T(8,128)(2,1)S(1)}, u32[]{:S(2)}, u32[]{:S(2)}) collective-permute-start(bf16[64,640]{1,0:T(8,128)(2,1)S(1)} %select_convert_fusion.1), channel_id=1, source_target_pairs={{0,8},{1,9},{2,10},{3,11},{4,12},{5,13},{6,14},{7,15},{8,0},{9,1},... | collective-permute-start | bytes 245768 | tf_op jit(solution)/shard_map/cond/branch_1_fun/ppermute | solution.py:108
  53.7 5.4 %collective-permute-start.2 = (bf16[64,640]{1,0:T(8,128)(2,1)S(1)}, bf16[64,640]{1,0:T(8,128)(2,1)S(1)}, u32[]{:S(2)}, u32[]{:S(2)}) collective-permute-start(bf16[64,640]{1,0:T(8,128)(2,1)S(1)} %add_convert_fusion), channel_id=1, source_target_pairs={{0,8},{1,9},{2,10},{3,11},{4,12},{5,13},{6,14},{7,15},{8,0},{9,1},... | collective-permute-start | bytes 245768 | tf_op jit(solution)/shard_map/cond/branch_1_fun/ppermute | solution.py:108
  59.2 5.4 %collective-permute-start.3 = (bf16[128,640]{1,0:T(8,128)(2,1)S(1)}, bf16[128,640]{1,0:T(8,128)(2,1)S(1)}, u32[]{:S(2)}, u32[]{:S(2)}) collective-permute-start(bf16[128,640]{1,0:T(8,128)(2,1)S(1)} %bitcast_select_fusion.1), channel_id=1, source_target_pairs={{0,4},{1,5},{2,6},{3,7},{4,0},{5,1},{6,2},{7,3},{8,12},{9,13},{10,... | collective-permute-start | bytes 491528 | tf_op jit(solution)/shard_map/cond/branch_1_fun/ppermute | solution.py:108
  64.7 55.7 %collective-permute-start.12 = (bf16[4096,256]{1,0:T(8,128)(2,1)}, bf16[4096,256]{1,0:T(8,128)(2,1)S(1)}, u32[]{:S(2)}, u32[]{:S(2)}) collective-permute-start(bf16[4096,256]{1,0:T(8,128)(2,1)} %get-tuple-element.70), channel_id=1, source_target_pairs={{0,16},{16,0},{1,17},{17,1},{2,18},{18,2},{3,19},{19,3},{4,20},{20... | collective-permute-start | bytes 6291464 | tf_op jit(solution)/shard_map/ppermute | solution.py:165
  81.0 2.4 %collective-permute-start.6 = (f32[512,384]{1,0:T(8,128)S(1)}, f32[512,384]{1,0:T(8,128)S(1)}, u32[]{:S(2)}, u32[]{:S(2)}) collective-permute-start(f32[512,384]{1,0:T(8,128)S(1)} %slice_select_fusion.1), channel_id=1, source_target_pairs={{0,1},{1,0},{2,3},{3,2},{4,5},{5,4},{6,7},{7,6},{8,9},{9,8},{10,11... | collective-permute-start | bytes 2359304 | tf_op jit(solution)/shard_map/cond/branch_1_fun/ppermute | solution.py:108
  84.2 17.8 %all-to-all-start = ((bf16[8,64,384]{2,1,0:T(8,128)(2,1)}), bf16[8,64,384]{2,1,0:T(8,128)(2,1)S(1)}, u32[]{:S(2)}, u32[]{:S(2)}) async-start(bf16[8,64,384]{2,1,0:T(8,128)(2,1)} %bitcast.7), calls=%async_computation | async-start | bytes 786432 | tf_op jit(solution)/shard_map/cond/branch_1_fun/all_to_all | solution.py:148
  90.0 17.0 %collective-permute-start.4 = (bf16[256,640]{1,0:T(8,128)(2,1)S(1)}, bf16[256,640]{1,0:T(8,128)(2,1)S(1)}, u32[]{:S(2)}, u32[]{:S(2)}) collective-permute-start(bf16[256,640]{1,0:T(8,128)(2,1)S(1)} %get-tuple-element.45), channel_id=1, source_target_pairs={{0,2},{1,3},{2,0},{3,1},{4,6},{5,7},{6,4},{7,5},{8,10},{9,11},{10,... | collective-permute-start | bytes 983048 | tf_op jit(solution)/shard_map/cond/branch_1_fun/ppermute | solution.py:108
  102.8 15.6 %all-to-all-start.1 = ((bf16[8,64,384]{2,1,0:T(8,128)(2,1)}), bf16[8,64,384]{2,1,0:T(8,128)(2,1)}, u32[]{:S(2)}, u32[]{:S(2)}) async-start(bf16[8,64,384]{2,1,0:T(8,128)(2,1)} %tile.0), calls=%async_computation.1 | async-start | bytes 786432 | tf_op jit(solution)/shard_map/cond/branch_1_fun/all_to_all | solution.py:148
  108.1 2.4 %collective-permute-start.5 = (bf16[512,640]{1,0:T(8,128)(2,1)}, bf16[512,640]{1,0:T(8,128)(2,1)}, u32[]{:S(2)}, u32[]{:S(2)}) collective-permute-start(bf16[512,640]{1,0:T(8,128)(2,1)} %bitcast_select_fusion.2), channel_id=1, source_target_pairs={{0,1},{1,0},{2,3},{3,2},{4,5},{5,4},{6,7},{7,6},{8,9},{9,8},{10,11... | collective-permute-start | bytes 1966088 | tf_op jit(solution)/shard_map/cond/branch_1_fun/ppermute | solution.py:108
  118.5 1.9 %collective-permute-start.11 = (bf16[512,384]{1,0:T(8,128)(2,1)}, bf16[512,384]{1,0:T(8,128)(2,1)S(1)}, u32[]{:S(2)}, u32[]{:S(2)}) collective-permute-start(bf16[512,384]{1,0:T(8,128)(2,1)} %get-tuple-element.69.refs_2_), channel_id=1, source_target_pairs={{0,1},{1,0},{2,3},{3,2},{4,5},{5,4},{6,7},{7,6},{8,9},{9,8},{10,11... | collective-permute-start | bytes 1179656 | tf_op jit(solution)/shard_map/ppermute | solution.py:108
  120.4 6.6 %copy-start.3 = (bf16[512,384]{1,0:T(8,128)(2,1)}, bf16[512,384]{1,0:T(8,128)(2,1)S(1)}, u32[]{:S(2)}) copy-start(bf16[512,384]{1,0:T(8,128)(2,1)S(1)} %collective-permute-done.11.refs_3_) | copy-start | bytes 1179652
  120.4 6.6 %copy-start = (bf16[4096,256]{1,0:T(8,128)(2,1)}, bf16[4096,256]{1,0:T(8,128)(2,1)S(1)}, u32[]{:S(2)}) copy-start(bf16[4096,256]{1,0:T(8,128)(2,1)S(1)} %collective-permute-done.12.refs_9_) | copy-start | bytes 6291460
  127.1 2.0 %collective-permute-start.13 = (f32[512,256]{1,0:T(8,128)S(1)}, f32[512,256]{1,0:T(8,128)S(1)}, u32[]{:S(2)}, u32[]{:S(2)}) collective-permute-start(f32[512,256]{1,0:T(8,128)S(1)} %slice_select_fusion.2), channel_id=1, source_target_pairs={{0,1},{1,0},{2,3},{3,2},{4,5},{5,4},{6,7},{7,6},{8,9},{9,8},{10,11... | collective-permute-start | bytes 1572872 | tf_op jit(solution)/shard_map/ppermute | solution.py:108
  154.3 1.5 copy-start.1
  154.3 1.5 collective-permute-start.14
  155.8 0.7 copy-start.4

commit v6 on v5

--- a/solution.py
+++ b/solution.py
@@ -1,3 +1,5 @@
+import functools
+
 import jax
 import jax.numpy as jnp
 from jax import lax
@@ -60,13 +62,16 @@
     )(amplitudes, vectors)
 
 
-def project_back(base, chis, pieces, upper, kind):
+def project_back(base, chis, pieces, upper, kind, share=(0, 1), earlier=None):
     rows, columns = base.shape
-    block = block_of(columns, 1024)
+    block = block_of(columns // share[1], 1024)
+    steps = columns // share[1] // block
+    first = share[0] * steps
     half = rows // 2
     widths = [mine.shape[1] for mine, _ in chis]
 
     def kernel(upper_ref, base_ref, *refs):
+        refs = refs if earlier is None else refs[1:]
         chi_refs, piece_refs, (out_ref, left_ref) = refs[: 2 * len(chis)], refs[2 * len(chis) : -2], refs[-2:]
 
         @pl.when(pl.program_id(0) == 0)
@@ -88,17 +93,23 @@
         kernel,
         grid_spec=pltpu.PrefetchScalarGridSpec(
             num_scalar_prefetch=1,
-            grid=(columns // block,),
-            in_specs=[pl.BlockSpec((rows, block), lambda i, u: (0, i))]
+            grid=(steps,),
+            in_specs=[pl.BlockSpec((rows, block), lambda i, u: (0, i + first))]
+            + ([] if earlier is None else [pl.BlockSpec(memory_space=pl.ANY)])
             + [pl.BlockSpec(h.shape, lambda i, u: (0, 0), pipeline_mode=pl.Buffered(1)) for h in halves]
-            + [pl.BlockSpec((block, piece.shape[1]), lambda i, u: (i, 0)) for piece in pieces],
-            out_specs=pl.BlockSpec((rows, block), lambda i, u: (0, i)),
+            + [pl.BlockSpec((block, piece.shape[1]), lambda i, u: (i + first, 0)) for piece in pieces],
+            out_specs=pl.BlockSpec((rows, block), lambda i, u: (0, i + first)),
             scratch_shapes=[pltpu.VMEM((rows, sum(widths)), jnp.bfloat16)],
         ),
         out_shape=jax.ShapeDtypeStruct(base.shape, kind),
+        input_output_aliases={} if earlier is None else {2: 0},
         compiler_params=pltpu.CompilerParams(vmem_limit_bytes=VMEM_BYTES),
-        cost_estimate=FREE,
-    )(upper, base, *halves, *pieces)
+        cost_estimate=pl.CostEstimate(
+            flops=2 * rows * steps * block * sum(widths),
+            bytes_accessed=rows * steps * block * (base.dtype.itemsize + jnp.dtype(kind).itemsize),
+            transcendentals=0,
+        ),
+    )(upper, base, *([] if earlier is None else [earlier]), *halves, *pieces)
 
 
 def solution(mesh):
@@ -134,7 +145,7 @@
             return jnp.where(mine, value, got).reshape(2 * value.shape[0], value.shape[1])
 
         def finish(value):
-            value = halve(halve(value, 2, jnp.bfloat16), 3, jnp.bfloat16).astype(jnp.bfloat16)
+            value = halve(halve(value, 2, jnp.float32), 3, jnp.float32).astype(jnp.bfloat16)
             return double(double(value, 3), 2)
 
         def both(value):
@@ -186,8 +197,17 @@
         part = jnp.concatenate([part_a, project(amplitudes, after(b, quarter))], axis=1)
         own, half_ab = boxed(last, quarter, part)
         pair_ab = both(half_ab)
-        pair_c = both(chain(project(amplitudes, after(c, *pair_ab))))
-        return project_back(residual_in, [own, pair_ab, pair_c], [cholesky, a, b, c], flag, jnp.bfloat16)
+        part_c = project(amplitudes, after(c, *pair_ab))
+
+        def tail(part, residual, own, pair, *pieces):
+            done = functools.partial(project_back, chis=[own, pair], pieces=pieces, upper=flag, kind=jnp.float32)
+            total = done(residual, share=(0, 2))
+            mine = after(scatter(part), total)
+            total = done(after(residual, mine), share=(1, 2), earlier=total)
+            return after(gather(mine), total), total
+
+        half_c, total = boxed(tail, part_c, residual_in, own, pair_ab, cholesky, a, b)
+        return project_back(total, [both(half_c)], [c], flag, jnp.bfloat16)
 
     in_specs = (P("row", "col"), P("row", "col"), P("col", "row"))
     return jax.shard_map(body, mesh=mesh, in_specs=in_specs, out_specs=P("row", "col"), check_vma=False)

time: 174 us -> 176 us (1.011)
  blocking collectives: 25 us -> 0 us
  Pallas kernels: 26.8 us -> 39.1 us
  starting transfers between devices: 28.2 us -> 32.8 us
  other arithmetic: 4.29 us -> 8.73 us
  waiting for transfers between devices: 60 us -> 63.9 us
    all_to_all x2 -> x0, blocking collectives: 25 us -> none  [spread(): lax.all_to_all(value, 'col', 0, 0, tiled=True, axis_index_groups=mates)]
    ppermute x12, waiting for transfers between devices: 32.6 us -> 45.9 us  [exchange(): return lax.ppermute(value, 'col', [(i, i ^ bit) for i in range(cols)])]
    pallas_call x1 -> x3, Pallas kernels: 17 us -> 29.3 us  [project_back(): pl.pallas_call(kernel, grid_spec=pltpu.PrefetchScalarGridSpec(num_scalar_...]
    all_to_all x2 -> x4, starting transfers between devices: 9.93 us -> 19.8 us  [spread(): lax.all_to_all(value, 'col', 0, 0, tiled=True, axis_index_groups=mates)]
    ppermute x3, waiting for transfers between devices: 9.51 us -> 0.02 us  [send_row(): lax.ppermute(vectors, 'row', [(i, (i + shift) % rows) for i in range(rows)])]
    ppermute x12, starting transfers between devices: 13.6 us -> 8.98 us  [exchange(): return lax.ppermute(value, 'col', [(i, i ^ bit) for i in range(cols)])]
    all_to_all x2 -> x4, waiting for transfers between devices: 17.9 us -> 18 us  [spread(): lax.all_to_all(value, 'col', 0, 0, tiled=True, axis_index_groups=mates)]
  transfers between devices with their start and end apart: 17 -> 19, of which waited for: 15 -> 13; matrix products, arithmetic and copies ran while one was open for 14% -> 15% of each run, Pallas kernels for 6% -> 16%
where the time goes in v6:
time: 176 us; the launch traced here: 175 us
  waiting for transfers between devices  63.9 us (36%)
  Pallas kernels  39.1 us (22%)
  starting transfers between devices  32.8 us (19%)
  matrix products  19 us (11%)
  local copies, waits for them, and re-layouts  11.5 us (7%)
  other arithmetic  8.73 us (5%)
    ppermute x12, waiting for transfers between devices, exchange(): return lax.ppermute(value, 'col', [(i, i ^ bit) for i in range(cols)])  45.9 us
    pallas_call x3, Pallas kernels, project_back(): pl.pallas_call(kernel, grid_spec=pltpu.PrefetchScalarGridSpec(num_scalar_...  29.3 us
    all_to_all x4, starting transfers between devices, spread(): lax.all_to_all(value, 'col', 0, 0, tiled=True, axis_index_groups=mates)  19.8 us
    dot_general x3, matrix products, project(): part = jnp.dot(amplitudes, vectors, preferred_element_type=jnp.float32)  19 us
    all_to_all x4, waiting for transfers between devices, spread(): lax.all_to_all(value, 'col', 0, 0, tiled=True, axis_index_groups=mates)  18 us
    pallas_call x1, Pallas kernels, project_wide(): pl.pallas_call(kernel, grid=(steps,), in_specs=[pl.BlockSpec((rows, block...  9.81 us
    ppermute x12, starting transfers between devices, exchange(): return lax.ppermute(value, 'col', [(i, i ^ bit) for i in range(cols)])  8.98 us
    slice x2, local copies, waits for them, and re-layouts, body(): cholesky[:, end - size:end]  6.82 us
  transfers between devices with their start and end apart: 19, of which 13 were waited for; matrix products, arithmetic and copies ran while one was open for 15% of the time, Pallas kernels for 16%

profile of v6, /device:TPU:0, one launch (start us, length us, event | category | flops | bytes accessed | tf_op | source)
XLA Modules:
  0.0 175.4 jit_solution(475870145258999476)
XLA Ops:
  0.0 2.3 %slice.10 = bf16[4096,128]{1,0:T(8,128)(2,1)} slice(bf16[4096,640]{1,0:T(8,128)(2,1)} %right_ref), slice={[0:4096], [0:128]} | slice | bytes 2097152 | tf_op jit(solution)/shard_map/slice | solution.py:187
  2.3 2.9 %collective-permute-start.9 = (bf16[4096,128]{1,0:T(8,128)(2,1)}, bf16[4096,128]{1,0:T(8,128)(2,1)S(1)}, u32[]{:S(2)}, u32[]{:S(2)}) collective-permute-start(bf16[4096,128]{1,0:T(8,128)(2,1)} %slice.10), channel_id=1, source_target_pairs={{0,16},{16,0},{1,17},{17,1},{2,18},{18,2},{3,19},{19,3},{4,20},{20... | collective-permute-start | bytes 3145736 | tf_op jit(solution)/shard_map/ppermute | solution.py:176
  5.2 4.6 %fusion.1 = (bf16[4096,256]{1,0:T(8,128)(2,1)}, bf16[4096,256]{1,0:T(8,128)(2,1)}) fusion(bf16[4096,640]{1,0:T(8,128)(2,1)} %right_ref), kind=kLoop, calls=%fused_computation.24 | loop fusion | bytes 8388608 | tf_op jit(solution)/shard_map/slice | solution.py:187
  9.8 9.8 %shard_map.38 = f32[1024,640]{1,0:T(8,128)S(1)} custom-call(bf16[1024,4096]{1,0:T(8,128)(2,1)} %left_ref.1, bf16[4096,640]{1,0:T(8,128)(2,1)} %right_ref), custom_call_target="tpu_custom_call" | custom-call | tf_op jit(solution)/shard_map/pallas_call | solution.py:53
  19.6 6.0 %conditional.4 = (f32[512,640]{1,0:T(8,128)}, f32[256,640]{1,0:T(8,128)S(1)}, f32[256,640]{1,0:T(8,128)S(1)}) conditional(s32[]{:T(128)} %convert_element_type.34, () %tuple.53, (pred[]{:T(512)}, f32[1024,640]{1,0:T(8,128)S(1)}) %tuple.55), branch_computations={%region_0.0_spmd, %region_1.2_spmd} | conditional | flops 983040 | bytes 17039426 | solution.py:129
  19.6 0.1 slice_select_fusion
  19.7 0.1 collective-permute-start.8
  19.8 3.0 %collective-permute-done.8 = f32[512,640]{1,0:T(8,128)S(1)} collective-permute-done((f32[512,640]{1,0:T(8,128)S(1)}, f32[512,640]{1,0:T(8,128)S(1)}, u32[]{:S(2)}, u32[]{:S(2)}) %collective-permute-start.8) | collective-permute-done | bytes 1310752 | tf_op jit(solution)/shard_map/cond/branch_1_fun/ppermute | solution.py:119
  22.8 1.3 select_add_fusion
  24.2 1.4 fusion
  25.5 1.0 broadcast_select_fusion
  26.5 2.1 %collective-permute-start.10 = (f32[256,640]{1,0:T(8,128)S(1)}, f32[256,640]{1,0:T(8,128)}, u32[]{:S(2)}, u32[]{:S(2)}) collective-permute-start(f32[256,640]{1,0:T(8,128)S(1)} %get-tuple-element.118), channel_id=1, source_target_pairs={{0,2},{1,3},{2,0},{3,1},{4,6},{5,7},{6,4},{7,5},{8,10},{9,11},{10,... | collective-permute-start | bytes 1966088 | tf_op jit(solution)/shard_map/ppermute | solution.py:119
  28.6 0.0 collective-permute-done.9
  28.6 6.9 %convolution_bitcast_fusion.2 = f32[1024,128]{1,0:T(8,128)} fusion(bf16[1024,4096]{1,0:T(8,128)(2,1)} %left_ref.1, bf16[4096,128]{1,0:T(8,128)(2,1)S(1)} %collective-permute-done.9), kind=kOutput, calls=%fused_computation.20 | convolution fusion | flops 1073741824 | bytes 9961472 | tf_op jit(solution)/shard_map/dot_general | solution.py:27
  35.5 7.9 %collective-permute-done.10 = f32[256,640]{1,0:T(8,128)} collective-permute-done((f32[256,640]{1,0:T(8,128)S(1)}, f32[256,640]{1,0:T(8,128)}, u32[]{:S(2)}, u32[]{:S(2)}) %collective-permute-start.10) | collective-permute-done | bytes 655392 | tf_op jit(solution)/shard_map/ppermute | solution.py:119
  43.4 31.4 %conditional.5 = (bf16[256,640]{1,0:T(8,128)(2,1)S(1)}) conditional(s32[]{:T(128)} %convert_element_type.34, () %tuple.52, (s32[]{:T(128)}, f32[256,640]{1,0:T(8,128)}, f32[256,640]{1,0:T(8,128)}) %tuple.59), branch_computations={%region_2.3_spmd, %region_3.4_spmd} | conditional | flops 819210 | bytes 9258224 | solution.py:129
  43.4 1.4 add.14
  44.8 1.9 %collective-permute-start = (f32[128,640]{1,0:T(8,128)S(1)}, f32[128,640]{1,0:T(8,128)S(1)}, u32[]{:S(2)}, u32[]{:S(2)}) collective-permute-start(f32[128,640]{1,0:T(8,128)S(1)} %slice_select_fusion.1), channel_id=1, source_target_pairs={{0,4},{1,5},{2,6},{3,7},{4,0},{5,1},{6,2},{7,3},{8,12},{9,13},{10,... | collective-permute-start | bytes 983048 | tf_op jit(solution)/shard_map/cond/branch_1_fun/ppermute | solution.py:119
  46.7 7.1 %collective-permute-done = f32[128,640]{1,0:T(8,128)S(1)} collective-permute-done((f32[128,640]{1,0:T(8,128)S(1)}, f32[128,640]{1,0:T(8,128)S(1)}, u32[]{:S(2)}, u32[]{:S(2)}) %collective-permute-start) | collective-permute-done | bytes 327712 | tf_op jit(solution)/shard_map/cond/branch_1_fun/ppermute | solution.py:119
  53.9 2.5 %collective-permute-start.1 = (f32[64,640]{1,0:T(8,128)S(1)}, f32[64,640]{1,0:T(8,128)S(1)}, u32[]{:S(2)}, u32[]{:S(2)}) collective-permute-start(f32[64,640]{1,0:T(8,128)S(1)} %slice_select_fusion.2), channel_id=1, source_target_pairs={{0,8},{1,9},{2,10},{3,11},{4,12},{5,13},{6,14},{7,15},{8,0},{9,1},... | collective-permute-start | bytes 491528 | tf_op jit(solution)/shard_map/cond/branch_1_fun/ppermute | solution.py:119
  56.4 0.1 broadcast_in_dim.54
  56.5 0.1 broadcast_in_dim.55
  56.6 6.2 %collective-permute-done.1 = f32[64,640]{1,0:T(8,128)S(1)} collective-permute-done((f32[64,640]{1,0:T(8,128)S(1)}, f32[64,640]{1,0:T(8,128)S(1)}, u32[]{:S(2)}, u32[]{:S(2)}) %collective-permute-start.1) | collective-permute-done | bytes 163872 | tf_op jit(solution)/shard_map/cond/branch_1_fun/ppermute | solution.py:119
  62.9 0.1 collective-permute-start.2
  63.0 6.2 %collective-permute-done.2 = bf16[64,640]{1,0:T(8,128)(2,1)S(1)} collective-permute-done((bf16[64,640]{1,0:T(8,128)(2,1)S(1)}, bf16[64,640]{1,0:T(8,128)(2,1)S(1)}, u32[]{:S(2)}, u32[]{:S(2)}) %collective-permute-start.2) | collective-permute-done | bytes 81952 | tf_op jit(solution)/shard_map/cond/branch_1_fun/ppermute | solution.py:119
  69.2 0.1 bitcast_select_fusion.1
  69.3 0.1 collective-permute-start.3
  69.3 0.1 broadcast_bitcast_fusion
  69.4 5.2 %collective-permute-done.3 = bf16[128,640]{1,0:T(8,128)(2,1)S(1)} collective-permute-done((bf16[128,640]{1,0:T(8,128)(2,1)S(1)}, bf16[128,640]{1,0:T(8,128)(2,1)S(1)}, u32[]{:S(2)}, u32[]{:S(2)}) %collective-permute-start.3) | collective-permute-done | bytes 163872 | tf_op jit(solution)/shard_map/cond/branch_1_fun/ppermute | solution.py:119
  74.6 0.1 bitcast_select_fusion
  74.8 1.1 collective-permute-start.11
  75.9 5.8 %convolution_bitcast_fusion.1 = f32[1024,256]{1,0:T(8,128)S(1)} fusion(bf16[1024,4096]{1,0:T(8,128)(2,1)} %left_ref.1, bf16[4096,256]{1,0:T(8,128)(2,1)S(1)} %collective-permute-done.12), kind=kOutput, calls=%fused_computation.19 | convolution fusion | flops 2147483648 | bytes 11534336 | tf_op jit(solution)/shard_map/dot_general | solution.py:27
  81.7 0.1 pad_maximum_fusion
  81.8 36.6 %conditional.6 = (bf16[512,640]{1,0:T(8,128)(2,1)}, bf16[512,640]{1,0:T(8,128)(2,1)}, bf16[512,384]{1,0:T(8,128)(2,1)}) conditional(s32[]{:T(128)} %convert_element_type.34, () %tuple.61, (pred[]{:T(512)}, bf16[256,640]{1,0:T(8,128)(2,1)S(1)}, pred[]{:T(512)}, f32[1024,384]{1,0:T(8,128)S(1)}) %tuple.63), branch_computations={%region_4.5_spmd, %region_5.7_spmd} | conditional | flops 1286147 | bytes 16746721 | solution.py:129
  81.8 0.1 slice_select_fusion.3
  81.9 0.1 collective-permute-start.6
  82.0 2.3 %collective-permute-done.6 = f32[512,384]{1,0:T(8,128)S(1)} collective-permute-done((f32[512,384]{1,0:T(8,128)S(1)}, f32[512,384]{1,0:T(8,128)S(1)}, u32[]{:S(2)}, u32[]{:S(2)}) %collective-permute-start.6) | collective-permute-done | bytes 786464 | tf_op jit(solution)/shard_map/cond/branch_1_fun/ppermute | solution.py:119
  84.3 0.9 add_convert_fusion.1
  85.1 4.8 %all-to-all-start = ((bf16[8,64,384]{2,1,0:T(8,128)(2,1)}), bf16[8,64,384]{2,1,0:T(8,128)(2,1)S(1)}, u32[]{:S(2)}, u32[]{:S(2)}) async-start(bf16[8,64,384]{2,1,0:T(8,128)(2,1)} %bitcast.7), calls=%async_computation | async-start | bytes 786432 | tf_op jit(solution)/shard_map/cond/branch_1_fun/all_to_all | solution.py:159
  90.0 2.0 %collective-permute-start.4 = (bf16[256,640]{1,0:T(8,128)(2,1)S(1)}, bf16[256,640]{1,0:T(8,128)(2,1)S(1)}, u32[]{:S(2)}, u32[]{:S(2)}) collective-permute-start(bf16[256,640]{1,0:T(8,128)(2,1)S(1)} %get-tuple-element.67), channel_id=1, source_target_pairs={{0,2},{1,3},{2,0},{3,1},{4,6},{5,7},{6,4},{7,5},{8,10},{9,11},{10,... | collective-permute-start | bytes 983048 | tf_op jit(solution)/shard_map/cond/branch_1_fun/ppermute | solution.py:119
  92.0 10.0 %all-to-all-done = bf16[8,64,384]{2,1,0:T(8,128)(2,1)S(1)} async-done(((bf16[8,64,384]{2,1,0:T(8,128)(2,1)}), bf16[8,64,384]{2,1,0:T(8,128)(2,1)S(1)}, u32[]{:S(2)}, u32[]{:S(2)}) %all-to-all-start) | async-done | bytes 393248 | tf_op jit(solution)/shard_map/cond/branch_1_fun/all_to_all | solution.py:159
  102.0 0.1 reduce_sum.22
  102.0 0.8 tile.0
  102.8 4.1 %all-to-all-start.1 = ((bf16[8,64,384]{2,1,0:T(8,128)(2,1)}), bf16[8,64,384]{2,1,0:T(8,128)(2,1)}, u32[]{:S(2)}, u32[]{:S(2)}) async-start(bf16[8,64,384]{2,1,0:T(8,128)(2,1)} %tile.0), calls=%async_computation.1 | async-start | bytes 786432 | tf_op jit(solution)/shard_map/cond/branch_1_fun/all_to_all | solution.py:159
  106.9 0.1 broadcast_in_dim.65
  107.0 1.0 bitcast_select_fusion.2
  108.0 2.4 %collective-permute-done.5 = bf16[512,640]{1,0:T(8,128)(2,1)} collective-permute-done((bf16[512,640]{1,0:T(8,128)(2,1)}, bf16[512,640]{1,0:T(8,128)(2,1)}, u32[]{:S(2)}, u32[]{:S(2)}) %collective-permute-start.5) | collective-permute-done | bytes 655392 | tf_op jit(solution)/shard_map/cond/branch_1_fun/ppermute | solution.py:119
  110.5 8.0 %all-to-all-done.1 = bf16[8,64,384]{2,1,0:T(8,128)(2,1)} async-done(((bf16[8,64,384]{2,1,0:T(8,128)(2,1)}), bf16[8,64,384]{2,1,0:T(8,128)(2,1)}, u32[]{:S(2)}, u32[]{:S(2)}) %all-to-all-start.1) | async-done | bytes 393248 | tf_op jit(solution)/shard_map/cond/branch_1_fun/all_to_all | solution.py:159
  118.5 1.9 %collective-permute-done.13 = bf16[512,384]{1,0:T(8,128)(2,1)S(1)} collective-permute-done((bf16[512,384]{1,0:T(8,128)(2,1)}, bf16[512,384]{1,0:T(8,128)(2,1)S(1)}, u32[]{:S(2)}, u32[]{:S(2)}) %collective-permute-start.13) | collective-permute-done | bytes 393248 | tf_op jit(solution)/shard_map/ppermute | solution.py:119
  120.4 6.3 %convolution_bitcast_fusion = f32[1024,256]{1,0:T(8,128)S(1)} fusion(bf16[1024,4096]{1,0:T(8,128)(2,1)} %left_ref.1, bf16[4096,256]{1,0:T(8,128)(2,1)} %collective-permute-done.11.refs_2_), kind=kOutput, calls=%fused_computation.18 | convolution fusion | flops 2147483648 | bytes 11534336 | tf_op jit(solution)/shard_map/dot_general | solution.py:27
  126.7 35.8 %conditional.7 = (bf16[512,256]{1,0:T(8,128)(2,1)}, f32[1024,4096]{1,0:T(8,128)}) conditional(s32[]{:T(128)} %convert_element_type.34, () %tuple.51, (pred[]{:T(512)}, f32[1024,256]{1,0:T(8,128)S(1)}, s32[1]{0:T(128)}, bf16[1024,4096]{1,0:T(8,128)(2,1)}, bf16[512,640]{1,0:T(8,128)(2,1)}, /*index=5*/bf16[512,640]{1,0:T(8,128)(2,1)}, ...), branch_computations={%region_7.8_spmd, %region_8.10_spmd} | conditional | flops 8590573568 | bytes 32833660 | solution.py:129
  126.9 0.1 slice_select_fusion.4
  127.0 0.2 collective-permute-start.7
  127.2 1.8 %collective-permute-done.7 = f32[512,256]{1,0:T(8,128)S(1)} collective-permute-done((f32[512,256]{1,0:T(8,128)S(1)}, f32[512,256]{1,0:T(8,128)S(1)}, u32[]{:S(2)}, u32[]{:S(2)}) %collective-permute-start.7) | collective-permute-done | bytes 524320 | tf_op jit(solution)/shard_map/cond/branch_1_fun/ppermute | solution.py:119
  129.0 0.8 add_convert_fusion.2
  129.8 4.9 %all-to-all-start.2 = ((bf16[8,64,256]{2,1,0:T(8,128)(2,1)}), bf16[8,64,256]{2,1,0:T(8,128)(2,1)}, u32[]{:S(2)}, u32[]{:S(2)}) async-start(bf16[8,64,256]{2,1,0:T(8,128)(2,1)} %bitcast.31), calls=%async_computation.2 | async-start | bytes 524288 | tf_op jit(solution)/shard_map/cond/branch_1_fun/all_to_all | solution.py:159
  134.6 9.4 %branch_1_fun.2.refs_0_ = f32[1024,4096]{1,0:T(8,128)} custom-call(s32[1]{0:T(128)} %get-tuple-element.72.upper_ref, bf16[1024,4096]{1,0:T(8,128)(2,1)} %get-tuple-element.82.base_ref, bf16[512,640]{1,0:T(8,128)(2,1)} %get-tuple-element.74.refs_0_.refs_1_, bf16[512,640]{1,0:T(8,128)(2,1)} %get-tuple-element.75.refs_1_.refs_2_, ...), custom_call_target="tpu_custom_call" | custom-call | flops 4294967296 | bytes 12582912 | tf_op jit(solution)/shard_map/cond/branch_1_fun/pallas_call | solution.py:92
  144.0 1.6 reduce_sum.23
  145.6 1.5 tile.2
  147.1 6.0 %all-to-all-start.3 = ((bf16[8,64,256]{2,1,0:T(8,128)(2,1)}), bf16[8,64,256]{2,1,0:T(8,128)(2,1)}, u32[]{:S(2)}, u32[]{:S(2)}) async-start(bf16[8,64,256]{2,1,0:T(8,128)(2,1)} %tile.2), calls=%async_computation.3 | async-start | bytes 524288 | tf_op jit(solution)/shard_map/cond/branch_1_fun/all_to_all | solution.py:159
  153.1 9.4 %branch_1_fun.3 = f32[1024,4096]{1,0:T(8,128)} custom-call(s32[1]{0:T(128)} %get-tuple-element.72.upper_ref, bf16[1024,4096]{1,0:T(8,128)(2,1)} %get-tuple-element.82.base_ref, f32[1024,4096]{1,0:T(8,128)} %branch_1_fun.2.refs_0_, bf16[512,640]{1,0:T(8,128)(2,1)} %get-tuple-element.74.refs_0_.refs_1_, ...), custom_call_target="tpu_custom_call", output_to_operand_aliasing={{}: (2, {})} | custom-call | flops 4294967296 | bytes 12582912 | tf_op jit(solution)/shard_map/cond/branch_1_fun/pallas_call | solution.py:92
  162.6 1.7 collective-permute-done.14.refs_1_
  164.3 0.7 copy-done.3
  165.0 10.4 %shard_map.39 = bf16[1024,4096]{1,0:T(8,128)(2,1)} custom-call(s32[1]{0:T(128)} %bitcast.11.upper_ref, f32[1024,4096]{1,0:T(8,128)} %get-tuple-element.110.base_ref, bf16[512,256]{1,0:T(8,128)(2,1)} %get-tuple-element.111.refs_0_, bf16[512,256]{1,0:T(8,128)(2,1)} %copy-done.3, bf16[4096,256]{1,0:T(8,128)(2,1)} %collective-permute-done.11.refs_2_), custom_call_target="tpu_custom_call" | custom-call | flops 2147483648 | bytes 25165824 | tf_op jit(solution)/shard_map/pallas_call | solution.py:92
  (24 shorter events, 0.2 us)
Async XLA Ops:
  2.3 26.3 %collective-permute-start.9 = (bf16[4096,128]{1,0:T(8,128)(2,1)}, bf16[4096,128]{1,0:T(8,128)(2,1)S(1)}, u32[]{:S(2)}, u32[]{:S(2)}) collective-permute-start(bf16[4096,128]{1,0:T(8,128)(2,1)} %slice.10), channel_id=1, source_target_pairs={{0,16},{16,0},{1,17},{17,1},{2,18},{18,2},{3,19},{19,3},{4,20},{20... | collective-permute-start | bytes 3145736 | tf_op jit(solution)/shard_map/ppermute | solution.py:176
  19.7 3.1 %collective-permute-start.8 = (f32[512,640]{1,0:T(8,128)S(1)}, f32[512,640]{1,0:T(8,128)S(1)}, u32[]{:S(2)}, u32[]{:S(2)}) collective-permute-start(f32[512,640]{1,0:T(8,128)S(1)} %slice_select_fusion), channel_id=1, source_target_pairs={{0,1},{1,0},{2,3},{3,2},{4,5},{5,4},{6,7},{7,6},{8,9},{9,8},{10,11... | collective-permute-start | bytes 3932168 | tf_op jit(solution)/shard_map/cond/branch_1_fun/ppermute | solution.py:119
  26.5 49.4 %collective-permute-start.12 = (bf16[4096,256]{1,0:T(8,128)(2,1)}, bf16[4096,256]{1,0:T(8,128)(2,1)S(1)}, u32[]{:S(2)}, u32[]{:S(2)}) collective-permute-start(bf16[4096,256]{1,0:T(8,128)(2,1)} %get-tuple-element.101), channel_id=1, source_target_pairs={{0,16},{16,0},{1,17},{17,1},{2,18},{18,2},{3,19},{19,3},{4,20},{20... | collective-permute-start | bytes 6291464 | tf_op jit(solution)/shard_map/ppermute | solution.py:176
  26.5 16.9 %collective-permute-start.10 = (f32[256,640]{1,0:T(8,128)S(1)}, f32[256,640]{1,0:T(8,128)}, u32[]{:S(2)}, u32[]{:S(2)}) collective-permute-start(f32[256,640]{1,0:T(8,128)S(1)} %get-tuple-element.118), channel_id=1, source_target_pairs={{0,2},{1,3},{2,0},{3,1},{4,6},{5,7},{6,4},{7,5},{8,10},{9,11},{10,... | collective-permute-start | bytes 1966088 | tf_op jit(solution)/shard_map/ppermute | solution.py:119
  28.6 6.9 %copy-start = (bf16[4096,128]{1,0:T(8,128)(2,1)}, bf16[4096,128]{1,0:T(8,128)(2,1)S(1)}, u32[]{:S(2)}) copy-start(bf16[4096,128]{1,0:T(8,128)(2,1)S(1)} %collective-permute-done.9) | copy-start | bytes 3145732
  44.8 9.0 %collective-permute-start = (f32[128,640]{1,0:T(8,128)S(1)}, f32[128,640]{1,0:T(8,128)S(1)}, u32[]{:S(2)}, u32[]{:S(2)}) collective-permute-start(f32[128,640]{1,0:T(8,128)S(1)} %slice_select_fusion.1), channel_id=1, source_target_pairs={{0,4},{1,5},{2,6},{3,7},{4,0},{5,1},{6,2},{7,3},{8,12},{9,13},{10,... | collective-permute-start | bytes 983048 | tf_op jit(solution)/shard_map/cond/branch_1_fun/ppermute | solution.py:119
  53.9 9.0 %collective-permute-start.1 = (f32[64,640]{1,0:T(8,128)S(1)}, f32[64,640]{1,0:T(8,128)S(1)}, u32[]{:S(2)}, u32[]{:S(2)}) collective-permute-start(f32[64,640]{1,0:T(8,128)S(1)} %slice_select_fusion.2), channel_id=1, source_target_pairs={{0,8},{1,9},{2,10},{3,11},{4,12},{5,13},{6,14},{7,15},{8,0},{9,1},... | collective-permute-start | bytes 491528 | tf_op jit(solution)/shard_map/cond/branch_1_fun/ppermute | solution.py:119
  62.9 6.3 %collective-permute-start.2 = (bf16[64,640]{1,0:T(8,128)(2,1)S(1)}, bf16[64,640]{1,0:T(8,128)(2,1)S(1)}, u32[]{:S(2)}, u32[]{:S(2)}) collective-permute-start(bf16[64,640]{1,0:T(8,128)(2,1)S(1)} %add_convert_fusion), channel_id=1, source_target_pairs={{0,8},{1,9},{2,10},{3,11},{4,12},{5,13},{6,14},{7,15},{8,0},{9,1},... | collective-permute-start | bytes 245768 | tf_op jit(solution)/shard_map/cond/branch_1_fun/ppermute | solution.py:119
  69.3 5.4 %collective-permute-start.3 = (bf16[128,640]{1,0:T(8,128)(2,1)S(1)}, bf16[128,640]{1,0:T(8,128)(2,1)S(1)}, u32[]{:S(2)}, u32[]{:S(2)}) collective-permute-start(bf16[128,640]{1,0:T(8,128)(2,1)S(1)} %bitcast_select_fusion.1), channel_id=1, source_target_pairs={{0,4},{1,5},{2,6},{3,7},{4,0},{5,1},{6,2},{7,3},{8,12},{9,13},{10,... | collective-permute-start | bytes 491528 | tf_op jit(solution)/shard_map/cond/branch_1_fun/ppermute | solution.py:119
  74.8 45.6 %collective-permute-start.11 = (bf16[4096,256]{1,0:T(8,128)(2,1)}, bf16[4096,256]{1,0:T(8,128)(2,1)}, u32[]{:S(2)}, u32[]{:S(2)}) collective-permute-start(bf16[4096,256]{1,0:T(8,128)(2,1)} %get-tuple-element.104), channel_id=1, source_target_pairs={{0,16},{16,0},{1,17},{17,1},{2,18},{18,2},{3,19},{19,3},{4,20},{20... | collective-permute-start | bytes 6291464 | tf_op jit(solution)/shard_map/ppermute | solution.py:176
  75.9 5.8 %copy-start.2 = (f32[1024,128]{1,0:T(8,128)S(1)}, f32[1024,128]{1,0:T(8,128)}, u32[]{:S(2)}) copy-start(f32[1024,128]{1,0:T(8,128)} %convolution_bitcast_fusion.2) | copy-start | bytes 1572868
  81.9 2.4 %collective-permute-start.6 = (f32[512,384]{1,0:T(8,128)S(1)}, f32[512,384]{1,0:T(8,128)S(1)}, u32[]{:S(2)}, u32[]{:S(2)}) collective-permute-start(f32[512,384]{1,0:T(8,128)S(1)} %slice_select_fusion.3), channel_id=1, source_target_pairs={{0,1},{1,0},{2,3},{3,2},{4,5},{5,4},{6,7},{7,6},{8,9},{9,8},{10,11... | collective-permute-start | bytes 2359304 | tf_op jit(solution)/shard_map/cond/branch_1_fun/ppermute | solution.py:119
  85.1 16.8 %all-to-all-start = ((bf16[8,64,384]{2,1,0:T(8,128)(2,1)}), bf16[8,64,384]{2,1,0:T(8,128)(2,1)S(1)}, u32[]{:S(2)}, u32[]{:S(2)}) async-start(bf16[8,64,384]{2,1,0:T(8,128)(2,1)} %bitcast.7), calls=%async_computation | async-start | bytes 786432 | tf_op jit(solution)/shard_map/cond/branch_1_fun/all_to_all | solution.py:159
  90.0 17.0 %collective-permute-start.4 = (bf16[256,640]{1,0:T(8,128)(2,1)S(1)}, bf16[256,640]{1,0:T(8,128)(2,1)S(1)}, u32[]{:S(2)}, u32[]{:S(2)}) collective-permute-start(bf16[256,640]{1,0:T(8,128)(2,1)S(1)} %get-tuple-element.67), channel_id=1, source_target_pairs={{0,2},{1,3},{2,0},{3,1},{4,6},{5,7},{6,4},{7,5},{8,10},{9,11},{10,... | collective-permute-start | bytes 983048 | tf_op jit(solution)/shard_map/cond/branch_1_fun/ppermute | solution.py:119
  102.8 15.6 %all-to-all-start.1 = ((bf16[8,64,384]{2,1,0:T(8,128)(2,1)}), bf16[8,64,384]{2,1,0:T(8,128)(2,1)}, u32[]{:S(2)}, u32[]{:S(2)}) async-start(bf16[8,64,384]{2,1,0:T(8,128)(2,1)} %tile.0), calls=%async_computation.1 | async-start | bytes 786432 | tf_op jit(solution)/shard_map/cond/branch_1_fun/all_to_all | solution.py:159
  108.0 2.4 %collective-permute-start.5 = (bf16[512,640]{1,0:T(8,128)(2,1)}, bf16[512,640]{1,0:T(8,128)(2,1)}, u32[]{:S(2)}, u32[]{:S(2)}) collective-permute-start(bf16[512,640]{1,0:T(8,128)(2,1)} %bitcast_select_fusion.2), channel_id=1, source_target_pairs={{0,1},{1,0},{2,3},{3,2},{4,5},{5,4},{6,7},{7,6},{8,9},{9,8},{10,11... | collective-permute-start | bytes 1966088 | tf_op jit(solution)/shard_map/cond/branch_1_fun/ppermute | solution.py:119
  118.4 1.9 %collective-permute-start.13 = (bf16[512,384]{1,0:T(8,128)(2,1)}, bf16[512,384]{1,0:T(8,128)(2,1)S(1)}, u32[]{:S(2)}, u32[]{:S(2)}) collective-permute-start(bf16[512,384]{1,0:T(8,128)(2,1)} %get-tuple-element.106), channel_id=1, source_target_pairs={{0,1},{1,0},{2,3},{3,2},{4,5},{5,4},{6,7},{7,6},{8,9},{9,8},{10,11... | collective-permute-start | bytes 1179656 | tf_op jit(solution)/shard_map/ppermute | solution.py:119
  118.5 8.3 %copy-start.1 = (bf16[4096,128]{1,0:T(8,128)(2,1)S(1)}, bf16[4096,128]{1,0:T(8,128)(2,1)}, u32[]{:S(2)}) copy-start(bf16[4096,128]{1,0:T(8,128)(2,1)} %copy-done) | copy-start | bytes 3145732
  127.0 2.0 %collective-permute-start.7 = (f32[512,256]{1,0:T(8,128)S(1)}, f32[512,256]{1,0:T(8,128)S(1)}, u32[]{:S(2)}, u32[]{:S(2)}) collective-permute-start(f32[512,256]{1,0:T(8,128)S(1)} %slice_select_fusion.4), channel_id=1, source_target_pairs={{0,1},{1,0},{2,3},{3,2},{4,5},{5,4},{6,7},{7,6},{8,9},{9,8},{10,11... | collective-permute-start | bytes 1572872 | tf_op jit(solution)/shard_map/cond/branch_1_fun/ppermute | solution.py:119
  129.8 14.3 %all-to-all-start.2 = ((bf16[8,64,256]{2,1,0:T(8,128)(2,1)}), bf16[8,64,256]{2,1,0:T(8,128)(2,1)}, u32[]{:S(2)}, u32[]{:S(2)}) async-start(bf16[8,64,256]{2,1,0:T(8,128)(2,1)} %bitcast.31), calls=%async_computation.2 | async-start | bytes 524288 | tf_op jit(solution)/shard_map/cond/branch_1_fun/all_to_all | solution.py:159
  147.1 15.4 %all-to-all-start.3 = ((bf16[8,64,256]{2,1,0:T(8,128)(2,1)}), bf16[8,64,256]{2,1,0:T(8,128)(2,1)}, u32[]{:S(2)}, u32[]{:S(2)}) async-start(bf16[8,64,256]{2,1,0:T(8,128)(2,1)} %tile.2), calls=%async_computation.3 | async-start | bytes 524288 | tf_op jit(solution)/shard_map/cond/branch_1_fun/all_to_all | solution.py:159
  162.5 1.7 collective-permute-start.14
  164.3 0.7 copy-start.3

commit v7 on v5

--- a/solution.py
+++ b/solution.py
@@ -2,7 +2,6 @@
 import jax.numpy as jnp
 from jax import lax
 from jax.experimental import pallas as pl
-from jax.experimental.layout import Layout, with_layout_constraint
 from jax.experimental.pallas import tpu as pltpu
 from jax.sharding import PartitionSpec as P
 
@@ -22,8 +21,33 @@
 
 
 def project(amplitudes, vectors):
-    part = jnp.dot(amplitudes, vectors, preferred_element_type=jnp.float32)
-    return with_layout_constraint(part, Layout(major_to_minor=(0, 1)))
+    rows, depth = amplitudes.shape
+    width = vectors.shape[1]
+    block = block_of(depth, 512)
+    part = block_of(rows, 256)
+
+    def kernel(left_ref, right_ref, out_ref):
+        for at in range(0, rows, part):
+            cut = slice(at, at + part)
+            term = jnp.dot(left_ref[cut, :], right_ref[...], preferred_element_type=jnp.float32)
+
+            @pl.when(pl.program_id(0) == 0)
+            def _():
+                out_ref[cut, :] = term
+
+            @pl.when(pl.program_id(0) > 0)
+            def _():
+                out_ref[cut, :] += term
+
+    return pl.pallas_call(
+        kernel,
+        grid=(depth // block,),
+        in_specs=[pl.BlockSpec((rows, block), lambda k: (0, k)), pl.BlockSpec((block, width), lambda k: (k, 0))],
+        out_specs=pl.BlockSpec((rows, width), lambda k: (0, 0)),
+        out_shape=jax.ShapeDtypeStruct((rows, width), jnp.float32),
+        compiler_params=pltpu.CompilerParams(vmem_limit_bytes=VMEM_BYTES),
+        cost_estimate=FREE,
+    )(amplitudes, vectors)
 
 
 def project_wide(amplitudes, vectors):
@@ -134,7 +158,7 @@
             return jnp.where(mine, value, got).reshape(2 * value.shape[0], value.shape[1])
 
         def finish(value):
-            value = halve(halve(value, 2, jnp.bfloat16), 3, jnp.bfloat16).astype(jnp.bfloat16)
+            value = halve(halve(value, 2, jnp.float32), 3, jnp.float32).astype(jnp.bfloat16)
             return double(double(value, 3), 2)
 
         def both(value):

time: 174 us -> 191 us (1.098)
  Pallas kernels: 26.8 us -> 61.6 us
  matrix products: 19 us -> 0 us
  starting transfers between devices: 28.2 us -> 22.5 us
  other arithmetic: 4.29 us -> 8.92 us
  local copies, waits for them, and re-layouts: 9.99 us -> 12.3 us
    pallas_call x0 -> x3, Pallas kernels: none -> 34.8 us  [project(): pl.pallas_call(kernel, grid=(depth // block,), in_specs=[pl.BlockSpec((ro...]
    dot_general x3 -> x0, matrix products: 19 us -> none  [project(): part = jnp.dot(amplitudes, vectors, preferred_element_type=jnp.float32)]
    ppermute x3, waiting for transfers between devices: 9.51 us -> 3.74 us  [send_row(): lax.ppermute(vectors, 'row', [(i, (i + shift) % rows) for i in range(rows)])]
    ppermute x12, waiting for transfers between devices: 32.6 us -> 37.8 us  [exchange(): return lax.ppermute(value, 'col', [(i, i ^ bit) for i in range(cols)])]
    ppermute x12, starting transfers between devices: 13.6 us -> 8.68 us  [exchange(): return lax.ppermute(value, 'col', [(i, i ^ bit) for i in range(cols)])]
    unnamed x10 -> x14, local copies, waits for them, and re-layouts: 0.71 us -> 3.03 us
    select_n x4 -> x6, other arithmetic: 0.38 us -> 2.56 us  [split(): jnp.where(upper[step], low, high)]
  transfers between devices with their start and end apart: 17 -> 17, of which waited for: 15 -> 14; matrix products, arithmetic and copies ran while one was open for 14% -> 8% of each run, Pallas kernels for 6% -> 17%
where the time goes in v7:
time: 191 us; the launch traced here: 190 us
  Pallas kernels  61.6 us (32%)
  waiting for transfers between devices  59.5 us (31%)
  blocking collectives  24.6 us (13%)
  starting transfers between devices  22.5 us (12%)
  local copies, waits for them, and re-layouts  12.3 us (6%)
  other arithmetic  8.92 us (5%)
    ppermute x12, waiting for transfers between devices, exchange(): return lax.ppermute(value, 'col', [(i, i ^ bit) for i in range(cols)])  37.8 us
    pallas_call x3, Pallas kernels, project(): pl.pallas_call(kernel, grid=(depth // block,), in_specs=[pl.BlockSpec((ro...  34.8 us
    all_to_all x2, blocking collectives, spread(): lax.all_to_all(value, 'col', 0, 0, tiled=True, axis_index_groups=mates)  24.6 us
    all_to_all x2, waiting for transfers between devices, spread(): lax.all_to_all(value, 'col', 0, 0, tiled=True, axis_index_groups=mates)  17.9 us
    pallas_call x1, Pallas kernels, project_back(): pl.pallas_call(kernel, grid_spec=pltpu.PrefetchScalarGridSpec(num_scalar_...  17 us
    pallas_call x1, Pallas kernels, project_wide(): pl.pallas_call(kernel, grid=(steps,), in_specs=[pl.BlockSpec((rows, block...  9.81 us
    all_to_all x2, starting transfers between devices, spread(): lax.all_to_all(value, 'col', 0, 0, tiled=True, axis_index_groups=mates)  8.98 us
    ppermute x12, starting transfers between devices, exchange(): return lax.ppermute(value, 'col', [(i, i ^ bit) for i in range(cols)])  8.68 us
  transfers between devices with their start and end apart: 17, of which 14 were waited for; matrix products, arithmetic and copies ran while one was open for 8% of the time, Pallas kernels for 17%

profile of v7, /device:TPU:0, one launch (start us, length us, event | category | flops | bytes accessed | tf_op | source)
XLA Modules:
  0.0 189.7 jit_solution(754425701640695994)
XLA Ops:
  0.0 2.3 %slice.9 = bf16[4096,128]{1,0:T(8,128)(2,1)} slice(bf16[4096,640]{1,0:T(8,128)(2,1)} %refs_6_.1), slice={[0:4096], [0:128]} | slice | bytes 2097152 | tf_op jit(solution)/shard_map/slice | solution.py:200
  2.3 2.9 %collective-permute-start.8 = (bf16[4096,128]{1,0:T(8,128)(2,1)}, bf16[4096,128]{1,0:T(8,128)(2,1)S(1)}, u32[]{:S(2)}, u32[]{:S(2)}) collective-permute-start(bf16[4096,128]{1,0:T(8,128)(2,1)} %slice.9), channel_id=1, source_target_pairs={{0,16},{16,0},{1,17},{17,1},{2,18},{18,2},{3,19},{19,3},{4,20},{20... | collective-permute-start | bytes 3145736 | tf_op jit(solution)/shard_map/ppermute | solution.py:189
  5.2 9.8 %shard_map.37 = f32[1024,640]{1,0:T(8,128)S(1)} custom-call(bf16[1024,4096]{1,0:T(8,128)(2,1)} %left_ref.7, bf16[4096,640]{1,0:T(8,128)(2,1)} %refs_6_.1), custom_call_target="tpu_custom_call" | custom-call | tf_op jit(solution)/shard_map/pallas_call | solution.py:75
  15.0 5.9 %conditional.3 = (f32[512,640]{1,0:T(8,128)}, f32[256,640]{1,0:T(8,128)S(1)}, f32[256,640]{1,0:T(8,128)S(1)}) conditional(s32[]{:T(128)} %convert_element_type.37, () %tuple.42, (pred[]{:T(512)}, f32[1024,640]{1,0:T(8,128)S(1)}) %tuple.44), branch_computations={%region_0.0_spmd, %region_1.2_spmd} | conditional | flops 983040 | bytes 17039426 | solution.py:142
  15.1 0.1 slice_select_fusion
  15.2 0.1 collective-permute-start.7
  15.3 3.0 %collective-permute-done.7 = f32[512,640]{1,0:T(8,128)S(1)} collective-permute-done((f32[512,640]{1,0:T(8,128)S(1)}, f32[512,640]{1,0:T(8,128)S(1)}, u32[]{:S(2)}, u32[]{:S(2)}) %collective-permute-start.7) | collective-permute-done | bytes 1310752 | tf_op jit(solution)/shard_map/cond/branch_1_fun/ppermute | solution.py:132
  18.3 1.3 select_add_fusion
  19.6 1.4 fusion
  21.0 0.9 broadcast_select_fusion
  21.9 1.5 collective-permute-start.9
  23.4 4.5 %fusion.1 = (bf16[4096,256]{1,0:T(8,128)(2,1)}, bf16[4096,256]{1,0:T(8,128)(2,1)}) fusion(bf16[4096,640]{1,0:T(8,128)(2,1)} %refs_6_.1), kind=kLoop, calls=%fused_computation.21 | loop fusion | bytes 8388608 | tf_op jit(solution)/shard_map/slice | solution.py:200
  27.9 0.5 collective-permute-start.10
  28.5 0.1 collective-permute-done.8.right_ref.refs_7_
  28.6 1.0 copy-done.2
  29.6 10.4 %shard_map.38 = f32[1024,128]{1,0:T(8,128)} custom-call(bf16[1024,4096]{1,0:T(8,128)(2,1)} %left_ref.7, bf16[4096,128]{1,0:T(8,128)(2,1)} %copy-done.2), custom_call_target="tpu_custom_call" | custom-call | tf_op jit(solution)/shard_map/pallas_call | solution.py:42
  40.0 0.0 collective-permute-done.9
  40.0 31.6 %conditional.4 = (bf16[256,640]{1,0:T(8,128)(2,1)S(1)}) conditional(s32[]{:T(128)} %convert_element_type.37, () %tuple.41, (s32[]{:T(128)}, f32[256,640]{1,0:T(8,128)}, f32[256,640]{1,0:T(8,128)}) %tuple.48), branch_computations={%region_2.3_spmd, %region_3.4_spmd} | conditional | flops 819210 | bytes 9258224 | solution.py:142
  40.0 1.4 add.14
  41.4 1.9 %collective-permute-start = (f32[128,640]{1,0:T(8,128)S(1)}, f32[128,640]{1,0:T(8,128)S(1)}, u32[]{:S(2)}, u32[]{:S(2)}) collective-permute-start(f32[128,640]{1,0:T(8,128)S(1)} %slice_select_fusion.1), channel_id=1, source_target_pairs={{0,4},{1,5},{2,6},{3,7},{4,0},{5,1},{6,2},{7,3},{8,12},{9,13},{10,... | collective-permute-start | bytes 983048 | tf_op jit(solution)/shard_map/cond/branch_1_fun/ppermute | solution.py:132
  43.3 7.2 %collective-permute-done = f32[128,640]{1,0:T(8,128)S(1)} collective-permute-done((f32[128,640]{1,0:T(8,128)S(1)}, f32[128,640]{1,0:T(8,128)S(1)}, u32[]{:S(2)}, u32[]{:S(2)}) %collective-permute-start) | collective-permute-done | bytes 327712 | tf_op jit(solution)/shard_map/cond/branch_1_fun/ppermute | solution.py:132
  50.6 2.7 %collective-permute-start.1 = (f32[64,640]{1,0:T(8,128)S(1)}, f32[64,640]{1,0:T(8,128)S(1)}, u32[]{:S(2)}, u32[]{:S(2)}) collective-permute-start(f32[64,640]{1,0:T(8,128)S(1)} %slice_select_fusion.2), channel_id=1, source_target_pairs={{0,8},{1,9},{2,10},{3,11},{4,12},{5,13},{6,14},{7,15},{8,0},{9,1},... | collective-permute-start | bytes 491528 | tf_op jit(solution)/shard_map/cond/branch_1_fun/ppermute | solution.py:132
  53.3 0.1 broadcast_in_dim.54
  53.3 0.1 broadcast_in_dim.55
  53.4 6.3 %collective-permute-done.1 = f32[64,640]{1,0:T(8,128)S(1)} collective-permute-done((f32[64,640]{1,0:T(8,128)S(1)}, f32[64,640]{1,0:T(8,128)S(1)}, u32[]{:S(2)}, u32[]{:S(2)}) %collective-permute-start.1) | collective-permute-done | bytes 163872 | tf_op jit(solution)/shard_map/cond/branch_1_fun/ppermute | solution.py:132
  59.7 0.1 collective-permute-start.2
  59.8 6.2 %collective-permute-done.2 = bf16[64,640]{1,0:T(8,128)(2,1)S(1)} collective-permute-done((bf16[64,640]{1,0:T(8,128)(2,1)S(1)}, bf16[64,640]{1,0:T(8,128)(2,1)S(1)}, u32[]{:S(2)}, u32[]{:S(2)}) %collective-permute-start.2) | collective-permute-done | bytes 81952 | tf_op jit(solution)/shard_map/cond/branch_1_fun/ppermute | solution.py:132
  66.0 0.1 bitcast_select_fusion.1
  66.1 0.2 collective-permute-start.3
  66.3 0.1 broadcast_bitcast_fusion
  66.4 5.1 %collective-permute-done.3 = bf16[128,640]{1,0:T(8,128)(2,1)S(1)} collective-permute-done((bf16[128,640]{1,0:T(8,128)(2,1)S(1)}, bf16[128,640]{1,0:T(8,128)(2,1)S(1)}, u32[]{:S(2)}, u32[]{:S(2)}) %collective-permute-start.3) | collective-permute-done | bytes 163872 | tf_op jit(solution)/shard_map/cond/branch_1_fun/ppermute | solution.py:132
  71.5 0.1 bitcast_select_fusion
  71.6 1.4 collective-permute-start.12
  73.0 3.6 %collective-permute-done.10.right_ref.refs_8_ = bf16[4096,256]{1,0:T(8,128)(2,1)S(1)} collective-permute-done((bf16[4096,256]{1,0:T(8,128)(2,1)}, bf16[4096,256]{1,0:T(8,128)(2,1)S(1)}, u32[]{:S(2)}, u32[]{:S(2)}) %collective-permute-start.10) | collective-permute-done | bytes 2097184 | tf_op jit(solution)/shard_map/ppermute | solution.py:189
  76.6 1.3 copy-done.1
  78.0 12.1 %shard_map.39 = f32[1024,256]{1,0:T(8,128)} custom-call(bf16[1024,4096]{1,0:T(8,128)(2,1)} %left_ref.7, bf16[4096,256]{1,0:T(8,128)(2,1)} %copy-done.1), custom_call_target="tpu_custom_call" | custom-call | tf_op jit(solution)/shard_map/pallas_call | solution.py:42
  90.1 1.3 pad_maximum_fusion
  91.4 36.7 %conditional.5 = (bf16[512,640]{1,0:T(8,128)(2,1)}, bf16[512,640]{1,0:T(8,128)(2,1)}, bf16[512,384]{1,0:T(8,128)(2,1)}) conditional(s32[]{:T(128)} %convert_element_type.37, () %tuple.40, (pred[]{:T(512)}, bf16[256,640]{1,0:T(8,128)(2,1)S(1)}, pred[]{:T(512)}, f32[1024,384]{1,0:T(8,128)S(1)}) %tuple.50), branch_computations={%region_4.5_spmd, %region_5.7_spmd} | conditional | flops 1286147 | bytes 16746721 | solution.py:142
  91.4 0.1 slice_select_fusion.3
  91.5 0.1 collective-permute-start.6
  91.6 2.3 %collective-permute-done.6 = f32[512,384]{1,0:T(8,128)S(1)} collective-permute-done((f32[512,384]{1,0:T(8,128)S(1)}, f32[512,384]{1,0:T(8,128)S(1)}, u32[]{:S(2)}, u32[]{:S(2)}) %collective-permute-start.6) | collective-permute-done | bytes 786464 | tf_op jit(solution)/shard_map/cond/branch_1_fun/ppermute | solution.py:132
  93.9 0.9 add_convert_fusion.1
  94.8 4.9 %all-to-all-start = ((bf16[8,64,384]{2,1,0:T(8,128)(2,1)}), bf16[8,64,384]{2,1,0:T(8,128)(2,1)S(1)}, u32[]{:S(2)}, u32[]{:S(2)}) async-start(bf16[8,64,384]{2,1,0:T(8,128)(2,1)} %bitcast.7), calls=%async_computation | async-start | bytes 786432 | tf_op jit(solution)/shard_map/cond/branch_1_fun/all_to_all | solution.py:172
  99.6 2.0 %collective-permute-start.4 = (bf16[256,640]{1,0:T(8,128)(2,1)S(1)}, bf16[256,640]{1,0:T(8,128)(2,1)S(1)}, u32[]{:S(2)}, u32[]{:S(2)}) collective-permute-start(bf16[256,640]{1,0:T(8,128)(2,1)S(1)} %get-tuple-element.45), channel_id=1, source_target_pairs={{0,2},{1,3},{2,0},{3,1},{4,6},{5,7},{6,4},{7,5},{8,10},{9,11},{10,... | collective-permute-start | bytes 983048 | tf_op jit(solution)/shard_map/cond/branch_1_fun/ppermute | solution.py:132
  101.7 10.0 %all-to-all-done = bf16[8,64,384]{2,1,0:T(8,128)(2,1)S(1)} async-done(((bf16[8,64,384]{2,1,0:T(8,128)(2,1)}), bf16[8,64,384]{2,1,0:T(8,128)(2,1)S(1)}, u32[]{:S(2)}, u32[]{:S(2)}) %all-to-all-start) | async-done | bytes 393248 | tf_op jit(solution)/shard_map/cond/branch_1_fun/all_to_all | solution.py:172
  111.6 0.1 reduce_sum.22
  111.7 0.8 tile.0
  112.5 4.1 %all-to-all-start.1 = ((bf16[8,64,384]{2,1,0:T(8,128)(2,1)}), bf16[8,64,384]{2,1,0:T(8,128)(2,1)}, u32[]{:S(2)}, u32[]{:S(2)}) async-start(bf16[8,64,384]{2,1,0:T(8,128)(2,1)} %tile.0), calls=%async_computation.1 | async-start | bytes 786432 | tf_op jit(solution)/shard_map/cond/branch_1_fun/all_to_all | solution.py:172
  116.6 0.1 broadcast_in_dim.65
  116.7 0.0 collective-permute-done.4
  116.7 1.0 bitcast_select_fusion.2
  117.7 2.4 %collective-permute-done.5 = bf16[512,640]{1,0:T(8,128)(2,1)} collective-permute-done((bf16[512,640]{1,0:T(8,128)(2,1)}, bf16[512,640]{1,0:T(8,128)(2,1)}, u32[]{:S(2)}, u32[]{:S(2)}) %collective-permute-start.5) | collective-permute-done | bytes 655392 | tf_op jit(solution)/shard_map/cond/branch_1_fun/ppermute | solution.py:132
  120.1 8.0 %all-to-all-done.1 = bf16[8,64,384]{2,1,0:T(8,128)(2,1)} async-done(((bf16[8,64,384]{2,1,0:T(8,128)(2,1)}), bf16[8,64,384]{2,1,0:T(8,128)(2,1)}, u32[]{:S(2)}, u32[]{:S(2)}) %all-to-all-start.1) | async-done | bytes 393248 | tf_op jit(solution)/shard_map/cond/branch_1_fun/all_to_all | solution.py:172
  128.1 1.9 %collective-permute-done.11.refs_3_ = bf16[512,384]{1,0:T(8,128)(2,1)S(1)} collective-permute-done((bf16[512,384]{1,0:T(8,128)(2,1)}, bf16[512,384]{1,0:T(8,128)(2,1)S(1)}, u32[]{:S(2)}, u32[]{:S(2)}) %collective-permute-start.11) | collective-permute-done | bytes 393248 | tf_op jit(solution)/shard_map/ppermute | solution.py:132
  130.1 12.3 %shard_map.40 = f32[1024,256]{1,0:T(8,128)} custom-call(bf16[1024,4096]{1,0:T(8,128)(2,1)} %left_ref.7, bf16[4096,256]{1,0:T(8,128)(2,1)} %collective-permute-done.12.right_ref.refs_9_), custom_call_target="tpu_custom_call" | custom-call | tf_op jit(solution)/shard_map/pallas_call | solution.py:42
  142.3 1.4 slice_select_fusion.4
  143.7 0.2 collective-permute-start.13
  143.9 1.8 collective-permute-done.13
  145.7 0.1 add_convert_fusion.2
  145.8 12.6 %all_to_all.31 = bf16[8,64,256]{2,1,0:T(8,128)(2,1)S(1)} all-to-all(bf16[8,64,256]{2,1,0:T(8,128)(2,1)S(1)} %bitcast.21), channel_id=1, replica_groups={{0,2,4,6,8,10,12,14},{1,3,5,7,9,11,13,15},{16,18,20,22,24,26,28,30},{17..., dimensions={0} | all-to-all | bytes 524288 | tf_op jit(solution)/shard_map/all_to_all | solution.py:172
  158.5 12.0 %all_to_all.32 = bf16[8,64,256]{2,1,0:T(8,128)(2,1)S(1)} all-to-all(bf16[8,64,256]{2,1,0:T(8,128)(2,1)S(1)} %tile.4), channel_id=1, replica_groups={{0,2,4,6,8,10,12,14},{1,3,5,7,9,11,13,15},{16,18,20,22,24,26,28,30},{17..., dimensions={0} | all-to-all | bytes 524288 | tf_op jit(solution)/shard_map/all_to_all | solution.py:172
  170.5 1.5 collective-permute-done.14.refs_5_
  172.0 0.7 copy-done.6
  172.7 17.0 %shard_map.41 = bf16[1024,4096]{1,0:T(8,128)(2,1)} custom-call(s32[1]{0:T(128)} %bitcast.9.upper_ref, bf16[1024,4096]{1,0:T(8,128)(2,1)} %base_ref.1, bf16[512,640]{1,0:T(8,128)(2,1)} %get-tuple-element.67.refs_0_, bf16[512,640]{1,0:T(8,128)(2,1)} %get-tuple-element.68.refs_1_, bf16[512,384]{1,0:T(8,128)(2,1)} %get-tuple-element.69.refs_2_, ...), custom_call_target="tpu_custom_call" | custom-call | tf_op jit(solution)/shard_map/pallas_call | solution.py:111
  (25 shorter events, 0.3 us)
Async XLA Ops:
  2.3 26.3 %collective-permute-start.8 = (bf16[4096,128]{1,0:T(8,128)(2,1)}, bf16[4096,128]{1,0:T(8,128)(2,1)S(1)}, u32[]{:S(2)}, u32[]{:S(2)}) collective-permute-start(bf16[4096,128]{1,0:T(8,128)(2,1)} %slice.9), channel_id=1, source_target_pairs={{0,16},{16,0},{1,17},{17,1},{2,18},{18,2},{3,19},{19,3},{4,20},{20... | collective-permute-start | bytes 3145736 | tf_op jit(solution)/shard_map/ppermute | solution.py:189
  15.2 3.1 %collective-permute-start.7 = (f32[512,640]{1,0:T(8,128)S(1)}, f32[512,640]{1,0:T(8,128)S(1)}, u32[]{:S(2)}, u32[]{:S(2)}) collective-permute-start(f32[512,640]{1,0:T(8,128)S(1)} %slice_select_fusion), channel_id=1, source_target_pairs={{0,1},{1,0},{2,3},{3,2},{4,5},{5,4},{6,7},{7,6},{8,9},{9,8},{10,11... | collective-permute-start | bytes 3932168 | tf_op jit(solution)/shard_map/cond/branch_1_fun/ppermute | solution.py:132
  21.9 18.1 %collective-permute-start.9 = (f32[256,640]{1,0:T(8,128)S(1)}, f32[256,640]{1,0:T(8,128)}, u32[]{:S(2)}, u32[]{:S(2)}) collective-permute-start(f32[256,640]{1,0:T(8,128)S(1)} %get-tuple-element.76), channel_id=1, source_target_pairs={{0,2},{1,3},{2,0},{3,1},{4,6},{5,7},{6,4},{7,5},{8,10},{9,11},{10,... | collective-permute-start | bytes 1966088 | tf_op jit(solution)/shard_map/ppermute | solution.py:132
  27.9 48.7 %collective-permute-start.10 = (bf16[4096,256]{1,0:T(8,128)(2,1)}, bf16[4096,256]{1,0:T(8,128)(2,1)S(1)}, u32[]{:S(2)}, u32[]{:S(2)}) collective-permute-start(bf16[4096,256]{1,0:T(8,128)(2,1)} %get-tuple-element.63), channel_id=1, source_target_pairs={{0,16},{16,0},{1,17},{17,1},{2,18},{18,2},{3,19},{19,3},{4,20},{20... | collective-permute-start | bytes 6291464 | tf_op jit(solution)/shard_map/ppermute | solution.py:189
  28.6 1.0 copy-start.2
  41.4 9.1 %collective-permute-start = (f32[128,640]{1,0:T(8,128)S(1)}, f32[128,640]{1,0:T(8,128)S(1)}, u32[]{:S(2)}, u32[]{:S(2)}) collective-permute-start(f32[128,640]{1,0:T(8,128)S(1)} %slice_select_fusion.1), channel_id=1, source_target_pairs={{0,4},{1,5},{2,6},{3,7},{4,0},{5,1},{6,2},{7,3},{8,12},{9,13},{10,... | collective-permute-start | bytes 983048 | tf_op jit(solution)/shard_map/cond/branch_1_fun/ppermute | solution.py:132
  50.6 9.1 %collective-permute-start.1 = (f32[64,640]{1,0:T(8,128)S(1)}, f32[64,640]{1,0:T(8,128)S(1)}, u32[]{:S(2)}, u32[]{:S(2)}) collective-permute-start(f32[64,640]{1,0:T(8,128)S(1)} %slice_select_fusion.2), channel_id=1, source_target_pairs={{0,8},{1,9},{2,10},{3,11},{4,12},{5,13},{6,14},{7,15},{8,0},{9,1},... | collective-permute-start | bytes 491528 | tf_op jit(solution)/shard_map/cond/branch_1_fun/ppermute | solution.py:132
  59.7 6.3 %collective-permute-start.2 = (bf16[64,640]{1,0:T(8,128)(2,1)S(1)}, bf16[64,640]{1,0:T(8,128)(2,1)S(1)}, u32[]{:S(2)}, u32[]{:S(2)}) collective-permute-start(bf16[64,640]{1,0:T(8,128)(2,1)S(1)} %add_convert_fusion), channel_id=1, source_target_pairs={{0,8},{1,9},{2,10},{3,11},{4,12},{5,13},{6,14},{7,15},{8,0},{9,1},... | collective-permute-start | bytes 245768 | tf_op jit(solution)/shard_map/cond/branch_1_fun/ppermute | solution.py:132
  66.1 5.4 %collective-permute-start.3 = (bf16[128,640]{1,0:T(8,128)(2,1)S(1)}, bf16[128,640]{1,0:T(8,128)(2,1)S(1)}, u32[]{:S(2)}, u32[]{:S(2)}) collective-permute-start(bf16[128,640]{1,0:T(8,128)(2,1)S(1)} %bitcast_select_fusion.1), channel_id=1, source_target_pairs={{0,4},{1,5},{2,6},{3,7},{4,0},{5,1},{6,2},{7,3},{8,12},{9,13},{10,... | collective-permute-start | bytes 491528 | tf_op jit(solution)/shard_map/cond/branch_1_fun/ppermute | solution.py:132
  71.6 58.4 %collective-permute-start.12 = (bf16[4096,256]{1,0:T(8,128)(2,1)}, bf16[4096,256]{1,0:T(8,128)(2,1)}, u32[]{:S(2)}, u32[]{:S(2)}) collective-permute-start(bf16[4096,256]{1,0:T(8,128)(2,1)} %get-tuple-element.70), channel_id=1, source_target_pairs={{0,16},{16,0},{1,17},{17,1},{2,18},{18,2},{3,19},{19,3},{4,20},{20... | collective-permute-start | bytes 6291464 | tf_op jit(solution)/shard_map/ppermute | solution.py:189
  73.0 17.1 %copy-start.3 = (f32[1024,128]{1,0:T(8,128)S(1)}, f32[1024,128]{1,0:T(8,128)}, u32[]{:S(2)}) copy-start(f32[1024,128]{1,0:T(8,128)} %shard_map.38) | copy-start | bytes 1572868
  76.6 1.3 copy-start.1
  91.5 2.4 %collective-permute-start.6 = (f32[512,384]{1,0:T(8,128)S(1)}, f32[512,384]{1,0:T(8,128)S(1)}, u32[]{:S(2)}, u32[]{:S(2)}) collective-permute-start(f32[512,384]{1,0:T(8,128)S(1)} %slice_select_fusion.3), channel_id=1, source_target_pairs={{0,1},{1,0},{2,3},{3,2},{4,5},{5,4},{6,7},{7,6},{8,9},{9,8},{10,11... | collective-permute-start | bytes 2359304 | tf_op jit(solution)/shard_map/cond/branch_1_fun/ppermute | solution.py:132
  94.8 16.9 %all-to-all-start = ((bf16[8,64,384]{2,1,0:T(8,128)(2,1)}), bf16[8,64,384]{2,1,0:T(8,128)(2,1)S(1)}, u32[]{:S(2)}, u32[]{:S(2)}) async-start(bf16[8,64,384]{2,1,0:T(8,128)(2,1)} %bitcast.7), calls=%async_computation | async-start | bytes 786432 | tf_op jit(solution)/shard_map/cond/branch_1_fun/all_to_all | solution.py:172
  99.6 17.1 %collective-permute-start.4 = (bf16[256,640]{1,0:T(8,128)(2,1)S(1)}, bf16[256,640]{1,0:T(8,128)(2,1)S(1)}, u32[]{:S(2)}, u32[]{:S(2)}) collective-permute-start(bf16[256,640]{1,0:T(8,128)(2,1)S(1)} %get-tuple-element.45), channel_id=1, source_target_pairs={{0,2},{1,3},{2,0},{3,1},{4,6},{5,7},{6,4},{7,5},{8,10},{9,11},{10,... | collective-permute-start | bytes 983048 | tf_op jit(solution)/shard_map/cond/branch_1_fun/ppermute | solution.py:132
  112.5 15.6 %all-to-all-start.1 = ((bf16[8,64,384]{2,1,0:T(8,128)(2,1)}), bf16[8,64,384]{2,1,0:T(8,128)(2,1)}, u32[]{:S(2)}, u32[]{:S(2)}) async-start(bf16[8,64,384]{2,1,0:T(8,128)(2,1)} %tile.0), calls=%async_computation.1 | async-start | bytes 786432 | tf_op jit(solution)/shard_map/cond/branch_1_fun/all_to_all | solution.py:172
  117.7 2.4 %collective-permute-start.5 = (bf16[512,640]{1,0:T(8,128)(2,1)}, bf16[512,640]{1,0:T(8,128)(2,1)}, u32[]{:S(2)}, u32[]{:S(2)}) collective-permute-start(bf16[512,640]{1,0:T(8,128)(2,1)} %bitcast_select_fusion.2), channel_id=1, source_target_pairs={{0,1},{1,0},{2,3},{3,2},{4,5},{5,4},{6,7},{7,6},{8,9},{9,8},{10,11... | collective-permute-start | bytes 1966088 | tf_op jit(solution)/shard_map/cond/branch_1_fun/ppermute | solution.py:132
  128.1 1.9 %collective-permute-start.11 = (bf16[512,384]{1,0:T(8,128)(2,1)}, bf16[512,384]{1,0:T(8,128)(2,1)S(1)}, u32[]{:S(2)}, u32[]{:S(2)}) collective-permute-start(bf16[512,384]{1,0:T(8,128)(2,1)} %get-tuple-element.69.refs_2_), channel_id=1, source_target_pairs={{0,1},{1,0},{2,3},{3,2},{4,5},{5,4},{6,7},{7,6},{8,9},{9,8},{10,11... | collective-permute-start | bytes 1179656 | tf_op jit(solution)/shard_map/ppermute | solution.py:132
  130.1 12.3 %copy-start.5 = (bf16[512,384]{1,0:T(8,128)(2,1)}, bf16[512,384]{1,0:T(8,128)(2,1)S(1)}, u32[]{:S(2)}) copy-start(bf16[512,384]{1,0:T(8,128)(2,1)S(1)} %collective-permute-done.11.refs_3_) | copy-start | bytes 1179652
  142.3 3.3 %copy-start = (f32[1024,256]{1,0:T(8,128)S(1)}, f32[1024,256]{1,0:T(8,128)}, u32[]{:S(2)}) copy-start(f32[1024,256]{1,0:T(8,128)} %shard_map.40) | copy-start | bytes 3145732
  143.7 2.0 %collective-permute-start.13 = (f32[512,256]{1,0:T(8,128)S(1)}, f32[512,256]{1,0:T(8,128)S(1)}, u32[]{:S(2)}, u32[]{:S(2)}) collective-permute-start(f32[512,256]{1,0:T(8,128)S(1)} %slice_select_fusion.4), channel_id=1, source_target_pairs={{0,1},{1,0},{2,3},{3,2},{4,5},{5,4},{6,7},{7,6},{8,9},{9,8},{10,11... | collective-permute-start | bytes 1572872 | tf_op jit(solution)/shard_map/ppermute | solution.py:132
  170.5 1.5 copy-start.4
  170.5 1.5 collective-permute-start.14
  172.0 0.7 copy-start.6

commit v8 on v6

--- a/solution.py
+++ b/solution.py
@@ -10,6 +10,7 @@
 
 GROUPS = (128, 256, 256)
 VMEM_BYTES = 58 * 1024 * 1024
+TAIL_VMEM_BYTES = 34 * 1024 * 1024
 FREE = pl.CostEstimate(flops=0, bytes_accessed=0, transcendentals=0)
 
 
@@ -103,7 +104,7 @@
         ),
         out_shape=jax.ShapeDtypeStruct(base.shape, kind),
         input_output_aliases={} if earlier is None else {2: 0},
-        compiler_params=pltpu.CompilerParams(vmem_limit_bytes=VMEM_BYTES),
+        compiler_params=pltpu.CompilerParams(vmem_limit_bytes=TAIL_VMEM_BYTES),
         cost_estimate=pl.CostEstimate(
             flops=2 * rows * steps * block * sum(widths),
             bytes_accessed=rows * steps * block * (base.dtype.itemsize + jnp.dtype(kind).itemsize),
@@ -204,10 +205,10 @@
             total = done(residual, share=(0, 2))
             mine = after(scatter(part), total)
             total = done(after(residual, mine), share=(1, 2), earlier=total)
-            return after(gather(mine), total), total
-
-        half_c, total = boxed(tail, part_c, residual_in, own, pair_ab, cholesky, a, b)
-        return project_back(total, [both(half_c)], [c], flag, jnp.bfloat16)
+            pair_c = both(after(gather(mine), total))
+            return project_back(total, [pair_c], [c], flag, jnp.bfloat16)
+
+        return boxed(tail, part_c, residual_in, own, pair_ab, cholesky, a, b)
 
     in_specs = (P("row", "col"), P("row", "col"), P("col", "row"))
     return jax.shard_map(body, mesh=mesh, in_specs=in_specs, out_specs=P("row", "col"), check_vma=False)

time: 176 us -> 191 us (1.085)
  local copies, waits for them, and re-layouts: 11.5 us -> 33.1 us
  Pallas kernels: 39.1 us -> 32.8 us
    cond x0 -> x10, local copies, waits for them, and re-layouts: none -> 23.1 us
    pallas_call x3, Pallas kernels: 29.3 us -> 23 us  [project_back(): pl.pallas_call(kernel, grid_spec=pltpu.PrefetchScalarGridSpec(num_scalar_...]
  transfers between devices with their start and end apart: 19 -> 19, of which waited for: 13 -> 14; matrix products, arithmetic and copies ran while one was open for 15% -> 14% of each run, Pallas kernels for 16% -> 14%
where the time goes in v8:
time: 191 us; the launch traced here: 190 us
  waiting for transfers between devices  63.7 us (33%)
  local copies, waits for them, and re-layouts  33.1 us (17%)
  starting transfers between devices  32.8 us (17%)
  Pallas kernels  32.8 us (17%)
  matrix products  19 us (10%)
  other arithmetic  8.09 us (4%)
    ppermute x12, waiting for transfers between devices, exchange(): return lax.ppermute(value, 'col', [(i, i ^ bit) for i in range(cols)])  45.7 us
    cond x10, local copies, waits for them, and re-layouts  23.1 us
    pallas_call x3, Pallas kernels, project_back(): pl.pallas_call(kernel, grid_spec=pltpu.PrefetchScalarGridSpec(num_scalar_...  23 us
    all_to_all x4, starting transfers between devices, spread(): lax.all_to_all(value, 'col', 0, 0, tiled=True, axis_index_groups=mates)  19.8 us
    dot_general x3, matrix products, project(): part = jnp.dot(amplitudes, vectors, preferred_element_type=jnp.float32)  19 us
    all_to_all x4, waiting for transfers between devices, spread(): lax.all_to_all(value, 'col', 0, 0, tiled=True, axis_index_groups=mates)  17.9 us
    pallas_call x1, Pallas kernels, project_wide(): pl.pallas_call(kernel, grid=(steps,), in_specs=[pl.BlockSpec((rows, block...  9.81 us
    ppermute x12, starting transfers between devices, exchange(): return lax.ppermute(value, 'col', [(i, i ^ bit) for i in range(cols)])  8.98 us
  transfers between devices with their start and end apart: 19, of which 14 were waited for; matrix products, arithmetic and copies ran while one was open for 14% of the time, Pallas kernels for 14%

profile of v8, /device:TPU:0, one launch (start us, length us, event | category | flops | bytes accessed | tf_op | source)
XLA Modules:
  0.0 189.9 jit_solution(14469273819071539109)
XLA Ops:
  0.0 2.3 %slice.10 = bf16[4096,128]{1,0:T(8,128)(2,1)} slice(bf16[4096,640]{1,0:T(8,128)(2,1)} %right_ref), slice={[0:4096], [0:128]} | slice | bytes 2097152 | tf_op jit(solution)/shard_map/slice | solution.py:188
  2.3 2.9 %collective-permute-start.10 = (bf16[4096,128]{1,0:T(8,128)(2,1)}, bf16[4096,128]{1,0:T(8,128)(2,1)S(1)}, u32[]{:S(2)}, u32[]{:S(2)}) collective-permute-start(bf16[4096,128]{1,0:T(8,128)(2,1)} %slice.10), channel_id=1, source_target_pairs={{0,16},{16,0},{1,17},{17,1},{2,18},{18,2},{3,19},{19,3},{4,20},{20... | collective-permute-start | bytes 3145736 | tf_op jit(solution)/shard_map/ppermute | solution.py:177
  5.2 4.5 %fusion.1 = (bf16[4096,256]{1,0:T(8,128)(2,1)}, bf16[4096,256]{1,0:T(8,128)(2,1)}) fusion(bf16[4096,640]{1,0:T(8,128)(2,1)} %right_ref), kind=kLoop, calls=%fused_computation.24 | loop fusion | bytes 8388608 | tf_op jit(solution)/shard_map/slice | solution.py:188
  9.7 9.8 %shard_map.40 = f32[1024,640]{1,0:T(8,128)S(1)} custom-call(bf16[1024,4096]{1,0:T(8,128)(2,1)} %left_ref.1, bf16[4096,640]{1,0:T(8,128)(2,1)} %right_ref), custom_call_target="tpu_custom_call" | custom-call | tf_op jit(solution)/shard_map/pallas_call | solution.py:54
  19.6 5.9 %conditional.4 = (f32[512,640]{1,0:T(8,128)}, f32[256,640]{1,0:T(8,128)S(1)}, f32[256,640]{1,0:T(8,128)S(1)}) conditional(s32[]{:T(128)} %convert_element_type.34, () %tuple.51, (pred[]{:T(512)}, f32[1024,640]{1,0:T(8,128)S(1)}) %tuple.53), branch_computations={%region_0.0_spmd, %region_1.2_spmd} | conditional | flops 983040 | bytes 17039426 | solution.py:130
  19.6 0.1 slice_select_fusion
  19.7 0.1 collective-permute-start.9
  19.8 3.0 %collective-permute-done.9 = f32[512,640]{1,0:T(8,128)S(1)} collective-permute-done((f32[512,640]{1,0:T(8,128)S(1)}, f32[512,640]{1,0:T(8,128)S(1)}, u32[]{:S(2)}, u32[]{:S(2)}) %collective-permute-start.9) | collective-permute-done | bytes 1310752 | tf_op jit(solution)/shard_map/cond/branch_1_fun/ppermute | solution.py:120
  22.8 1.3 select_add_fusion
  24.1 1.4 fusion
  25.5 0.9 broadcast_select_fusion
  26.4 2.0 %collective-permute-start.11 = (f32[256,640]{1,0:T(8,128)S(1)}, f32[256,640]{1,0:T(8,128)}, u32[]{:S(2)}, u32[]{:S(2)}) collective-permute-start(f32[256,640]{1,0:T(8,128)S(1)} %get-tuple-element.122), channel_id=1, source_target_pairs={{0,2},{1,3},{2,0},{3,1},{4,6},{5,7},{6,4},{7,5},{8,10},{9,11},{10,... | collective-permute-start | bytes 1966088 | tf_op jit(solution)/shard_map/ppermute | solution.py:120
  28.5 0.1 collective-permute-done.10
  28.6 6.9 %convolution_bitcast_fusion.2 = f32[1024,128]{1,0:T(8,128)} fusion(bf16[1024,4096]{1,0:T(8,128)(2,1)} %left_ref.1, bf16[4096,128]{1,0:T(8,128)(2,1)S(1)} %collective-permute-done.10), kind=kOutput, calls=%fused_computation.20 | convolution fusion | flops 1073741824 | bytes 9961472 | tf_op jit(solution)/shard_map/dot_general | solution.py:28
  35.5 7.9 %collective-permute-done.11 = f32[256,640]{1,0:T(8,128)} collective-permute-done((f32[256,640]{1,0:T(8,128)S(1)}, f32[256,640]{1,0:T(8,128)}, u32[]{:S(2)}, u32[]{:S(2)}) %collective-permute-start.11) | collective-permute-done | bytes 655392 | tf_op jit(solution)/shard_map/ppermute | solution.py:120
  43.3 31.4 %conditional.5 = (bf16[256,640]{1,0:T(8,128)(2,1)S(1)}) conditional(s32[]{:T(128)} %convert_element_type.34, () %tuple.50, (s32[]{:T(128)}, f32[256,640]{1,0:T(8,128)}, f32[256,640]{1,0:T(8,128)}) %tuple.57), branch_computations={%region_2.3_spmd, %region_3.4_spmd} | conditional | flops 819210 | bytes 9258224 | solution.py:130
  43.3 1.4 add.14
  44.7 1.9 collective-permute-start
  46.6 7.1 %collective-permute-done = f32[128,640]{1,0:T(8,128)S(1)} collective-permute-done((f32[128,640]{1,0:T(8,128)S(1)}, f32[128,640]{1,0:T(8,128)S(1)}, u32[]{:S(2)}, u32[]{:S(2)}) %collective-permute-start) | collective-permute-done | bytes 327712 | tf_op jit(solution)/shard_map/cond/branch_1_fun/ppermute | solution.py:120
  53.8 2.6 %collective-permute-start.1 = (f32[64,640]{1,0:T(8,128)S(1)}, f32[64,640]{1,0:T(8,128)S(1)}, u32[]{:S(2)}, u32[]{:S(2)}) collective-permute-start(f32[64,640]{1,0:T(8,128)S(1)} %slice_select_fusion.2), channel_id=1, source_target_pairs={{0,8},{1,9},{2,10},{3,11},{4,12},{5,13},{6,14},{7,15},{8,0},{9,1},... | collective-permute-start | bytes 491528 | tf_op jit(solution)/shard_map/cond/branch_1_fun/ppermute | solution.py:120
  56.4 0.1 broadcast_in_dim.54
  56.5 0.1 broadcast_in_dim.55
  56.5 6.2 %collective-permute-done.1 = f32[64,640]{1,0:T(8,128)S(1)} collective-permute-done((f32[64,640]{1,0:T(8,128)S(1)}, f32[64,640]{1,0:T(8,128)S(1)}, u32[]{:S(2)}, u32[]{:S(2)}) %collective-permute-start.1) | collective-permute-done | bytes 163872 | tf_op jit(solution)/shard_map/cond/branch_1_fun/ppermute | solution.py:120
  62.8 0.1 collective-permute-start.2
  62.9 6.2 %collective-permute-done.2 = bf16[64,640]{1,0:T(8,128)(2,1)S(1)} collective-permute-done((bf16[64,640]{1,0:T(8,128)(2,1)S(1)}, bf16[64,640]{1,0:T(8,128)(2,1)S(1)}, u32[]{:S(2)}, u32[]{:S(2)}) %collective-permute-start.2) | collective-permute-done | bytes 81952 | tf_op jit(solution)/shard_map/cond/branch_1_fun/ppermute | solution.py:120
  69.1 0.1 bitcast_select_fusion.1
  69.2 0.1 collective-permute-start.3
  69.3 0.1 broadcast_bitcast_fusion
  69.4 5.2 %collective-permute-done.3 = bf16[128,640]{1,0:T(8,128)(2,1)S(1)} collective-permute-done((bf16[128,640]{1,0:T(8,128)(2,1)S(1)}, bf16[128,640]{1,0:T(8,128)(2,1)S(1)}, u32[]{:S(2)}, u32[]{:S(2)}) %collective-permute-start.3) | collective-permute-done | bytes 163872 | tf_op jit(solution)/shard_map/cond/branch_1_fun/ppermute | solution.py:120
  74.6 0.1 bitcast_select_fusion
  74.7 1.1 collective-permute-start.12
  75.8 5.8 %convolution_bitcast_fusion.1 = f32[1024,256]{1,0:T(8,128)S(1)} fusion(bf16[1024,4096]{1,0:T(8,128)(2,1)} %left_ref.1, bf16[4096,256]{1,0:T(8,128)(2,1)S(1)} %collective-permute-done.13), kind=kOutput, calls=%fused_computation.19 | convolution fusion | flops 2147483648 | bytes 11534336 | tf_op jit(solution)/shard_map/dot_general | solution.py:28
  81.6 0.1 pad_maximum_fusion
  81.7 36.6 %conditional.6 = (bf16[512,640]{1,0:T(8,128)(2,1)}, bf16[512,640]{1,0:T(8,128)(2,1)}, bf16[512,384]{1,0:T(8,128)(2,1)}) conditional(s32[]{:T(128)} %convert_element_type.34, () %tuple.59, (pred[]{:T(512)}, bf16[256,640]{1,0:T(8,128)(2,1)S(1)}, pred[]{:T(512)}, f32[1024,384]{1,0:T(8,128)S(1)}) %tuple.61), branch_computations={%region_4.5_spmd, %region_5.7_spmd} | conditional | flops 1286147 | bytes 16746721 | solution.py:130
  81.8 0.1 slice_select_fusion.3
  81.9 2.3 %collective-permute-done.6 = f32[512,384]{1,0:T(8,128)S(1)} collective-permute-done((f32[512,384]{1,0:T(8,128)S(1)}, f32[512,384]{1,0:T(8,128)S(1)}, u32[]{:S(2)}, u32[]{:S(2)}) %collective-permute-start.6) | collective-permute-done | bytes 786464 | tf_op jit(solution)/shard_map/cond/branch_1_fun/ppermute | solution.py:120
  84.2 0.9 add_convert_fusion.1
  85.1 4.8 %all-to-all-start = ((bf16[8,64,384]{2,1,0:T(8,128)(2,1)}), bf16[8,64,384]{2,1,0:T(8,128)(2,1)S(1)}, u32[]{:S(2)}, u32[]{:S(2)}) async-start(bf16[8,64,384]{2,1,0:T(8,128)(2,1)} %bitcast.7), calls=%async_computation | async-start | bytes 786432 | tf_op jit(solution)/shard_map/cond/branch_1_fun/all_to_all | solution.py:160
  89.9 2.0 %collective-permute-start.4 = (bf16[256,640]{1,0:T(8,128)(2,1)S(1)}, bf16[256,640]{1,0:T(8,128)(2,1)S(1)}, u32[]{:S(2)}, u32[]{:S(2)}) collective-permute-start(bf16[256,640]{1,0:T(8,128)(2,1)S(1)} %get-tuple-element.73), channel_id=1, source_target_pairs={{0,2},{1,3},{2,0},{3,1},{4,6},{5,7},{6,4},{7,5},{8,10},{9,11},{10,... | collective-permute-start | bytes 983048 | tf_op jit(solution)/shard_map/cond/branch_1_fun/ppermute | solution.py:120
  91.9 10.0 %all-to-all-done = bf16[8,64,384]{2,1,0:T(8,128)(2,1)S(1)} async-done(((bf16[8,64,384]{2,1,0:T(8,128)(2,1)}), bf16[8,64,384]{2,1,0:T(8,128)(2,1)S(1)}, u32[]{:S(2)}, u32[]{:S(2)}) %all-to-all-start) | async-done | bytes 393248 | tf_op jit(solution)/shard_map/cond/branch_1_fun/all_to_all | solution.py:160
  102.0 0.8 tile.0
  102.7 4.1 %all-to-all-start.1 = ((bf16[8,64,384]{2,1,0:T(8,128)(2,1)}), bf16[8,64,384]{2,1,0:T(8,128)(2,1)}, u32[]{:S(2)}, u32[]{:S(2)}) async-start(bf16[8,64,384]{2,1,0:T(8,128)(2,1)} %tile.0), calls=%async_computation.1 | async-start | bytes 786432 | tf_op jit(solution)/shard_map/cond/branch_1_fun/all_to_all | solution.py:160
  106.9 0.1 broadcast_in_dim.65
  107.0 1.0 bitcast_select_fusion.2
  108.0 2.4 %collective-permute-done.5 = bf16[512,640]{1,0:T(8,128)(2,1)} collective-permute-done((bf16[512,640]{1,0:T(8,128)(2,1)}, bf16[512,640]{1,0:T(8,128)(2,1)}, u32[]{:S(2)}, u32[]{:S(2)}) %collective-permute-start.5) | collective-permute-done | bytes 655392 | tf_op jit(solution)/shard_map/cond/branch_1_fun/ppermute | solution.py:120
  110.4 8.0 %all-to-all-done.1 = bf16[8,64,384]{2,1,0:T(8,128)(2,1)} async-done(((bf16[8,64,384]{2,1,0:T(8,128)(2,1)}), bf16[8,64,384]{2,1,0:T(8,128)(2,1)}, u32[]{:S(2)}, u32[]{:S(2)}) %all-to-all-start.1) | async-done | bytes 393248 | tf_op jit(solution)/shard_map/cond/branch_1_fun/all_to_all | solution.py:160
  118.4 1.9 %collective-permute-done.14 = bf16[512,384]{1,0:T(8,128)(2,1)S(1)} collective-permute-done((bf16[512,384]{1,0:T(8,128)(2,1)}, bf16[512,384]{1,0:T(8,128)(2,1)S(1)}, u32[]{:S(2)}, u32[]{:S(2)}) %collective-permute-start.14) | collective-permute-done | bytes 393248 | tf_op jit(solution)/shard_map/ppermute | solution.py:120
  120.3 6.3 %convolution_bitcast_fusion = f32[1024,256]{1,0:T(8,128)S(1)} fusion(bf16[1024,4096]{1,0:T(8,128)(2,1)} %left_ref.1, bf16[4096,256]{1,0:T(8,128)(2,1)} %collective-permute-done.12), kind=kOutput, calls=%fused_computation.18 | convolution fusion | flops 2147483648 | bytes 11534336 | tf_op jit(solution)/shard_map/dot_general | solution.py:28
  126.7 63.3 %conditional.7 = (bf16[1024,4096]{1,0:T(8,128)(2,1)}) conditional(s32[]{:T(128)} %convert_element_type.34, () %tuple.49, (s32[]{:T(128)}, pred[]{:T(512)}, f32[1024,256]{1,0:T(8,128)S(1)}, bf16[1024,4096]{1,0:T(8,128)(2,1)}, bf16[512,640]{1,0:T(8,128)(2,1)}, /*index=5*/bf16[512,640]{1,0:T(8,128)(2,1)}, bf16[512,384]{1,0:T(8,128)(2,1)}, ...), branch_computations={%region_7.8_spmd, %region_8.10_spmd} | conditional | flops 10738057216 | bytes 329056544 | solution.py:130
  126.9 0.2 collective-permute-start.7
  127.1 1.8 collective-permute-done.7
  128.9 0.8 add_convert_fusion.2
  129.7 4.9 %all-to-all-start.2 = ((bf16[8,64,256]{2,1,0:T(8,128)(2,1)}), bf16[8,64,256]{2,1,0:T(8,128)(2,1)}, u32[]{:S(2)}, u32[]{:S(2)}) async-start(bf16[8,64,256]{2,1,0:T(8,128)(2,1)} %bitcast.33), calls=%async_computation.2 | async-start | bytes 524288 | tf_op jit(solution)/shard_map/cond/branch_1_fun/all_to_all | solution.py:160
  134.6 7.9 %branch_1_fun.3.refs_0_ = f32[1024,4096]{1,0:T(8,128)S(1)} custom-call(s32[1]{0:T(128)} %bitcast.9.upper_ref, bf16[1024,4096]{1,0:T(8,128)(2,1)} %get-tuple-element.88.base_ref, bf16[512,640]{1,0:T(8,128)(2,1)} %get-tuple-element.80.refs_0_.refs_1_, bf16[512,640]{1,0:T(8,128)(2,1)} %get-tuple-element.81.refs_1_.refs_2_, ...), custom_call_target="tpu_custom_call" | custom-call | flops 4294967296 | bytes 12582912 | tf_op jit(solution)/shard_map/cond/branch_1_fun/pallas_call | solution.py:93
  142.6 5.8 %copy-done = f32[1024,4096]{1,0:T(8,128)} copy-done((f32[1024,4096]{1,0:T(8,128)}, f32[1024,4096]{1,0:T(8,128)S(1)}, u32[]{:S(2)}) %copy-start) | copy-done | bytes 16777240 | tf_op jit(solution)/shard_map/cond
  148.3 1.0 reduce_sum.23
  149.3 0.7 tile.2
  150.0 6.0 %all-to-all-start.3 = ((bf16[8,64,256]{2,1,0:T(8,128)(2,1)}), bf16[8,64,256]{2,1,0:T(8,128)(2,1)S(1)}, u32[]{:S(2)}, u32[]{:S(2)}) async-start(bf16[8,64,256]{2,1,0:T(8,128)(2,1)} %tile.2), calls=%async_computation.3 | async-start | bytes 524288 | tf_op jit(solution)/shard_map/cond/branch_1_fun/all_to_all | solution.py:160
  156.0 5.8 %copy-done.1 = f32[1024,4096]{1,0:T(8,128)S(1)} copy-done((f32[1024,4096]{1,0:T(8,128)S(1)}, f32[1024,4096]{1,0:T(8,128)}, u32[]{:S(2)}) %copy-start.1) | copy-done | bytes 16777240 | tf_op jit(solution)/shard_map/cond
  161.8 8.1 %branch_1_fun.4.base_ref = f32[1024,4096]{1,0:T(8,128)S(1)} custom-call(s32[1]{0:T(128)} %bitcast.9.upper_ref, bf16[1024,4096]{1,0:T(8,128)(2,1)} %get-tuple-element.88.base_ref, f32[1024,4096]{1,0:T(8,128)S(1)} %copy-done.1, bf16[512,640]{1,0:T(8,128)(2,1)} %get-tuple-element.80.refs_0_.refs_1_, ...), custom_call_target="tpu_custom_call", output_to_operand_aliasing={{}: (2, {})} | custom-call | flops 4294967296 | bytes 12582912 | tf_op jit(solution)/shard_map/cond/branch_1_fun/pallas_call | solution.py:93
  169.9 5.8 %copy-done.2 = f32[1024,4096]{1,0:T(8,128)} copy-done((f32[1024,4096]{1,0:T(8,128)}, f32[1024,4096]{1,0:T(8,128)S(1)}, u32[]{:S(2)}) %copy-start.2) | copy-done | bytes 16777240 | tf_op jit(solution)/shard_map/cond
  175.6 1.5 collective-permute-done.8.refs_1_
  177.2 5.8 %copy-done.3 = f32[1024,4096]{1,0:T(8,128)S(1)} copy-done((f32[1024,4096]{1,0:T(8,128)S(1)}, f32[1024,4096]{1,0:T(8,128)}, u32[]{:S(2)}) %copy-start.3) | copy-done | bytes 16777240 | tf_op jit(solution)/shard_map/cond
  182.9 7.0 %branch_1_fun.5 = bf16[1024,4096]{1,0:T(8,128)(2,1)} custom-call(s32[1]{0:T(128)} %bitcast.9.upper_ref, f32[1024,4096]{1,0:T(8,128)S(1)} %copy-done.3, bf16[512,256]{1,0:T(8,128)(2,1)S(1)} %bitcast.32, bf16[512,256]{1,0:T(8,128)(2,1)S(1)} %collective-permute-done.8.refs_1_, bf16[4096,256]{1,0:T(8,128)(2,1)} %get-tuple-element.90.refs_2_), custom_call_target="tpu_custom_call" | custom-call | flops 2147483648 | bytes 25165824 | tf_op jit(solution)/shard_map/cond/branch_1_fun/pallas_call | solution.py:93
  (32 shorter events, 0.4 us)
Async XLA Ops:
  2.3 26.3 %collective-permute-start.10 = (bf16[4096,128]{1,0:T(8,128)(2,1)}, bf16[4096,128]{1,0:T(8,128)(2,1)S(1)}, u32[]{:S(2)}, u32[]{:S(2)}) collective-permute-start(bf16[4096,128]{1,0:T(8,128)(2,1)} %slice.10), channel_id=1, source_target_pairs={{0,16},{16,0},{1,17},{17,1},{2,18},{18,2},{3,19},{19,3},{4,20},{20... | collective-permute-start | bytes 3145736 | tf_op jit(solution)/shard_map/ppermute | solution.py:177
  19.7 3.1 %collective-permute-start.9 = (f32[512,640]{1,0:T(8,128)S(1)}, f32[512,640]{1,0:T(8,128)S(1)}, u32[]{:S(2)}, u32[]{:S(2)}) collective-permute-start(f32[512,640]{1,0:T(8,128)S(1)} %slice_select_fusion), channel_id=1, source_target_pairs={{0,1},{1,0},{2,3},{3,2},{4,5},{5,4},{6,7},{7,6},{8,9},{9,8},{10,11... | collective-permute-start | bytes 3932168 | tf_op jit(solution)/shard_map/cond/branch_1_fun/ppermute | solution.py:120
  26.4 49.4 %collective-permute-start.13 = (bf16[4096,256]{1,0:T(8,128)(2,1)}, bf16[4096,256]{1,0:T(8,128)(2,1)S(1)}, u32[]{:S(2)}, u32[]{:S(2)}) collective-permute-start(bf16[4096,256]{1,0:T(8,128)(2,1)} %get-tuple-element.106), channel_id=1, source_target_pairs={{0,16},{16,0},{1,17},{17,1},{2,18},{18,2},{3,19},{19,3},{4,20},{20... | collective-permute-start | bytes 6291464 | tf_op jit(solution)/shard_map/ppermute | solution.py:177
  26.4 16.9 %collective-permute-start.11 = (f32[256,640]{1,0:T(8,128)S(1)}, f32[256,640]{1,0:T(8,128)}, u32[]{:S(2)}, u32[]{:S(2)}) collective-permute-start(f32[256,640]{1,0:T(8,128)S(1)} %get-tuple-element.122), channel_id=1, source_target_pairs={{0,2},{1,3},{2,0},{3,1},{4,6},{5,7},{6,4},{7,5},{8,10},{9,11},{10,... | collective-permute-start | bytes 1966088 | tf_op jit(solution)/shard_map/ppermute | solution.py:120
  28.6 6.9 %copy-start.4 = (bf16[4096,128]{1,0:T(8,128)(2,1)}, bf16[4096,128]{1,0:T(8,128)(2,1)S(1)}, u32[]{:S(2)}) copy-start(bf16[4096,128]{1,0:T(8,128)(2,1)S(1)} %collective-permute-done.10) | copy-start | bytes 3145732
  44.7 9.0 %collective-permute-start = (f32[128,640]{1,0:T(8,128)S(1)}, f32[128,640]{1,0:T(8,128)S(1)}, u32[]{:S(2)}, u32[]{:S(2)}) collective-permute-start(f32[128,640]{1,0:T(8,128)S(1)} %slice_select_fusion.1), channel_id=1, source_target_pairs={{0,4},{1,5},{2,6},{3,7},{4,0},{5,1},{6,2},{7,3},{8,12},{9,13},{10,... | collective-permute-start | bytes 983048 | tf_op jit(solution)/shard_map/cond/branch_1_fun/ppermute | solution.py:120
  53.8 9.0 %collective-permute-start.1 = (f32[64,640]{1,0:T(8,128)S(1)}, f32[64,640]{1,0:T(8,128)S(1)}, u32[]{:S(2)}, u32[]{:S(2)}) collective-permute-start(f32[64,640]{1,0:T(8,128)S(1)} %slice_select_fusion.2), channel_id=1, source_target_pairs={{0,8},{1,9},{2,10},{3,11},{4,12},{5,13},{6,14},{7,15},{8,0},{9,1},... | collective-permute-start | bytes 491528 | tf_op jit(solution)/shard_map/cond/branch_1_fun/ppermute | solution.py:120
  62.8 6.3 %collective-permute-start.2 = (bf16[64,640]{1,0:T(8,128)(2,1)S(1)}, bf16[64,640]{1,0:T(8,128)(2,1)S(1)}, u32[]{:S(2)}, u32[]{:S(2)}) collective-permute-start(bf16[64,640]{1,0:T(8,128)(2,1)S(1)} %add_convert_fusion), channel_id=1, source_target_pairs={{0,8},{1,9},{2,10},{3,11},{4,12},{5,13},{6,14},{7,15},{8,0},{9,1},... | collective-permute-start | bytes 245768 | tf_op jit(solution)/shard_map/cond/branch_1_fun/ppermute | solution.py:120
  69.2 5.4 %collective-permute-start.3 = (bf16[128,640]{1,0:T(8,128)(2,1)S(1)}, bf16[128,640]{1,0:T(8,128)(2,1)S(1)}, u32[]{:S(2)}, u32[]{:S(2)}) collective-permute-start(bf16[128,640]{1,0:T(8,128)(2,1)S(1)} %bitcast_select_fusion.1), channel_id=1, source_target_pairs={{0,4},{1,5},{2,6},{3,7},{4,0},{5,1},{6,2},{7,3},{8,12},{9,13},{10,... | collective-permute-start | bytes 491528 | tf_op jit(solution)/shard_map/cond/branch_1_fun/ppermute | solution.py:120
  74.7 45.6 %collective-permute-start.12 = (bf16[4096,256]{1,0:T(8,128)(2,1)}, bf16[4096,256]{1,0:T(8,128)(2,1)}, u32[]{:S(2)}, u32[]{:S(2)}) collective-permute-start(bf16[4096,256]{1,0:T(8,128)(2,1)} %get-tuple-element.109), channel_id=1, source_target_pairs={{0,16},{16,0},{1,17},{17,1},{2,18},{18,2},{3,19},{19,3},{4,20},{20... | collective-permute-start | bytes 6291464 | tf_op jit(solution)/shard_map/ppermute | solution.py:177
  75.8 5.8 %copy-start.7 = (f32[1024,128]{1,0:T(8,128)S(1)}, f32[1024,128]{1,0:T(8,128)}, u32[]{:S(2)}) copy-start(f32[1024,128]{1,0:T(8,128)} %convolution_bitcast_fusion.2) | copy-start | bytes 1572868
  81.9 2.4 %collective-permute-start.6 = (f32[512,384]{1,0:T(8,128)S(1)}, f32[512,384]{1,0:T(8,128)S(1)}, u32[]{:S(2)}, u32[]{:S(2)}) collective-permute-start(f32[512,384]{1,0:T(8,128)S(1)} %slice_select_fusion.3), channel_id=1, source_target_pairs={{0,1},{1,0},{2,3},{3,2},{4,5},{5,4},{6,7},{7,6},{8,9},{9,8},{10,11... | collective-permute-start | bytes 2359304 | tf_op jit(solution)/shard_map/cond/branch_1_fun/ppermute | solution.py:120
  85.1 16.8 %all-to-all-start = ((bf16[8,64,384]{2,1,0:T(8,128)(2,1)}), bf16[8,64,384]{2,1,0:T(8,128)(2,1)S(1)}, u32[]{:S(2)}, u32[]{:S(2)}) async-start(bf16[8,64,384]{2,1,0:T(8,128)(2,1)} %bitcast.7), calls=%async_computation | async-start | bytes 786432 | tf_op jit(solution)/shard_map/cond/branch_1_fun/all_to_all | solution.py:160
  89.9 17.0 %collective-permute-start.4 = (bf16[256,640]{1,0:T(8,128)(2,1)S(1)}, bf16[256,640]{1,0:T(8,128)(2,1)S(1)}, u32[]{:S(2)}, u32[]{:S(2)}) collective-permute-start(bf16[256,640]{1,0:T(8,128)(2,1)S(1)} %get-tuple-element.73), channel_id=1, source_target_pairs={{0,2},{1,3},{2,0},{3,1},{4,6},{5,7},{6,4},{7,5},{8,10},{9,11},{10,... | collective-permute-start | bytes 983048 | tf_op jit(solution)/shard_map/cond/branch_1_fun/ppermute | solution.py:120
  102.7 15.6 %all-to-all-start.1 = ((bf16[8,64,384]{2,1,0:T(8,128)(2,1)}), bf16[8,64,384]{2,1,0:T(8,128)(2,1)}, u32[]{:S(2)}, u32[]{:S(2)}) async-start(bf16[8,64,384]{2,1,0:T(8,128)(2,1)} %tile.0), calls=%async_computation.1 | async-start | bytes 786432 | tf_op jit(solution)/shard_map/cond/branch_1_fun/all_to_all | solution.py:160
  108.0 2.4 %collective-permute-start.5 = (bf16[512,640]{1,0:T(8,128)(2,1)}, bf16[512,640]{1,0:T(8,128)(2,1)}, u32[]{:S(2)}, u32[]{:S(2)}) collective-permute-start(bf16[512,640]{1,0:T(8,128)(2,1)} %bitcast_select_fusion.2), channel_id=1, source_target_pairs={{0,1},{1,0},{2,3},{3,2},{4,5},{5,4},{6,7},{7,6},{8,9},{9,8},{10,11... | collective-permute-start | bytes 1966088 | tf_op jit(solution)/shard_map/cond/branch_1_fun/ppermute | solution.py:120
  118.4 1.9 %collective-permute-start.14 = (bf16[512,384]{1,0:T(8,128)(2,1)}, bf16[512,384]{1,0:T(8,128)(2,1)S(1)}, u32[]{:S(2)}, u32[]{:S(2)}) collective-permute-start(bf16[512,384]{1,0:T(8,128)(2,1)} %get-tuple-element.111), channel_id=1, source_target_pairs={{0,1},{1,0},{2,3},{3,2},{4,5},{5,4},{6,7},{7,6},{8,9},{9,8},{10,11... | collective-permute-start | bytes 1179656 | tf_op jit(solution)/shard_map/ppermute | solution.py:120
  118.4 8.3 %copy-start.5 = (bf16[4096,128]{1,0:T(8,128)(2,1)S(1)}, bf16[4096,128]{1,0:T(8,128)(2,1)}, u32[]{:S(2)}) copy-start(bf16[4096,128]{1,0:T(8,128)(2,1)} %copy-done.4) | copy-start | bytes 3145732
  126.9 15.7 %copy-start.6 = (bf16[512,384]{1,0:T(8,128)(2,1)}, bf16[512,384]{1,0:T(8,128)(2,1)S(1)}, u32[]{:S(2)}) copy-start(bf16[512,384]{1,0:T(8,128)(2,1)S(1)} %get-tuple-element.83.refs_3_.refs_4_) | copy-start | bytes 1179652 | tf_op jit(solution)/shard_map/cond
  126.9 2.0 %collective-permute-start.7 = (f32[512,256]{1,0:T(8,128)S(1)}, f32[512,256]{1,0:T(8,128)S(1)}, u32[]{:S(2)}, u32[]{:S(2)}) collective-permute-start(f32[512,256]{1,0:T(8,128)S(1)} %slice_select_fusion.4), channel_id=1, source_target_pairs={{0,1},{1,0},{2,3},{3,2},{4,5},{5,4},{6,7},{7,6},{8,9},{9,8},{10,11... | collective-permute-start | bytes 1572872 | tf_op jit(solution)/shard_map/cond/branch_1_fun/ppermute | solution.py:120
  129.7 18.6 %all-to-all-start.2 = ((bf16[8,64,256]{2,1,0:T(8,128)(2,1)}), bf16[8,64,256]{2,1,0:T(8,128)(2,1)}, u32[]{:S(2)}, u32[]{:S(2)}) async-start(bf16[8,64,256]{2,1,0:T(8,128)(2,1)} %bitcast.33), calls=%async_computation.2 | async-start | bytes 524288 | tf_op jit(solution)/shard_map/cond/branch_1_fun/all_to_all | solution.py:160
  142.5 5.8 %copy-start = (f32[1024,4096]{1,0:T(8,128)}, f32[1024,4096]{1,0:T(8,128)S(1)}, u32[]{:S(2)}) copy-start(f32[1024,4096]{1,0:T(8,128)S(1)} %branch_1_fun.3.refs_0_) | copy-start | bytes 50331652 | tf_op jit(solution)/shard_map/cond
  150.0 25.6 %all-to-all-start.3 = ((bf16[8,64,256]{2,1,0:T(8,128)(2,1)}), bf16[8,64,256]{2,1,0:T(8,128)(2,1)S(1)}, u32[]{:S(2)}, u32[]{:S(2)}) async-start(bf16[8,64,256]{2,1,0:T(8,128)(2,1)} %tile.2), calls=%async_computation.3 | async-start | bytes 524288 | tf_op jit(solution)/shard_map/cond/branch_1_fun/all_to_all | solution.py:160
  156.0 5.8 %copy-start.1 = (f32[1024,4096]{1,0:T(8,128)S(1)}, f32[1024,4096]{1,0:T(8,128)}, u32[]{:S(2)}) copy-start(f32[1024,4096]{1,0:T(8,128)} %copy-done) | copy-start | bytes 50331652 | tf_op jit(solution)/shard_map/cond
  169.8 5.8 %copy-start.2 = (f32[1024,4096]{1,0:T(8,128)}, f32[1024,4096]{1,0:T(8,128)S(1)}, u32[]{:S(2)}) copy-start(f32[1024,4096]{1,0:T(8,128)S(1)} %branch_1_fun.4.base_ref) | copy-start | bytes 50331652 | tf_op jit(solution)/shard_map/cond
  175.6 1.5 collective-permute-start.8
  177.2 5.8 %copy-start.3 = (f32[1024,4096]{1,0:T(8,128)S(1)}, f32[1024,4096]{1,0:T(8,128)}, u32[]{:S(2)}) copy-start(f32[1024,4096]{1,0:T(8,128)} %copy-done.2) | copy-start | bytes 50331652 | tf_op jit(solution)/shard_map/cond

commit v9 on v6

--- a/solution.py
+++ b/solution.py
@@ -9,7 +9,7 @@
 from jax.sharding import PartitionSpec as P
 
 GROUPS = (128, 256, 256)
-VMEM_BYTES = 58 * 1024 * 1024
+VMEM_BYTES = 50 * 1024 * 1024
 FREE = pl.CostEstimate(flops=0, bytes_accessed=0, transcendentals=0)
 
 
@@ -199,15 +199,15 @@
         pair_ab = both(half_ab)
         part_c = project(amplitudes, after(c, *pair_ab))
 
-        def tail(part, residual, own, pair, *pieces):
-            done = functools.partial(project_back, chis=[own, pair], pieces=pieces, upper=flag, kind=jnp.float32)
+        def tail(part, residual, own, vectors):
+            done = functools.partial(project_back, chis=[own], pieces=[vectors], upper=flag, kind=jnp.float32)
             total = done(residual, share=(0, 2))
             mine = after(scatter(part), total)
             total = done(after(residual, mine), share=(1, 2), earlier=total)
             return after(gather(mine), total), total
 
-        half_c, total = boxed(tail, part_c, residual_in, own, pair_ab, cholesky, a, b)
-        return project_back(total, [both(half_c)], [c], flag, jnp.bfloat16)
+        half_c, total = boxed(tail, part_c, residual_in, own, cholesky)
+        return project_back(total, [pair_ab, both(half_c)], [a, b, c], flag, jnp.bfloat16)
 
     in_specs = (P("row", "col"), P("row", "col"), P("col", "row"))
     return jax.shard_map(body, mesh=mesh, in_specs=in_specs, out_specs=P("row", "col"), check_vma=False)

time: 176 us -> 181 us (1.028)
  other arithmetic: 8.73 us -> 13.1 us
  starting transfers between devices: 32.8 us -> 30.4 us
  waiting for transfers between devices: 63.9 us -> 66.1 us
    all_to_all x4, starting transfers between devices: 19.8 us -> 17.4 us  [spread(): lax.all_to_all(value, 'col', 0, 0, tiled=True, axis_index_groups=mates)]
  transfers between devices with their start and end apart: 19 -> 19, of which waited for: 13 -> 16; matrix products, arithmetic and copies ran while one was open for 15% -> 17% of each run, Pallas kernels for 16% -> 14%
where the time goes in v9:
time: 181 us; the launch traced here: 180 us
  waiting for transfers between devices  66.1 us (37%)
  Pallas kernels  39.2 us (22%)
  starting transfers between devices  30.4 us (17%)
  matrix products  18.6 us (10%)
  other arithmetic  13.1 us (7%)
  local copies, waits for them, and re-layouts  12.4 us (7%)
    ppermute x12, waiting for transfers between devices, exchange(): return lax.ppermute(value, 'col', [(i, i ^ bit) for i in range(cols)])  46.7 us
    pallas_call x3, Pallas kernels, project_back(): pl.pallas_call(kernel, grid_spec=pltpu.PrefetchScalarGridSpec(num_scalar_...  29.4 us
    all_to_all x4, waiting for transfers between devices, spread(): lax.all_to_all(value, 'col', 0, 0, tiled=True, axis_index_groups=mates)  19.3 us
    dot_general x3, matrix products, project(): part = jnp.dot(amplitudes, vectors, preferred_element_type=jnp.float32)  18.6 us
    all_to_all x4, starting transfers between devices, spread(): lax.all_to_all(value, 'col', 0, 0, tiled=True, axis_index_groups=mates)  17.4 us
    pallas_call x1, Pallas kernels, project_wide(): pl.pallas_call(kernel, grid=(steps,), in_specs=[pl.BlockSpec((rows, block...  9.81 us
    ppermute x12, starting transfers between devices, exchange(): return lax.ppermute(value, 'col', [(i, i ^ bit) for i in range(cols)])  8.92 us
    slice x2, local copies, waits for them, and re-layouts, body(): cholesky[:, end - size:end]  6.82 us
  transfers between devices with their start and end apart: 19, of which 16 were waited for; matrix products, arithmetic and copies ran while one was open for 17% of the time, Pallas kernels for 14%

profile of v9, /device:TPU:0, one launch (start us, length us, event | category | flops | bytes accessed | tf_op | source)
XLA Modules:
  0.0 180.2 jit_solution(6150427189314198731)
XLA Ops:
  0.0 2.3 %slice.10 = bf16[4096,128]{1,0:T(8,128)(2,1)} slice(bf16[4096,640]{1,0:T(8,128)(2,1)} %right_ref), slice={[0:4096], [0:128]} | slice | bytes 2097152 | tf_op jit(solution)/shard_map/slice | solution.py:187
  2.3 2.9 %collective-permute-start.9 = (bf16[4096,128]{1,0:T(8,128)(2,1)}, bf16[4096,128]{1,0:T(8,128)(2,1)S(1)}, u32[]{:S(2)}, u32[]{:S(2)}) collective-permute-start(bf16[4096,128]{1,0:T(8,128)(2,1)} %slice.10), channel_id=1, source_target_pairs={{0,16},{16,0},{1,17},{17,1},{2,18},{18,2},{3,19},{19,3},{4,20},{20... | collective-permute-start | bytes 3145736 | tf_op jit(solution)/shard_map/ppermute | solution.py:176
  5.2 4.5 %fusion.1 = (bf16[4096,256]{1,0:T(8,128)(2,1)}, bf16[4096,256]{1,0:T(8,128)(2,1)}) fusion(bf16[4096,640]{1,0:T(8,128)(2,1)} %right_ref), kind=kLoop, calls=%fused_computation.24 | loop fusion | bytes 8388608 | tf_op jit(solution)/shard_map/slice | solution.py:187
  9.8 9.8 %shard_map.38 = f32[1024,640]{1,0:T(8,128)S(1)} custom-call(bf16[1024,4096]{1,0:T(8,128)(2,1)} %left_ref.1, bf16[4096,640]{1,0:T(8,128)(2,1)} %right_ref), custom_call_target="tpu_custom_call" | custom-call | tf_op jit(solution)/shard_map/pallas_call | solution.py:53
  19.6 6.0 %conditional.4 = (f32[512,640]{1,0:T(8,128)}, f32[256,640]{1,0:T(8,128)S(1)}, f32[256,640]{1,0:T(8,128)S(1)}) conditional(s32[]{:T(128)} %convert_element_type.34, () %tuple.53, (pred[]{:T(512)}, f32[1024,640]{1,0:T(8,128)S(1)}) %tuple.55), branch_computations={%region_0.0_spmd, %region_1.2_spmd} | conditional | flops 983040 | bytes 17039426 | solution.py:129
  19.6 0.1 slice_select_fusion
  19.7 0.1 collective-permute-start.8
  19.8 3.0 %collective-permute-done.8 = f32[512,640]{1,0:T(8,128)S(1)} collective-permute-done((f32[512,640]{1,0:T(8,128)S(1)}, f32[512,640]{1,0:T(8,128)S(1)}, u32[]{:S(2)}, u32[]{:S(2)}) %collective-permute-start.8) | collective-permute-done | bytes 1310752 | tf_op jit(solution)/shard_map/cond/branch_1_fun/ppermute | solution.py:119
  22.8 1.3 select_add_fusion
  24.2 1.4 fusion
  25.5 0.9 broadcast_select_fusion
  26.5 2.0 %collective-permute-start.10 = (f32[256,640]{1,0:T(8,128)S(1)}, f32[256,640]{1,0:T(8,128)}, u32[]{:S(2)}, u32[]{:S(2)}) collective-permute-start(f32[256,640]{1,0:T(8,128)S(1)} %get-tuple-element.106), channel_id=1, source_target_pairs={{0,2},{1,3},{2,0},{3,1},{4,6},{5,7},{6,4},{7,5},{8,10},{9,11},{10,... | collective-permute-start | bytes 1966088 | tf_op jit(solution)/shard_map/ppermute | solution.py:119
  28.6 6.5 %convolution_bitcast_fusion.2 = f32[1024,128]{1,0:T(8,128)} fusion(bf16[1024,4096]{1,0:T(8,128)(2,1)} %left_ref.1, bf16[4096,128]{1,0:T(8,128)(2,1)S(1)} %collective-permute-done.9.refs_4_), kind=kOutput, calls=%fused_computation.20 | convolution fusion | flops 1073741824 | bytes 9961472 | tf_op jit(solution)/shard_map/dot_general | solution.py:27
  35.1 8.3 %collective-permute-done.10 = f32[256,640]{1,0:T(8,128)} collective-permute-done((f32[256,640]{1,0:T(8,128)S(1)}, f32[256,640]{1,0:T(8,128)}, u32[]{:S(2)}, u32[]{:S(2)}) %collective-permute-start.10) | collective-permute-done | bytes 655392 | tf_op jit(solution)/shard_map/ppermute | solution.py:119
  43.4 35.3 %conditional.5 = (bf16[256,640]{1,0:T(8,128)(2,1)S(1)}) conditional(s32[]{:T(128)} %convert_element_type.34, () %tuple.52, (s32[]{:T(128)}, f32[256,640]{1,0:T(8,128)}, f32[256,640]{1,0:T(8,128)}) %tuple.59), branch_computations={%region_2.3_spmd, %region_3.4_spmd} | conditional | flops 819210 | bytes 11879692 | solution.py:129
  43.4 1.4 add.14
  44.7 0.8 copy-done
  45.6 1.9 %collective-permute-start = (f32[128,640]{1,0:T(8,128)S(1)}, f32[128,640]{1,0:T(8,128)}, u32[]{:S(2)}, u32[]{:S(2)}) collective-permute-start(f32[128,640]{1,0:T(8,128)S(1)} %slice_select_fusion.1), channel_id=1, source_target_pairs={{0,4},{1,5},{2,6},{3,7},{4,0},{5,1},{6,2},{7,3},{8,12},{9,13},{10,... | collective-permute-start | bytes 983048 | tf_op jit(solution)/shard_map/cond/branch_1_fun/ppermute | solution.py:119
  47.5 7.2 %collective-permute-done = f32[128,640]{1,0:T(8,128)} collective-permute-done((f32[128,640]{1,0:T(8,128)S(1)}, f32[128,640]{1,0:T(8,128)}, u32[]{:S(2)}, u32[]{:S(2)}) %collective-permute-start) | collective-permute-done | bytes 327712 | tf_op jit(solution)/shard_map/cond/branch_1_fun/ppermute | solution.py:119
  54.7 1.2 select_add_fusion.1
  55.9 0.7 slice_select_fusion.2
  56.6 2.5 %collective-permute-start.1 = (f32[64,640]{1,0:T(8,128)}, f32[64,640]{1,0:T(8,128)}, u32[]{:S(2)}, u32[]{:S(2)}) collective-permute-start(f32[64,640]{1,0:T(8,128)} %slice_select_fusion.2), channel_id=1, source_target_pairs={{0,8},{1,9},{2,10},{3,11},{4,12},{5,13},{6,14},{7,15},{8,0},{9,1},... | collective-permute-start | bytes 491528 | tf_op jit(solution)/shard_map/cond/branch_1_fun/ppermute | solution.py:119
  59.1 0.1 broadcast_in_dim.54
  59.2 0.1 broadcast_in_dim.55
  59.3 6.6 %collective-permute-done.1 = f32[64,640]{1,0:T(8,128)} collective-permute-done((f32[64,640]{1,0:T(8,128)}, f32[64,640]{1,0:T(8,128)}, u32[]{:S(2)}, u32[]{:S(2)}) %collective-permute-start.1) | collective-permute-done | bytes 163872 | tf_op jit(solution)/shard_map/cond/branch_1_fun/ppermute | solution.py:119
  65.8 0.9 add_convert_fusion
  66.9 6.2 %collective-permute-done.2 = bf16[64,640]{1,0:T(8,128)(2,1)S(1)} collective-permute-done((bf16[64,640]{1,0:T(8,128)(2,1)S(1)}, bf16[64,640]{1,0:T(8,128)(2,1)S(1)}, u32[]{:S(2)}, u32[]{:S(2)}) %collective-permute-start.2) | collective-permute-done | bytes 81952 | tf_op jit(solution)/shard_map/cond/branch_1_fun/ppermute | solution.py:119
  73.1 0.1 bitcast_select_fusion.1
  73.2 0.1 broadcast_bitcast_fusion
  73.3 5.2 %collective-permute-done.3 = bf16[128,640]{1,0:T(8,128)(2,1)S(1)} collective-permute-done((bf16[128,640]{1,0:T(8,128)(2,1)S(1)}, bf16[128,640]{1,0:T(8,128)(2,1)S(1)}, u32[]{:S(2)}, u32[]{:S(2)}) %collective-permute-start.3) | collective-permute-done | bytes 163872 | tf_op jit(solution)/shard_map/cond/branch_1_fun/ppermute | solution.py:119
  78.5 0.1 bitcast_select_fusion
  78.7 1.1 collective-permute-start.11
  79.8 5.8 %convolution_bitcast_fusion.1 = f32[1024,256]{1,0:T(8,128)S(1)} fusion(bf16[1024,4096]{1,0:T(8,128)(2,1)} %left_ref.1, bf16[4096,256]{1,0:T(8,128)(2,1)S(1)} %collective-permute-done.12.refs_5_), kind=kOutput, calls=%fused_computation.19 | convolution fusion | flops 2147483648 | bytes 11534336 | tf_op jit(solution)/shard_map/dot_general | solution.py:27
  85.6 0.1 pad_maximum_fusion
  85.7 38.1 %conditional.6 = (bf16[512,640]{1,0:T(8,128)(2,1)}, bf16[512,640]{1,0:T(8,128)(2,1)}, bf16[512,384]{1,0:T(8,128)(2,1)}) conditional(s32[]{:T(128)} %convert_element_type.34, () %tuple.61, (pred[]{:T(512)}, bf16[256,640]{1,0:T(8,128)(2,1)S(1)}, pred[]{:T(512)}, f32[1024,384]{1,0:T(8,128)S(1)}) %tuple.63), branch_computations={%region_4.5_spmd, %region_5.7_spmd} | conditional | flops 1286147 | bytes 18057468 | solution.py:129
  85.7 0.1 slice_select_fusion.3
  85.9 2.3 %collective-permute-done.6 = f32[512,384]{1,0:T(8,128)S(1)} collective-permute-done((f32[512,384]{1,0:T(8,128)S(1)}, f32[512,384]{1,0:T(8,128)S(1)}, u32[]{:S(2)}, u32[]{:S(2)}) %collective-permute-start.6) | collective-permute-done | bytes 786464 | tf_op jit(solution)/shard_map/cond/branch_1_fun/ppermute | solution.py:119
  88.2 0.9 add_convert_fusion.1
  89.0 4.8 %all-to-all-start = ((bf16[8,64,384]{2,1,0:T(8,128)(2,1)}), bf16[8,64,384]{2,1,0:T(8,128)(2,1)S(1)}, u32[]{:S(2)}, u32[]{:S(2)}) async-start(bf16[8,64,384]{2,1,0:T(8,128)(2,1)} %bitcast.31), calls=%async_computation | async-start | bytes 786432 | tf_op jit(solution)/shard_map/cond/branch_1_fun/all_to_all | solution.py:159
  93.9 2.0 %collective-permute-start.4 = (bf16[256,640]{1,0:T(8,128)(2,1)}, bf16[256,640]{1,0:T(8,128)(2,1)}, u32[]{:S(2)}, u32[]{:S(2)}) collective-permute-start(bf16[256,640]{1,0:T(8,128)(2,1)} %copy-done.1), channel_id=1, source_target_pairs={{0,2},{1,3},{2,0},{3,1},{4,6},{5,7},{6,4},{7,5},{8,10},{9,11},{10,... | collective-permute-start | bytes 983048 | tf_op jit(solution)/shard_map/cond/branch_1_fun/ppermute | solution.py:119
  95.9 10.0 %all-to-all-done = bf16[8,64,384]{2,1,0:T(8,128)(2,1)S(1)} async-done(((bf16[8,64,384]{2,1,0:T(8,128)(2,1)}), bf16[8,64,384]{2,1,0:T(8,128)(2,1)S(1)}, u32[]{:S(2)}, u32[]{:S(2)}) %all-to-all-start) | async-done | bytes 393248 | tf_op jit(solution)/shard_map/cond/branch_1_fun/all_to_all | solution.py:159
  105.9 0.7 reduce_sum.22
  106.5 1.6 tile.0
  108.1 4.1 %all-to-all-start.1 = ((bf16[8,64,384]{2,1,0:T(8,128)(2,1)}), bf16[8,64,384]{2,1,0:T(8,128)(2,1)}, u32[]{:S(2)}, u32[]{:S(2)}) async-start(bf16[8,64,384]{2,1,0:T(8,128)(2,1)} %tile.0), calls=%async_computation.1 | async-start | bytes 786432 | tf_op jit(solution)/shard_map/cond/branch_1_fun/all_to_all | solution.py:159
  112.2 0.1 broadcast_in_dim.65
  112.3 2.1 %bitcast_select_fusion.2 = bf16[512,640]{1,0:T(8,128)(2,1)} fusion(pred[512]{0:T(512)(128)(4,1)S(1)} %broadcast_in_dim.66, bf16[256,640]{1,0:T(8,128)(2,1)} %collective-permute-done.4, bf16[256,640]{1,0:T(8,128)(2,1)} %copy-done.1), kind=kLoop, calls=%fused_computation.13 | loop fusion | flops 327680 | bytes 1311232 | tf_op jit(solution)/shard_map/cond/branch_1_fun/jit(_where)/select_n | solution.py:145
  114.4 2.4 %collective-permute-done.5 = bf16[512,640]{1,0:T(8,128)(2,1)} collective-permute-done((bf16[512,640]{1,0:T(8,128)(2,1)}, bf16[512,640]{1,0:T(8,128)(2,1)}, u32[]{:S(2)}, u32[]{:S(2)}) %collective-permute-start.5) | collective-permute-done | bytes 655392 | tf_op jit(solution)/shard_map/cond/branch_1_fun/ppermute | solution.py:119
  116.9 6.9 %all-to-all-done.1 = bf16[8,64,384]{2,1,0:T(8,128)(2,1)} async-done(((bf16[8,64,384]{2,1,0:T(8,128)(2,1)}), bf16[8,64,384]{2,1,0:T(8,128)(2,1)}, u32[]{:S(2)}, u32[]{:S(2)}) %all-to-all-start.1) | async-done | bytes 393248 | tf_op jit(solution)/shard_map/cond/branch_1_fun/all_to_all | solution.py:159
  123.8 1.9 %collective-permute-done.13.refs_1_ = bf16[512,384]{1,0:T(8,128)(2,1)S(1)} collective-permute-done((bf16[512,384]{1,0:T(8,128)(2,1)}, bf16[512,384]{1,0:T(8,128)(2,1)S(1)}, u32[]{:S(2)}, u32[]{:S(2)}) %collective-permute-start.13) | collective-permute-done | bytes 393248 | tf_op jit(solution)/shard_map/ppermute | solution.py:119
  125.7 6.3 %convolution_bitcast_fusion = f32[1024,256]{1,0:T(8,128)S(1)} fusion(bf16[1024,4096]{1,0:T(8,128)(2,1)} %left_ref.1, bf16[4096,256]{1,0:T(8,128)(2,1)} %collective-permute-done.11.refs_6_), kind=kOutput, calls=%fused_computation.18 | convolution fusion | flops 2147483648 | bytes 11534336 | tf_op jit(solution)/shard_map/dot_general | solution.py:27
  132.0 33.1 %conditional.7 = (bf16[512,256]{1,0:T(8,128)(2,1)}, f32[1024,4096]{1,0:T(8,128)}) conditional(s32[]{:T(128)} %convert_element_type.34, () %tuple.51, (pred[]{:T(512)}, f32[1024,256]{1,0:T(8,128)S(1)}, s32[1]{0:T(128)}, bf16[1024,4096]{1,0:T(8,128)(2,1)}, bf16[512,640]{1,0:T(8,128)(2,1)}, /*index=5*/bf16[512,640]{1,0:T(8,128)(2,1)}, ...), branch_computations={%region_7.8_spmd, %region_8.10_spmd} | conditional | flops 5369348096 | bytes 32833660 | solution.py:129
  132.3 0.2 collective-permute-start.7
  132.5 1.8 collective-permute-done.7
  134.3 0.8 add_convert_fusion.2
  135.1 4.0 %all-to-all-start.2 = ((bf16[8,64,256]{2,1,0:T(8,128)(2,1)}), bf16[8,64,256]{2,1,0:T(8,128)(2,1)}, u32[]{:S(2)}, u32[]{:S(2)}) async-start(bf16[8,64,256]{2,1,0:T(8,128)(2,1)} %bitcast.32), calls=%async_computation.2 | async-start | bytes 524288 | tf_op jit(solution)/shard_map/cond/branch_1_fun/all_to_all | solution.py:159
  139.1 8.0 %branch_1_fun.2.refs_0_ = f32[1024,4096]{1,0:T(8,128)} custom-call(s32[1]{0:T(128)} %get-tuple-element.64.upper_ref, bf16[1024,4096]{1,0:T(8,128)(2,1)} %get-tuple-element.70.base_ref, bf16[512,640]{1,0:T(8,128)(2,1)} %get-tuple-element.66.refs_0_.refs_1_, bf16[512,640]{1,0:T(8,128)(2,1)} %get-tuple-element.67.refs_1_.refs_2_, ...), custom_call_target="tpu_custom_call" | custom-call | flops 2684354560 | bytes 12582912 | tf_op jit(solution)/shard_map/cond/branch_1_fun/pallas_call | solution.py:92
  147.2 1.5 all-to-all-done.2
  148.6 1.6 reduce_sum.23
  150.2 1.5 tile.2
  151.7 4.4 %all-to-all-start.3 = ((bf16[8,64,256]{2,1,0:T(8,128)(2,1)}), bf16[8,64,256]{2,1,0:T(8,128)(2,1)}, u32[]{:S(2)}, u32[]{:S(2)}) async-start(bf16[8,64,256]{2,1,0:T(8,128)(2,1)} %tile.2), calls=%async_computation.3 | async-start | bytes 524288 | tf_op jit(solution)/shard_map/cond/branch_1_fun/all_to_all | solution.py:159
  156.1 8.1 %branch_1_fun.3 = f32[1024,4096]{1,0:T(8,128)} custom-call(s32[1]{0:T(128)} %get-tuple-element.64.upper_ref, bf16[1024,4096]{1,0:T(8,128)(2,1)} %get-tuple-element.70.base_ref, f32[1024,4096]{1,0:T(8,128)} %branch_1_fun.2.refs_0_, bf16[512,640]{1,0:T(8,128)(2,1)} %get-tuple-element.66.refs_0_.refs_1_, ...), custom_call_target="tpu_custom_call", output_to_operand_aliasing={{}: (2, {})} | custom-call | flops 2684354560 | bytes 12582912 | tf_op jit(solution)/shard_map/cond/branch_1_fun/pallas_call | solution.py:92
  164.2 1.0 all-to-all-done.3
  165.2 1.7 collective-permute-done.14.refs_3_
  166.9 13.3 %shard_map.39 = bf16[1024,4096]{1,0:T(8,128)(2,1)} custom-call(s32[1]{0:T(128)} %bitcast.11.upper_ref, f32[1024,4096]{1,0:T(8,128)} %get-tuple-element.98.base_ref, bf16[512,384]{1,0:T(8,128)(2,1)} %get-tuple-element.94.refs_0_, bf16[512,384]{1,0:T(8,128)(2,1)S(1)} %collective-permute-done.13.refs_1_, bf16[512,256]{1,0:T(8,128)(2,1)} %get-tuple-element.99.refs_2_, ...), custom_call_target="tpu_custom_call" | custom-call | flops 5368709120 | bytes 25165824 | tf_op jit(solution)/shard_map/pallas_call | solution.py:92
  (22 shorter events, 0.4 us)
Async XLA Ops:
  2.3 26.3 %collective-permute-start.9 = (bf16[4096,128]{1,0:T(8,128)(2,1)}, bf16[4096,128]{1,0:T(8,128)(2,1)S(1)}, u32[]{:S(2)}, u32[]{:S(2)}) collective-permute-start(bf16[4096,128]{1,0:T(8,128)(2,1)} %slice.10), channel_id=1, source_target_pairs={{0,16},{16,0},{1,17},{17,1},{2,18},{18,2},{3,19},{19,3},{4,20},{20... | collective-permute-start | bytes 3145736 | tf_op jit(solution)/shard_map/ppermute | solution.py:176
  19.7 3.1 %collective-permute-start.8 = (f32[512,640]{1,0:T(8,128)S(1)}, f32[512,640]{1,0:T(8,128)S(1)}, u32[]{:S(2)}, u32[]{:S(2)}) collective-permute-start(f32[512,640]{1,0:T(8,128)S(1)} %slice_select_fusion), channel_id=1, source_target_pairs={{0,1},{1,0},{2,3},{3,2},{4,5},{5,4},{6,7},{7,6},{8,9},{9,8},{10,11... | collective-permute-start | bytes 3932168 | tf_op jit(solution)/shard_map/cond/branch_1_fun/ppermute | solution.py:119
  26.5 53.3 %collective-permute-start.12 = (bf16[4096,256]{1,0:T(8,128)(2,1)}, bf16[4096,256]{1,0:T(8,128)(2,1)S(1)}, u32[]{:S(2)}, u32[]{:S(2)}) collective-permute-start(bf16[4096,256]{1,0:T(8,128)(2,1)} %get-tuple-element.89), channel_id=1, source_target_pairs={{0,16},{16,0},{1,17},{17,1},{2,18},{18,2},{3,19},{19,3},{4,20},{20... | collective-permute-start | bytes 6291464 | tf_op jit(solution)/shard_map/ppermute | solution.py:176
  26.5 16.9 %collective-permute-start.10 = (f32[256,640]{1,0:T(8,128)S(1)}, f32[256,640]{1,0:T(8,128)}, u32[]{:S(2)}, u32[]{:S(2)}) collective-permute-start(f32[256,640]{1,0:T(8,128)S(1)} %get-tuple-element.106), channel_id=1, source_target_pairs={{0,2},{1,3},{2,0},{3,1},{4,6},{5,7},{6,4},{7,5},{8,10},{9,11},{10,... | collective-permute-start | bytes 1966088 | tf_op jit(solution)/shard_map/ppermute | solution.py:119
  44.7 0.8 copy-start
  45.6 9.1 %collective-permute-start = (f32[128,640]{1,0:T(8,128)S(1)}, f32[128,640]{1,0:T(8,128)}, u32[]{:S(2)}, u32[]{:S(2)}) collective-permute-start(f32[128,640]{1,0:T(8,128)S(1)} %slice_select_fusion.1), channel_id=1, source_target_pairs={{0,4},{1,5},{2,6},{3,7},{4,0},{5,1},{6,2},{7,3},{8,12},{9,13},{10,... | collective-permute-start | bytes 983048 | tf_op jit(solution)/shard_map/cond/branch_1_fun/ppermute | solution.py:119
  56.6 9.2 %collective-permute-start.1 = (f32[64,640]{1,0:T(8,128)}, f32[64,640]{1,0:T(8,128)}, u32[]{:S(2)}, u32[]{:S(2)}) collective-permute-start(f32[64,640]{1,0:T(8,128)} %slice_select_fusion.2), channel_id=1, source_target_pairs={{0,8},{1,9},{2,10},{3,11},{4,12},{5,13},{6,14},{7,15},{8,0},{9,1},... | collective-permute-start | bytes 491528 | tf_op jit(solution)/shard_map/cond/branch_1_fun/ppermute | solution.py:119
  66.8 6.3 %collective-permute-start.2 = (bf16[64,640]{1,0:T(8,128)(2,1)S(1)}, bf16[64,640]{1,0:T(8,128)(2,1)S(1)}, u32[]{:S(2)}, u32[]{:S(2)}) collective-permute-start(bf16[64,640]{1,0:T(8,128)(2,1)S(1)} %add_convert_fusion), channel_id=1, source_target_pairs={{0,8},{1,9},{2,10},{3,11},{4,12},{5,13},{6,14},{7,15},{8,0},{9,1},... | collective-permute-start | bytes 245768 | tf_op jit(solution)/shard_map/cond/branch_1_fun/ppermute | solution.py:119
  73.2 5.4 %collective-permute-start.3 = (bf16[128,640]{1,0:T(8,128)(2,1)S(1)}, bf16[128,640]{1,0:T(8,128)(2,1)S(1)}, u32[]{:S(2)}, u32[]{:S(2)}) collective-permute-start(bf16[128,640]{1,0:T(8,128)(2,1)S(1)} %bitcast_select_fusion.1), channel_id=1, source_target_pairs={{0,4},{1,5},{2,6},{3,7},{4,0},{5,1},{6,2},{7,3},{8,12},{9,13},{10,... | collective-permute-start | bytes 491528 | tf_op jit(solution)/shard_map/cond/branch_1_fun/ppermute | solution.py:119
  78.7 47.0 %collective-permute-start.11 = (bf16[4096,256]{1,0:T(8,128)(2,1)}, bf16[4096,256]{1,0:T(8,128)(2,1)}, u32[]{:S(2)}, u32[]{:S(2)}) collective-permute-start(bf16[4096,256]{1,0:T(8,128)(2,1)} %get-tuple-element.92), channel_id=1, source_target_pairs={{0,16},{16,0},{1,17},{17,1},{2,18},{18,2},{3,19},{19,3},{4,20},{20... | collective-permute-start | bytes 6291464 | tf_op jit(solution)/shard_map/ppermute | solution.py:176
  79.8 5.8 %copy-start.2 = (f32[1024,128]{1,0:T(8,128)S(1)}, f32[1024,128]{1,0:T(8,128)}, u32[]{:S(2)}) copy-start(f32[1024,128]{1,0:T(8,128)} %convolution_bitcast_fusion.2) | copy-start | bytes 1572868
  85.7 3.3 %copy-start.1 = (bf16[256,640]{1,0:T(8,128)(2,1)}, bf16[256,640]{1,0:T(8,128)(2,1)S(1)}, u32[]{:S(2)}) copy-start(bf16[256,640]{1,0:T(8,128)(2,1)S(1)} %get-tuple-element.59) | copy-start | bytes 983044 | tf_op jit(solution)/shard_map/cond
  85.8 2.4 %collective-permute-start.6 = (f32[512,384]{1,0:T(8,128)S(1)}, f32[512,384]{1,0:T(8,128)S(1)}, u32[]{:S(2)}, u32[]{:S(2)}) collective-permute-start(f32[512,384]{1,0:T(8,128)S(1)} %slice_select_fusion.3), channel_id=1, source_target_pairs={{0,1},{1,0},{2,3},{3,2},{4,5},{5,4},{6,7},{7,6},{8,9},{9,8},{10,11... | collective-permute-start | bytes 2359304 | tf_op jit(solution)/shard_map/cond/branch_1_fun/ppermute | solution.py:119
  89.0 16.8 %all-to-all-start = ((bf16[8,64,384]{2,1,0:T(8,128)(2,1)}), bf16[8,64,384]{2,1,0:T(8,128)(2,1)S(1)}, u32[]{:S(2)}, u32[]{:S(2)}) async-start(bf16[8,64,384]{2,1,0:T(8,128)(2,1)} %bitcast.31), calls=%async_computation | async-start | bytes 786432 | tf_op jit(solution)/shard_map/cond/branch_1_fun/all_to_all | solution.py:159
  93.9 18.4 %collective-permute-start.4 = (bf16[256,640]{1,0:T(8,128)(2,1)}, bf16[256,640]{1,0:T(8,128)(2,1)}, u32[]{:S(2)}, u32[]{:S(2)}) collective-permute-start(bf16[256,640]{1,0:T(8,128)(2,1)} %copy-done.1), channel_id=1, source_target_pairs={{0,2},{1,3},{2,0},{3,1},{4,6},{5,7},{6,4},{7,5},{8,10},{9,11},{10,... | collective-permute-start | bytes 983048 | tf_op jit(solution)/shard_map/cond/branch_1_fun/ppermute | solution.py:119
  108.1 15.6 %all-to-all-start.1 = ((bf16[8,64,384]{2,1,0:T(8,128)(2,1)}), bf16[8,64,384]{2,1,0:T(8,128)(2,1)}, u32[]{:S(2)}, u32[]{:S(2)}) async-start(bf16[8,64,384]{2,1,0:T(8,128)(2,1)} %tile.0), calls=%async_computation.1 | async-start | bytes 786432 | tf_op jit(solution)/shard_map/cond/branch_1_fun/all_to_all | solution.py:159
  114.4 2.4 %collective-permute-start.5 = (bf16[512,640]{1,0:T(8,128)(2,1)}, bf16[512,640]{1,0:T(8,128)(2,1)}, u32[]{:S(2)}, u32[]{:S(2)}) collective-permute-start(bf16[512,640]{1,0:T(8,128)(2,1)} %bitcast_select_fusion.2), channel_id=1, source_target_pairs={{0,1},{1,0},{2,3},{3,2},{4,5},{5,4},{6,7},{7,6},{8,9},{9,8},{10,11... | collective-permute-start | bytes 1966088 | tf_op jit(solution)/shard_map/cond/branch_1_fun/ppermute | solution.py:119
  123.8 1.9 %collective-permute-start.13 = (bf16[512,384]{1,0:T(8,128)(2,1)}, bf16[512,384]{1,0:T(8,128)(2,1)S(1)}, u32[]{:S(2)}, u32[]{:S(2)}) collective-permute-start(bf16[512,384]{1,0:T(8,128)(2,1)} %get-tuple-element.94.refs_0_), channel_id=1, source_target_pairs={{0,1},{1,0},{2,3},{3,2},{4,5},{5,4},{6,7},{7,6},{8,9},{9,8},{10,11... | collective-permute-start | bytes 1179656 | tf_op jit(solution)/shard_map/ppermute | solution.py:119
  132.3 2.0 %collective-permute-start.7 = (f32[512,256]{1,0:T(8,128)S(1)}, f32[512,256]{1,0:T(8,128)S(1)}, u32[]{:S(2)}, u32[]{:S(2)}) collective-permute-start(f32[512,256]{1,0:T(8,128)S(1)} %slice_select_fusion.4), channel_id=1, source_target_pairs={{0,1},{1,0},{2,3},{3,2},{4,5},{5,4},{6,7},{7,6},{8,9},{9,8},{10,11... | collective-permute-start | bytes 1572872 | tf_op jit(solution)/shard_map/cond/branch_1_fun/ppermute | solution.py:119
  135.1 13.6 %all-to-all-start.2 = ((bf16[8,64,256]{2,1,0:T(8,128)(2,1)}), bf16[8,64,256]{2,1,0:T(8,128)(2,1)}, u32[]{:S(2)}, u32[]{:S(2)}) async-start(bf16[8,64,256]{2,1,0:T(8,128)(2,1)} %bitcast.32), calls=%async_computation.2 | async-start | bytes 524288 | tf_op jit(solution)/shard_map/cond/branch_1_fun/all_to_all | solution.py:159
  151.7 13.5 %all-to-all-start.3 = ((bf16[8,64,256]{2,1,0:T(8,128)(2,1)}), bf16[8,64,256]{2,1,0:T(8,128)(2,1)}, u32[]{:S(2)}, u32[]{:S(2)}) async-start(bf16[8,64,256]{2,1,0:T(8,128)(2,1)} %tile.2), calls=%async_computation.3 | async-start | bytes 524288 | tf_op jit(solution)/shard_map/cond/branch_1_fun/all_to_all | solution.py:159
  165.2 1.7 collective-permute-start.14

commit v10 on v9

--- a/solution.py
+++ b/solution.py
@@ -9,7 +9,7 @@
 from jax.sharding import PartitionSpec as P
 
 GROUPS = (128, 256, 256)
-VMEM_BYTES = 50 * 1024 * 1024
+VMEM_BYTES = 58 * 1024 * 1024
 FREE = pl.CostEstimate(flops=0, bytes_accessed=0, transcendentals=0)
 
 
@@ -145,7 +145,7 @@
             return jnp.where(mine, value, got).reshape(2 * value.shape[0], value.shape[1])
 
         def finish(value):
-            value = halve(halve(value, 2, jnp.float32), 3, jnp.float32).astype(jnp.bfloat16)
+            value = halve(halve(value, 2, jnp.bfloat16), 3, jnp.bfloat16).astype(jnp.bfloat16)
             return double(double(value, 3), 2)
 
         def both(value):
@@ -167,10 +167,6 @@
 
         def chain(value):
             return gather(scatter(value))
-
-        def last(quarter, part):
-            mine = scatter(part)
-            return both(after(double(quarter, 1), mine)), gather(mine)
 
         def send_row(vectors, shift):
             return lax.ppermute(vectors, "row", [(i, (i + shift) % rows) for i in range(rows)])
@@ -194,20 +190,21 @@
         part_a = project(amplitudes, after(a, out_b))
         quarter = boxed(finish, after(keep, part_a) + got)
         c = send_row(after(out_c, quarter), 1)
-        part = jnp.concatenate([part_a, project(amplitudes, after(b, quarter))], axis=1)
-        own, half_ab = boxed(last, quarter, part)
-        pair_ab = both(half_ab)
-        part_c = project(amplitudes, after(c, *pair_ab))
-
-        def tail(part, residual, own, vectors):
+        half_own = double(quarter, 1)
+        own = both(half_own)
+        part = jnp.concatenate([part_a, project(amplitudes, after(b, half_own))], axis=1)
+
+        def beside(part, residual, own, vectors):
             done = functools.partial(project_back, chis=[own], pieces=[vectors], upper=flag, kind=jnp.float32)
             total = done(residual, share=(0, 2))
             mine = after(scatter(part), total)
             total = done(after(residual, mine), share=(1, 2), earlier=total)
             return after(gather(mine), total), total
 
-        half_c, total = boxed(tail, part_c, residual_in, own, cholesky)
-        return project_back(total, [pair_ab, both(half_c)], [a, b, c], flag, jnp.bfloat16)
+        half_ab, total = boxed(beside, part, residual_in, own, cholesky)
+        pair_ab = both(half_ab)
+        pair_c = both(chain(project(amplitudes, after(c, *pair_ab))))
+        return project_back(total, [pair_ab, pair_c], [a, b, c], flag, jnp.bfloat16)
 
     in_specs = (P("row", "col"), P("row", "col"), P("col", "row"))
     return jax.shard_map(body, mesh=mesh, in_specs=in_specs, out_specs=P("row", "col"), check_vma=False)

time: 181 us -> 173 us (0.956)
  blocking collectives: 0 us -> 24.6 us
  waiting for transfers between devices: 66.1 us -> 45.3 us
  other arithmetic: 13.1 us -> 4.48 us
  local copies, waits for them, and re-layouts: 12.4 us -> 10 us
  starting transfers between devices: 30.4 us -> 28.3 us
    all_to_all x0 -> x2, blocking collectives: none -> 24.6 us  [spread(): lax.all_to_all(value, 'col', 0, 0, tiled=True, axis_index_groups=mates)]
    ppermute x12, waiting for transfers between devices: 46.7 us -> 34.9 us  [exchange(): return lax.ppermute(value, 'col', [(i, i ^ bit) for i in range(cols)])]
    all_to_all x4 -> x2, waiting for transfers between devices: 19.3 us -> 8.34 us  [spread(): lax.all_to_all(value, 'col', 0, 0, tiled=True, axis_index_groups=mates)]
    all_to_all x4 -> x2, starting transfers between devices: 17.4 us -> 10.5 us  [spread(): lax.all_to_all(value, 'col', 0, 0, tiled=True, axis_index_groups=mates)]
    ppermute x12, starting transfers between devices: 8.92 us -> 13.2 us  [exchange(): return lax.ppermute(value, 'col', [(i, i ^ bit) for i in range(cols)])]
    another operation x2, local copies, waits for them, and re-layouts: 3.05 us -> 0.8 us  [gather(): return spread(jnp.tile(mine, (count, 1)))]
    ppermute x3, waiting for transfers between devices: 0.06 us -> 2.12 us  [send_row(): lax.ppermute(vectors, 'row', [(i, (i + shift) % rows) for i in range(rows)])]
    select_n x3, other arithmetic: 2.28 us -> 0.37 us  [double(): jnp.where(mine, value, got).reshape(2 * value.shape[0], value.shape[1])]
  transfers between devices with their start and end apart: 19 -> 17, of which waited for: 16 -> 15; matrix products, arithmetic and copies ran while one was open for 17% -> 14% of each run, Pallas kernels for 14% -> 15%
where the time goes in v10:
time: 173 us; the launch traced here: 172 us
  waiting for transfers between devices  45.3 us (26%)
  Pallas kernels  39.4 us (23%)
  starting transfers between devices  28.3 us (16%)
  blocking collectives  24.6 us (14%)
  matrix products  19.8 us (11%)
  local copies, waits for them, and re-layouts  10 us (6%)
  other arithmetic  4.48 us (3%)
    ppermute x12, waiting for transfers between devices, exchange(): return lax.ppermute(value, 'col', [(i, i ^ bit) for i in range(cols)])  34.9 us
    pallas_call x3, Pallas kernels, project_back(): pl.pallas_call(kernel, grid_spec=pltpu.PrefetchScalarGridSpec(num_scalar_...  29.6 us
    all_to_all x2, blocking collectives, spread(): lax.all_to_all(value, 'col', 0, 0, tiled=True, axis_index_groups=mates)  24.6 us
    dot_general x3, matrix products, project(): part = jnp.dot(amplitudes, vectors, preferred_element_type=jnp.float32)  19.8 us
    ppermute x12, starting transfers between devices, exchange(): return lax.ppermute(value, 'col', [(i, i ^ bit) for i in range(cols)])  13.2 us
    all_to_all x2, starting transfers between devices, spread(): lax.all_to_all(value, 'col', 0, 0, tiled=True, axis_index_groups=mates)  10.5 us
    pallas_call x1, Pallas kernels, project_wide(): pl.pallas_call(kernel, grid=(steps,), in_specs=[pl.BlockSpec((rows, block...  9.81 us
    all_to_all x2, waiting for transfers between devices, spread(): lax.all_to_all(value, 'col', 0, 0, tiled=True, axis_index_groups=mates)  8.34 us
  transfers between devices with their start and end apart: 17, of which 15 were waited for; matrix products, arithmetic and copies ran while one was open for 14% of the time, Pallas kernels for 15%

profile of v10, /device:TPU:0, one launch (start us, length us, event | category | flops | bytes accessed | tf_op | source)
XLA Modules:
  0.0 172.2 jit_solution(3492561399942388782)
XLA Ops:
  0.0 2.3 %slice.9 = bf16[4096,128]{1,0:T(8,128)(2,1)} slice(bf16[4096,640]{1,0:T(8,128)(2,1)} %right_ref), slice={[0:4096], [0:128]} | slice | bytes 2097152 | tf_op jit(solution)/shard_map/slice | solution.py:183
  2.3 2.9 %collective-permute-start.6 = (bf16[4096,128]{1,0:T(8,128)(2,1)}, bf16[4096,128]{1,0:T(8,128)(2,1)S(1)}, u32[]{:S(2)}, u32[]{:S(2)}) collective-permute-start(bf16[4096,128]{1,0:T(8,128)(2,1)} %slice.9), channel_id=1, source_target_pairs={{0,16},{16,0},{1,17},{17,1},{2,18},{18,2},{3,19},{19,3},{4,20},{20... | collective-permute-start | bytes 3145736 | tf_op jit(solution)/shard_map/ppermute | solution.py:172
  5.2 4.5 %fusion.1 = (bf16[4096,256]{1,0:T(8,128)(2,1)}, bf16[4096,256]{1,0:T(8,128)(2,1)}) fusion(bf16[4096,640]{1,0:T(8,128)(2,1)} %right_ref), kind=kLoop, calls=%fused_computation.24 | loop fusion | bytes 8388608 | tf_op jit(solution)/shard_map/slice | solution.py:183
  9.8 9.8 %shard_map.38 = f32[1024,640]{1,0:T(8,128)S(1)} custom-call(bf16[1024,4096]{1,0:T(8,128)(2,1)} %left_ref.1, bf16[4096,640]{1,0:T(8,128)(2,1)} %right_ref), custom_call_target="tpu_custom_call" | custom-call | tf_op jit(solution)/shard_map/pallas_call | solution.py:53
  19.6 6.0 %conditional.3 = (f32[512,640]{1,0:T(8,128)}, f32[256,640]{1,0:T(8,128)S(1)}, f32[256,640]{1,0:T(8,128)S(1)}) conditional(s32[]{:T(128)} %convert_element_type.45, () %tuple.43, (pred[]{:T(512)}, f32[1024,640]{1,0:T(8,128)S(1)}) %tuple.45), branch_computations={%region_0.0_spmd, %region_1.2_spmd} | conditional | flops 983040 | bytes 17039426 | solution.py:129
  19.6 0.1 slice_select_fusion
  19.7 0.1 collective-permute-start.5
  19.8 3.0 %collective-permute-done.5 = f32[512,640]{1,0:T(8,128)S(1)} collective-permute-done((f32[512,640]{1,0:T(8,128)S(1)}, f32[512,640]{1,0:T(8,128)S(1)}, u32[]{:S(2)}, u32[]{:S(2)}) %collective-permute-start.5) | collective-permute-done | bytes 1310752 | tf_op jit(solution)/shard_map/cond/branch_1_fun/ppermute | solution.py:119
  22.8 1.3 select_add_fusion
  24.2 1.4 fusion
  25.5 0.1 broadcast_select_fusion
  25.6 0.1 collective-permute-start.7
  25.7 2.0 %collective-permute-start.8 = (f32[256,640]{1,0:T(8,128)S(1)}, f32[256,640]{1,0:T(8,128)S(1)}, u32[]{:S(2)}, u32[]{:S(2)}) collective-permute-start(f32[256,640]{1,0:T(8,128)S(1)} %get-tuple-element.89), channel_id=1, source_target_pairs={{0,2},{1,3},{2,0},{3,1},{4,6},{5,7},{6,4},{7,5},{8,10},{9,11},{10,... | collective-permute-start | bytes 1966088 | tf_op jit(solution)/shard_map/ppermute | solution.py:119
  27.7 1.3 collective-permute-done.6.refs_4_
  29.1 6.9 %convolution_bitcast_fusion.2 = f32[1024,128]{1,0:T(8,128)} fusion(bf16[1024,4096]{1,0:T(8,128)(2,1)} %left_ref.1, bf16[4096,128]{1,0:T(8,128)(2,1)S(1)} %collective-permute-done.6.refs_4_), kind=kOutput, calls=%fused_computation.16 | convolution fusion | flops 1073741824 | bytes 9961472 | tf_op jit(solution)/shard_map/dot_general | solution.py:27
  36.0 6.5 %collective-permute-done.8 = f32[256,640]{1,0:T(8,128)S(1)} collective-permute-done((f32[256,640]{1,0:T(8,128)S(1)}, f32[256,640]{1,0:T(8,128)S(1)}, u32[]{:S(2)}, u32[]{:S(2)}) %collective-permute-start.8) | collective-permute-done | bytes 655392 | tf_op jit(solution)/shard_map/ppermute | solution.py:119
  42.5 22.2 %conditional.4 = (bf16[256,640]{1,0:T(8,128)(2,1)S(1)}) conditional(s32[]{:T(128)} %convert_element_type.45, () %tuple.48, (s32[]{:T(128)}, f32[256,640]{1,0:T(8,128)S(1)}, f32[256,640]{1,0:T(8,128)S(1)}) %tuple.50), branch_computations={%region_2.3_spmd, %region_3.4_spmd} | conditional | flops 942090 | bytes 7292144 | solution.py:129
  42.5 0.1 add.14
  42.7 1.8 %collective-permute-start = (bf16[128,640]{1,0:T(8,128)(2,1)S(1)}, bf16[128,640]{1,0:T(8,128)(2,1)S(1)}, u32[]{:S(2)}, u32[]{:S(2)}) collective-permute-start(bf16[128,640]{1,0:T(8,128)(2,1)S(1)} %select_convert_fusion), channel_id=1, source_target_pairs={{0,4},{1,5},{2,6},{3,7},{4,0},{5,1},{6,2},{7,3},{8,12},{9,13},{10,... | collective-permute-start | bytes 491528 | tf_op jit(solution)/shard_map/cond/branch_1_fun/ppermute | solution.py:119
  44.5 3.8 %collective-permute-done = bf16[128,640]{1,0:T(8,128)(2,1)S(1)} collective-permute-done((bf16[128,640]{1,0:T(8,128)(2,1)S(1)}, bf16[128,640]{1,0:T(8,128)(2,1)S(1)}, u32[]{:S(2)}, u32[]{:S(2)}) %collective-permute-start) | collective-permute-done | bytes 163872 | tf_op jit(solution)/shard_map/cond/branch_1_fun/ppermute | solution.py:119
  48.3 2.6 %collective-permute-start.1 = (bf16[64,640]{1,0:T(8,128)(2,1)S(1)}, bf16[64,640]{1,0:T(8,128)(2,1)S(1)}, u32[]{:S(2)}, u32[]{:S(2)}) collective-permute-start(bf16[64,640]{1,0:T(8,128)(2,1)S(1)} %select_convert_fusion.1), channel_id=1, source_target_pairs={{0,8},{1,9},{2,10},{3,11},{4,12},{5,13},{6,14},{7,15},{8,0},{9,1},... | collective-permute-start | bytes 245768 | tf_op jit(solution)/shard_map/cond/branch_1_fun/ppermute | solution.py:119
  51.0 0.1 broadcast_in_dim.54
  51.0 0.1 broadcast_in_dim.55
  51.1 2.6 %collective-permute-done.1 = bf16[64,640]{1,0:T(8,128)(2,1)S(1)} collective-permute-done((bf16[64,640]{1,0:T(8,128)(2,1)S(1)}, bf16[64,640]{1,0:T(8,128)(2,1)S(1)}, u32[]{:S(2)}, u32[]{:S(2)}) %collective-permute-start.1) | collective-permute-done | bytes 81952 | tf_op jit(solution)/shard_map/cond/branch_1_fun/ppermute | solution.py:119
  53.8 2.7 %collective-permute-start.2 = (bf16[64,640]{1,0:T(8,128)(2,1)S(1)}, bf16[64,640]{1,0:T(8,128)(2,1)S(1)}, u32[]{:S(2)}, u32[]{:S(2)}) collective-permute-start(bf16[64,640]{1,0:T(8,128)(2,1)S(1)} %add_convert_fusion), channel_id=1, source_target_pairs={{0,8},{1,9},{2,10},{3,11},{4,12},{5,13},{6,14},{7,15},{8,0},{9,1},... | collective-permute-start | bytes 245768 | tf_op jit(solution)/shard_map/cond/branch_1_fun/ppermute | solution.py:119
  56.5 2.7 %collective-permute-done.2 = bf16[64,640]{1,0:T(8,128)(2,1)S(1)} collective-permute-done((bf16[64,640]{1,0:T(8,128)(2,1)S(1)}, bf16[64,640]{1,0:T(8,128)(2,1)S(1)}, u32[]{:S(2)}, u32[]{:S(2)}) %collective-permute-start.2) | collective-permute-done | bytes 81952 | tf_op jit(solution)/shard_map/cond/branch_1_fun/ppermute | solution.py:119
  59.2 0.1 bitcast_select_fusion.1
  59.3 2.1 %collective-permute-start.3 = (bf16[128,640]{1,0:T(8,128)(2,1)S(1)}, bf16[128,640]{1,0:T(8,128)(2,1)S(1)}, u32[]{:S(2)}, u32[]{:S(2)}) collective-permute-start(bf16[128,640]{1,0:T(8,128)(2,1)S(1)} %bitcast_select_fusion.1), channel_id=1, source_target_pairs={{0,4},{1,5},{2,6},{3,7},{4,0},{5,1},{6,2},{7,3},{8,12},{9,13},{10,... | collective-permute-start | bytes 491528 | tf_op jit(solution)/shard_map/cond/branch_1_fun/ppermute | solution.py:119
  61.3 0.1 broadcast_bitcast_fusion
  61.4 3.3 %collective-permute-done.3 = bf16[128,640]{1,0:T(8,128)(2,1)S(1)} collective-permute-done((bf16[128,640]{1,0:T(8,128)(2,1)S(1)}, bf16[128,640]{1,0:T(8,128)(2,1)S(1)}, u32[]{:S(2)}, u32[]{:S(2)}) %collective-permute-start.3) | collective-permute-done | bytes 163872 | tf_op jit(solution)/shard_map/cond/branch_1_fun/ppermute | solution.py:119
  64.6 0.1 bitcast_select_fusion
  64.8 1.6 collective-permute-start.12
  66.4 1.5 collective-permute-start.9
  67.9 0.1 broadcast_in_dim.72
  68.0 5.5 %collective-permute-done.9 = bf16[256,640]{1,0:T(8,128)(2,1)S(1)} collective-permute-done((bf16[256,640]{1,0:T(8,128)(2,1)S(1)}, bf16[256,640]{1,0:T(8,128)(2,1)S(1)}, u32[]{:S(2)}, u32[]{:S(2)}) %collective-permute-start.9) | collective-permute-done | bytes 327712 | tf_op jit(solution)/shard_map/ppermute | solution.py:119
  73.5 0.2 bitcast_select_fusion.2
  73.6 0.1 collective-permute-start.10
  73.7 0.8 collective-permute-done.7.refs_5_
  74.5 6.3 %convolution_bitcast_fusion.1 = f32[1024,256]{1,0:T(8,128)S(1)} fusion(bf16[1024,4096]{1,0:T(8,128)(2,1)} %left_ref.1, bf16[4096,256]{1,0:T(8,128)(2,1)} %collective-permute-done.7.refs_5_), kind=kOutput, calls=%fused_computation.15 | convolution fusion | flops 2147483648 | bytes 11534336 | tf_op jit(solution)/shard_map/dot_general | solution.py:27
  80.8 0.1 pad_maximum_fusion
  80.9 39.6 %conditional.5 = (bf16[512,384]{1,0:T(8,128)(2,1)}, f32[1024,4096]{1,0:T(8,128)}) conditional(s32[]{:T(128)} %convert_element_type.45, () %tuple.42, (pred[]{:T(512)}, f32[1024,384]{1,0:T(8,128)S(1)}, s32[1]{0:T(128)}, bf16[1024,4096]{1,0:T(8,128)(2,1)}, bf16[512,640]{1,0:T(8,128)(2,1)S(1)}, /*index=5*/bf16[512,640]{1,0:T(8,128)(2,1)S(1)}, ...), branch_computations={%region_4.5_spmd, %region_5.7_spmd} | conditional | flops 5369667584 | bytes 36667516 | solution.py:129
  80.9 0.1 slice_select_fusion.1
  81.0 0.1 collective-permute-start.4
  81.1 2.3 %collective-permute-done.4 = f32[512,384]{1,0:T(8,128)S(1)} collective-permute-done((f32[512,384]{1,0:T(8,128)S(1)}, f32[512,384]{1,0:T(8,128)S(1)}, u32[]{:S(2)}, u32[]{:S(2)}) %collective-permute-start.4) | collective-permute-done | bytes 786464 | tf_op jit(solution)/shard_map/cond/branch_1_fun/ppermute | solution.py:119
  83.4 0.9 add_convert_fusion.1
  84.3 6.4 %all-to-all-start = ((bf16[8,64,384]{2,1,0:T(8,128)(2,1)}), bf16[8,64,384]{2,1,0:T(8,128)(2,1)}, u32[]{:S(2)}, u32[]{:S(2)}) async-start(bf16[8,64,384]{2,1,0:T(8,128)(2,1)} %bitcast.31), calls=%async_computation | async-start | bytes 786432 | tf_op jit(solution)/shard_map/cond/branch_1_fun/all_to_all | solution.py:159
  90.7 7.8 %branch_1_fun.2.refs_0_ = f32[1024,4096]{1,0:T(8,128)} custom-call(s32[1]{0:T(128)} %get-tuple-element.52.upper_ref, bf16[1024,4096]{1,0:T(8,128)(2,1)} %get-tuple-element.58.base_ref, bf16[512,640]{1,0:T(8,128)(2,1)S(1)} %get-tuple-element.54.refs_0_.refs_1_, bf16[512,640]{1,0:T(8,128)(2,1)S(1)} %get-tuple-element.55.refs_1_.refs_2_, ...), custom_call_target="tpu_custom_call" | custom-call | flops 2684354560 | bytes 12582912 | tf_op jit(solution)/shard_map/cond/branch_1_fun/pallas_call | solution.py:92
  98.5 4.5 %all-to-all-done = bf16[8,64,384]{2,1,0:T(8,128)(2,1)} async-done(((bf16[8,64,384]{2,1,0:T(8,128)(2,1)}), bf16[8,64,384]{2,1,0:T(8,128)(2,1)}, u32[]{:S(2)}, u32[]{:S(2)}) %all-to-all-start) | async-done | bytes 393248 | tf_op jit(solution)/shard_map/cond/branch_1_fun/all_to_all | solution.py:159
  103.0 1.1 reduce_sum.22
  104.0 0.8 tile.0
  104.8 4.1 %all-to-all-start.1 = ((bf16[8,64,384]{2,1,0:T(8,128)(2,1)}), bf16[8,64,384]{2,1,0:T(8,128)(2,1)}, u32[]{:S(2)}, u32[]{:S(2)}) async-start(bf16[8,64,384]{2,1,0:T(8,128)(2,1)} %tile.0), calls=%async_computation.1 | async-start | bytes 786432 | tf_op jit(solution)/shard_map/cond/branch_1_fun/all_to_all | solution.py:159
  108.9 7.7 %branch_1_fun.3 = f32[1024,4096]{1,0:T(8,128)} custom-call(s32[1]{0:T(128)} %get-tuple-element.52.upper_ref, bf16[1024,4096]{1,0:T(8,128)(2,1)} %get-tuple-element.58.base_ref, f32[1024,4096]{1,0:T(8,128)} %branch_1_fun.2.refs_0_, bf16[512,640]{1,0:T(8,128)(2,1)S(1)} %get-tuple-element.54.refs_0_.refs_1_, ...), custom_call_target="tpu_custom_call", output_to_operand_aliasing={{}: (2, {})} | custom-call | flops 2684354560 | bytes 12582912 | tf_op jit(solution)/shard_map/cond/branch_1_fun/pallas_call | solution.py:92
  116.7 3.8 %all-to-all-done.1 = bf16[8,64,384]{2,1,0:T(8,128)(2,1)} async-done(((bf16[8,64,384]{2,1,0:T(8,128)(2,1)}), bf16[8,64,384]{2,1,0:T(8,128)(2,1)}, u32[]{:S(2)}, u32[]{:S(2)}) %all-to-all-start.1) | async-done | bytes 393248 | tf_op jit(solution)/shard_map/cond/branch_1_fun/all_to_all | solution.py:159
  120.5 1.9 %collective-permute-done.11.refs_1_ = bf16[512,384]{1,0:T(8,128)(2,1)S(1)} collective-permute-done((bf16[512,384]{1,0:T(8,128)(2,1)}, bf16[512,384]{1,0:T(8,128)(2,1)S(1)}, u32[]{:S(2)}, u32[]{:S(2)}) %collective-permute-start.11) | collective-permute-done | bytes 393248 | tf_op jit(solution)/shard_map/ppermute | solution.py:119
  122.4 6.6 %convolution_bitcast_fusion = f32[1024,256]{1,0:T(8,128)S(1)} fusion(bf16[1024,4096]{1,0:T(8,128)(2,1)} %left_ref.1, bf16[4096,256]{1,0:T(8,128)(2,1)S(1)} %collective-permute-done.12.refs_6_), kind=kOutput, calls=%fused_computation.14 | convolution fusion | flops 2147483648 | bytes 11534336 | tf_op jit(solution)/shard_map/dot_general | solution.py:27
  129.1 0.1 slice_select_fusion.2
  129.1 0.2 collective-permute-start.13
  129.3 1.8 %collective-permute-done.13 = f32[512,256]{1,0:T(8,128)S(1)} collective-permute-done((f32[512,256]{1,0:T(8,128)S(1)}, f32[512,256]{1,0:T(8,128)S(1)}, u32[]{:S(2)}, u32[]{:S(2)}) %collective-permute-start.13) | collective-permute-done | bytes 524320 | tf_op jit(solution)/shard_map/ppermute | solution.py:119
  131.1 0.1 add_convert_fusion.2
  131.2 12.7 %all_to_all.31 = bf16[8,64,256]{2,1,0:T(8,128)(2,1)S(1)} all-to-all(bf16[8,64,256]{2,1,0:T(8,128)(2,1)S(1)} %bitcast.34), channel_id=1, replica_groups={{0,2,4,6,8,10,12,14},{1,3,5,7,9,11,13,15},{16,18,20,22,24,26,28,30},{17..., dimensions={0} | all-to-all | bytes 524288 | tf_op jit(solution)/shard_map/all_to_all | solution.py:159
  143.9 12.0 %all_to_all.32 = bf16[8,64,256]{2,1,0:T(8,128)(2,1)S(1)} all-to-all(bf16[8,64,256]{2,1,0:T(8,128)(2,1)S(1)} %tile.4), channel_id=1, replica_groups={{0,2,4,6,8,10,12,14},{1,3,5,7,9,11,13,15},{16,18,20,22,24,26,28,30},{17..., dimensions={0} | all-to-all | bytes 524288 | tf_op jit(solution)/shard_map/all_to_all | solution.py:159
  155.9 1.5 collective-permute-done.14.refs_3_
  157.4 0.7 copy-done.5
  158.1 14.1 %shard_map.39 = bf16[1024,4096]{1,0:T(8,128)(2,1)} custom-call(s32[1]{0:T(128)} %bitcast.7.upper_ref, f32[1024,4096]{1,0:T(8,128)} %get-tuple-element.78.base_ref, bf16[512,384]{1,0:T(8,128)(2,1)} %get-tuple-element.79.refs_0_, bf16[512,384]{1,0:T(8,128)(2,1)} %copy-done.4, bf16[512,256]{1,0:T(8,128)(2,1)} %bitcast.33, bf16[512,256]{1,0:T(8,128)(2,1)} %copy-done.5, ...), custom_call_target="tpu_custom_call" | custom-call | flops 5368709120 | bytes 25165824 | tf_op jit(solution)/shard_map/pallas_call | solution.py:92
  (25 shorter events, 0.2 us)
Async XLA Ops:
  2.3 26.8 %collective-permute-start.6 = (bf16[4096,128]{1,0:T(8,128)(2,1)}, bf16[4096,128]{1,0:T(8,128)(2,1)S(1)}, u32[]{:S(2)}, u32[]{:S(2)}) collective-permute-start(bf16[4096,128]{1,0:T(8,128)(2,1)} %slice.9), channel_id=1, source_target_pairs={{0,16},{16,0},{1,17},{17,1},{2,18},{18,2},{3,19},{19,3},{4,20},{20... | collective-permute-start | bytes 3145736 | tf_op jit(solution)/shard_map/ppermute | solution.py:172
  19.7 3.1 %collective-permute-start.5 = (f32[512,640]{1,0:T(8,128)S(1)}, f32[512,640]{1,0:T(8,128)S(1)}, u32[]{:S(2)}, u32[]{:S(2)}) collective-permute-start(f32[512,640]{1,0:T(8,128)S(1)} %slice_select_fusion), channel_id=1, source_target_pairs={{0,1},{1,0},{2,3},{3,2},{4,5},{5,4},{6,7},{7,6},{8,9},{9,8},{10,11... | collective-permute-start | bytes 3932168 | tf_op jit(solution)/shard_map/cond/branch_1_fun/ppermute | solution.py:119
  25.6 48.9 %collective-permute-start.7 = (bf16[4096,256]{1,0:T(8,128)(2,1)}, bf16[4096,256]{1,0:T(8,128)(2,1)}, u32[]{:S(2)}, u32[]{:S(2)}) collective-permute-start(bf16[4096,256]{1,0:T(8,128)(2,1)} %get-tuple-element.74), channel_id=1, source_target_pairs={{0,16},{16,0},{1,17},{17,1},{2,18},{18,2},{3,19},{19,3},{4,20},{20... | collective-permute-start | bytes 6291464 | tf_op jit(solution)/shard_map/ppermute | solution.py:172
  25.7 16.8 %collective-permute-start.8 = (f32[256,640]{1,0:T(8,128)S(1)}, f32[256,640]{1,0:T(8,128)S(1)}, u32[]{:S(2)}, u32[]{:S(2)}) collective-permute-start(f32[256,640]{1,0:T(8,128)S(1)} %get-tuple-element.89), channel_id=1, source_target_pairs={{0,2},{1,3},{2,0},{3,1},{4,6},{5,7},{6,4},{7,5},{8,10},{9,11},{10,... | collective-permute-start | bytes 1966088 | tf_op jit(solution)/shard_map/ppermute | solution.py:119
  29.1 6.9 %copy-start.2 = (bf16[4096,128]{1,0:T(8,128)(2,1)}, bf16[4096,128]{1,0:T(8,128)(2,1)S(1)}, u32[]{:S(2)}) copy-start(bf16[4096,128]{1,0:T(8,128)(2,1)S(1)} %collective-permute-done.6.refs_4_) | copy-start | bytes 3145732
  42.7 5.6 %collective-permute-start = (bf16[128,640]{1,0:T(8,128)(2,1)S(1)}, bf16[128,640]{1,0:T(8,128)(2,1)S(1)}, u32[]{:S(2)}, u32[]{:S(2)}) collective-permute-start(bf16[128,640]{1,0:T(8,128)(2,1)S(1)} %select_convert_fusion), channel_id=1, source_target_pairs={{0,4},{1,5},{2,6},{3,7},{4,0},{5,1},{6,2},{7,3},{8,12},{9,13},{10,... | collective-permute-start | bytes 491528 | tf_op jit(solution)/shard_map/cond/branch_1_fun/ppermute | solution.py:119
  48.3 5.4 %collective-permute-start.1 = (bf16[64,640]{1,0:T(8,128)(2,1)S(1)}, bf16[64,640]{1,0:T(8,128)(2,1)S(1)}, u32[]{:S(2)}, u32[]{:S(2)}) collective-permute-start(bf16[64,640]{1,0:T(8,128)(2,1)S(1)} %select_convert_fusion.1), channel_id=1, source_target_pairs={{0,8},{1,9},{2,10},{3,11},{4,12},{5,13},{6,14},{7,15},{8,0},{9,1},... | collective-permute-start | bytes 245768 | tf_op jit(solution)/shard_map/cond/branch_1_fun/ppermute | solution.py:119
  53.8 5.4 %collective-permute-start.2 = (bf16[64,640]{1,0:T(8,128)(2,1)S(1)}, bf16[64,640]{1,0:T(8,128)(2,1)S(1)}, u32[]{:S(2)}, u32[]{:S(2)}) collective-permute-start(bf16[64,640]{1,0:T(8,128)(2,1)S(1)} %add_convert_fusion), channel_id=1, source_target_pairs={{0,8},{1,9},{2,10},{3,11},{4,12},{5,13},{6,14},{7,15},{8,0},{9,1},... | collective-permute-start | bytes 245768 | tf_op jit(solution)/shard_map/cond/branch_1_fun/ppermute | solution.py:119
  59.3 5.4 %collective-permute-start.3 = (bf16[128,640]{1,0:T(8,128)(2,1)S(1)}, bf16[128,640]{1,0:T(8,128)(2,1)S(1)}, u32[]{:S(2)}, u32[]{:S(2)}) collective-permute-start(bf16[128,640]{1,0:T(8,128)(2,1)S(1)} %bitcast_select_fusion.1), channel_id=1, source_target_pairs={{0,4},{1,5},{2,6},{3,7},{4,0},{5,1},{6,2},{7,3},{8,12},{9,13},{10,... | collective-permute-start | bytes 491528 | tf_op jit(solution)/shard_map/cond/branch_1_fun/ppermute | solution.py:119
  64.8 57.6 %collective-permute-start.12 = (bf16[4096,256]{1,0:T(8,128)(2,1)}, bf16[4096,256]{1,0:T(8,128)(2,1)S(1)}, u32[]{:S(2)}, u32[]{:S(2)}) collective-permute-start(bf16[4096,256]{1,0:T(8,128)(2,1)} %get-tuple-element.80), channel_id=1, source_target_pairs={{0,16},{16,0},{1,17},{17,1},{2,18},{18,2},{3,19},{19,3},{4,20},{20... | collective-permute-start | bytes 6291464 | tf_op jit(solution)/shard_map/ppermute | solution.py:172
  66.4 7.1 %collective-permute-start.9 = (bf16[256,640]{1,0:T(8,128)(2,1)S(1)}, bf16[256,640]{1,0:T(8,128)(2,1)S(1)}, u32[]{:S(2)}, u32[]{:S(2)}) collective-permute-start(bf16[256,640]{1,0:T(8,128)(2,1)S(1)} %get-tuple-element.100), channel_id=1, source_target_pairs={{0,2},{1,3},{2,0},{3,1},{4,6},{5,7},{6,4},{7,5},{8,10},{9,11},{10,... | collective-permute-start | bytes 983048 | tf_op jit(solution)/shard_map/ppermute | solution.py:119
  73.6 7.2 %copy-start.3 = (f32[1024,128]{1,0:T(8,128)S(1)}, f32[1024,128]{1,0:T(8,128)}, u32[]{:S(2)}) copy-start(f32[1024,128]{1,0:T(8,128)} %convolution_bitcast_fusion.2) | copy-start | bytes 1572868
  73.6 7.3 %collective-permute-start.10 = (bf16[512,640]{1,0:T(8,128)(2,1)S(1)}, bf16[512,640]{1,0:T(8,128)(2,1)S(1)}, u32[]{:S(2)}, u32[]{:S(2)}) collective-permute-start(bf16[512,640]{1,0:T(8,128)(2,1)S(1)} %bitcast_select_fusion.2), channel_id=1, source_target_pairs={{0,1},{1,0},{2,3},{3,2},{4,5},{5,4},{6,7},{7,6},{8,9},{9,8},{10,11... | collective-permute-start | bytes 1966088 | tf_op jit(solution)/shard_map/ppermute | solution.py:119
  81.0 2.4 %collective-permute-start.4 = (f32[512,384]{1,0:T(8,128)S(1)}, f32[512,384]{1,0:T(8,128)S(1)}, u32[]{:S(2)}, u32[]{:S(2)}) collective-permute-start(f32[512,384]{1,0:T(8,128)S(1)} %slice_select_fusion.1), channel_id=1, source_target_pairs={{0,1},{1,0},{2,3},{3,2},{4,5},{5,4},{6,7},{7,6},{8,9},{9,8},{10,11... | collective-permute-start | bytes 2359304 | tf_op jit(solution)/shard_map/cond/branch_1_fun/ppermute | solution.py:119
  84.3 18.7 %all-to-all-start = ((bf16[8,64,384]{2,1,0:T(8,128)(2,1)}), bf16[8,64,384]{2,1,0:T(8,128)(2,1)}, u32[]{:S(2)}, u32[]{:S(2)}) async-start(bf16[8,64,384]{2,1,0:T(8,128)(2,1)} %bitcast.31), calls=%async_computation | async-start | bytes 786432 | tf_op jit(solution)/shard_map/cond/branch_1_fun/all_to_all | solution.py:159
  104.8 15.7 %all-to-all-start.1 = ((bf16[8,64,384]{2,1,0:T(8,128)(2,1)}), bf16[8,64,384]{2,1,0:T(8,128)(2,1)}, u32[]{:S(2)}, u32[]{:S(2)}) async-start(bf16[8,64,384]{2,1,0:T(8,128)(2,1)} %tile.0), calls=%async_computation.1 | async-start | bytes 786432 | tf_op jit(solution)/shard_map/cond/branch_1_fun/all_to_all | solution.py:159
  120.5 1.9 %collective-permute-start.11 = (bf16[512,384]{1,0:T(8,128)(2,1)}, bf16[512,384]{1,0:T(8,128)(2,1)S(1)}, u32[]{:S(2)}, u32[]{:S(2)}) collective-permute-start(bf16[512,384]{1,0:T(8,128)(2,1)} %get-tuple-element.79.refs_0_), channel_id=1, source_target_pairs={{0,1},{1,0},{2,3},{3,2},{4,5},{5,4},{6,7},{7,6},{8,9},{9,8},{10,11... | collective-permute-start | bytes 1179656 | tf_op jit(solution)/shard_map/ppermute | solution.py:119
  122.4 6.6 %copy-start.4 = (bf16[512,384]{1,0:T(8,128)(2,1)}, bf16[512,384]{1,0:T(8,128)(2,1)S(1)}, u32[]{:S(2)}) copy-start(bf16[512,384]{1,0:T(8,128)(2,1)S(1)} %collective-permute-done.11.refs_1_) | copy-start | bytes 1179652
  122.4 6.6 %copy-start = (bf16[4096,256]{1,0:T(8,128)(2,1)}, bf16[4096,256]{1,0:T(8,128)(2,1)S(1)}, u32[]{:S(2)}) copy-start(bf16[4096,256]{1,0:T(8,128)(2,1)S(1)} %collective-permute-done.12.refs_6_) | copy-start | bytes 6291460
  129.1 2.0 %collective-permute-start.13 = (f32[512,256]{1,0:T(8,128)S(1)}, f32[512,256]{1,0:T(8,128)S(1)}, u32[]{:S(2)}, u32[]{:S(2)}) collective-permute-start(f32[512,256]{1,0:T(8,128)S(1)} %slice_select_fusion.2), channel_id=1, source_target_pairs={{0,1},{1,0},{2,3},{3,2},{4,5},{5,4},{6,7},{7,6},{8,9},{9,8},{10,11... | collective-permute-start | bytes 1572872 | tf_op jit(solution)/shard_map/ppermute | solution.py:119
  155.9 1.5 copy-start.1
  155.9 1.5 collective-permute-start.14
  157.4 0.7 copy-start.5

commit v11 on v10

--- a/solution.py
+++ b/solution.py
@@ -203,7 +203,7 @@
 
         half_ab, total = boxed(beside, part, residual_in, own, cholesky)
         pair_ab = both(half_ab)
-        pair_c = both(chain(project(amplitudes, after(c, *pair_ab))))
+        pair_c = both(chain(project(amplitudes, after(c, half_ab))))
         return project_back(total, [pair_ab, pair_c], [a, b, c], flag, jnp.bfloat16)
 
     in_specs = (P("row", "col"), P("row", "col"), P("col", "row"))

time: 173 us -> 172 us (level)
  blocking collectives: 24.6 us -> 13.2 us
  waiting for transfers between devices: 45.3 us -> 52 us
  starting transfers between devices: 28.3 us -> 31.8 us
    all_to_all x2 -> x1, blocking collectives: 24.6 us -> 13.2 us  [spread(): lax.all_to_all(value, 'col', 0, 0, tiled=True, axis_index_groups=mates)]
    all_to_all x2 -> x3, waiting for transfers between devices: 8.34 us -> 16.9 us  [spread(): lax.all_to_all(value, 'col', 0, 0, tiled=True, axis_index_groups=mates)]
    all_to_all x2 -> x3, starting transfers between devices: 10.5 us -> 14.1 us  [spread(): lax.all_to_all(value, 'col', 0, 0, tiled=True, axis_index_groups=mates)]
    ppermute x12, waiting for transfers between devices: 34.9 us -> 32.8 us  [exchange(): return lax.ppermute(value, 'col', [(i, i ^ bit) for i in range(cols)])]
  transfers between devices with their start and end apart: 17 -> 18, of which waited for: 15 -> 15; matrix products, arithmetic and copies ran while one was open for 14% -> 14% of each run, Pallas kernels for 15% -> 15%
where the time goes in v11:
time: 172 us; the launch traced here: 171 us
  waiting for transfers between devices  52 us (30%)
  Pallas kernels  39.3 us (23%)
  starting transfers between devices  31.8 us (18%)
  matrix products  19.7 us (11%)
  blocking collectives  13.2 us (8%)
  local copies, waits for them, and re-layouts  10.8 us (6%)
  other arithmetic  4.45 us (3%)
    ppermute x12, waiting for transfers between devices, exchange(): return lax.ppermute(value, 'col', [(i, i ^ bit) for i in range(cols)])  32.8 us
    pallas_call x3, Pallas kernels, project_back(): pl.pallas_call(kernel, grid_spec=pltpu.PrefetchScalarGridSpec(num_scalar_...  29.5 us
    dot_general x3, matrix products, project(): part = jnp.dot(amplitudes, vectors, preferred_element_type=jnp.float32)  19.7 us
    all_to_all x3, waiting for transfers between devices, spread(): lax.all_to_all(value, 'col', 0, 0, tiled=True, axis_index_groups=mates)  16.9 us
    all_to_all x3, starting transfers between devices, spread(): lax.all_to_all(value, 'col', 0, 0, tiled=True, axis_index_groups=mates)  14.1 us
    ppermute x12, starting transfers between devices, exchange(): return lax.ppermute(value, 'col', [(i, i ^ bit) for i in range(cols)])  13.2 us
    all_to_all x1, blocking collectives, spread(): lax.all_to_all(value, 'col', 0, 0, tiled=True, axis_index_groups=mates)  13.2 us
    pallas_call x1, Pallas kernels, project_wide(): pl.pallas_call(kernel, grid=(steps,), in_specs=[pl.BlockSpec((rows, block...  9.81 us
  transfers between devices with their start and end apart: 18, of which 15 were waited for; matrix products, arithmetic and copies ran while one was open for 14% of the time, Pallas kernels for 15%

profile of v11, /device:TPU:0, one launch (start us, length us, event | category | flops | bytes accessed | tf_op | source)
XLA Modules:
  0.0 171.4 jit_solution(10065276216148154317)
XLA Ops:
  0.0 2.3 %slice.9 = bf16[4096,128]{1,0:T(8,128)(2,1)} slice(bf16[4096,640]{1,0:T(8,128)(2,1)} %right_ref), slice={[0:4096], [0:128]} | slice | bytes 2097152 | tf_op jit(solution)/shard_map/slice | solution.py:183
  2.3 2.9 %collective-permute-start.6 = (bf16[4096,128]{1,0:T(8,128)(2,1)}, bf16[4096,128]{1,0:T(8,128)(2,1)S(1)}, u32[]{:S(2)}, u32[]{:S(2)}) collective-permute-start(bf16[4096,128]{1,0:T(8,128)(2,1)} %slice.9), channel_id=1, source_target_pairs={{0,16},{16,0},{1,17},{17,1},{2,18},{18,2},{3,19},{19,3},{4,20},{20... | collective-permute-start | bytes 3145736 | tf_op jit(solution)/shard_map/ppermute | solution.py:172
  5.2 9.8 %shard_map.38 = f32[1024,640]{1,0:T(8,128)S(1)} custom-call(bf16[1024,4096]{1,0:T(8,128)(2,1)} %left_ref.1, bf16[4096,640]{1,0:T(8,128)(2,1)} %right_ref), custom_call_target="tpu_custom_call" | custom-call | tf_op jit(solution)/shard_map/pallas_call | solution.py:53
  15.0 5.9 %conditional.3 = (f32[512,640]{1,0:T(8,128)}, f32[256,640]{1,0:T(8,128)S(1)}, f32[256,640]{1,0:T(8,128)S(1)}) conditional(s32[]{:T(128)} %convert_element_type.45, () %tuple.43, (pred[]{:T(512)}, f32[1024,640]{1,0:T(8,128)S(1)}) %tuple.45), branch_computations={%region_0.0_spmd, %region_1.2_spmd} | conditional | flops 983040 | bytes 17039426 | solution.py:129
  15.0 0.1 slice_select_fusion
  15.2 0.1 collective-permute-start.5
  15.3 3.0 %collective-permute-done.5 = f32[512,640]{1,0:T(8,128)S(1)} collective-permute-done((f32[512,640]{1,0:T(8,128)S(1)}, f32[512,640]{1,0:T(8,128)S(1)}, u32[]{:S(2)}, u32[]{:S(2)}) %collective-permute-start.5) | collective-permute-done | bytes 1310752 | tf_op jit(solution)/shard_map/cond/branch_1_fun/ppermute | solution.py:119
  18.3 1.3 select_add_fusion
  19.6 1.4 fusion
  21.0 0.1 broadcast_select_fusion
  21.1 4.6 %fusion.1 = (bf16[4096,256]{1,0:T(8,128)(2,1)}, bf16[4096,256]{1,0:T(8,128)(2,1)}) fusion(bf16[4096,640]{1,0:T(8,128)(2,1)} %right_ref), kind=kLoop, calls=%fused_computation.24 | loop fusion | bytes 8388608 | tf_op jit(solution)/shard_map/slice | solution.py:183
  25.6 2.0 %collective-permute-start.8 = (f32[256,640]{1,0:T(8,128)S(1)}, f32[256,640]{1,0:T(8,128)S(1)}, u32[]{:S(2)}, u32[]{:S(2)}) collective-permute-start(f32[256,640]{1,0:T(8,128)S(1)} %get-tuple-element.89), channel_id=1, source_target_pairs={{0,2},{1,3},{2,0},{3,1},{4,6},{5,7},{6,4},{7,5},{8,10},{9,11},{10,... | collective-permute-start | bytes 1966088 | tf_op jit(solution)/shard_map/ppermute | solution.py:119
  27.7 1.4 collective-permute-done.6.refs_4_
  29.1 6.9 %convolution_bitcast_fusion.2 = f32[1024,128]{1,0:T(8,128)} fusion(bf16[1024,4096]{1,0:T(8,128)(2,1)} %left_ref.1, bf16[4096,128]{1,0:T(8,128)(2,1)S(1)} %collective-permute-done.6.refs_4_), kind=kOutput, calls=%fused_computation.16 | convolution fusion | flops 1073741824 | bytes 9961472 | tf_op jit(solution)/shard_map/dot_general | solution.py:27
  36.0 6.4 %collective-permute-done.8 = f32[256,640]{1,0:T(8,128)S(1)} collective-permute-done((f32[256,640]{1,0:T(8,128)S(1)}, f32[256,640]{1,0:T(8,128)S(1)}, u32[]{:S(2)}, u32[]{:S(2)}) %collective-permute-start.8) | collective-permute-done | bytes 655392 | tf_op jit(solution)/shard_map/ppermute | solution.py:119
  42.4 22.3 %conditional.4 = (bf16[256,640]{1,0:T(8,128)(2,1)S(1)}) conditional(s32[]{:T(128)} %convert_element_type.45, () %tuple.48, (s32[]{:T(128)}, f32[256,640]{1,0:T(8,128)S(1)}, f32[256,640]{1,0:T(8,128)S(1)}) %tuple.50), branch_computations={%region_2.3_spmd, %region_3.4_spmd} | conditional | flops 942090 | bytes 7292144 | solution.py:129
  42.4 0.1 add.14
  42.5 1.9 %collective-permute-start = (bf16[128,640]{1,0:T(8,128)(2,1)S(1)}, bf16[128,640]{1,0:T(8,128)(2,1)S(1)}, u32[]{:S(2)}, u32[]{:S(2)}) collective-permute-start(bf16[128,640]{1,0:T(8,128)(2,1)S(1)} %select_convert_fusion), channel_id=1, source_target_pairs={{0,4},{1,5},{2,6},{3,7},{4,0},{5,1},{6,2},{7,3},{8,12},{9,13},{10,... | collective-permute-start | bytes 491528 | tf_op jit(solution)/shard_map/cond/branch_1_fun/ppermute | solution.py:119
  44.4 3.7 %collective-permute-done = bf16[128,640]{1,0:T(8,128)(2,1)S(1)} collective-permute-done((bf16[128,640]{1,0:T(8,128)(2,1)S(1)}, bf16[128,640]{1,0:T(8,128)(2,1)S(1)}, u32[]{:S(2)}, u32[]{:S(2)}) %collective-permute-start) | collective-permute-done | bytes 163872 | tf_op jit(solution)/shard_map/cond/branch_1_fun/ppermute | solution.py:119
  48.2 2.7 %collective-permute-start.1 = (bf16[64,640]{1,0:T(8,128)(2,1)S(1)}, bf16[64,640]{1,0:T(8,128)(2,1)S(1)}, u32[]{:S(2)}, u32[]{:S(2)}) collective-permute-start(bf16[64,640]{1,0:T(8,128)(2,1)S(1)} %select_convert_fusion.1), channel_id=1, source_target_pairs={{0,8},{1,9},{2,10},{3,11},{4,12},{5,13},{6,14},{7,15},{8,0},{9,1},... | collective-permute-start | bytes 245768 | tf_op jit(solution)/shard_map/cond/branch_1_fun/ppermute | solution.py:119
  50.9 0.1 broadcast_in_dim.54
  51.0 0.1 broadcast_in_dim.55
  51.0 2.6 %collective-permute-done.1 = bf16[64,640]{1,0:T(8,128)(2,1)S(1)} collective-permute-done((bf16[64,640]{1,0:T(8,128)(2,1)S(1)}, bf16[64,640]{1,0:T(8,128)(2,1)S(1)}, u32[]{:S(2)}, u32[]{:S(2)}) %collective-permute-start.1) | collective-permute-done | bytes 81952 | tf_op jit(solution)/shard_map/cond/branch_1_fun/ppermute | solution.py:119
  53.6 2.8 %collective-permute-start.2 = (bf16[64,640]{1,0:T(8,128)(2,1)S(1)}, bf16[64,640]{1,0:T(8,128)(2,1)S(1)}, u32[]{:S(2)}, u32[]{:S(2)}) collective-permute-start(bf16[64,640]{1,0:T(8,128)(2,1)S(1)} %add_convert_fusion), channel_id=1, source_target_pairs={{0,8},{1,9},{2,10},{3,11},{4,12},{5,13},{6,14},{7,15},{8,0},{9,1},... | collective-permute-start | bytes 245768 | tf_op jit(solution)/shard_map/cond/branch_1_fun/ppermute | solution.py:119
  56.4 2.7 %collective-permute-done.2 = bf16[64,640]{1,0:T(8,128)(2,1)S(1)} collective-permute-done((bf16[64,640]{1,0:T(8,128)(2,1)S(1)}, bf16[64,640]{1,0:T(8,128)(2,1)S(1)}, u32[]{:S(2)}, u32[]{:S(2)}) %collective-permute-start.2) | collective-permute-done | bytes 81952 | tf_op jit(solution)/shard_map/cond/branch_1_fun/ppermute | solution.py:119
  59.1 0.1 bitcast_select_fusion.1
  59.2 2.0 %collective-permute-start.3 = (bf16[128,640]{1,0:T(8,128)(2,1)S(1)}, bf16[128,640]{1,0:T(8,128)(2,1)S(1)}, u32[]{:S(2)}, u32[]{:S(2)}) collective-permute-start(bf16[128,640]{1,0:T(8,128)(2,1)S(1)} %bitcast_select_fusion.1), channel_id=1, source_target_pairs={{0,4},{1,5},{2,6},{3,7},{4,0},{5,1},{6,2},{7,3},{8,12},{9,13},{10,... | collective-permute-start | bytes 491528 | tf_op jit(solution)/shard_map/cond/branch_1_fun/ppermute | solution.py:119
  61.2 0.1 broadcast_bitcast_fusion
  61.3 3.3 %collective-permute-done.3 = bf16[128,640]{1,0:T(8,128)(2,1)S(1)} collective-permute-done((bf16[128,640]{1,0:T(8,128)(2,1)S(1)}, bf16[128,640]{1,0:T(8,128)(2,1)S(1)}, u32[]{:S(2)}, u32[]{:S(2)}) %collective-permute-start.3) | collective-permute-done | bytes 163872 | tf_op jit(solution)/shard_map/cond/branch_1_fun/ppermute | solution.py:119
  64.6 0.1 bitcast_select_fusion
  64.7 1.6 collective-permute-start.12
  66.3 1.5 collective-permute-start.9
  67.8 0.1 broadcast_in_dim.72
  67.9 5.5 %collective-permute-done.9 = bf16[256,640]{1,0:T(8,128)(2,1)S(1)} collective-permute-done((bf16[256,640]{1,0:T(8,128)(2,1)S(1)}, bf16[256,640]{1,0:T(8,128)(2,1)S(1)}, u32[]{:S(2)}, u32[]{:S(2)}) %collective-permute-start.9) | collective-permute-done | bytes 327712 | tf_op jit(solution)/shard_map/ppermute | solution.py:119
  73.4 0.2 bitcast_select_fusion.2
  73.5 0.1 collective-permute-start.10
  73.6 0.8 collective-permute-done.7.refs_5_
  74.4 6.3 %convolution_bitcast_fusion.1 = f32[1024,256]{1,0:T(8,128)S(1)} fusion(bf16[1024,4096]{1,0:T(8,128)(2,1)} %left_ref.1, bf16[4096,256]{1,0:T(8,128)(2,1)} %collective-permute-done.7.refs_5_), kind=kOutput, calls=%fused_computation.15 | convolution fusion | flops 2147483648 | bytes 11534336 | tf_op jit(solution)/shard_map/dot_general | solution.py:27
  80.7 0.1 pad_maximum_fusion
  80.9 39.6 %conditional.5 = (bf16[512,384]{1,0:T(8,128)(2,1)}, f32[1024,4096]{1,0:T(8,128)}) conditional(s32[]{:T(128)} %convert_element_type.45, () %tuple.42, (pred[]{:T(512)}, f32[1024,384]{1,0:T(8,128)S(1)}, s32[1]{0:T(128)}, bf16[1024,4096]{1,0:T(8,128)(2,1)}, bf16[512,640]{1,0:T(8,128)(2,1)S(1)}, /*index=5*/bf16[512,640]{1,0:T(8,128)(2,1)S(1)}, ...), branch_computations={%region_4.5_spmd, %region_5.7_spmd} | conditional | flops 5369667584 | bytes 36667516 | solution.py:129
  80.9 0.1 slice_select_fusion.1
  81.0 0.1 collective-permute-start.4
  81.0 2.3 %collective-permute-done.4 = f32[512,384]{1,0:T(8,128)S(1)} collective-permute-done((f32[512,384]{1,0:T(8,128)S(1)}, f32[512,384]{1,0:T(8,128)S(1)}, u32[]{:S(2)}, u32[]{:S(2)}) %collective-permute-start.4) | collective-permute-done | bytes 786464 | tf_op jit(solution)/shard_map/cond/branch_1_fun/ppermute | solution.py:119
  83.3 0.9 add_convert_fusion.1
  84.2 6.4 %all-to-all-start = ((bf16[8,64,384]{2,1,0:T(8,128)(2,1)}), bf16[8,64,384]{2,1,0:T(8,128)(2,1)}, u32[]{:S(2)}, u32[]{:S(2)}) async-start(bf16[8,64,384]{2,1,0:T(8,128)(2,1)} %bitcast.31), calls=%async_computation | async-start | bytes 786432 | tf_op jit(solution)/shard_map/cond/branch_1_fun/all_to_all | solution.py:159
  90.6 7.8 %branch_1_fun.2.refs_0_ = f32[1024,4096]{1,0:T(8,128)} custom-call(s32[1]{0:T(128)} %get-tuple-element.52.upper_ref, bf16[1024,4096]{1,0:T(8,128)(2,1)} %get-tuple-element.58.base_ref, bf16[512,640]{1,0:T(8,128)(2,1)S(1)} %get-tuple-element.54.refs_0_.refs_1_, bf16[512,640]{1,0:T(8,128)(2,1)S(1)} %get-tuple-element.55.refs_1_.refs_2_, ...), custom_call_target="tpu_custom_call" | custom-call | flops 2684354560 | bytes 12582912 | tf_op jit(solution)/shard_map/cond/branch_1_fun/pallas_call | solution.py:92
  98.4 4.5 %all-to-all-done = bf16[8,64,384]{2,1,0:T(8,128)(2,1)} async-done(((bf16[8,64,384]{2,1,0:T(8,128)(2,1)}), bf16[8,64,384]{2,1,0:T(8,128)(2,1)}, u32[]{:S(2)}, u32[]{:S(2)}) %all-to-all-start) | async-done | bytes 393248 | tf_op jit(solution)/shard_map/cond/branch_1_fun/all_to_all | solution.py:159
  102.9 1.1 reduce_sum.22
  104.0 0.8 tile.0
  104.7 4.1 %all-to-all-start.1 = ((bf16[8,64,384]{2,1,0:T(8,128)(2,1)}), bf16[8,64,384]{2,1,0:T(8,128)(2,1)}, u32[]{:S(2)}, u32[]{:S(2)}) async-start(bf16[8,64,384]{2,1,0:T(8,128)(2,1)} %tile.0), calls=%async_computation.1 | async-start | bytes 786432 | tf_op jit(solution)/shard_map/cond/branch_1_fun/all_to_all | solution.py:159
  108.8 7.7 %branch_1_fun.3 = f32[1024,4096]{1,0:T(8,128)} custom-call(s32[1]{0:T(128)} %get-tuple-element.52.upper_ref, bf16[1024,4096]{1,0:T(8,128)(2,1)} %get-tuple-element.58.base_ref, f32[1024,4096]{1,0:T(8,128)} %branch_1_fun.2.refs_0_, bf16[512,640]{1,0:T(8,128)(2,1)S(1)} %get-tuple-element.54.refs_0_.refs_1_, ...), custom_call_target="tpu_custom_call", output_to_operand_aliasing={{}: (2, {})} | custom-call | flops 2684354560 | bytes 12582912 | tf_op jit(solution)/shard_map/cond/branch_1_fun/pallas_call | solution.py:92
  116.6 3.8 %all-to-all-done.1 = bf16[8,64,384]{2,1,0:T(8,128)(2,1)} async-done(((bf16[8,64,384]{2,1,0:T(8,128)(2,1)}), bf16[8,64,384]{2,1,0:T(8,128)(2,1)}, u32[]{:S(2)}, u32[]{:S(2)}) %all-to-all-start.1) | async-done | bytes 393248 | tf_op jit(solution)/shard_map/cond/branch_1_fun/all_to_all | solution.py:159
  120.4 6.5 %convolution_bitcast_fusion = f32[1024,256]{1,0:T(8,128)S(1)} fusion(bf16[1024,4096]{1,0:T(8,128)(2,1)} %left_ref.1, bf16[4096,256]{1,0:T(8,128)(2,1)S(1)} %collective-permute-done.12.refs_6_), kind=kOutput, calls=%fused_computation.14 | convolution fusion | flops 2147483648 | bytes 11534336 | tf_op jit(solution)/shard_map/dot_general | solution.py:27
  126.9 0.1 slice_select_fusion.2
  127.0 0.1 collective-permute-start.13
  127.0 1.9 %collective-permute-done.13 = f32[512,256]{1,0:T(8,128)S(1)} collective-permute-done((f32[512,256]{1,0:T(8,128)S(1)}, f32[512,256]{1,0:T(8,128)S(1)}, u32[]{:S(2)}, u32[]{:S(2)}) %collective-permute-start.13) | collective-permute-done | bytes 524320 | tf_op jit(solution)/shard_map/ppermute | solution.py:119
  128.9 0.1 add_convert_fusion.2
  129.1 13.2 %all_to_all.31 = bf16[8,64,256]{2,1,0:T(8,128)(2,1)S(1)} all-to-all(bf16[8,64,256]{2,1,0:T(8,128)(2,1)S(1)} %bitcast.34), channel_id=1, replica_groups={{0,2,4,6,8,10,12,14},{1,3,5,7,9,11,13,15},{16,18,20,22,24,26,28,30},{17..., dimensions={0} | all-to-all | bytes 524288 | tf_op jit(solution)/shard_map/all_to_all | solution.py:159
  142.3 0.7 tile.4
  143.0 3.6 %all-to-all-start.3 = ((bf16[8,64,256]{2,1,0:T(8,128)(2,1)}), bf16[8,64,256]{2,1,0:T(8,128)(2,1)S(1)}, u32[]{:S(2)}, u32[]{:S(2)}) async-start(bf16[8,64,256]{2,1,0:T(8,128)(2,1)} %tile.4), calls=%async_computation.3 | async-start | bytes 524288 | tf_op jit(solution)/shard_map/all_to_all | solution.py:159
  146.6 8.6 %all-to-all-done.3 = bf16[8,64,256]{2,1,0:T(8,128)(2,1)S(1)} async-done(((bf16[8,64,256]{2,1,0:T(8,128)(2,1)}), bf16[8,64,256]{2,1,0:T(8,128)(2,1)S(1)}, u32[]{:S(2)}, u32[]{:S(2)}) %all-to-all-start.3) | async-done | bytes 262176 | tf_op jit(solution)/shard_map/all_to_all | solution.py:159
  155.2 1.5 collective-permute-done.14.refs_3_
  156.7 0.7 copy-done.5
  157.4 14.1 %shard_map.39 = bf16[1024,4096]{1,0:T(8,128)(2,1)} custom-call(s32[1]{0:T(128)} %bitcast.7.upper_ref, f32[1024,4096]{1,0:T(8,128)} %get-tuple-element.78.base_ref, bf16[512,384]{1,0:T(8,128)(2,1)} %get-tuple-element.79.refs_0_, bf16[512,384]{1,0:T(8,128)(2,1)} %copy-done.4, bf16[512,256]{1,0:T(8,128)(2,1)} %bitcast.33, bf16[512,256]{1,0:T(8,128)(2,1)} %copy-done.5, ...), custom_call_target="tpu_custom_call" | custom-call | flops 5368709120 | bytes 25165824 | tf_op jit(solution)/shard_map/pallas_call | solution.py:92
  (26 shorter events, 0.2 us)
Async XLA Ops:
  2.3 26.8 %collective-permute-start.6 = (bf16[4096,128]{1,0:T(8,128)(2,1)}, bf16[4096,128]{1,0:T(8,128)(2,1)S(1)}, u32[]{:S(2)}, u32[]{:S(2)}) collective-permute-start(bf16[4096,128]{1,0:T(8,128)(2,1)} %slice.9), channel_id=1, source_target_pairs={{0,16},{16,0},{1,17},{17,1},{2,18},{18,2},{3,19},{19,3},{4,20},{20... | collective-permute-start | bytes 3145736 | tf_op jit(solution)/shard_map/ppermute | solution.py:172
  15.2 3.1 %collective-permute-start.5 = (f32[512,640]{1,0:T(8,128)S(1)}, f32[512,640]{1,0:T(8,128)S(1)}, u32[]{:S(2)}, u32[]{:S(2)}) collective-permute-start(f32[512,640]{1,0:T(8,128)S(1)} %slice_select_fusion), channel_id=1, source_target_pairs={{0,1},{1,0},{2,3},{3,2},{4,5},{5,4},{6,7},{7,6},{8,9},{9,8},{10,11... | collective-permute-start | bytes 3932168 | tf_op jit(solution)/shard_map/cond/branch_1_fun/ppermute | solution.py:119
  25.6 48.8 %collective-permute-start.7 = (bf16[4096,256]{1,0:T(8,128)(2,1)}, bf16[4096,256]{1,0:T(8,128)(2,1)}, u32[]{:S(2)}, u32[]{:S(2)}) collective-permute-start(bf16[4096,256]{1,0:T(8,128)(2,1)} %get-tuple-element.74), channel_id=1, source_target_pairs={{0,16},{16,0},{1,17},{17,1},{2,18},{18,2},{3,19},{19,3},{4,20},{20... | collective-permute-start | bytes 6291464 | tf_op jit(solution)/shard_map/ppermute | solution.py:172
  25.6 16.8 %collective-permute-start.8 = (f32[256,640]{1,0:T(8,128)S(1)}, f32[256,640]{1,0:T(8,128)S(1)}, u32[]{:S(2)}, u32[]{:S(2)}) collective-permute-start(f32[256,640]{1,0:T(8,128)S(1)} %get-tuple-element.89), channel_id=1, source_target_pairs={{0,2},{1,3},{2,0},{3,1},{4,6},{5,7},{6,4},{7,5},{8,10},{9,11},{10,... | collective-permute-start | bytes 1966088 | tf_op jit(solution)/shard_map/ppermute | solution.py:119
  29.1 6.9 %copy-start.2 = (bf16[4096,128]{1,0:T(8,128)(2,1)}, bf16[4096,128]{1,0:T(8,128)(2,1)S(1)}, u32[]{:S(2)}) copy-start(bf16[4096,128]{1,0:T(8,128)(2,1)S(1)} %collective-permute-done.6.refs_4_) | copy-start | bytes 3145732
  42.5 5.6 %collective-permute-start = (bf16[128,640]{1,0:T(8,128)(2,1)S(1)}, bf16[128,640]{1,0:T(8,128)(2,1)S(1)}, u32[]{:S(2)}, u32[]{:S(2)}) collective-permute-start(bf16[128,640]{1,0:T(8,128)(2,1)S(1)} %select_convert_fusion), channel_id=1, source_target_pairs={{0,4},{1,5},{2,6},{3,7},{4,0},{5,1},{6,2},{7,3},{8,12},{9,13},{10,... | collective-permute-start | bytes 491528 | tf_op jit(solution)/shard_map/cond/branch_1_fun/ppermute | solution.py:119
  48.2 5.4 %collective-permute-start.1 = (bf16[64,640]{1,0:T(8,128)(2,1)S(1)}, bf16[64,640]{1,0:T(8,128)(2,1)S(1)}, u32[]{:S(2)}, u32[]{:S(2)}) collective-permute-start(bf16[64,640]{1,0:T(8,128)(2,1)S(1)} %select_convert_fusion.1), channel_id=1, source_target_pairs={{0,8},{1,9},{2,10},{3,11},{4,12},{5,13},{6,14},{7,15},{8,0},{9,1},... | collective-permute-start | bytes 245768 | tf_op jit(solution)/shard_map/cond/branch_1_fun/ppermute | solution.py:119
  53.6 5.5 %collective-permute-start.2 = (bf16[64,640]{1,0:T(8,128)(2,1)S(1)}, bf16[64,640]{1,0:T(8,128)(2,1)S(1)}, u32[]{:S(2)}, u32[]{:S(2)}) collective-permute-start(bf16[64,640]{1,0:T(8,128)(2,1)S(1)} %add_convert_fusion), channel_id=1, source_target_pairs={{0,8},{1,9},{2,10},{3,11},{4,12},{5,13},{6,14},{7,15},{8,0},{9,1},... | collective-permute-start | bytes 245768 | tf_op jit(solution)/shard_map/cond/branch_1_fun/ppermute | solution.py:119
  59.2 5.4 %collective-permute-start.3 = (bf16[128,640]{1,0:T(8,128)(2,1)S(1)}, bf16[128,640]{1,0:T(8,128)(2,1)S(1)}, u32[]{:S(2)}, u32[]{:S(2)}) collective-permute-start(bf16[128,640]{1,0:T(8,128)(2,1)S(1)} %bitcast_select_fusion.1), channel_id=1, source_target_pairs={{0,4},{1,5},{2,6},{3,7},{4,0},{5,1},{6,2},{7,3},{8,12},{9,13},{10,... | collective-permute-start | bytes 491528 | tf_op jit(solution)/shard_map/cond/branch_1_fun/ppermute | solution.py:119
  64.7 55.7 %collective-permute-start.12 = (bf16[4096,256]{1,0:T(8,128)(2,1)}, bf16[4096,256]{1,0:T(8,128)(2,1)S(1)}, u32[]{:S(2)}, u32[]{:S(2)}) collective-permute-start(bf16[4096,256]{1,0:T(8,128)(2,1)} %get-tuple-element.80), channel_id=1, source_target_pairs={{0,16},{16,0},{1,17},{17,1},{2,18},{18,2},{3,19},{19,3},{4,20},{20... | collective-permute-start | bytes 6291464 | tf_op jit(solution)/shard_map/ppermute | solution.py:172
  66.3 7.1 %collective-permute-start.9 = (bf16[256,640]{1,0:T(8,128)(2,1)S(1)}, bf16[256,640]{1,0:T(8,128)(2,1)S(1)}, u32[]{:S(2)}, u32[]{:S(2)}) collective-permute-start(bf16[256,640]{1,0:T(8,128)(2,1)S(1)} %get-tuple-element.100), channel_id=1, source_target_pairs={{0,2},{1,3},{2,0},{3,1},{4,6},{5,7},{6,4},{7,5},{8,10},{9,11},{10,... | collective-permute-start | bytes 983048 | tf_op jit(solution)/shard_map/ppermute | solution.py:119
  73.5 7.2 %copy-start.3 = (f32[1024,128]{1,0:T(8,128)S(1)}, f32[1024,128]{1,0:T(8,128)}, u32[]{:S(2)}) copy-start(f32[1024,128]{1,0:T(8,128)} %convolution_bitcast_fusion.2) | copy-start | bytes 1572868
  73.5 7.3 %collective-permute-start.10 = (bf16[512,640]{1,0:T(8,128)(2,1)S(1)}, bf16[512,640]{1,0:T(8,128)(2,1)S(1)}, u32[]{:S(2)}, u32[]{:S(2)}) collective-permute-start(bf16[512,640]{1,0:T(8,128)(2,1)S(1)} %bitcast_select_fusion.2), channel_id=1, source_target_pairs={{0,1},{1,0},{2,3},{3,2},{4,5},{5,4},{6,7},{7,6},{8,9},{9,8},{10,11... | collective-permute-start | bytes 1966088 | tf_op jit(solution)/shard_map/ppermute | solution.py:119
  81.0 2.4 %collective-permute-start.4 = (f32[512,384]{1,0:T(8,128)S(1)}, f32[512,384]{1,0:T(8,128)S(1)}, u32[]{:S(2)}, u32[]{:S(2)}) collective-permute-start(f32[512,384]{1,0:T(8,128)S(1)} %slice_select_fusion.1), channel_id=1, source_target_pairs={{0,1},{1,0},{2,3},{3,2},{4,5},{5,4},{6,7},{7,6},{8,9},{9,8},{10,11... | collective-permute-start | bytes 2359304 | tf_op jit(solution)/shard_map/cond/branch_1_fun/ppermute | solution.py:119
  84.2 18.7 %all-to-all-start = ((bf16[8,64,384]{2,1,0:T(8,128)(2,1)}), bf16[8,64,384]{2,1,0:T(8,128)(2,1)}, u32[]{:S(2)}, u32[]{:S(2)}) async-start(bf16[8,64,384]{2,1,0:T(8,128)(2,1)} %bitcast.31), calls=%async_computation | async-start | bytes 786432 | tf_op jit(solution)/shard_map/cond/branch_1_fun/all_to_all | solution.py:159
  104.7 15.7 %all-to-all-start.1 = ((bf16[8,64,384]{2,1,0:T(8,128)(2,1)}), bf16[8,64,384]{2,1,0:T(8,128)(2,1)}, u32[]{:S(2)}, u32[]{:S(2)}) async-start(bf16[8,64,384]{2,1,0:T(8,128)(2,1)} %tile.0), calls=%async_computation.1 | async-start | bytes 786432 | tf_op jit(solution)/shard_map/cond/branch_1_fun/all_to_all | solution.py:159
  120.4 6.5 %copy-start = (bf16[4096,256]{1,0:T(8,128)(2,1)}, bf16[4096,256]{1,0:T(8,128)(2,1)S(1)}, u32[]{:S(2)}) copy-start(bf16[4096,256]{1,0:T(8,128)(2,1)S(1)} %collective-permute-done.12.refs_6_) | copy-start | bytes 6291460
  127.0 2.0 %collective-permute-start.13 = (f32[512,256]{1,0:T(8,128)S(1)}, f32[512,256]{1,0:T(8,128)S(1)}, u32[]{:S(2)}, u32[]{:S(2)}) collective-permute-start(f32[512,256]{1,0:T(8,128)S(1)} %slice_select_fusion.2), channel_id=1, source_target_pairs={{0,1},{1,0},{2,3},{3,2},{4,5},{5,4},{6,7},{7,6},{8,9},{9,8},{10,11... | collective-permute-start | bytes 1572872 | tf_op jit(solution)/shard_map/ppermute | solution.py:119
  143.0 12.2 %all-to-all-start.3 = ((bf16[8,64,256]{2,1,0:T(8,128)(2,1)}), bf16[8,64,256]{2,1,0:T(8,128)(2,1)S(1)}, u32[]{:S(2)}, u32[]{:S(2)}) async-start(bf16[8,64,256]{2,1,0:T(8,128)(2,1)} %tile.4), calls=%async_computation.3 | async-start | bytes 524288 | tf_op jit(solution)/shard_map/all_to_all | solution.py:159
  146.6 8.6 %collective-permute-start.11 = (bf16[512,384]{1,0:T(8,128)(2,1)}, bf16[512,384]{1,0:T(8,128)(2,1)S(1)}, u32[]{:S(2)}, u32[]{:S(2)}) collective-permute-start(bf16[512,384]{1,0:T(8,128)(2,1)} %get-tuple-element.79.refs_0_), channel_id=1, source_target_pairs={{0,1},{1,0},{2,3},{3,2},{4,5},{5,4},{6,7},{7,6},{8,9},{9,8},{10,11... | collective-permute-start | bytes 1179656 | tf_op jit(solution)/shard_map/ppermute | solution.py:119
  155.1 1.5 copy-start.1
  155.1 1.5 collective-permute-start.14
  155.1 1.5 copy-start.4
  156.7 0.7 copy-start.5

commit v12 on v11

--- a/solution.py
+++ b/solution.py
@@ -9,7 +9,8 @@
 from jax.sharding import PartitionSpec as P
 
 GROUPS = (128, 256, 256)
-VMEM_BYTES = 58 * 1024 * 1024
+VMEM_BYTES = 52 * 1024 * 1024
+WIDE_VMEM_BYTES = 24 * 1024 * 1024
 FREE = pl.CostEstimate(flops=0, bytes_accessed=0, transcendentals=0)
 
 
@@ -57,7 +58,7 @@
         out_specs=pl.BlockSpec((rows, width), lambda k: (0, 0)),
         out_shape=jax.ShapeDtypeStruct((rows, width), jnp.float32),
         scratch_shapes=[pltpu.VMEM((width, rows), jnp.float32)],
-        compiler_params=pltpu.CompilerParams(vmem_limit_bytes=VMEM_BYTES),
+        compiler_params=pltpu.CompilerParams(vmem_limit_bytes=WIDE_VMEM_BYTES),
         cost_estimate=FREE,
     )(amplitudes, vectors)
 

time: 172 us -> 174 us (1.012)
  local copies, waits for them, and re-layouts: 10.8 us -> 13.4 us
    unnamed x12 -> x4, local copies, waits for them, and re-layouts: 0.72 us -> 3.39 us
    ppermute x12, waiting for transfers between devices: 32.8 us -> 34.7 us  [exchange(): return lax.ppermute(value, 'col', [(i, i ^ bit) for i in range(cols)])]
  transfers between devices with their start and end apart: 18 -> 18, of which waited for: 15 -> 14; matrix products, arithmetic and copies ran while one was open for 14% -> 13% of each run, Pallas kernels for 15% -> 14%
where the time goes in v12:
time: 174 us; the launch traced here: 173 us
  waiting for transfers between devices  52.3 us (30%)
  Pallas kernels  38.6 us (22%)
  starting transfers between devices  31.8 us (18%)
  matrix products  19.1 us (11%)
  blocking collectives  14.1 us (8%)
  local copies, waits for them, and re-layouts  13.4 us (8%)
  other arithmetic  3.44 us (2%)
    ppermute x12, waiting for transfers between devices, exchange(): return lax.ppermute(value, 'col', [(i, i ^ bit) for i in range(cols)])  34.7 us
    pallas_call x3, Pallas kernels, project_back(): pl.pallas_call(kernel, grid_spec=pltpu.PrefetchScalarGridSpec(num_scalar_...  29.2 us
    dot_general x3, matrix products, project(): part = jnp.dot(amplitudes, vectors, preferred_element_type=jnp.float32)  19.1 us
    all_to_all x3, waiting for transfers between devices, spread(): lax.all_to_all(value, 'col', 0, 0, tiled=True, axis_index_groups=mates)  16.8 us
    all_to_all x1, blocking collectives, spread(): lax.all_to_all(value, 'col', 0, 0, tiled=True, axis_index_groups=mates)  14.1 us
    all_to_all x3, starting transfers between devices, spread(): lax.all_to_all(value, 'col', 0, 0, tiled=True, axis_index_groups=mates)  14.1 us
    ppermute x12, starting transfers between devices, exchange(): return lax.ppermute(value, 'col', [(i, i ^ bit) for i in range(cols)])  13.2 us
    pallas_call x1, Pallas kernels, project_wide(): pl.pallas_call(kernel, grid=(steps,), in_specs=[pl.BlockSpec((rows, block...  9.42 us
  transfers between devices with their start and end apart: 18, of which 14 were waited for; matrix products, arithmetic and copies ran while one was open for 13% of the time, Pallas kernels for 14%

profile of v12, /device:TPU:0, one launch (start us, length us, event | category | flops | bytes accessed | tf_op | source)
XLA Modules:
  0.0 173.0 jit_solution(8682792914922155159)
XLA Ops:
  0.0 2.3 %slice.9 = bf16[4096,128]{1,0:T(8,128)(2,1)} slice(bf16[4096,640]{1,0:T(8,128)(2,1)} %right_ref), slice={[0:4096], [0:128]} | slice | bytes 2097152 | tf_op jit(solution)/shard_map/slice | solution.py:184
  2.3 2.9 %collective-permute-start.6 = (bf16[4096,128]{1,0:T(8,128)(2,1)}, bf16[4096,128]{1,0:T(8,128)(2,1)S(1)}, u32[]{:S(2)}, u32[]{:S(2)}) collective-permute-start(bf16[4096,128]{1,0:T(8,128)(2,1)} %slice.9), channel_id=1, source_target_pairs={{0,16},{16,0},{1,17},{17,1},{2,18},{18,2},{3,19},{19,3},{4,20},{20... | collective-permute-start | bytes 3145736 | tf_op jit(solution)/shard_map/ppermute | solution.py:173
  5.2 3.4 %copy-done = bf16[1024,4096]{1,0:T(8,128)(2,1)S(1)} copy-done((bf16[1024,4096]{1,0:T(8,128)(2,1)S(1)}, bf16[1024,4096]{1,0:T(8,128)(2,1)}, u32[]{:S(2)}) %copy-start) | copy-done | bytes 8388632
  8.6 9.4 %shard_map.38 = f32[1024,640]{1,0:T(8,128)S(1)} custom-call(bf16[1024,4096]{1,0:T(8,128)(2,1)S(1)} %copy-done, bf16[4096,640]{1,0:T(8,128)(2,1)} %right_ref), custom_call_target="tpu_custom_call" | custom-call | tf_op jit(solution)/shard_map/pallas_call | solution.py:54
  18.0 5.9 %conditional.3 = (f32[512,640]{1,0:T(8,128)}, f32[256,640]{1,0:T(8,128)S(1)}, f32[256,640]{1,0:T(8,128)S(1)}) conditional(s32[]{:T(128)} %convert_element_type.45, () %tuple.43, (pred[]{:T(512)}, f32[1024,640]{1,0:T(8,128)S(1)}) %tuple.45), branch_computations={%region_0.0_spmd, %region_1.2_spmd} | conditional | flops 983040 | bytes 17039426 | solution.py:130
  18.0 0.1 slice_select_fusion
  18.2 0.1 collective-permute-start.5
  18.3 3.0 %collective-permute-done.5 = f32[512,640]{1,0:T(8,128)S(1)} collective-permute-done((f32[512,640]{1,0:T(8,128)S(1)}, f32[512,640]{1,0:T(8,128)S(1)}, u32[]{:S(2)}, u32[]{:S(2)}) %collective-permute-start.5) | collective-permute-done | bytes 1310752 | tf_op jit(solution)/shard_map/cond/branch_1_fun/ppermute | solution.py:120
  21.3 1.3 select_add_fusion
  22.6 1.4 fusion
  24.0 0.1 broadcast_select_fusion
  24.1 4.5 %fusion.1 = (bf16[4096,256]{1,0:T(8,128)(2,1)}, bf16[4096,256]{1,0:T(8,128)(2,1)}) fusion(bf16[4096,640]{1,0:T(8,128)(2,1)} %right_ref), kind=kLoop, calls=%fused_computation.24 | loop fusion | bytes 8388608 | tf_op jit(solution)/shard_map/slice | solution.py:184
  28.6 0.0 collective-permute-start.7
  28.6 2.0 %collective-permute-start.8 = (f32[256,640]{1,0:T(8,128)S(1)}, f32[256,640]{1,0:T(8,128)S(1)}, u32[]{:S(2)}, u32[]{:S(2)}) collective-permute-start(f32[256,640]{1,0:T(8,128)S(1)} %get-tuple-element.89), channel_id=1, source_target_pairs={{0,2},{1,3},{2,0},{3,1},{4,6},{5,7},{6,4},{7,5},{8,10},{9,11},{10,... | collective-permute-start | bytes 1966088 | tf_op jit(solution)/shard_map/ppermute | solution.py:120
  30.6 6.5 %convolution_bitcast_fusion.2 = f32[1024,128]{1,0:T(8,128)} fusion(bf16[1024,4096]{1,0:T(8,128)(2,1)} %left_ref.1, bf16[4096,128]{1,0:T(8,128)(2,1)S(1)} %collective-permute-done.6.refs_4_), kind=kOutput, calls=%fused_computation.16 | convolution fusion | flops 1073741824 | bytes 9961472 | tf_op jit(solution)/shard_map/dot_general | solution.py:28
  37.2 8.2 %collective-permute-done.8 = f32[256,640]{1,0:T(8,128)S(1)} collective-permute-done((f32[256,640]{1,0:T(8,128)S(1)}, f32[256,640]{1,0:T(8,128)S(1)}, u32[]{:S(2)}, u32[]{:S(2)}) %collective-permute-start.8) | collective-permute-done | bytes 655392 | tf_op jit(solution)/shard_map/ppermute | solution.py:120
  45.4 22.3 %conditional.4 = (bf16[256,640]{1,0:T(8,128)(2,1)S(1)}) conditional(s32[]{:T(128)} %convert_element_type.45, () %tuple.48, (s32[]{:T(128)}, f32[256,640]{1,0:T(8,128)S(1)}, f32[256,640]{1,0:T(8,128)S(1)}) %tuple.50), branch_computations={%region_2.3_spmd, %region_3.4_spmd} | conditional | flops 942090 | bytes 7292144 | solution.py:130
  45.4 0.1 add.14
  45.5 1.9 %collective-permute-start = (bf16[128,640]{1,0:T(8,128)(2,1)S(1)}, bf16[128,640]{1,0:T(8,128)(2,1)S(1)}, u32[]{:S(2)}, u32[]{:S(2)}) collective-permute-start(bf16[128,640]{1,0:T(8,128)(2,1)S(1)} %select_convert_fusion), channel_id=1, source_target_pairs={{0,4},{1,5},{2,6},{3,7},{4,0},{5,1},{6,2},{7,3},{8,12},{9,13},{10,... | collective-permute-start | bytes 491528 | tf_op jit(solution)/shard_map/cond/branch_1_fun/ppermute | solution.py:120
  47.4 3.7 %collective-permute-done = bf16[128,640]{1,0:T(8,128)(2,1)S(1)} collective-permute-done((bf16[128,640]{1,0:T(8,128)(2,1)S(1)}, bf16[128,640]{1,0:T(8,128)(2,1)S(1)}, u32[]{:S(2)}, u32[]{:S(2)}) %collective-permute-start) | collective-permute-done | bytes 163872 | tf_op jit(solution)/shard_map/cond/branch_1_fun/ppermute | solution.py:120
  51.2 2.7 %collective-permute-start.1 = (bf16[64,640]{1,0:T(8,128)(2,1)S(1)}, bf16[64,640]{1,0:T(8,128)(2,1)S(1)}, u32[]{:S(2)}, u32[]{:S(2)}) collective-permute-start(bf16[64,640]{1,0:T(8,128)(2,1)S(1)} %select_convert_fusion.1), channel_id=1, source_target_pairs={{0,8},{1,9},{2,10},{3,11},{4,12},{5,13},{6,14},{7,15},{8,0},{9,1},... | collective-permute-start | bytes 245768 | tf_op jit(solution)/shard_map/cond/branch_1_fun/ppermute | solution.py:120
  53.9 0.1 broadcast_in_dim.54
  53.9 0.1 broadcast_in_dim.55
  54.0 2.6 %collective-permute-done.1 = bf16[64,640]{1,0:T(8,128)(2,1)S(1)} collective-permute-done((bf16[64,640]{1,0:T(8,128)(2,1)S(1)}, bf16[64,640]{1,0:T(8,128)(2,1)S(1)}, u32[]{:S(2)}, u32[]{:S(2)}) %collective-permute-start.1) | collective-permute-done | bytes 81952 | tf_op jit(solution)/shard_map/cond/branch_1_fun/ppermute | solution.py:120
  56.6 2.8 %collective-permute-start.2 = (bf16[64,640]{1,0:T(8,128)(2,1)S(1)}, bf16[64,640]{1,0:T(8,128)(2,1)S(1)}, u32[]{:S(2)}, u32[]{:S(2)}) collective-permute-start(bf16[64,640]{1,0:T(8,128)(2,1)S(1)} %add_convert_fusion), channel_id=1, source_target_pairs={{0,8},{1,9},{2,10},{3,11},{4,12},{5,13},{6,14},{7,15},{8,0},{9,1},... | collective-permute-start | bytes 245768 | tf_op jit(solution)/shard_map/cond/branch_1_fun/ppermute | solution.py:120
  59.4 2.7 %collective-permute-done.2 = bf16[64,640]{1,0:T(8,128)(2,1)S(1)} collective-permute-done((bf16[64,640]{1,0:T(8,128)(2,1)S(1)}, bf16[64,640]{1,0:T(8,128)(2,1)S(1)}, u32[]{:S(2)}, u32[]{:S(2)}) %collective-permute-start.2) | collective-permute-done | bytes 81952 | tf_op jit(solution)/shard_map/cond/branch_1_fun/ppermute | solution.py:120
  62.1 0.1 bitcast_select_fusion.1
  62.2 2.0 %collective-permute-start.3 = (bf16[128,640]{1,0:T(8,128)(2,1)S(1)}, bf16[128,640]{1,0:T(8,128)(2,1)S(1)}, u32[]{:S(2)}, u32[]{:S(2)}) collective-permute-start(bf16[128,640]{1,0:T(8,128)(2,1)S(1)} %bitcast_select_fusion.1), channel_id=1, source_target_pairs={{0,4},{1,5},{2,6},{3,7},{4,0},{5,1},{6,2},{7,3},{8,12},{9,13},{10,... | collective-permute-start | bytes 491528 | tf_op jit(solution)/shard_map/cond/branch_1_fun/ppermute | solution.py:120
  64.2 0.1 broadcast_bitcast_fusion
  64.3 3.3 %collective-permute-done.3 = bf16[128,640]{1,0:T(8,128)(2,1)S(1)} collective-permute-done((bf16[128,640]{1,0:T(8,128)(2,1)S(1)}, bf16[128,640]{1,0:T(8,128)(2,1)S(1)}, u32[]{:S(2)}, u32[]{:S(2)}) %collective-permute-start.3) | collective-permute-done | bytes 163872 | tf_op jit(solution)/shard_map/cond/branch_1_fun/ppermute | solution.py:120
  67.6 0.1 bitcast_select_fusion
  67.7 1.6 collective-permute-start.12
  69.3 1.5 collective-permute-start.9
  70.8 0.1 broadcast_in_dim.72
  70.9 5.5 %collective-permute-done.9 = bf16[256,640]{1,0:T(8,128)(2,1)S(1)} collective-permute-done((bf16[256,640]{1,0:T(8,128)(2,1)S(1)}, bf16[256,640]{1,0:T(8,128)(2,1)S(1)}, u32[]{:S(2)}, u32[]{:S(2)}) %collective-permute-start.9) | collective-permute-done | bytes 327712 | tf_op jit(solution)/shard_map/ppermute | solution.py:120
  76.3 0.2 bitcast_select_fusion.2
  76.5 0.1 collective-permute-start.10
  76.6 0.8 collective-permute-done.7.refs_5_
  77.4 6.3 %convolution_bitcast_fusion.1 = f32[1024,256]{1,0:T(8,128)S(1)} fusion(bf16[1024,4096]{1,0:T(8,128)(2,1)} %left_ref.1, bf16[4096,256]{1,0:T(8,128)(2,1)} %collective-permute-done.7.refs_5_), kind=kOutput, calls=%fused_computation.15 | convolution fusion | flops 2147483648 | bytes 11534336 | tf_op jit(solution)/shard_map/dot_general | solution.py:28
  83.7 0.1 pad_maximum_fusion
  83.8 38.4 %conditional.5 = (bf16[512,384]{1,0:T(8,128)(2,1)}, f32[1024,4096]{1,0:T(8,128)}) conditional(s32[]{:T(128)} %convert_element_type.45, () %tuple.42, (pred[]{:T(512)}, f32[1024,384]{1,0:T(8,128)S(1)}, s32[1]{0:T(128)}, bf16[1024,4096]{1,0:T(8,128)(2,1)}, bf16[512,640]{1,0:T(8,128)(2,1)S(1)}, /*index=5*/bf16[512,640]{1,0:T(8,128)(2,1)S(1)}, ...), branch_computations={%region_4.5_spmd, %region_5.7_spmd} | conditional | flops 5369667584 | bytes 36667516 | solution.py:130
  83.8 0.1 slice_select_fusion.1
  83.9 0.1 collective-permute-start.4
  84.0 2.3 %collective-permute-done.4 = f32[512,384]{1,0:T(8,128)S(1)} collective-permute-done((f32[512,384]{1,0:T(8,128)S(1)}, f32[512,384]{1,0:T(8,128)S(1)}, u32[]{:S(2)}, u32[]{:S(2)}) %collective-permute-start.4) | collective-permute-done | bytes 786464 | tf_op jit(solution)/shard_map/cond/branch_1_fun/ppermute | solution.py:120
  86.3 0.9 add_convert_fusion.1
  87.2 6.4 %all-to-all-start = ((bf16[8,64,384]{2,1,0:T(8,128)(2,1)}), bf16[8,64,384]{2,1,0:T(8,128)(2,1)S(1)}, u32[]{:S(2)}, u32[]{:S(2)}) async-start(bf16[8,64,384]{2,1,0:T(8,128)(2,1)} %bitcast.5), calls=%async_computation | async-start | bytes 786432 | tf_op jit(solution)/shard_map/cond/branch_1_fun/all_to_all | solution.py:160
  93.6 7.7 %branch_1_fun.2.refs_0_ = f32[1024,4096]{1,0:T(8,128)} custom-call(s32[1]{0:T(128)} %get-tuple-element.52.upper_ref, bf16[1024,4096]{1,0:T(8,128)(2,1)} %get-tuple-element.58.base_ref, bf16[512,640]{1,0:T(8,128)(2,1)S(1)} %get-tuple-element.54.refs_0_.refs_1_, bf16[512,640]{1,0:T(8,128)(2,1)S(1)} %get-tuple-element.55.refs_1_.refs_2_, ...), custom_call_target="tpu_custom_call" | custom-call | flops 2684354560 | bytes 12582912 | tf_op jit(solution)/shard_map/cond/branch_1_fun/pallas_call | solution.py:93
  101.3 4.5 %all-to-all-done = bf16[8,64,384]{2,1,0:T(8,128)(2,1)S(1)} async-done(((bf16[8,64,384]{2,1,0:T(8,128)(2,1)}), bf16[8,64,384]{2,1,0:T(8,128)(2,1)S(1)}, u32[]{:S(2)}, u32[]{:S(2)}) %all-to-all-start) | async-done | bytes 393248 | tf_op jit(solution)/shard_map/cond/branch_1_fun/all_to_all | solution.py:160
  105.8 0.1 reduce_sum.22
  105.8 0.8 tile.0
  106.6 4.1 %all-to-all-start.1 = ((bf16[8,64,384]{2,1,0:T(8,128)(2,1)}), bf16[8,64,384]{2,1,0:T(8,128)(2,1)}, u32[]{:S(2)}, u32[]{:S(2)}) async-start(bf16[8,64,384]{2,1,0:T(8,128)(2,1)} %tile.0), calls=%async_computation.1 | async-start | bytes 786432 | tf_op jit(solution)/shard_map/cond/branch_1_fun/all_to_all | solution.py:160
  110.7 7.8 %branch_1_fun.3 = f32[1024,4096]{1,0:T(8,128)} custom-call(s32[1]{0:T(128)} %get-tuple-element.52.upper_ref, bf16[1024,4096]{1,0:T(8,128)(2,1)} %get-tuple-element.58.base_ref, f32[1024,4096]{1,0:T(8,128)} %branch_1_fun.2.refs_0_, bf16[512,640]{1,0:T(8,128)(2,1)S(1)} %get-tuple-element.54.refs_0_.refs_1_, ...), custom_call_target="tpu_custom_call", output_to_operand_aliasing={{}: (2, {})} | custom-call | flops 2684354560 | bytes 12582912 | tf_op jit(solution)/shard_map/cond/branch_1_fun/pallas_call | solution.py:93
  118.5 3.8 %all-to-all-done.1 = bf16[8,64,384]{2,1,0:T(8,128)(2,1)} async-done(((bf16[8,64,384]{2,1,0:T(8,128)(2,1)}), bf16[8,64,384]{2,1,0:T(8,128)(2,1)}, u32[]{:S(2)}, u32[]{:S(2)}) %all-to-all-start.1) | async-done | bytes 393248 | tf_op jit(solution)/shard_map/cond/branch_1_fun/all_to_all | solution.py:160
  122.3 6.3 %convolution_bitcast_fusion = f32[1024,256]{1,0:T(8,128)S(1)} fusion(bf16[1024,4096]{1,0:T(8,128)(2,1)} %left_ref.1, bf16[4096,256]{1,0:T(8,128)(2,1)} %collective-permute-done.12.refs_6_), kind=kOutput, calls=%fused_computation.14 | convolution fusion | flops 2147483648 | bytes 11534336 | tf_op jit(solution)/shard_map/dot_general | solution.py:28
  128.6 0.1 slice_select_fusion.2
  128.7 0.1 collective-permute-start.13
  128.7 1.9 %collective-permute-done.13 = f32[512,256]{1,0:T(8,128)S(1)} collective-permute-done((f32[512,256]{1,0:T(8,128)S(1)}, f32[512,256]{1,0:T(8,128)S(1)}, u32[]{:S(2)}, u32[]{:S(2)}) %collective-permute-start.13) | collective-permute-done | bytes 524320 | tf_op jit(solution)/shard_map/ppermute | solution.py:120
  130.6 0.1 add_convert_fusion.2
  130.8 14.1 %all_to_all.31 = bf16[8,64,256]{2,1,0:T(8,128)(2,1)S(1)} all-to-all(bf16[8,64,256]{2,1,0:T(8,128)(2,1)S(1)} %bitcast.33), channel_id=1, replica_groups={{0,2,4,6,8,10,12,14},{1,3,5,7,9,11,13,15},{16,18,20,22,24,26,28,30},{17..., dimensions={0} | all-to-all | bytes 524288 | tf_op jit(solution)/shard_map/all_to_all | solution.py:160
  144.9 0.7 tile.4
  145.6 3.6 %all-to-all-start.3 = ((bf16[8,64,256]{2,1,0:T(8,128)(2,1)}), bf16[8,64,256]{2,1,0:T(8,128)(2,1)S(1)}, u32[]{:S(2)}, u32[]{:S(2)}) async-start(bf16[8,64,256]{2,1,0:T(8,128)(2,1)} %tile.4), calls=%async_computation.3 | async-start | bytes 524288 | tf_op jit(solution)/shard_map/all_to_all | solution.py:160
  149.2 8.6 %all-to-all-done.3 = bf16[8,64,256]{2,1,0:T(8,128)(2,1)S(1)} async-done(((bf16[8,64,256]{2,1,0:T(8,128)(2,1)}), bf16[8,64,256]{2,1,0:T(8,128)(2,1)S(1)}, u32[]{:S(2)}, u32[]{:S(2)}) %all-to-all-start.3) | async-done | bytes 262176 | tf_op jit(solution)/shard_map/all_to_all | solution.py:160
  157.8 1.5 collective-permute-done.14.refs_3_
  159.3 13.7 %shard_map.39 = bf16[1024,4096]{1,0:T(8,128)(2,1)} custom-call(s32[1]{0:T(128)} %bitcast.7.upper_ref, f32[1024,4096]{1,0:T(8,128)} %get-tuple-element.78.base_ref, bf16[512,384]{1,0:T(8,128)(2,1)} %get-tuple-element.79.refs_0_, bf16[512,384]{1,0:T(8,128)(2,1)S(1)} %collective-permute-done.11.refs_1_, bf16[512,256]{1,0:T(8,128)(2,1)S(1)} %bitcast.32, ...), custom_call_target="tpu_custom_call" | custom-call | flops 5368709120 | bytes 25165824 | tf_op jit(solution)/shard_map/pallas_call | solution.py:93
  (18 shorter events, 0.2 us)
Async XLA Ops:
  2.3 28.4 %collective-permute-start.6 = (bf16[4096,128]{1,0:T(8,128)(2,1)}, bf16[4096,128]{1,0:T(8,128)(2,1)S(1)}, u32[]{:S(2)}, u32[]{:S(2)}) collective-permute-start(bf16[4096,128]{1,0:T(8,128)(2,1)} %slice.9), channel_id=1, source_target_pairs={{0,16},{16,0},{1,17},{17,1},{2,18},{18,2},{3,19},{19,3},{4,20},{20... | collective-permute-start | bytes 3145736 | tf_op jit(solution)/shard_map/ppermute | solution.py:173
  5.2 3.4 %copy-start = (bf16[1024,4096]{1,0:T(8,128)(2,1)S(1)}, bf16[1024,4096]{1,0:T(8,128)(2,1)}, u32[]{:S(2)}) copy-start(bf16[1024,4096]{1,0:T(8,128)(2,1)} %left_ref.1) | copy-start | bytes 25165828
  18.2 3.1 %collective-permute-start.5 = (f32[512,640]{1,0:T(8,128)S(1)}, f32[512,640]{1,0:T(8,128)S(1)}, u32[]{:S(2)}, u32[]{:S(2)}) collective-permute-start(f32[512,640]{1,0:T(8,128)S(1)} %slice_select_fusion), channel_id=1, source_target_pairs={{0,1},{1,0},{2,3},{3,2},{4,5},{5,4},{6,7},{7,6},{8,9},{9,8},{10,11... | collective-permute-start | bytes 3932168 | tf_op jit(solution)/shard_map/cond/branch_1_fun/ppermute | solution.py:120
  28.6 48.8 %collective-permute-start.7 = (bf16[4096,256]{1,0:T(8,128)(2,1)}, bf16[4096,256]{1,0:T(8,128)(2,1)}, u32[]{:S(2)}, u32[]{:S(2)}) collective-permute-start(bf16[4096,256]{1,0:T(8,128)(2,1)} %get-tuple-element.74), channel_id=1, source_target_pairs={{0,16},{16,0},{1,17},{17,1},{2,18},{18,2},{3,19},{19,3},{4,20},{20... | collective-permute-start | bytes 6291464 | tf_op jit(solution)/shard_map/ppermute | solution.py:173
  28.6 16.8 %collective-permute-start.8 = (f32[256,640]{1,0:T(8,128)S(1)}, f32[256,640]{1,0:T(8,128)S(1)}, u32[]{:S(2)}, u32[]{:S(2)}) collective-permute-start(f32[256,640]{1,0:T(8,128)S(1)} %get-tuple-element.89), channel_id=1, source_target_pairs={{0,2},{1,3},{2,0},{3,1},{4,6},{5,7},{6,4},{7,5},{8,10},{9,11},{10,... | collective-permute-start | bytes 1966088 | tf_op jit(solution)/shard_map/ppermute | solution.py:120
  45.5 5.6 %collective-permute-start = (bf16[128,640]{1,0:T(8,128)(2,1)S(1)}, bf16[128,640]{1,0:T(8,128)(2,1)S(1)}, u32[]{:S(2)}, u32[]{:S(2)}) collective-permute-start(bf16[128,640]{1,0:T(8,128)(2,1)S(1)} %select_convert_fusion), channel_id=1, source_target_pairs={{0,4},{1,5},{2,6},{3,7},{4,0},{5,1},{6,2},{7,3},{8,12},{9,13},{10,... | collective-permute-start | bytes 491528 | tf_op jit(solution)/shard_map/cond/branch_1_fun/ppermute | solution.py:120
  51.2 5.4 %collective-permute-start.1 = (bf16[64,640]{1,0:T(8,128)(2,1)S(1)}, bf16[64,640]{1,0:T(8,128)(2,1)S(1)}, u32[]{:S(2)}, u32[]{:S(2)}) collective-permute-start(bf16[64,640]{1,0:T(8,128)(2,1)S(1)} %select_convert_fusion.1), channel_id=1, source_target_pairs={{0,8},{1,9},{2,10},{3,11},{4,12},{5,13},{6,14},{7,15},{8,0},{9,1},... | collective-permute-start | bytes 245768 | tf_op jit(solution)/shard_map/cond/branch_1_fun/ppermute | solution.py:120
  56.6 5.5 %collective-permute-start.2 = (bf16[64,640]{1,0:T(8,128)(2,1)S(1)}, bf16[64,640]{1,0:T(8,128)(2,1)S(1)}, u32[]{:S(2)}, u32[]{:S(2)}) collective-permute-start(bf16[64,640]{1,0:T(8,128)(2,1)S(1)} %add_convert_fusion), channel_id=1, source_target_pairs={{0,8},{1,9},{2,10},{3,11},{4,12},{5,13},{6,14},{7,15},{8,0},{9,1},... | collective-permute-start | bytes 245768 | tf_op jit(solution)/shard_map/cond/branch_1_fun/ppermute | solution.py:120
  62.2 5.4 %collective-permute-start.3 = (bf16[128,640]{1,0:T(8,128)(2,1)S(1)}, bf16[128,640]{1,0:T(8,128)(2,1)S(1)}, u32[]{:S(2)}, u32[]{:S(2)}) collective-permute-start(bf16[128,640]{1,0:T(8,128)(2,1)S(1)} %bitcast_select_fusion.1), channel_id=1, source_target_pairs={{0,4},{1,5},{2,6},{3,7},{4,0},{5,1},{6,2},{7,3},{8,12},{9,13},{10,... | collective-permute-start | bytes 491528 | tf_op jit(solution)/shard_map/cond/branch_1_fun/ppermute | solution.py:120
  67.7 54.6 %collective-permute-start.12 = (bf16[4096,256]{1,0:T(8,128)(2,1)}, bf16[4096,256]{1,0:T(8,128)(2,1)}, u32[]{:S(2)}, u32[]{:S(2)}) collective-permute-start(bf16[4096,256]{1,0:T(8,128)(2,1)} %get-tuple-element.80), channel_id=1, source_target_pairs={{0,16},{16,0},{1,17},{17,1},{2,18},{18,2},{3,19},{19,3},{4,20},{20... | collective-permute-start | bytes 6291464 | tf_op jit(solution)/shard_map/ppermute | solution.py:173
  69.3 7.1 %collective-permute-start.9 = (bf16[256,640]{1,0:T(8,128)(2,1)S(1)}, bf16[256,640]{1,0:T(8,128)(2,1)S(1)}, u32[]{:S(2)}, u32[]{:S(2)}) collective-permute-start(bf16[256,640]{1,0:T(8,128)(2,1)S(1)} %get-tuple-element.100), channel_id=1, source_target_pairs={{0,2},{1,3},{2,0},{3,1},{4,6},{5,7},{6,4},{7,5},{8,10},{9,11},{10,... | collective-permute-start | bytes 983048 | tf_op jit(solution)/shard_map/ppermute | solution.py:120
  76.5 7.2 %copy-start.1 = (f32[1024,128]{1,0:T(8,128)S(1)}, f32[1024,128]{1,0:T(8,128)}, u32[]{:S(2)}) copy-start(f32[1024,128]{1,0:T(8,128)} %convolution_bitcast_fusion.2) | copy-start | bytes 1572868
  76.5 7.3 %collective-permute-start.10 = (bf16[512,640]{1,0:T(8,128)(2,1)S(1)}, bf16[512,640]{1,0:T(8,128)(2,1)S(1)}, u32[]{:S(2)}, u32[]{:S(2)}) collective-permute-start(bf16[512,640]{1,0:T(8,128)(2,1)S(1)} %bitcast_select_fusion.2), channel_id=1, source_target_pairs={{0,1},{1,0},{2,3},{3,2},{4,5},{5,4},{6,7},{7,6},{8,9},{9,8},{10,11... | collective-permute-start | bytes 1966088 | tf_op jit(solution)/shard_map/ppermute | solution.py:120
  83.9 2.4 %collective-permute-start.4 = (f32[512,384]{1,0:T(8,128)S(1)}, f32[512,384]{1,0:T(8,128)S(1)}, u32[]{:S(2)}, u32[]{:S(2)}) collective-permute-start(f32[512,384]{1,0:T(8,128)S(1)} %slice_select_fusion.1), channel_id=1, source_target_pairs={{0,1},{1,0},{2,3},{3,2},{4,5},{5,4},{6,7},{7,6},{8,9},{9,8},{10,11... | collective-permute-start | bytes 2359304 | tf_op jit(solution)/shard_map/cond/branch_1_fun/ppermute | solution.py:120
  87.2 18.6 %all-to-all-start = ((bf16[8,64,384]{2,1,0:T(8,128)(2,1)}), bf16[8,64,384]{2,1,0:T(8,128)(2,1)S(1)}, u32[]{:S(2)}, u32[]{:S(2)}) async-start(bf16[8,64,384]{2,1,0:T(8,128)(2,1)} %bitcast.5), calls=%async_computation | async-start | bytes 786432 | tf_op jit(solution)/shard_map/cond/branch_1_fun/all_to_all | solution.py:160
  106.6 15.7 %all-to-all-start.1 = ((bf16[8,64,384]{2,1,0:T(8,128)(2,1)}), bf16[8,64,384]{2,1,0:T(8,128)(2,1)}, u32[]{:S(2)}, u32[]{:S(2)}) async-start(bf16[8,64,384]{2,1,0:T(8,128)(2,1)} %tile.0), calls=%async_computation.1 | async-start | bytes 786432 | tf_op jit(solution)/shard_map/cond/branch_1_fun/all_to_all | solution.py:160
  128.7 2.0 %collective-permute-start.13 = (f32[512,256]{1,0:T(8,128)S(1)}, f32[512,256]{1,0:T(8,128)S(1)}, u32[]{:S(2)}, u32[]{:S(2)}) collective-permute-start(f32[512,256]{1,0:T(8,128)S(1)} %slice_select_fusion.2), channel_id=1, source_target_pairs={{0,1},{1,0},{2,3},{3,2},{4,5},{5,4},{6,7},{7,6},{8,9},{9,8},{10,11... | collective-permute-start | bytes 1572872 | tf_op jit(solution)/shard_map/ppermute | solution.py:120
  145.6 12.2 %all-to-all-start.3 = ((bf16[8,64,256]{2,1,0:T(8,128)(2,1)}), bf16[8,64,256]{2,1,0:T(8,128)(2,1)S(1)}, u32[]{:S(2)}, u32[]{:S(2)}) async-start(bf16[8,64,256]{2,1,0:T(8,128)(2,1)} %tile.4), calls=%async_computation.3 | async-start | bytes 524288 | tf_op jit(solution)/shard_map/all_to_all | solution.py:160
  149.2 8.6 %collective-permute-start.11 = (bf16[512,384]{1,0:T(8,128)(2,1)}, bf16[512,384]{1,0:T(8,128)(2,1)S(1)}, u32[]{:S(2)}, u32[]{:S(2)}) collective-permute-start(bf16[512,384]{1,0:T(8,128)(2,1)} %get-tuple-element.79.refs_0_), channel_id=1, source_target_pairs={{0,1},{1,0},{2,3},{3,2},{4,5},{5,4},{6,7},{7,6},{8,9},{9,8},{10,11... | collective-permute-start | bytes 1179656 | tf_op jit(solution)/shard_map/ppermute | solution.py:120
  157.8 1.5 collective-permute-start.14

commit v13 on v12

--- a/solution.py
+++ b/solution.py
@@ -10,7 +10,7 @@
 
 GROUPS = (128, 256, 256)
 VMEM_BYTES = 52 * 1024 * 1024
-WIDE_VMEM_BYTES = 24 * 1024 * 1024
+WIDE_VMEM_BYTES = 58 * 1024 * 1024
 FREE = pl.CostEstimate(flops=0, bytes_accessed=0, transcendentals=0)
 
 

time: 174 us -> 171 us (0.983)
  local copies, waits for them, and re-layouts: 13.4 us -> 10 us
    unnamed x4 -> x2, local copies, waits for them, and re-layouts: 3.39 us -> 0.01 us
  transfers between devices with their start and end apart: 18 -> 18, of which waited for: 14 -> 15; matrix products, arithmetic and copies ran while one was open for 13% -> 14% of each run, Pallas kernels for 14% -> 15%
where the time goes in v13:
time: 171 us; the launch traced here: 170 us
  waiting for transfers between devices  52.4 us (31%)
  Pallas kernels  38.9 us (23%)
  starting transfers between devices  31.8 us (19%)
  matrix products  19.1 us (11%)
  blocking collectives  14.4 us (8%)
  local copies, waits for them, and re-layouts  10 us (6%)
  other arithmetic  3.43 us (2%)
    ppermute x12, waiting for transfers between devices, exchange(): return lax.ppermute(value, 'col', [(i, i ^ bit) for i in range(cols)])  33.2 us
    pallas_call x3, Pallas kernels, project_back(): pl.pallas_call(kernel, grid_spec=pltpu.PrefetchScalarGridSpec(num_scalar_...  29.1 us
    dot_general x3, matrix products, project(): part = jnp.dot(amplitudes, vectors, preferred_element_type=jnp.float32)  19.1 us
    all_to_all x3, waiting for transfers between devices, spread(): lax.all_to_all(value, 'col', 0, 0, tiled=True, axis_index_groups=mates)  16.9 us
    all_to_all x1, blocking collectives, spread(): lax.all_to_all(value, 'col', 0, 0, tiled=True, axis_index_groups=mates)  14.4 us
    all_to_all x3, starting transfers between devices, spread(): lax.all_to_all(value, 'col', 0, 0, tiled=True, axis_index_groups=mates)  14.1 us
    ppermute x12, starting transfers between devices, exchange(): return lax.ppermute(value, 'col', [(i, i ^ bit) for i in range(cols)])  13.2 us
    pallas_call x1, Pallas kernels, project_wide(): pl.pallas_call(kernel, grid=(steps,), in_specs=[pl.BlockSpec((rows, block...  9.81 us
  transfers between devices with their start and end apart: 18, of which 15 were waited for; matrix products, arithmetic and copies ran while one was open for 14% of the time, Pallas kernels for 15%

profile of v13, /device:TPU:0, one launch (start us, length us, event | category | flops | bytes accessed | tf_op | source)
XLA Modules:
  0.0 170.3 jit_solution(12619331346750965131)
XLA Ops:
  0.0 2.3 %slice.9 = bf16[4096,128]{1,0:T(8,128)(2,1)} slice(bf16[4096,640]{1,0:T(8,128)(2,1)} %right_ref), slice={[0:4096], [0:128]} | slice | bytes 2097152 | tf_op jit(solution)/shard_map/slice | solution.py:184
  2.3 2.9 %collective-permute-start.6 = (bf16[4096,128]{1,0:T(8,128)(2,1)}, bf16[4096,128]{1,0:T(8,128)(2,1)S(1)}, u32[]{:S(2)}, u32[]{:S(2)}) collective-permute-start(bf16[4096,128]{1,0:T(8,128)(2,1)} %slice.9), channel_id=1, source_target_pairs={{0,16},{16,0},{1,17},{17,1},{2,18},{18,2},{3,19},{19,3},{4,20},{20... | collective-permute-start | bytes 3145736 | tf_op jit(solution)/shard_map/ppermute | solution.py:173
  5.2 9.8 %shard_map.38 = f32[1024,640]{1,0:T(8,128)S(1)} custom-call(bf16[1024,4096]{1,0:T(8,128)(2,1)} %left_ref.1, bf16[4096,640]{1,0:T(8,128)(2,1)} %right_ref), custom_call_target="tpu_custom_call" | custom-call | tf_op jit(solution)/shard_map/pallas_call | solution.py:54
  15.0 5.9 %conditional.3 = (f32[512,640]{1,0:T(8,128)}, f32[256,640]{1,0:T(8,128)S(1)}, f32[256,640]{1,0:T(8,128)S(1)}) conditional(s32[]{:T(128)} %convert_element_type.45, () %tuple.43, (pred[]{:T(512)}, f32[1024,640]{1,0:T(8,128)S(1)}) %tuple.45), branch_computations={%region_0.0_spmd, %region_1.2_spmd} | conditional | flops 983040 | bytes 17039426 | solution.py:130
  15.1 0.1 slice_select_fusion
  15.2 0.1 collective-permute-start.5
  15.3 3.0 %collective-permute-done.5 = f32[512,640]{1,0:T(8,128)S(1)} collective-permute-done((f32[512,640]{1,0:T(8,128)S(1)}, f32[512,640]{1,0:T(8,128)S(1)}, u32[]{:S(2)}, u32[]{:S(2)}) %collective-permute-start.5) | collective-permute-done | bytes 1310752 | tf_op jit(solution)/shard_map/cond/branch_1_fun/ppermute | solution.py:120
  18.3 1.3 select_add_fusion
  19.6 1.4 fusion
  21.0 0.1 broadcast_select_fusion
  21.1 4.5 %fusion.1 = (bf16[4096,256]{1,0:T(8,128)(2,1)}, bf16[4096,256]{1,0:T(8,128)(2,1)}) fusion(bf16[4096,640]{1,0:T(8,128)(2,1)} %right_ref), kind=kLoop, calls=%fused_computation.24 | loop fusion | bytes 8388608 | tf_op jit(solution)/shard_map/slice | solution.py:184
  25.6 0.0 collective-permute-start.7
  25.6 2.0 %collective-permute-start.8 = (f32[256,640]{1,0:T(8,128)S(1)}, f32[256,640]{1,0:T(8,128)S(1)}, u32[]{:S(2)}, u32[]{:S(2)}) collective-permute-start(f32[256,640]{1,0:T(8,128)S(1)} %get-tuple-element.89), channel_id=1, source_target_pairs={{0,2},{1,3},{2,0},{3,1},{4,6},{5,7},{6,4},{7,5},{8,10},{9,11},{10,... | collective-permute-start | bytes 1966088 | tf_op jit(solution)/shard_map/ppermute | solution.py:120
  27.7 1.4 collective-permute-done.6.refs_4_
  29.1 6.5 %convolution_bitcast_fusion.2 = f32[1024,128]{1,0:T(8,128)} fusion(bf16[1024,4096]{1,0:T(8,128)(2,1)} %left_ref.1, bf16[4096,128]{1,0:T(8,128)(2,1)S(1)} %collective-permute-done.6.refs_4_), kind=kOutput, calls=%fused_computation.16 | convolution fusion | flops 1073741824 | bytes 9961472 | tf_op jit(solution)/shard_map/dot_general | solution.py:28
  35.6 6.8 %collective-permute-done.8 = f32[256,640]{1,0:T(8,128)S(1)} collective-permute-done((f32[256,640]{1,0:T(8,128)S(1)}, f32[256,640]{1,0:T(8,128)S(1)}, u32[]{:S(2)}, u32[]{:S(2)}) %collective-permute-start.8) | collective-permute-done | bytes 655392 | tf_op jit(solution)/shard_map/ppermute | solution.py:120
  42.4 22.3 %conditional.4 = (bf16[256,640]{1,0:T(8,128)(2,1)S(1)}) conditional(s32[]{:T(128)} %convert_element_type.45, () %tuple.48, (s32[]{:T(128)}, f32[256,640]{1,0:T(8,128)S(1)}, f32[256,640]{1,0:T(8,128)S(1)}) %tuple.50), branch_computations={%region_2.3_spmd, %region_3.4_spmd} | conditional | flops 942090 | bytes 7292144 | solution.py:130
  42.4 0.1 add.14
  42.5 1.9 %collective-permute-start = (bf16[128,640]{1,0:T(8,128)(2,1)S(1)}, bf16[128,640]{1,0:T(8,128)(2,1)S(1)}, u32[]{:S(2)}, u32[]{:S(2)}) collective-permute-start(bf16[128,640]{1,0:T(8,128)(2,1)S(1)} %select_convert_fusion), channel_id=1, source_target_pairs={{0,4},{1,5},{2,6},{3,7},{4,0},{5,1},{6,2},{7,3},{8,12},{9,13},{10,... | collective-permute-start | bytes 491528 | tf_op jit(solution)/shard_map/cond/branch_1_fun/ppermute | solution.py:120
  44.4 3.7 %collective-permute-done = bf16[128,640]{1,0:T(8,128)(2,1)S(1)} collective-permute-done((bf16[128,640]{1,0:T(8,128)(2,1)S(1)}, bf16[128,640]{1,0:T(8,128)(2,1)S(1)}, u32[]{:S(2)}, u32[]{:S(2)}) %collective-permute-start) | collective-permute-done | bytes 163872 | tf_op jit(solution)/shard_map/cond/branch_1_fun/ppermute | solution.py:120
  48.2 2.7 %collective-permute-start.1 = (bf16[64,640]{1,0:T(8,128)(2,1)S(1)}, bf16[64,640]{1,0:T(8,128)(2,1)S(1)}, u32[]{:S(2)}, u32[]{:S(2)}) collective-permute-start(bf16[64,640]{1,0:T(8,128)(2,1)S(1)} %select_convert_fusion.1), channel_id=1, source_target_pairs={{0,8},{1,9},{2,10},{3,11},{4,12},{5,13},{6,14},{7,15},{8,0},{9,1},... | collective-permute-start | bytes 245768 | tf_op jit(solution)/shard_map/cond/branch_1_fun/ppermute | solution.py:120
  50.9 0.1 broadcast_in_dim.54
  50.9 0.1 broadcast_in_dim.55
  51.0 2.6 %collective-permute-done.1 = bf16[64,640]{1,0:T(8,128)(2,1)S(1)} collective-permute-done((bf16[64,640]{1,0:T(8,128)(2,1)S(1)}, bf16[64,640]{1,0:T(8,128)(2,1)S(1)}, u32[]{:S(2)}, u32[]{:S(2)}) %collective-permute-start.1) | collective-permute-done | bytes 81952 | tf_op jit(solution)/shard_map/cond/branch_1_fun/ppermute | solution.py:120
  53.6 2.8 %collective-permute-start.2 = (bf16[64,640]{1,0:T(8,128)(2,1)S(1)}, bf16[64,640]{1,0:T(8,128)(2,1)S(1)}, u32[]{:S(2)}, u32[]{:S(2)}) collective-permute-start(bf16[64,640]{1,0:T(8,128)(2,1)S(1)} %add_convert_fusion), channel_id=1, source_target_pairs={{0,8},{1,9},{2,10},{3,11},{4,12},{5,13},{6,14},{7,15},{8,0},{9,1},... | collective-permute-start | bytes 245768 | tf_op jit(solution)/shard_map/cond/branch_1_fun/ppermute | solution.py:120
  56.4 2.7 %collective-permute-done.2 = bf16[64,640]{1,0:T(8,128)(2,1)S(1)} collective-permute-done((bf16[64,640]{1,0:T(8,128)(2,1)S(1)}, bf16[64,640]{1,0:T(8,128)(2,1)S(1)}, u32[]{:S(2)}, u32[]{:S(2)}) %collective-permute-start.2) | collective-permute-done | bytes 81952 | tf_op jit(solution)/shard_map/cond/branch_1_fun/ppermute | solution.py:120
  59.1 0.1 bitcast_select_fusion.1
  59.2 2.0 %collective-permute-start.3 = (bf16[128,640]{1,0:T(8,128)(2,1)S(1)}, bf16[128,640]{1,0:T(8,128)(2,1)S(1)}, u32[]{:S(2)}, u32[]{:S(2)}) collective-permute-start(bf16[128,640]{1,0:T(8,128)(2,1)S(1)} %bitcast_select_fusion.1), channel_id=1, source_target_pairs={{0,4},{1,5},{2,6},{3,7},{4,0},{5,1},{6,2},{7,3},{8,12},{9,13},{10,... | collective-permute-start | bytes 491528 | tf_op jit(solution)/shard_map/cond/branch_1_fun/ppermute | solution.py:120
  61.2 0.1 broadcast_bitcast_fusion
  61.3 3.3 %collective-permute-done.3 = bf16[128,640]{1,0:T(8,128)(2,1)S(1)} collective-permute-done((bf16[128,640]{1,0:T(8,128)(2,1)S(1)}, bf16[128,640]{1,0:T(8,128)(2,1)S(1)}, u32[]{:S(2)}, u32[]{:S(2)}) %collective-permute-start.3) | collective-permute-done | bytes 163872 | tf_op jit(solution)/shard_map/cond/branch_1_fun/ppermute | solution.py:120
  64.6 0.1 bitcast_select_fusion
  64.7 1.6 collective-permute-start.12
  66.3 1.5 collective-permute-start.9
  67.8 0.1 broadcast_in_dim.72
  67.9 5.4 %collective-permute-done.9 = bf16[256,640]{1,0:T(8,128)(2,1)S(1)} collective-permute-done((bf16[256,640]{1,0:T(8,128)(2,1)S(1)}, bf16[256,640]{1,0:T(8,128)(2,1)S(1)}, u32[]{:S(2)}, u32[]{:S(2)}) %collective-permute-start.9) | collective-permute-done | bytes 327712 | tf_op jit(solution)/shard_map/ppermute | solution.py:120
  73.4 0.2 bitcast_select_fusion.2
  73.5 0.1 collective-permute-start.10
  73.6 0.8 collective-permute-done.7.refs_5_
  74.4 6.3 %convolution_bitcast_fusion.1 = f32[1024,256]{1,0:T(8,128)S(1)} fusion(bf16[1024,4096]{1,0:T(8,128)(2,1)} %left_ref.1, bf16[4096,256]{1,0:T(8,128)(2,1)} %collective-permute-done.7.refs_5_), kind=kOutput, calls=%fused_computation.15 | convolution fusion | flops 2147483648 | bytes 11534336 | tf_op jit(solution)/shard_map/dot_general | solution.py:28
  80.7 0.1 pad_maximum_fusion
  80.8 38.4 %conditional.5 = (bf16[512,384]{1,0:T(8,128)(2,1)}, f32[1024,4096]{1,0:T(8,128)}) conditional(s32[]{:T(128)} %convert_element_type.45, () %tuple.42, (pred[]{:T(512)}, f32[1024,384]{1,0:T(8,128)S(1)}, s32[1]{0:T(128)}, bf16[1024,4096]{1,0:T(8,128)(2,1)}, bf16[512,640]{1,0:T(8,128)(2,1)S(1)}, /*index=5*/bf16[512,640]{1,0:T(8,128)(2,1)S(1)}, ...), branch_computations={%region_4.5_spmd, %region_5.7_spmd} | conditional | flops 5369667584 | bytes 36667516 | solution.py:130
  80.9 0.1 slice_select_fusion.1
  81.0 0.1 collective-permute-start.4
  81.0 2.3 %collective-permute-done.4 = f32[512,384]{1,0:T(8,128)S(1)} collective-permute-done((f32[512,384]{1,0:T(8,128)S(1)}, f32[512,384]{1,0:T(8,128)S(1)}, u32[]{:S(2)}, u32[]{:S(2)}) %collective-permute-start.4) | collective-permute-done | bytes 786464 | tf_op jit(solution)/shard_map/cond/branch_1_fun/ppermute | solution.py:120
  83.3 0.9 add_convert_fusion.1
  84.2 6.4 %all-to-all-start = ((bf16[8,64,384]{2,1,0:T(8,128)(2,1)}), bf16[8,64,384]{2,1,0:T(8,128)(2,1)S(1)}, u32[]{:S(2)}, u32[]{:S(2)}) async-start(bf16[8,64,384]{2,1,0:T(8,128)(2,1)} %bitcast.5), calls=%async_computation | async-start | bytes 786432 | tf_op jit(solution)/shard_map/cond/branch_1_fun/all_to_all | solution.py:160
  90.6 7.7 %branch_1_fun.2.refs_0_ = f32[1024,4096]{1,0:T(8,128)} custom-call(s32[1]{0:T(128)} %get-tuple-element.52.upper_ref, bf16[1024,4096]{1,0:T(8,128)(2,1)} %get-tuple-element.58.base_ref, bf16[512,640]{1,0:T(8,128)(2,1)S(1)} %get-tuple-element.54.refs_0_.refs_1_, bf16[512,640]{1,0:T(8,128)(2,1)S(1)} %get-tuple-element.55.refs_1_.refs_2_, ...), custom_call_target="tpu_custom_call" | custom-call | flops 2684354560 | bytes 12582912 | tf_op jit(solution)/shard_map/cond/branch_1_fun/pallas_call | solution.py:93
  98.3 4.5 %all-to-all-done = bf16[8,64,384]{2,1,0:T(8,128)(2,1)S(1)} async-done(((bf16[8,64,384]{2,1,0:T(8,128)(2,1)}), bf16[8,64,384]{2,1,0:T(8,128)(2,1)S(1)}, u32[]{:S(2)}, u32[]{:S(2)}) %all-to-all-start) | async-done | bytes 393248 | tf_op jit(solution)/shard_map/cond/branch_1_fun/all_to_all | solution.py:160
  102.8 0.1 reduce_sum.22
  102.8 0.8 tile.0
  103.6 4.1 %all-to-all-start.1 = ((bf16[8,64,384]{2,1,0:T(8,128)(2,1)}), bf16[8,64,384]{2,1,0:T(8,128)(2,1)}, u32[]{:S(2)}, u32[]{:S(2)}) async-start(bf16[8,64,384]{2,1,0:T(8,128)(2,1)} %tile.0), calls=%async_computation.1 | async-start | bytes 786432 | tf_op jit(solution)/shard_map/cond/branch_1_fun/all_to_all | solution.py:160
  107.7 7.7 %branch_1_fun.3 = f32[1024,4096]{1,0:T(8,128)} custom-call(s32[1]{0:T(128)} %get-tuple-element.52.upper_ref, bf16[1024,4096]{1,0:T(8,128)(2,1)} %get-tuple-element.58.base_ref, f32[1024,4096]{1,0:T(8,128)} %branch_1_fun.2.refs_0_, bf16[512,640]{1,0:T(8,128)(2,1)S(1)} %get-tuple-element.54.refs_0_.refs_1_, ...), custom_call_target="tpu_custom_call", output_to_operand_aliasing={{}: (2, {})} | custom-call | flops 2684354560 | bytes 12582912 | tf_op jit(solution)/shard_map/cond/branch_1_fun/pallas_call | solution.py:93
  115.4 3.8 %all-to-all-done.1 = bf16[8,64,384]{2,1,0:T(8,128)(2,1)} async-done(((bf16[8,64,384]{2,1,0:T(8,128)(2,1)}), bf16[8,64,384]{2,1,0:T(8,128)(2,1)}, u32[]{:S(2)}, u32[]{:S(2)}) %all-to-all-start.1) | async-done | bytes 393248 | tf_op jit(solution)/shard_map/cond/branch_1_fun/all_to_all | solution.py:160
  119.3 6.3 %convolution_bitcast_fusion = f32[1024,256]{1,0:T(8,128)S(1)} fusion(bf16[1024,4096]{1,0:T(8,128)(2,1)} %left_ref.1, bf16[4096,256]{1,0:T(8,128)(2,1)} %collective-permute-done.12.refs_6_), kind=kOutput, calls=%fused_computation.14 | convolution fusion | flops 2147483648 | bytes 11534336 | tf_op jit(solution)/shard_map/dot_general | solution.py:28
  125.6 0.1 slice_select_fusion.2
  125.7 0.1 collective-permute-start.13
  125.7 1.9 %collective-permute-done.13 = f32[512,256]{1,0:T(8,128)S(1)} collective-permute-done((f32[512,256]{1,0:T(8,128)S(1)}, f32[512,256]{1,0:T(8,128)S(1)}, u32[]{:S(2)}, u32[]{:S(2)}) %collective-permute-start.13) | collective-permute-done | bytes 524320 | tf_op jit(solution)/shard_map/ppermute | solution.py:120
  127.6 0.1 add_convert_fusion.2
  127.8 14.4 %all_to_all.31 = bf16[8,64,256]{2,1,0:T(8,128)(2,1)S(1)} all-to-all(bf16[8,64,256]{2,1,0:T(8,128)(2,1)S(1)} %bitcast.33), channel_id=1, replica_groups={{0,2,4,6,8,10,12,14},{1,3,5,7,9,11,13,15},{16,18,20,22,24,26,28,30},{17..., dimensions={0} | all-to-all | bytes 524288 | tf_op jit(solution)/shard_map/all_to_all | solution.py:160
  142.2 0.7 tile.4
  142.9 3.6 %all-to-all-start.3 = ((bf16[8,64,256]{2,1,0:T(8,128)(2,1)}), bf16[8,64,256]{2,1,0:T(8,128)(2,1)S(1)}, u32[]{:S(2)}, u32[]{:S(2)}) async-start(bf16[8,64,256]{2,1,0:T(8,128)(2,1)} %tile.4), calls=%async_computation.3 | async-start | bytes 524288 | tf_op jit(solution)/shard_map/all_to_all | solution.py:160
  146.5 8.6 %all-to-all-done.3 = bf16[8,64,256]{2,1,0:T(8,128)(2,1)S(1)} async-done(((bf16[8,64,256]{2,1,0:T(8,128)(2,1)}), bf16[8,64,256]{2,1,0:T(8,128)(2,1)S(1)}, u32[]{:S(2)}, u32[]{:S(2)}) %all-to-all-start.3) | async-done | bytes 262176 | tf_op jit(solution)/shard_map/all_to_all | solution.py:160
  155.1 1.5 collective-permute-done.14.refs_3_
  156.6 13.7 %shard_map.39 = bf16[1024,4096]{1,0:T(8,128)(2,1)} custom-call(s32[1]{0:T(128)} %bitcast.7.upper_ref, f32[1024,4096]{1,0:T(8,128)} %get-tuple-element.78.base_ref, bf16[512,384]{1,0:T(8,128)(2,1)} %get-tuple-element.79.refs_0_, bf16[512,384]{1,0:T(8,128)(2,1)S(1)} %collective-permute-done.11.refs_1_, bf16[512,256]{1,0:T(8,128)(2,1)S(1)} %bitcast.32, ...), custom_call_target="tpu_custom_call" | custom-call | flops 5368709120 | bytes 25165824 | tf_op jit(solution)/shard_map/pallas_call | solution.py:93
  (16 shorter events, 0.2 us)
Async XLA Ops:
  2.3 26.8 %collective-permute-start.6 = (bf16[4096,128]{1,0:T(8,128)(2,1)}, bf16[4096,128]{1,0:T(8,128)(2,1)S(1)}, u32[]{:S(2)}, u32[]{:S(2)}) collective-permute-start(bf16[4096,128]{1,0:T(8,128)(2,1)} %slice.9), channel_id=1, source_target_pairs={{0,16},{16,0},{1,17},{17,1},{2,18},{18,2},{3,19},{19,3},{4,20},{20... | collective-permute-start | bytes 3145736 | tf_op jit(solution)/shard_map/ppermute | solution.py:173
  15.2 3.1 %collective-permute-start.5 = (f32[512,640]{1,0:T(8,128)S(1)}, f32[512,640]{1,0:T(8,128)S(1)}, u32[]{:S(2)}, u32[]{:S(2)}) collective-permute-start(f32[512,640]{1,0:T(8,128)S(1)} %slice_select_fusion), channel_id=1, source_target_pairs={{0,1},{1,0},{2,3},{3,2},{4,5},{5,4},{6,7},{7,6},{8,9},{9,8},{10,11... | collective-permute-start | bytes 3932168 | tf_op jit(solution)/shard_map/cond/branch_1_fun/ppermute | solution.py:120
  25.6 48.8 %collective-permute-start.7 = (bf16[4096,256]{1,0:T(8,128)(2,1)}, bf16[4096,256]{1,0:T(8,128)(2,1)}, u32[]{:S(2)}, u32[]{:S(2)}) collective-permute-start(bf16[4096,256]{1,0:T(8,128)(2,1)} %get-tuple-element.74), channel_id=1, source_target_pairs={{0,16},{16,0},{1,17},{17,1},{2,18},{18,2},{3,19},{19,3},{4,20},{20... | collective-permute-start | bytes 6291464 | tf_op jit(solution)/shard_map/ppermute | solution.py:173
  25.6 16.8 %collective-permute-start.8 = (f32[256,640]{1,0:T(8,128)S(1)}, f32[256,640]{1,0:T(8,128)S(1)}, u32[]{:S(2)}, u32[]{:S(2)}) collective-permute-start(f32[256,640]{1,0:T(8,128)S(1)} %get-tuple-element.89), channel_id=1, source_target_pairs={{0,2},{1,3},{2,0},{3,1},{4,6},{5,7},{6,4},{7,5},{8,10},{9,11},{10,... | collective-permute-start | bytes 1966088 | tf_op jit(solution)/shard_map/ppermute | solution.py:120
  42.5 5.6 %collective-permute-start = (bf16[128,640]{1,0:T(8,128)(2,1)S(1)}, bf16[128,640]{1,0:T(8,128)(2,1)S(1)}, u32[]{:S(2)}, u32[]{:S(2)}) collective-permute-start(bf16[128,640]{1,0:T(8,128)(2,1)S(1)} %select_convert_fusion), channel_id=1, source_target_pairs={{0,4},{1,5},{2,6},{3,7},{4,0},{5,1},{6,2},{7,3},{8,12},{9,13},{10,... | collective-permute-start | bytes 491528 | tf_op jit(solution)/shard_map/cond/branch_1_fun/ppermute | solution.py:120
  48.2 5.4 %collective-permute-start.1 = (bf16[64,640]{1,0:T(8,128)(2,1)S(1)}, bf16[64,640]{1,0:T(8,128)(2,1)S(1)}, u32[]{:S(2)}, u32[]{:S(2)}) collective-permute-start(bf16[64,640]{1,0:T(8,128)(2,1)S(1)} %select_convert_fusion.1), channel_id=1, source_target_pairs={{0,8},{1,9},{2,10},{3,11},{4,12},{5,13},{6,14},{7,15},{8,0},{9,1},... | collective-permute-start | bytes 245768 | tf_op jit(solution)/shard_map/cond/branch_1_fun/ppermute | solution.py:120
  53.6 5.5 %collective-permute-start.2 = (bf16[64,640]{1,0:T(8,128)(2,1)S(1)}, bf16[64,640]{1,0:T(8,128)(2,1)S(1)}, u32[]{:S(2)}, u32[]{:S(2)}) collective-permute-start(bf16[64,640]{1,0:T(8,128)(2,1)S(1)} %add_convert_fusion), channel_id=1, source_target_pairs={{0,8},{1,9},{2,10},{3,11},{4,12},{5,13},{6,14},{7,15},{8,0},{9,1},... | collective-permute-start | bytes 245768 | tf_op jit(solution)/shard_map/cond/branch_1_fun/ppermute | solution.py:120
  59.2 5.4 %collective-permute-start.3 = (bf16[128,640]{1,0:T(8,128)(2,1)S(1)}, bf16[128,640]{1,0:T(8,128)(2,1)S(1)}, u32[]{:S(2)}, u32[]{:S(2)}) collective-permute-start(bf16[128,640]{1,0:T(8,128)(2,1)S(1)} %bitcast_select_fusion.1), channel_id=1, source_target_pairs={{0,4},{1,5},{2,6},{3,7},{4,0},{5,1},{6,2},{7,3},{8,12},{9,13},{10,... | collective-permute-start | bytes 491528 | tf_op jit(solution)/shard_map/cond/branch_1_fun/ppermute | solution.py:120
  64.7 54.6 %collective-permute-start.12 = (bf16[4096,256]{1,0:T(8,128)(2,1)}, bf16[4096,256]{1,0:T(8,128)(2,1)}, u32[]{:S(2)}, u32[]{:S(2)}) collective-permute-start(bf16[4096,256]{1,0:T(8,128)(2,1)} %get-tuple-element.80), channel_id=1, source_target_pairs={{0,16},{16,0},{1,17},{17,1},{2,18},{18,2},{3,19},{19,3},{4,20},{20... | collective-permute-start | bytes 6291464 | tf_op jit(solution)/shard_map/ppermute | solution.py:173
  66.3 7.1 %collective-permute-start.9 = (bf16[256,640]{1,0:T(8,128)(2,1)S(1)}, bf16[256,640]{1,0:T(8,128)(2,1)S(1)}, u32[]{:S(2)}, u32[]{:S(2)}) collective-permute-start(bf16[256,640]{1,0:T(8,128)(2,1)S(1)} %get-tuple-element.100), channel_id=1, source_target_pairs={{0,2},{1,3},{2,0},{3,1},{4,6},{5,7},{6,4},{7,5},{8,10},{9,11},{10,... | collective-permute-start | bytes 983048 | tf_op jit(solution)/shard_map/ppermute | solution.py:120
  73.5 7.2 %copy-start = (f32[1024,128]{1,0:T(8,128)S(1)}, f32[1024,128]{1,0:T(8,128)}, u32[]{:S(2)}) copy-start(f32[1024,128]{1,0:T(8,128)} %convolution_bitcast_fusion.2) | copy-start | bytes 1572868
  73.5 7.3 %collective-permute-start.10 = (bf16[512,640]{1,0:T(8,128)(2,1)S(1)}, bf16[512,640]{1,0:T(8,128)(2,1)S(1)}, u32[]{:S(2)}, u32[]{:S(2)}) collective-permute-start(bf16[512,640]{1,0:T(8,128)(2,1)S(1)} %bitcast_select_fusion.2), channel_id=1, source_target_pairs={{0,1},{1,0},{2,3},{3,2},{4,5},{5,4},{6,7},{7,6},{8,9},{9,8},{10,11... | collective-permute-start | bytes 1966088 | tf_op jit(solution)/shard_map/ppermute | solution.py:120
  81.0 2.4 %collective-permute-start.4 = (f32[512,384]{1,0:T(8,128)S(1)}, f32[512,384]{1,0:T(8,128)S(1)}, u32[]{:S(2)}, u32[]{:S(2)}) collective-permute-start(f32[512,384]{1,0:T(8,128)S(1)} %slice_select_fusion.1), channel_id=1, source_target_pairs={{0,1},{1,0},{2,3},{3,2},{4,5},{5,4},{6,7},{7,6},{8,9},{9,8},{10,11... | collective-permute-start | bytes 2359304 | tf_op jit(solution)/shard_map/cond/branch_1_fun/ppermute | solution.py:120
  84.2 18.6 %all-to-all-start = ((bf16[8,64,384]{2,1,0:T(8,128)(2,1)}), bf16[8,64,384]{2,1,0:T(8,128)(2,1)S(1)}, u32[]{:S(2)}, u32[]{:S(2)}) async-start(bf16[8,64,384]{2,1,0:T(8,128)(2,1)} %bitcast.5), calls=%async_computation | async-start | bytes 786432 | tf_op jit(solution)/shard_map/cond/branch_1_fun/all_to_all | solution.py:160
  103.6 15.7 %all-to-all-start.1 = ((bf16[8,64,384]{2,1,0:T(8,128)(2,1)}), bf16[8,64,384]{2,1,0:T(8,128)(2,1)}, u32[]{:S(2)}, u32[]{:S(2)}) async-start(bf16[8,64,384]{2,1,0:T(8,128)(2,1)} %tile.0), calls=%async_computation.1 | async-start | bytes 786432 | tf_op jit(solution)/shard_map/cond/branch_1_fun/all_to_all | solution.py:160
  125.7 2.0 %collective-permute-start.13 = (f32[512,256]{1,0:T(8,128)S(1)}, f32[512,256]{1,0:T(8,128)S(1)}, u32[]{:S(2)}, u32[]{:S(2)}) collective-permute-start(f32[512,256]{1,0:T(8,128)S(1)} %slice_select_fusion.2), channel_id=1, source_target_pairs={{0,1},{1,0},{2,3},{3,2},{4,5},{5,4},{6,7},{7,6},{8,9},{9,8},{10,11... | collective-permute-start | bytes 1572872 | tf_op jit(solution)/shard_map/ppermute | solution.py:120
  142.9 12.2 %all-to-all-start.3 = ((bf16[8,64,256]{2,1,0:T(8,128)(2,1)}), bf16[8,64,256]{2,1,0:T(8,128)(2,1)S(1)}, u32[]{:S(2)}, u32[]{:S(2)}) async-start(bf16[8,64,256]{2,1,0:T(8,128)(2,1)} %tile.4), calls=%async_computation.3 | async-start | bytes 524288 | tf_op jit(solution)/shard_map/all_to_all | solution.py:160
  146.5 8.6 %collective-permute-start.11 = (bf16[512,384]{1,0:T(8,128)(2,1)}, bf16[512,384]{1,0:T(8,128)(2,1)S(1)}, u32[]{:S(2)}, u32[]{:S(2)}) collective-permute-start(bf16[512,384]{1,0:T(8,128)(2,1)} %get-tuple-element.79.refs_0_), channel_id=1, source_target_pairs={{0,1},{1,0},{2,3},{3,2},{4,5},{5,4},{6,7},{7,6},{8,9},{9,8},{10,11... | collective-permute-start | bytes 1179656 | tf_op jit(solution)/shard_map/ppermute | solution.py:120
  155.1 1.5 collective-permute-start.14
